TPU v7x, 256 devices: a whole 4x4x8 slice. The times are simulated.
256 devices in a mesh: ens: 4 (over y), space: 64 (over z, x, core).
Axes of the slice: x: 4, y: 4, z: 8, core: 2. Of those that a mesh axis runs over, the one named last changes fastest.
Arguments:
- hidden: bfloat16 [16, 32768, 1024], P('ens', 'space'), as said below
- decoder_weight: float32 [99, 1024], replicated, may hold values from -0.1875 to 0.1875
- decoder_intercept: float32 [99], replicated, may hold values from -3 to 3
- analysis_truth: float32 [99, 32768], P(None, 'space'), may hold values from -12 to 12
- var_weight: float32 [99], replicated, may hold values from 1 to 10
- lat_weight: float32 [640], replicated, as said below
- area_bin: int32 [32768], P('space'), may hold values from 0 to 639
- train_step: int32 [1], replicated, may hold values from 500 to 999
Outputs:
- grad_hidden: bfloat16 [16, 32768, 1024], P('ens', 'space')
- new_weight: float32 [99, 1024], replicated
- new_bias: float32 [99], replicated
Inputs may be any that keep to these rules, and one draw needn't show every extreme that they name: `hidden`: decoder input features. `lat_weight`: positive area weights.
All inputs are finite; a program needn't handle non-finite values.
Results may differ from a plain program's by a relative error of at most 0.0015.
The roundings to bfloat16 on the way count: a program that leaves them out, or rounds other values in their place, can miss the bound.
Values may be sent and summed in bfloat16 or wider, within the bound.
No kernel may reach another device: no remote copies, remote signals or barrier semaphores. Data moves between devices by JAX's collectives and lax.ppermute only.
A program may use at most 64 MiB of HBM per device.

v0:
```python
import jax
import jax.numpy as jnp
from jax import lax
from jax.sharding import PartitionSpec as P

WARMUP = 1000


smooth_sq = 0.0025
fair_alpha = 0.95


def smoothed_signum(difference):
    return difference / jnp.sqrt(difference * difference + smooth_sq)


def on_device(
    hidden,
    decoder_weight,
    decoder_intercept,
    analysis_truth,
    var_weight,
    lat_weight,
    area_bin,
    train_step,
):
    members_local, points, features = hidden.shape
    groups = lax.axis_size("ens")
    spatial_count = lax.axis_size("space")
    ensemble_realizations = members_local * groups
    fair_eps = (1.0 - fair_alpha) / ensemble_realizations
    couple_normalizer = (1.0 - fair_eps) / (ensemble_realizations * (ensemble_realizations - 1))
    half_weight = decoder_weight.astype(jnp.bfloat16)
    decoded_prognosis = jnp.einsum(
        "zl,srl->szr", half_weight, hidden, preferred_element_type=jnp.float32
    )
    prognosis_misfit = decoded_prognosis + decoder_intercept[None, :, None] - analysis_truth[None]
    collected_rows = lax.all_to_all(
        prognosis_misfit, "ens", split_axis=2, concat_axis=0, tiled=True
    )
    couple_grand_figure = jnp.sum(
        smoothed_signum(collected_rows[:, None] - collected_rows[None, :]), axis=1
    )
    bracket_local = (
        smoothed_signum(collected_rows) / ensemble_realizations
        - couple_normalizer * couple_grand_figure
    ).astype(jnp.bfloat16)
    ensemble_rank_interval = lax.all_to_all(
        bracket_local, "ens", split_axis=0, concat_axis=2, tiled=True
    )
    nlat = lat_weight.shape[0]
    matches = area_bin[:, None] == jnp.arange(nlat, dtype=jnp.int32)[None, :]
    area_weight = jnp.sum(jnp.where(matches, lat_weight[None, :], 0.0), axis=1)
    weighted = (
        area_weight[None, None, :]
        * var_weight[None, :, None]
        * ensemble_rank_interval.astype(jnp.float32)
    ).astype(jnp.bfloat16)
    hidden_raw = jnp.einsum(
        "mvp,vd->mpd", weighted, half_weight, preferred_element_type=jnp.float32
    )
    weight_raw = jnp.einsum("mvp,mpd->vd", weighted, hidden, preferred_element_type=jnp.float32)
    bias_raw = jnp.sum(weighted.astype(jnp.float32), axis=(0, 2))
    area_local = jnp.sum(area_weight)
    replicas = points * spatial_count * groups
    param_count = decoder_weight.shape[0] * decoder_weight.shape[1] + decoder_weight.shape[0]
    warm_rate = (train_step[0] + 1).astype(jnp.float32) / WARMUP
    weight_sum, bias_sum, area_total = lax.psum(
        (weight_raw, bias_raw, area_local), ("ens", "space")
    )
    mean_area = area_total / replicas
    weight_grad = weight_sum / mean_area
    bias_grad = bias_sum / mean_area
    square_sum = jnp.sum(weight_grad * weight_grad) + jnp.sum(bias_grad * bias_grad)
    grad_rms = jnp.sqrt(square_sum / param_count + 1e-06)
    step_scale = warm_rate * jnp.minimum(1.0, 1.0 / grad_rms)
    new_weight = decoder_weight - step_scale * weight_grad
    grad_hidden = (hidden_raw / mean_area).astype(jnp.bfloat16)
    new_bias = decoder_intercept - step_scale * bias_grad
    return (grad_hidden, new_weight, new_bias)


def solution(mesh):
    return jax.shard_map(
        on_device,
        mesh=mesh,
        in_specs=(P("ens", "space", None), P(), P(), P(None, "space"), P(), P(), P("space"), P()),
        out_specs=(P("ens", "space", None), P(), P()),
        check_vma=False,
    )
```

profile of v0, /device:TPU:1, one launch (start us, length us, event | category | flops | bytes accessed | tf_op | source)
XLA Modules:
  0.0 320.4 jit_solution(18085609913307315437)
XLA Ops:
  7.2 0.0 copy-start.4
  7.2 0.0 copy-start.2
  7.2 3.8 %fusion.4 = f32[4,99,512]{2,1,0:T(8,128)S(1)} fusion(bf16[4,512,1024]{2,1,0:T(8,128)(2,1)} %param.8, f32[99,512]{1,0:T(8,128)} %param.11, f32[99]{0:T(128)} %param.10, f32[99,1024]{1,0:T(8,128)} %param.9), kind=kOutput, calls=%fused_computation.10 | convolution fusion | flops 415742976 | bytes 5613964 | tf_op jit(solution)/shard_map/zl,srl->szr/dot_general | solution.py:34
  11.0 1.3 copy.32
  12.3 5.0 %all-to-all-start = ((f32[4,99,512]{1,0,2:T(4,128)}), f32[4,99,512]{1,0,2:T(4,128)S(1)}, u32[]{:S(2)}, u32[]{:S(2)}) async-start(f32[4,99,512]{1,0,2:T(4,128)} %copy.32), calls=%async_computation | async-start | bytes 2097152 | tf_op jit(solution)/shard_map/all_to_all | solution.py:38
  17.3 0.0 copy-done.4
  17.3 0.0 copy-done.2
  17.3 1.1 select_reduce_fusion.1
  18.4 12.3 %all-to-all-done = f32[4,99,512]{1,0,2:T(4,128)S(1)} async-done(((f32[4,99,512]{1,0,2:T(4,128)}), f32[4,99,512]{1,0,2:T(4,128)S(1)}, u32[]{:S(2)}, u32[]{:S(2)}) %all-to-all-start) | async-done | bytes 811040 | tf_op jit(solution)/shard_map/all_to_all | solution.py:38
  30.7 0.6 copy.34
  31.4 0.3 copy.35
  31.6 0.0 copy-start.3
  31.6 9.1 %fusion.2 = f32[16,99,128]{2,1,0:T(8,128)S(1)} fusion(f32[16,99,128]{2,0,1:T(8,128)S(1)} %bitcast.29, f32[16,99,128]{2,1,0:T(8,128)S(1)} %copy.35), kind=kLoop, calls=%fused_computation.4 | loop fusion | flops 16017408 | bytes 2433024 | tf_op jit(solution)/shard_map/reduce_sum | solution.py:41
  40.7 0.3 fusion.6
  41.0 0.9 copy.37
  41.8 3.5 %all-to-all-start.1 = ((bf16[16,99,128]{2,1,0:T(8,128)(2,1)}), bf16[16,99,128]{2,1,0:T(8,128)(2,1)S(1)}, u32[]{:S(2)}, u32[]{:S(2)}) async-start(bf16[16,99,128]{2,1,0:T(8,128)(2,1)} %copy.37), calls=%async_computation.1 | async-start | bytes 851968 | tf_op jit(solution)/shard_map/all_to_all | solution.py:48
  45.3 0.0 all-reduce.3.cloned.1.call-start
  45.4 0.0 copy-done.3
  45.4 0.2 broadcast_multiply_fusion.1
  46.2 0.1 broadcast_multiply_fusion
  46.3 5.4 %all-to-all-done.1 = bf16[16,99,128]{2,1,0:T(8,128)(2,1)S(1)} async-done(((bf16[16,99,128]{2,1,0:T(8,128)(2,1)}), bf16[16,99,128]{2,1,0:T(8,128)(2,1)S(1)}, u32[]{:S(2)}, u32[]{:S(2)}) %all-to-all-start.1) | async-done | bytes 405536 | tf_op jit(solution)/shard_map/all_to_all | solution.py:48
  51.7 0.1 copy.42
  51.7 0.2 copy.39
  52.0 0.3 reshape.67
  52.3 0.0 copy-start
  52.3 3.8 %convolution_bitcast_fusion = f32[99,1024]{1,0:T(8,128)} fusion(bf16[4,512,1024]{2,1,0:T(8,128)(2,1)} %param.8, f32[4,99,512]{2,1,0:T(8,128)S(1)} %reshape.67, f32[99,512]{1,0:T(8,128)S(1)} %broadcast_multiply_fusion), kind=kOutput, calls=%fused_computation.12 | convolution fusion | flops 415641600 | bytes 5613568 | tf_op jit(solution)/shard_map/mvp,mpd->vd/dot_general | solution.py:62
  56.1 0.0 all-reduce.3.cloned.1.call-update
  56.1 0.8 convert_reduce_fusion
  56.9 82.1 %all-reduce = (f32[]{:T(128)}, f32[99]{0:T(128)S(1)}) all-reduce(f32[]{:T(128)} %get-tuple-element.4, f32[99]{0:T(128)S(1)} %convert_reduce_fusion), channel_id=1, replica_groups=mesh['ens'=4,'space'=64] {'ens','space'}, use_global_device_ids=true, to_apply=%region_3.4 | all-reduce | flops 100 | bytes 800 | tf_op jit(solution)/shard_map/psum | solution.py:68
  139.7 0.0 copy-done
  139.7 0.0 copy-start.1
  139.7 3.3 %divide_convert_fusion = bf16[4,512,1024]{2,1,0:T(8,128)(2,1)} fusion(f32[]{:T(128)S(6)} %div.46, f32[99,1024]{1,0:T(8,128)S(1)} %copy-done, f32[4,99,512]{2,1,0:T(8,128)S(1)} %reshape.67, f32[99,512]{1,0:T(8,128)S(1)} %broadcast_multiply_fusion), kind=kOutput, calls=%fused_computation.5 | convolution fusion | flops 419937280 | bytes 5613572 | tf_op jit(solution)/shard_map/mvp,vd->mpd/dot_general | solution.py:59
  143.1 0.6 multiply_reduce_fusion.1
  143.7 164.6 %all-reduce.3.cloned.1.call-done = f32[99,1024]{1,0:T(8,128)} async-done(((f32[99,1024]{1,0:T(8,128)}), f32[99,1024]{1,0:T(8,128)}) %all-reduce.3.cloned.1.call-update) | async-done | bytes 405520 | tf_op jit(solution)/shard_map/psum | solution.py:68
  308.3 1.7 multiply_reduce_fusion
  311.2 0.0 copy-done.1
  311.3 0.5 multiply_subtract_fusion.1
  311.8 1.8 multiply_subtract_fusion
Async XLA Ops:
  7.2 10.1 %copy-start.4 = (s32[512]{0:T(512)S(1)}, s32[512]{0:T(512)}, u32[]{:S(2)}) copy-start(s32[512]{0:T(512)} %param.14) | copy-start | bytes 6148
  7.2 10.1 %copy-start.2 = (f32[640]{0:T(1024)S(1)}, f32[640]{0:T(1024)}, u32[]{:S(2)}) copy-start(f32[640]{0:T(1024)} %param.13) | copy-start | bytes 7684
  12.3 18.4 %all-to-all-start = ((f32[4,99,512]{1,0,2:T(4,128)}), f32[4,99,512]{1,0,2:T(4,128)S(1)}, u32[]{:S(2)}, u32[]{:S(2)}) async-start(f32[4,99,512]{1,0,2:T(4,128)} %copy.32), calls=%async_computation | async-start | bytes 2097152 | tf_op jit(solution)/shard_map/all_to_all | solution.py:38
  31.6 13.7 %copy-start.3 = (f32[99]{0:T(128)S(1)}, f32[99]{0:T(128)}, u32[]{:S(2)}) copy-start(f32[99]{0:T(128)} %param.12) | copy-start | bytes 1192
  41.8 9.8 %all-to-all-start.1 = ((bf16[16,99,128]{2,1,0:T(8,128)(2,1)}), bf16[16,99,128]{2,1,0:T(8,128)(2,1)S(1)}, u32[]{:S(2)}, u32[]{:S(2)}) async-start(bf16[16,99,128]{2,1,0:T(8,128)(2,1)} %copy.37), calls=%async_computation.1 | async-start | bytes 851968 | tf_op jit(solution)/shard_map/all_to_all | solution.py:48
  45.3 262.9 %all-reduce.3.cloned.1.call-start = ((), (), s32[]{:S(2)}) async-start(), calls=%async_computation.2 | async-start | bytes 851968 | tf_op jit(solution)/shard_map/psum | solution.py:68
  52.3 87.4 %copy-start = (f32[99,1024]{1,0:T(8,128)S(1)}, f32[99,1024]{1,0:T(8,128)}, u32[]{:S(2)}) copy-start(f32[99,1024]{1,0:T(8,128)} %param.9) | copy-start | bytes 1216516
  139.7 171.5 %copy-start.1 = (f32[99]{0:T(128)S(1)}, f32[99]{0:T(128)}, u32[]{:S(2)}) copy-start(f32[99]{0:T(128)} %param.10) | copy-start | bytes 1192
Sparse Core Ops, SparseCore 0:
  56.2 251.9 all-reduce.2
where the time goes:
time: 321 us; the launch traced here: 320 us
  waiting for transfers between devices  182 us (57%)
  blocking collectives  82.1 us (26%)
  between operations  16.8 us (5%)
  other arithmetic  16.1 us (5%)
  matrix products  10.9 us (3%)
  starting transfers between devices  8.52 us (3%)
  local copies, waits for them, and re-layouts  3.71 us (1%)
    psum x1, waiting for transfers between devices, on_device(): lax.psum((weight_raw, bias_raw, area_local), ('ens', 'space'))  165 us
    psum x1, blocking collectives, on_device(): lax.psum((weight_raw, bias_raw, area_local), ('ens', 'space'))  82.1 us
    all_to_all x1, waiting for transfers between devices, on_device(): lax.all_to_all(prognosis_misfit, 'ens', split_axis=2, concat_axis=0, tile...  12.3 us
    reduce_sum x1, other arithmetic, on_device(): jnp.sum(smoothed_signum(collected_rows[:, None] - collected_rows[None, :]...  9.05 us
  transfers between devices with their start and end apart: 3, of which 3 were waited for; matrix products, arithmetic and copies ran while one was open for 2% of the time, Pallas kernels for 0%

commit v1 on v0

v1 whole, which is shorter than its diff:
```python
import jax
import jax.numpy as jnp
from jax import lax
from jax.experimental import pallas as pl
from jax.experimental.pallas import tpu as pltpu
from jax.sharding import Mesh, PartitionSpec as P

WARMUP = 1000
smooth_sq = 0.0025
fair_alpha = 0.95

GROUPS = 4
PIECES = 16
PIECE_ROWS = 7
BIG = 48 * 1024 * 1024
VMEM = pl.BlockSpec(memory_space=pltpu.VMEM)
SMEM = pl.BlockSpec(memory_space=pltpu.SMEM)
ANY = pl.BlockSpec(memory_space=pl.ANY)
F32 = jnp.float32
BF16 = jnp.bfloat16


def soft(d):
    return d * lax.rsqrt(d * d + smooth_sq)


def as_column(row, rows):
    n = row.shape[1]
    pick = lax.broadcasted_iota(jnp.int32, (rows, n), 0) == lax.broadcasted_iota(jnp.int32, (rows, n), 1)
    return jnp.sum(jnp.where(pick, jnp.broadcast_to(row, (rows, n)), 0.0), axis=1, keepdims=True)


def padded(value, rows):
    return jnp.concatenate([value, jnp.zeros((rows - value.shape[0], value.shape[1]), value.dtype)], axis=0)


def forward_kernel(where, hidden, weight, intercept, truth, *rest):
    outs, (held, half, sem) = rest[:GROUPS], rest[GROUPS:]
    rows = half.shape[0]
    chunk = outs[0].shape[2]
    copies = []
    for k in range(GROUPS):
        start = pl.multiple_of(lax.rem(where[0] + k, GROUPS) * chunk, chunk)
        copies.append(pltpu.make_async_copy(hidden.at[:, pl.ds(start, chunk), :], held.at[k], sem.at[k]))
    for k in (2, 1, 3, 0):
        copies[k].start()
    half[...] = padded(weight[...], rows).astype(BF16)
    bias = as_column(intercept[...], rows)
    for k in (2, 1, 3, 0):
        start = pl.multiple_of(lax.rem(where[0] + k, GROUPS) * chunk, chunk)
        shift = bias - padded(truth[:, pl.ds(start, chunk)], rows)
        copies[k].wait()
        for m in range(outs[0].shape[0]):
            outs[k][m] = lax.dot_general(
                half[...], held[k, m], (((1,), (1,)), ((), ())), preferred_element_type=F32
            ) + shift


def pairs_kernel(members, *rest):
    ins, outs, (scratch,) = rest[:GROUPS], rest[GROUPS : 2 * GROUPS], rest[2 * GROUPS :]
    local = ins[0].shape[0]
    eps = (1.0 - fair_alpha) / members
    normalizer = (1.0 - eps) / (members * (members - 1))

    def tile(t, carry):
        at = pl.ds(pl.multiple_of(t * 8, 8), 8)
        r = [ins[j // local][j % local, at, :] for j in range(members)]
        total = [None] * members
        for i in range(members):
            for j in range(i + 1, members):
                s = soft(r[i] - r[j])
                total[i] = s if total[i] is None else total[i] + s
                total[j] = -s if total[j] is None else total[j] - s
        for j in range(members):
            scratch[j, at, :] = soft(r[j]) * (1.0 / members) - normalizer * total[j]
        return carry

    lax.fori_loop(0, ins[0].shape[1] // 8, tile, 0)
    for j in range(members):
        outs[j // local][j % local] = scratch[j].astype(BF16)


def area_kernel(lat, area_bin, out):
    cells, width = lat.shape
    points = area_bin.shape[1]
    bins = jnp.broadcast_to(area_bin[...], (width, points))
    level = lax.broadcasted_iota(jnp.int32, (width, points), 0)
    total = jnp.zeros((width, points), F32)
    for q in range(cells):
        column = as_column(lat[q : q + 1, :], width)
        total = total + jnp.where(bins == level + q * width, column, 0.0)
    out[...] = jnp.sum(total, axis=0, keepdims=True)


def backward_kernel(where, hidden, b0, b1, b2, b3, var, area, weighted, mine, other, held, acc, sem):
    brackets = (b0, b1, b2, b3)
    local, rows, chunk = b0.shape
    depth = local * chunk
    features = held.shape[-1]
    copies = []
    for k in range(GROUPS):
        start = pl.multiple_of(lax.rem(where[0] + k, GROUPS) * chunk, chunk)
        copies.append(pltpu.make_async_copy(hidden.at[:, pl.ds(start, chunk), :], held.at[k], sem.at[k]))
        copies[-1].start()
    scale = as_column(var[...], rows)
    ones = jnp.ones((8, depth), BF16)
    bias = jnp.zeros((8, rows), F32)
    for k in range(GROUPS):
        start = pl.multiple_of(lax.rem(where[0] + k, GROUPS) * chunk, chunk)
        point_scale = area[:, pl.ds(start, chunk)] * scale
        w = jnp.concatenate(
            [(point_scale * brackets[k][m].astype(F32)).astype(BF16) for m in range(local)], axis=1
        )
        weighted[k] = w
        bias = bias + lax.dot_general(ones, w, (((1,), (1,)), ((), ())), preferred_element_type=F32)
        copies[k].wait()
        product = jnp.dot(w, held[k].reshape(depth, features), preferred_element_type=F32)
        if k == 0:
            acc[0:rows, :] = product
        else:
            acc[0:rows, :] += product
    acc[rows:, :] = jnp.zeros((acc.shape[0] - rows, features), F32)
    half = features // 2
    total = jnp.sum(area[...], axis=1, keepdims=True)
    extra = jnp.concatenate(
        [
            bias[0:1],
            jnp.zeros((1, 128 - rows), F32),
            jnp.broadcast_to(total, (1, 128)),
            jnp.zeros((1, half - 256), F32),
        ],
        axis=1,
    )
    extra = jnp.broadcast_to(extra, (8, half))
    last = lax.broadcasted_iota(jnp.int32, (8, half), 0) == PIECE_ROWS
    for side, out in ((where[1], mine), (1 - where[1], other)):
        lanes = pl.ds(pl.multiple_of(side * half, half), half)
        for r in range(PIECES):
            out[r] = jnp.where(last, extra, acc[PIECE_ROWS * r : PIECE_ROWS * r + 8, lanes])


def grad_hidden_kernel(where, weighted, weight, piece, out, half, *, replicas):
    rows = half.shape[0]

    @pl.when(pl.program_id(0) == 0)
    def _():
        half[...] = padded(weight[...], rows).astype(BF16)

    inverse = 1.0 / (piece[PIECE_ROWS : PIECE_ROWS + 1, 128:129] * (1.0 / replicas))
    chunk = out.shape[1]
    for m in range(out.shape[0]):
        product = lax.dot_general(
            weighted[0, :, m * chunk : (m + 1) * chunk], half[...], (((0,), (0,)), ((), ())), preferred_element_type=F32
        )
        out[m] = (product * inverse).astype(BF16)


def update_kernel(where, step, own, partner, weight, intercept, new_weight, new_bias, *, replicas):
    variables, features = weight.shape
    half = features // 2
    first = where[1] == 0
    mean_area = own[0, PIECE_ROWS : PIECE_ROWS + 1, 128:129] * (1.0 / replicas)
    bias_grad = own[0, PIECE_ROWS : PIECE_ROWS + 1, 0:variables] / mean_area
    keep = lax.broadcasted_iota(jnp.int32, (8, half), 0) < PIECE_ROWS
    squares = jnp.zeros((8, half), F32)
    for r in range(PIECES):
        for side in (own, partner):
            g = jnp.where(keep, side[r] / mean_area, 0.0)
            squares = squares + g * g
    total = jnp.sum(jnp.sum(squares, axis=0, keepdims=True), axis=1, keepdims=True)
    total = total + jnp.sum(bias_grad * bias_grad, axis=1, keepdims=True)
    count = variables * features + variables
    rms = jnp.sqrt(total / count + 1e-06)
    warm = (step[0] + 1).astype(F32) / WARMUP
    scale = warm * jnp.minimum(1.0, 1.0 / rms)
    for r in range(PIECES):
        low = PIECE_ROWS * r
        n = min(PIECE_ROWS, variables - low)
        if n <= 0:
            continue
        a, b = own[r, 0:n, :], partner[r, 0:n, :]
        left, right = jnp.where(first, a, b), jnp.where(first, b, a)
        new_weight[low : low + n, :half] = weight[low : low + n, :half] - scale * (left / mean_area)
        new_weight[low : low + n, half:] = weight[low : low + n, half:] - scale * (right / mean_area)
    new_bias[...] = intercept[...] - scale * bias_grad


def on_device(hidden, decoder_weight, decoder_intercept, analysis_truth, var_weight, lat_weight, area_bin, train_step):
    local, points, features = hidden.shape
    variables = decoder_weight.shape[0]
    rows = -(-variables // 8) * 8
    chunk = points // GROUPS
    members = local * GROUPS
    replicas = points * lax.axis_size("z") * lax.axis_size("x") * lax.axis_size("c") * GROUPS
    me, core = lax.axis_index("y"), lax.axis_index("c")
    where = jnp.stack([me, core]).astype(jnp.int32)
    big = pltpu.CompilerParams(vmem_limit_bytes=BIG)
    intercept_row = decoder_intercept.reshape(1, variables)
    var_row = var_weight.reshape(1, variables)

    def turn(value, k):
        return value if k % GROUPS == 0 else lax.ppermute(value, "y", [(i, (i + k) % GROUPS) for i in range(GROUPS)])

    with jax.named_scope("forward"):
        residual = pl.pallas_call(
            forward_kernel,
            out_shape=[jax.ShapeDtypeStruct((local, rows, chunk), F32)] * GROUPS,
            in_specs=[SMEM, ANY, VMEM, VMEM, VMEM],
            out_specs=[VMEM] * GROUPS,
            scratch_shapes=[
                pltpu.VMEM((GROUPS, local, chunk, features), BF16),
                pltpu.VMEM((rows, features), BF16),
                pltpu.SemaphoreType.DMA((GROUPS,)),
            ],
            compiler_params=big,
            name="forward",
        )(where, hidden, decoder_weight, intercept_row, analysis_truth)
    with jax.named_scope("residual_exchange"):
        gathered = [residual[0], None, None, None]
        for k in (2, 1, 3):
            gathered[k] = turn(residual[k], k)
    with jax.named_scope("area"):
        area = pl.pallas_call(
            area_kernel,
            out_shape=jax.ShapeDtypeStruct((1, points), F32),
            in_specs=[VMEM, VMEM],
            out_specs=VMEM,
            name="area",
        )(lat_weight.reshape(-1, 128), area_bin.reshape(1, points))
    with jax.named_scope("pairs"):
        brackets = pl.pallas_call(
            lambda *refs: pairs_kernel(members, *refs),
            out_shape=[jax.ShapeDtypeStruct((local, rows, chunk), BF16)] * GROUPS,
            in_specs=[VMEM] * GROUPS,
            out_specs=[VMEM] * GROUPS,
            scratch_shapes=[pltpu.VMEM((members, rows, chunk), F32)],
            compiler_params=big,
            name="pairs",
        )(*gathered)
    with jax.named_scope("bracket_exchange"):
        returned = [brackets[0], None, None, None]
        for k in (2, 1, 3):
            returned[k] = turn(brackets[k], -k)
    with jax.named_scope("backward"):
        half = features // 2
        weighted, mine, other = pl.pallas_call(
            backward_kernel,
            out_shape=[
                jax.ShapeDtypeStruct((GROUPS, rows, local * chunk), BF16),
                jax.ShapeDtypeStruct((PIECES, 8, half), F32),
                jax.ShapeDtypeStruct((PIECES, 8, half), F32),
            ],
            in_specs=[SMEM, ANY] + [VMEM] * 6,
            out_specs=[VMEM] * 3,
            scratch_shapes=[
                pltpu.VMEM((GROUPS, local, chunk, features), BF16),
                pltpu.VMEM((PIECES * 8, features), F32),
                pltpu.SemaphoreType.DMA((GROUPS,)),
            ],
            compiler_params=big,
            name="backward",
        )(where, hidden, *returned, var_row, area)
    with jax.named_scope("gradient_sum"):
        swap = [(0, 1), (1, 0)]
        part = mine + lax.ppermute(other, "c", swap)
        part = lax.all_to_all(part, ("y", "x"), 0, 0, tiled=True)
        depth = lax.axis_size("z")
        part = jnp.broadcast_to(jnp.sum(part, axis=0), (depth, 8, half))
        part = lax.all_to_all(part, "z", 0, 0, tiled=True)
        piece = jnp.sum(part, axis=0)
        own = lax.all_to_all(jnp.broadcast_to(piece, (PIECES, 8, half)), ("y", "x"), 0, 0, tiled=True)
        partner = lax.ppermute(own, "c", swap)
    with jax.named_scope("grad_hidden"):
        grad_hidden = pl.pallas_call(
            lambda *refs: grad_hidden_kernel(*refs, replicas=replicas),
            out_shape=jax.ShapeDtypeStruct(hidden.shape, BF16),
            grid_spec=pltpu.PrefetchScalarGridSpec(
                num_scalar_prefetch=1,
                grid=(GROUPS,),
                in_specs=[
                    pl.BlockSpec((1, rows, local * chunk), lambda g, s: (g, 0, 0)),
                    pl.BlockSpec((variables, features), lambda g, s: (0, 0)),
                    pl.BlockSpec((8, half), lambda g, s: (0, 0)),
                ],
                out_specs=pl.BlockSpec((local, chunk, features), lambda g, s: (0, lax.rem(s[0] + g, GROUPS), 0)),
                scratch_shapes=[pltpu.VMEM((rows, features), BF16)],
            ),
            compiler_params=big,
            cost_estimate=pl.CostEstimate(
                flops=2 * rows * local * points * features, bytes_accessed=2 * hidden.size, transcendentals=0
            ),
            name="grad_hidden",
        )(where, weighted, decoder_weight, piece)
    with jax.named_scope("update"):
        new_weight, new_bias = pl.pallas_call(
            lambda *refs: update_kernel(*refs, replicas=replicas),
            out_shape=[
                jax.ShapeDtypeStruct((variables, features), F32),
                jax.ShapeDtypeStruct((1, variables), F32),
            ],
            in_specs=[SMEM, SMEM] + [VMEM] * 4,
            out_specs=[VMEM] * 2,
            compiler_params=big,
            name="update",
        )(where, train_step, own, partner, decoder_weight, intercept_row)
    return grad_hidden, new_weight, new_bias.reshape(variables)


def solution(mesh):
    fine = Mesh(mesh.devices.reshape(GROUPS, 8, 4, 2), ("y", "z", "x", "c"))
    space = ("z", "x", "c")
    return jax.shard_map(
        on_device,
        mesh=fine,
        in_specs=(P("y", space, None), P(), P(), P(None, space), P(), P(), P(space), P()),
        out_specs=(P("y", space, None), P(), P()),
        check_vma=False,
    )
```

time: 321 us -> 92 us (0.29)
  waiting for transfers between devices: 182 us -> 12.9 us
  blocking collectives: 82.1 us -> 39.1 us
  other arithmetic: 16.1 us -> 0.15 us
  between operations: 16.8 us -> 1.38 us
  Pallas kernels: 0 us -> 13.9 us
  matrix products: 10.9 us -> 0 us
  starting transfers between devices: 8.52 us -> 16.5 us
  local copies, waits for them, and re-layouts: 3.71 us -> 7.7 us
    psum x1 -> x0, waiting for transfers between devices: 165 us -> none  [on_device(): lax.psum((weight_raw, bias_raw, area_local), ('ens', 'space'))]
    psum x1 -> x0, blocking collectives: 82.1 us -> none  [on_device(): lax.psum((weight_raw, bias_raw, area_local), ('ens', 'space'))]
    all_to_all x0 -> x3, blocking collectives: none -> 39.1 us  [the longest x1 15.9 us: on_device(): part = lax.all_to_all(part, 'z', 0, 0, tiled=True)]
    all_to_all x2 -> x0, waiting for transfers between devices: 17.7 us -> none  [the longest x1 12.3 us: on_device(): lax.all_to_all(prognosis_misfit, 'ens', split_axis=2, concat_axis=0, tile...]
    ppermute x0 -> x8, starting transfers between devices: none -> 16.5 us  [the longest x6 9.03 us: turn(): lax.ppermute(value, 'y', [(i, (i + k) % GROUPS) for i in range(GROUPS)])]
    pallas_call x0 -> x6, Pallas kernels: none -> 13.9 us  [the longest x1 3.94 us: on_device(): pl.pallas_call(lambda *refs: grad_hidden_kernel(*refs, replicas=replicas)...]
    reduce_sum x5 -> x2, other arithmetic: 13.3 us -> 0.03 us  [the longest x1 0.02 us: on_device(): part = jnp.broadcast_to(jnp.sum(part, axis=0), (depth, 8, half))]
    ppermute x0 -> x8, waiting for transfers between devices: none -> 12.9 us  [the longest x6 11.7 us: turn(): lax.ppermute(value, 'y', [(i, (i + k) % GROUPS) for i in range(GROUPS)])]
  transfers between devices with their start and end apart: 3 -> 8, of which waited for: 3 -> 5; matrix products, arithmetic and copies ran while one was open for 2% -> 0% of each run, Pallas kernels for 0% -> 6%
where the time goes in v1:
time: 92 us; the launch traced here: 91.6 us
  blocking collectives  39.1 us (42%)
  starting transfers between devices  16.5 us (18%)
  Pallas kernels  13.9 us (15%)
  waiting for transfers between devices  12.9 us (14%)
  local copies, waits for them, and re-layouts  7.7 us (8%)
  between operations  1.38 us (2%)
    all_to_all x1, blocking collectives, on_device(): part = lax.all_to_all(part, 'z', 0, 0, tiled=True)  15.9 us
    all_to_all x1, blocking collectives, on_device(): part = lax.all_to_all(part, ('y', 'x'), 0, 0, tiled=True)  13.1 us
    ppermute x6, waiting for transfers between devices, turn(): lax.ppermute(value, 'y', [(i, (i + k) % GROUPS) for i in range(GROUPS)])  11.7 us
    all_to_all x1, blocking collectives, on_device(): lax.all_to_all(jnp.broadcast_to(piece, (PIECES, 8, half)), ('y', 'x'), 0,...  10.1 us
    ppermute x6, starting transfers between devices, turn(): lax.ppermute(value, 'y', [(i, (i + k) % GROUPS) for i in range(GROUPS)])  9.03 us
    unnamed x18, local copies, waits for them, and re-layouts  7.67 us
    ppermute x1, starting transfers between devices, on_device(): partner = lax.ppermute(own, 'c', swap)  4.4 us
    pallas_call x1, Pallas kernels, on_device(): pl.pallas_call(lambda *refs: grad_hidden_kernel(*refs, replicas=replicas)...  3.94 us
  transfers between devices with their start and end apart: 8, of which 5 were waited for; matrix products, arithmetic and copies ran while one was open for 0% of the time, Pallas kernels for 6%

profile of v1, /device:TPU:1, one launch (start us, length us, event | category | flops | bytes accessed | tf_op | source)
XLA Modules:
  0.0 91.6 jit_solution(16378110513210180973)
XLA Ops:
  0.6 0.0 copy-start.8
  0.6 0.1 pad_add_fusion.where.refs_0_
  0.7 0.0 copy-start
  0.7 2.2 %copy-done = bf16[4,512,1024]{2,1,0:T(8,128)(2,1)S(1)} copy-done((bf16[4,512,1024]{2,1,0:T(8,128)(2,1)S(1)}, bf16[4,512,1024]{2,1,0:T(8,128)(2,1)}, u32[]{:S(2)}) %copy-start) | copy-done | bytes 4194328
  2.9 0.0 copy-start.2
  2.9 1.0 %copy-done.2 = f32[99,1024]{1,0:T(8,128)S(1)} copy-done((f32[99,1024]{1,0:T(8,128)S(1)}, f32[99,1024]{1,0:T(8,128)}, u32[]{:S(2)}) %copy-start.2) | copy-done | bytes 405528
  3.9 0.0 copy-start.4
  3.9 0.9 %copy-done.4 = f32[99,512]{1,0:T(8,128)S(1)} copy-done((f32[99,512]{1,0:T(8,128)S(1)}, f32[99,512]{1,0:T(8,128)}, u32[]{:S(2)}) %copy-start.4) | copy-done | bytes 202776
  4.9 0.0 copy-start.6
  4.9 0.7 copy-done.6
  5.5 2.7 %forward.1 = (f32[4,104,128]{2,1,0:T(8,128)S(1)}, f32[4,104,128]{2,1,0:T(8,128)S(1)}, f32[4,104,128]{2,1,0:T(8,128)S(1)}, f32[4,104,128]{2,1,0:T(8,128)S(1)}) custom-call(s32[2]{0:T(128)S(1)} %pad_add_fusion.where.refs_0_, bf16[4,512,1024]{2,1,0:T(8,128)(2,1)S(1)} %copy-done, f32[99,1024]{1,0:T(8,128)S(1)} %copy-done.2, f32[1,99]{1,0:T(1,128)S(1)} %bitcast.7, ...), custom_call_target="tpu_custom_call" | custom-call | tf_op jit(solution)/shard_map/forward/forward/pallas_call | solution.py:205
  8.2 2.2 %collective-permute-start = (f32[4,104,128]{2,1,0:T(8,128)S(1)}, f32[4,104,128]{2,1,0:T(8,128)S(1)}, u32[]{:S(2)}, u32[]{:S(2)}) collective-permute-start(f32[4,104,128]{2,1,0:T(8,128)S(1)} %get-tuple-element.17), channel_id=1, source_target_pairs={{0,64},{64,128},{128,192},{192,0},{1,65},{65,129},{129,193},{193,1... | collective-permute-start | bytes 638984 | tf_op jit(solution)/shard_map/residual_exchange/ppermute | solution.py:202
  10.4 2.6 %collective-permute-start.1 = (f32[4,104,128]{2,1,0:T(8,128)S(1)}, f32[4,104,128]{2,1,0:T(8,128)S(1)}, u32[]{:S(2)}, u32[]{:S(2)}) collective-permute-start(f32[4,104,128]{2,1,0:T(8,128)S(1)} %get-tuple-element.18), channel_id=1, source_target_pairs={{0,128},{64,192},{128,0},{192,64},{1,129},{65,193},{129,1},{193,65... | collective-permute-start | bytes 638984 | tf_op jit(solution)/shard_map/residual_exchange/ppermute | solution.py:202
  13.0 1.1 %collective-permute-start.2 = (f32[4,104,128]{2,1,0:T(8,128)S(1)}, f32[4,104,128]{2,1,0:T(8,128)S(1)}, u32[]{:S(2)}, u32[]{:S(2)}) collective-permute-start(f32[4,104,128]{2,1,0:T(8,128)S(1)} %get-tuple-element.19), channel_id=1, source_target_pairs={{0,192},{64,0},{128,64},{192,128},{1,193},{65,1},{129,65},{193,129... | collective-permute-start | bytes 638984 | tf_op jit(solution)/shard_map/residual_exchange/ppermute | solution.py:202
  14.1 1.0 %collective-permute-done.refs_1_ = f32[4,104,128]{2,1,0:T(8,128)S(1)} collective-permute-done((f32[4,104,128]{2,1,0:T(8,128)S(1)}, f32[4,104,128]{2,1,0:T(8,128)S(1)}, u32[]{:S(2)}, u32[]{:S(2)}) %collective-permute-start) | collective-permute-done | bytes 213024 | tf_op jit(solution)/shard_map/residual_exchange/ppermute | solution.py:202
  15.1 7.2 %collective-permute-done.1.refs_2_ = f32[4,104,128]{2,1,0:T(8,128)S(1)} collective-permute-done((f32[4,104,128]{2,1,0:T(8,128)S(1)}, f32[4,104,128]{2,1,0:T(8,128)S(1)}, u32[]{:S(2)}, u32[]{:S(2)}) %collective-permute-start.1) | collective-permute-done | bytes 213024 | tf_op jit(solution)/shard_map/residual_exchange/ppermute | solution.py:202
  22.2 0.0 collective-permute-done.2.refs_3_
  22.2 0.0 copy-start.3
  22.2 1.8 %pairs.1 = (bf16[4,104,128]{2,1,0:T(8,128)(2,1)S(1)}, bf16[4,104,128]{2,1,0:T(8,128)(2,1)S(1)}, bf16[4,104,128]{2,1,0:T(8,128)(2,1)S(1)}, bf16[4,104,128]{2,1,0:T(8,128)(2,1)S(1)}) custom-call(f32[4,104,128]{2,1,0:T(8,128)S(1)} %get-tuple-element.16.refs_0_, f32[4,104,128]{2,1,0:T(8,128)S(1)} %collective-permute-done.refs_1_, ...), custom_call_target="tpu_custom_call" | custom-call | tf_op jit(solution)/shard_map/pairs/pairs/pallas_call | solution.py:231
  24.0 2.0 %collective-permute-start.3 = (bf16[4,104,128]{2,1,0:T(8,128)(2,1)S(1)}, bf16[4,104,128]{2,1,0:T(8,128)(2,1)S(1)}, u32[]{:S(2)}, u32[]{:S(2)}) collective-permute-start(bf16[4,104,128]{2,1,0:T(8,128)(2,1)S(1)} %get-tuple-element.21), channel_id=1, source_target_pairs={{0,192},{64,0},{128,64},{192,128},{1,193},{65,1},{129,65},{193,129... | collective-permute-start | bytes 319496 | tf_op jit(solution)/shard_map/bracket_exchange/ppermute | solution.py:202
  26.0 1.1 %collective-permute-start.4 = (bf16[4,104,128]{2,1,0:T(8,128)(2,1)S(1)}, bf16[4,104,128]{2,1,0:T(8,128)(2,1)S(1)}, u32[]{:S(2)}, u32[]{:S(2)}) collective-permute-start(bf16[4,104,128]{2,1,0:T(8,128)(2,1)S(1)} %get-tuple-element.22), channel_id=1, source_target_pairs={{0,128},{64,192},{128,0},{192,64},{1,129},{65,193},{129,1},{193,65... | collective-permute-start | bytes 319496 | tf_op jit(solution)/shard_map/bracket_exchange/ppermute | solution.py:202
  27.2 0.0 collective-permute-start.5
  27.2 1.5 %area.1 = f32[1,512]{1,0:T(1,128)} custom-call(f32[5,128]{1,0:T(8,128)} %bitcast.10, s32[1,512]{1,0:T(1,128)} %bitcast.11), custom_call_target="tpu_custom_call" | custom-call | tf_op jit(solution)/shard_map/area/area/pallas_call | solution.py:223
  28.7 0.0 collective-permute-done.3.b1
  28.7 2.5 %collective-permute-done.4.b2 = bf16[4,104,128]{2,1,0:T(8,128)(2,1)S(1)} collective-permute-done((bf16[4,104,128]{2,1,0:T(8,128)(2,1)S(1)}, bf16[4,104,128]{2,1,0:T(8,128)(2,1)S(1)}, u32[]{:S(2)}, u32[]{:S(2)}) %collective-permute-start.4) | collective-permute-done | bytes 106528 | tf_op jit(solution)/shard_map/bracket_exchange/ppermute | solution.py:202
  31.1 1.1 %collective-permute-done.5.b3 = bf16[4,104,128]{2,1,0:T(8,128)(2,1)S(1)} collective-permute-done((bf16[4,104,128]{2,1,0:T(8,128)(2,1)S(1)}, bf16[4,104,128]{2,1,0:T(8,128)(2,1)S(1)}, u32[]{:S(2)}, u32[]{:S(2)}) %collective-permute-start.5) | collective-permute-done | bytes 106528 | tf_op jit(solution)/shard_map/bracket_exchange/ppermute | solution.py:202
  32.2 0.0 copy-done.8
  32.2 0.0 copy-start.1
  32.2 2.2 %copy-done.1 = bf16[4,512,1024]{2,1,0:T(8,128)(2,1)S(1)} copy-done((bf16[4,512,1024]{2,1,0:T(8,128)(2,1)S(1)}, bf16[4,512,1024]{2,1,0:T(8,128)(2,1)}, u32[]{:S(2)}) %copy-start.1) | copy-done | bytes 4194328
  34.4 0.0 copy-start.5
  34.4 0.7 copy-done.5
  35.1 2.3 %backward.1 = (bf16[4,104,512]{2,1,0:T(8,128)(2,1)S(1)}, f32[16,8,512]{2,1,0:T(8,128)S(1)}, f32[16,8,512]{2,1,0:T(8,128)S(1)}) custom-call(s32[2]{0:T(128)S(1)} %pad_add_fusion.where.refs_0_, bf16[4,512,1024]{2,1,0:T(8,128)(2,1)S(1)} %copy-done.1, bf16[4,104,128]{2,1,0:T(8,128)(2,1)S(1)} %get-tuple-element.20.b0, ...), custom_call_target="tpu_custom_call" | custom-call | tf_op jit(solution)/shard_map/backward/backward/pallas_call | solution.py:246
  37.5 0.0 copy-start.7
  37.5 3.1 %collective-permute-start.6 = (f32[16,8,512]{2,1,0:T(8,128)S(1)}, f32[16,8,512]{2,1,0:T(8,128)S(1)}, u32[]{:S(2)}, u32[]{:S(2)}) collective-permute-start(f32[16,8,512]{2,1,0:T(8,128)S(1)} %get-tuple-element.26), channel_id=1, source_target_pairs={{0,1},{1,0},{2,3},{3,2},{4,5},{5,4},{6,7},{7,6},{8,9},{9,8},{10,11... | collective-permute-start | bytes 786440 | tf_op jit(solution)/shard_map/gradient_sum/ppermute | solution.py:265
  40.5 1.2 %collective-permute-done.6 = f32[16,8,512]{2,1,0:T(8,128)S(1)} collective-permute-done((f32[16,8,512]{2,1,0:T(8,128)S(1)}, f32[16,8,512]{2,1,0:T(8,128)S(1)}, u32[]{:S(2)}, u32[]{:S(2)}) %collective-permute-start.6) | collective-permute-done | bytes 262176 | tf_op jit(solution)/shard_map/gradient_sum/ppermute | solution.py:265
  41.7 13.1 %all_to_all.15 = f32[16,8,512]{2,1,0:T(8,128)S(1)} all-to-all(f32[16,8,512]{2,1,0:T(8,128)S(1)} %add.3), channel_id=1, replica_groups=mesh['y'=4,'z'=8,'x'=4,'c'=2] {'y','x'}, dimensions={0} | all-to-all | bytes 524288 | tf_op jit(solution)/shard_map/gradient_sum/all_to_all | solution.py:266
  54.9 15.9 %all_to_all.16 = f32[8,8,512]{2,1,0:T(8,128)S(1)} all-to-all(f32[8,8,512]{2,1,0:T(8,128)S(1)} %broadcast_in_dim.6), channel_id=1, replica_groups=mesh['y'=4,'z'=8,'x'=4,'c'=2] {'z'}, dimensions={0} | all-to-all | bytes 262144 | tf_op jit(solution)/shard_map/gradient_sum/all_to_all | solution.py:269
  70.8 10.1 %all_to_all.17.refs_2_ = f32[16,8,512]{2,1,0:T(8,128)S(1)} all-to-all(f32[16,8,512]{2,1,0:T(8,128)S(1)} %broadcast_in_dim.7), channel_id=1, replica_groups=mesh['y'=4,'z'=8,'x'=4,'c'=2] {'y','x'}, dimensions={0} | all-to-all | bytes 524288 | tf_op jit(solution)/shard_map/gradient_sum/all_to_all | solution.py:271
  80.9 4.4 %collective-permute-start.7 = (f32[16,8,512]{2,1,0:T(8,128)S(1)}, f32[16,8,512]{2,1,0:T(8,128)S(1)}, u32[]{:S(2)}, u32[]{:S(2)}) collective-permute-start(f32[16,8,512]{2,1,0:T(8,128)S(1)} %all_to_all.17.refs_2_), channel_id=1, source_target_pairs={{0,1},{1,0},{2,3},{3,2},{4,5},{5,4},{6,7},{7,6},{8,9},{9,8},{10,11... | collective-permute-start | bytes 786440 | tf_op jit(solution)/shard_map/gradient_sum/ppermute | solution.py:272
  86.0 0.0 copy-done.3
  86.0 3.9 %grad_hidden.1 = bf16[4,512,1024]{2,1,0:T(8,128)(2,1)} custom-call(s32[2]{0:T(128)S(1)} %pad_add_fusion.where.refs_0_, bf16[4,104,512]{2,1,0:T(8,128)(2,1)S(1)} %get-tuple-element.24.refs_1_, f32[99,1024]{1,0:T(8,128)S(1)} %copy-done.3, f32[8,512]{1,0:T(8,128)S(1)} %reduce_sum.19.refs_3_), custom_call_target="tpu_custom_call" | custom-call | flops 436207616 | bytes 4194304 | tf_op jit(solution)/shard_map/grad_hidden/grad_hidden/pallas_call | solution.py:274
  89.9 0.0 collective-permute-done.7.refs_3_
  90.0 0.0 copy-done.7
  90.0 1.6 %update.1 = (f32[99,1024]{1,0:T(8,128)}, f32[1,99]{1,0:T(1,128)}) custom-call(s32[2]{0:T(128)S(1)} %pad_add_fusion.where.refs_0_, s32[1]{0:T(128)S(6)} %copy.11.refs_1_, f32[16,8,512]{2,1,0:T(8,128)S(1)} %all_to_all.17.refs_2_, f32[16,8,512]{2,1,0:T(8,128)S(1)} %collective-permute-done.7.refs_3_, f32[99,1024]{1,0:T(8,128)S(1)} %copy-done.3, f32[1,99]{1,0:T(1,128)S(1)} %bitcast.8), custom_call_target="tpu_custom_call" | custom-call | tf_op jit(solution)/shard_map/update/update/pallas_call | solution.py:295
  (5 shorter events, 0.1 us)
Async XLA Ops:
  0.6 31.6 %copy-start.8 = (f32[99]{0:T(128)S(1)}, f32[99]{0:T(128)}, u32[]{:S(2)}) copy-start(f32[99]{0:T(128)} %param.12) | copy-start | bytes 1192
  0.7 2.2 %copy-start = (bf16[4,512,1024]{2,1,0:T(8,128)(2,1)S(1)}, bf16[4,512,1024]{2,1,0:T(8,128)(2,1)}, u32[]{:S(2)}) copy-start(bf16[4,512,1024]{2,1,0:T(8,128)(2,1)} %hidden.3) | copy-start | bytes 12582916
  2.9 1.0 %copy-start.2 = (f32[99,1024]{1,0:T(8,128)S(1)}, f32[99,1024]{1,0:T(8,128)}, u32[]{:S(2)}) copy-start(f32[99,1024]{1,0:T(8,128)} %refs_4_.1) | copy-start | bytes 1216516
  3.9 0.9 %copy-start.4 = (f32[99,512]{1,0:T(8,128)S(1)}, f32[99,512]{1,0:T(8,128)}, u32[]{:S(2)}) copy-start(f32[99,512]{1,0:T(8,128)} %truth.1) | copy-start | bytes 608260
  4.9 0.7 copy-start.6
  8.2 6.9 %collective-permute-start = (f32[4,104,128]{2,1,0:T(8,128)S(1)}, f32[4,104,128]{2,1,0:T(8,128)S(1)}, u32[]{:S(2)}, u32[]{:S(2)}) collective-permute-start(f32[4,104,128]{2,1,0:T(8,128)S(1)} %get-tuple-element.17), channel_id=1, source_target_pairs={{0,64},{64,128},{128,192},{192,0},{1,65},{65,129},{129,193},{193,1... | collective-permute-start | bytes 638984 | tf_op jit(solution)/shard_map/residual_exchange/ppermute | solution.py:202
  10.4 11.8 %collective-permute-start.1 = (f32[4,104,128]{2,1,0:T(8,128)S(1)}, f32[4,104,128]{2,1,0:T(8,128)S(1)}, u32[]{:S(2)}, u32[]{:S(2)}) collective-permute-start(f32[4,104,128]{2,1,0:T(8,128)S(1)} %get-tuple-element.18), channel_id=1, source_target_pairs={{0,128},{64,192},{128,0},{192,64},{1,129},{65,193},{129,1},{193,65... | collective-permute-start | bytes 638984 | tf_op jit(solution)/shard_map/residual_exchange/ppermute | solution.py:202
  13.0 9.2 %collective-permute-start.2 = (f32[4,104,128]{2,1,0:T(8,128)S(1)}, f32[4,104,128]{2,1,0:T(8,128)S(1)}, u32[]{:S(2)}, u32[]{:S(2)}) collective-permute-start(f32[4,104,128]{2,1,0:T(8,128)S(1)} %get-tuple-element.19), channel_id=1, source_target_pairs={{0,192},{64,0},{128,64},{192,128},{1,193},{65,1},{129,65},{193,129... | collective-permute-start | bytes 638984 | tf_op jit(solution)/shard_map/residual_exchange/ppermute | solution.py:202
  22.2 63.8 %copy-start.3 = (f32[99,1024]{1,0:T(8,128)S(1)}, f32[99,1024]{1,0:T(8,128)}, u32[]{:S(2)}) copy-start(f32[99,1024]{1,0:T(8,128)} %refs_4_.1) | copy-start | bytes 1216516
  24.0 4.7 %collective-permute-start.3 = (bf16[4,104,128]{2,1,0:T(8,128)(2,1)S(1)}, bf16[4,104,128]{2,1,0:T(8,128)(2,1)S(1)}, u32[]{:S(2)}, u32[]{:S(2)}) collective-permute-start(bf16[4,104,128]{2,1,0:T(8,128)(2,1)S(1)} %get-tuple-element.21), channel_id=1, source_target_pairs={{0,192},{64,0},{128,64},{192,128},{1,193},{65,1},{129,65},{193,129... | collective-permute-start | bytes 319496 | tf_op jit(solution)/shard_map/bracket_exchange/ppermute | solution.py:202
  26.0 5.1 %collective-permute-start.4 = (bf16[4,104,128]{2,1,0:T(8,128)(2,1)S(1)}, bf16[4,104,128]{2,1,0:T(8,128)(2,1)S(1)}, u32[]{:S(2)}, u32[]{:S(2)}) collective-permute-start(bf16[4,104,128]{2,1,0:T(8,128)(2,1)S(1)} %get-tuple-element.22), channel_id=1, source_target_pairs={{0,128},{64,192},{128,0},{192,64},{1,129},{65,193},{129,1},{193,65... | collective-permute-start | bytes 319496 | tf_op jit(solution)/shard_map/bracket_exchange/ppermute | solution.py:202
  27.2 5.1 %collective-permute-start.5 = (bf16[4,104,128]{2,1,0:T(8,128)(2,1)S(1)}, bf16[4,104,128]{2,1,0:T(8,128)(2,1)S(1)}, u32[]{:S(2)}, u32[]{:S(2)}) collective-permute-start(bf16[4,104,128]{2,1,0:T(8,128)(2,1)S(1)} %get-tuple-element.23), channel_id=1, source_target_pairs={{0,64},{64,128},{128,192},{192,0},{1,65},{65,129},{129,193},{193,1... | collective-permute-start | bytes 319496 | tf_op jit(solution)/shard_map/bracket_exchange/ppermute | solution.py:202
  32.2 2.2 %copy-start.1 = (bf16[4,512,1024]{2,1,0:T(8,128)(2,1)S(1)}, bf16[4,512,1024]{2,1,0:T(8,128)(2,1)}, u32[]{:S(2)}) copy-start(bf16[4,512,1024]{2,1,0:T(8,128)(2,1)} %hidden.3) | copy-start | bytes 12582916
  34.4 0.7 copy-start.5
  37.5 52.5 %copy-start.7 = (f32[99]{0:T(128)S(1)}, f32[99]{0:T(128)}, u32[]{:S(2)}) copy-start(f32[99]{0:T(128)} %param.10) | copy-start | bytes 1192
  37.5 4.2 %collective-permute-start.6 = (f32[16,8,512]{2,1,0:T(8,128)S(1)}, f32[16,8,512]{2,1,0:T(8,128)S(1)}, u32[]{:S(2)}, u32[]{:S(2)}) collective-permute-start(f32[16,8,512]{2,1,0:T(8,128)S(1)} %get-tuple-element.26), channel_id=1, source_target_pairs={{0,1},{1,0},{2,3},{3,2},{4,5},{5,4},{6,7},{7,6},{8,9},{9,8},{10,11... | collective-permute-start | bytes 786440 | tf_op jit(solution)/shard_map/gradient_sum/ppermute | solution.py:265
  80.9 9.0 %collective-permute-start.7 = (f32[16,8,512]{2,1,0:T(8,128)S(1)}, f32[16,8,512]{2,1,0:T(8,128)S(1)}, u32[]{:S(2)}, u32[]{:S(2)}) collective-permute-start(f32[16,8,512]{2,1,0:T(8,128)S(1)} %all_to_all.17.refs_2_), channel_id=1, source_target_pairs={{0,1},{1,0},{2,3},{3,2},{4,5},{5,4},{6,7},{7,6},{8,9},{9,8},{10,11... | collective-permute-start | bytes 786440 | tf_op jit(solution)/shard_map/gradient_sum/ppermute | solution.py:272

commit v2 on v1

--- a/solution.py
+++ b/solution.py
@@ -12,10 +12,11 @@
 GROUPS = 4
 PIECES = 16
 PIECE_ROWS = 7
-BIG = 48 * 1024 * 1024
+MIB = 1024 * 1024
+ORDER = (2, 1, 3, 0)
 VMEM = pl.BlockSpec(memory_space=pltpu.VMEM)
 SMEM = pl.BlockSpec(memory_space=pltpu.SMEM)
-ANY = pl.BlockSpec(memory_space=pl.ANY)
+HBM = pl.BlockSpec(memory_space=pltpu.HBM)
 F32 = jnp.float32
 BF16 = jnp.bfloat16
 
@@ -34,37 +35,37 @@
     return jnp.concatenate([value, jnp.zeros((rows - value.shape[0], value.shape[1]), value.dtype)], axis=0)
 
 
-def forward_kernel(where, hidden, weight, intercept, truth, *rest):
-    outs, (held, half, sem) = rest[:GROUPS], rest[GROUPS:]
+def forward_kernel(where, hidden, weight, *rest):
+    outs, half = rest[:GROUPS], rest[GROUPS]
+    held, w, sem, weight_sem = rest[GROUPS + 1 :]
     rows = half.shape[0]
     chunk = outs[0].shape[2]
-    copies = []
-    for k in range(GROUPS):
+    fetch = pltpu.make_async_copy(weight, w, weight_sem)
+    fetch.start()
+    copies = {}
+    for k in ORDER:
         start = pl.multiple_of(lax.rem(where[0] + k, GROUPS) * chunk, chunk)
-        copies.append(pltpu.make_async_copy(hidden.at[:, pl.ds(start, chunk), :], held.at[k], sem.at[k]))
-    for k in (2, 1, 3, 0):
+        copies[k] = pltpu.make_async_copy(hidden.at[:, pl.ds(start, chunk), :], held.at[k], sem.at[k])
         copies[k].start()
-    half[...] = padded(weight[...], rows).astype(BF16)
-    bias = as_column(intercept[...], rows)
-    for k in (2, 1, 3, 0):
-        start = pl.multiple_of(lax.rem(where[0] + k, GROUPS) * chunk, chunk)
-        shift = bias - padded(truth[:, pl.ds(start, chunk)], rows)
+    fetch.wait()
+    half[...] = padded(w[...], rows).astype(BF16)
+    for k in ORDER:
         copies[k].wait()
         for m in range(outs[0].shape[0]):
             outs[k][m] = lax.dot_general(
                 half[...], held[k, m], (((1,), (1,)), ((), ())), preferred_element_type=F32
-            ) + shift
+            )
 
 
 def pairs_kernel(members, *rest):
-    ins, outs, (scratch,) = rest[:GROUPS], rest[GROUPS : 2 * GROUPS], rest[2 * GROUPS :]
+    ins, shift, outs, scratch = rest[:GROUPS], rest[GROUPS], rest[GROUPS + 1 : 2 * GROUPS + 1], rest[2 * GROUPS + 1]
     local = ins[0].shape[0]
     eps = (1.0 - fair_alpha) / members
     normalizer = (1.0 - eps) / (members * (members - 1))
 
     def tile(t, carry):
         at = pl.ds(pl.multiple_of(t * 8, 8), 8)
-        r = [ins[j // local][j % local, at, :] for j in range(members)]
+        r = [ins[j // local][j % local, at, :] + shift[at, :] for j in range(members)]
         total = [None] * members
         for i in range(members):
             for j in range(i + 1, members):
@@ -80,7 +81,13 @@
         outs[j // local][j % local] = scratch[j].astype(BF16)
 
 
-def area_kernel(lat, area_bin, out):
+def area_kernel(where, hidden, lat, area_bin, intercept, truth, out, shift, held, sem):
+    chunk = held.shape[2]
+    copies = []
+    for k in range(GROUPS):
+        start = pl.multiple_of(lax.rem(where[0] + k, GROUPS) * chunk, chunk)
+        copies.append(pltpu.make_async_copy(hidden.at[:, pl.ds(start, chunk), :], held.at[k], sem.at[k]))
+        copies[k].start()
     cells, width = lat.shape
     points = area_bin.shape[1]
     bins = jnp.broadcast_to(area_bin[...], (width, points))
@@ -90,18 +97,17 @@
         column = as_column(lat[q : q + 1, :], width)
         total = total + jnp.where(bins == level + q * width, column, 0.0)
     out[...] = jnp.sum(total, axis=0, keepdims=True)
-
-
-def backward_kernel(where, hidden, b0, b1, b2, b3, var, area, weighted, mine, other, held, acc, sem):
+    mine = pl.multiple_of(where[0] * chunk, chunk)
+    shift[...] = as_column(intercept[...], shift.shape[0]) - padded(truth[:, pl.ds(mine, chunk)], shift.shape[0])
+    for copy in copies:
+        copy.wait()
+
+
+def backward_kernel(where, held, b0, b1, b2, b3, var, area, weighted, mine, other, acc):
     brackets = (b0, b1, b2, b3)
     local, rows, chunk = b0.shape
     depth = local * chunk
     features = held.shape[-1]
-    copies = []
-    for k in range(GROUPS):
-        start = pl.multiple_of(lax.rem(where[0] + k, GROUPS) * chunk, chunk)
-        copies.append(pltpu.make_async_copy(hidden.at[:, pl.ds(start, chunk), :], held.at[k], sem.at[k]))
-        copies[-1].start()
     scale = as_column(var[...], rows)
     ones = jnp.ones((8, depth), BF16)
     bias = jnp.zeros((8, rows), F32)
@@ -113,7 +119,6 @@
         )
         weighted[k] = w
         bias = bias + lax.dot_general(ones, w, (((1,), (1,)), ((), ())), preferred_element_type=F32)
-        copies[k].wait()
         product = jnp.dot(w, held[k].reshape(depth, features), preferred_element_type=F32)
         if k == 0:
             acc[0:rows, :] = product
@@ -139,13 +144,7 @@
             out[r] = jnp.where(last, extra, acc[PIECE_ROWS * r : PIECE_ROWS * r + 8, lanes])
 
 
-def grad_hidden_kernel(where, weighted, weight, piece, out, half, *, replicas):
-    rows = half.shape[0]
-
-    @pl.when(pl.program_id(0) == 0)
-    def _():
-        half[...] = padded(weight[...], rows).astype(BF16)
-
+def grad_hidden_kernel(where, weighted, half, piece, out, *, replicas):
     inverse = 1.0 / (piece[PIECE_ROWS : PIECE_ROWS + 1, 128:129] * (1.0 / replicas))
     chunk = out.shape[1]
     for m in range(out.shape[0]):
@@ -160,12 +159,13 @@
     half = features // 2
     first = where[1] == 0
     mean_area = own[0, PIECE_ROWS : PIECE_ROWS + 1, 128:129] * (1.0 / replicas)
-    bias_grad = own[0, PIECE_ROWS : PIECE_ROWS + 1, 0:variables] / mean_area
+    inverse = 1.0 / mean_area
+    bias_grad = own[0, PIECE_ROWS : PIECE_ROWS + 1, 0:variables] * inverse
     keep = lax.broadcasted_iota(jnp.int32, (8, half), 0) < PIECE_ROWS
     squares = jnp.zeros((8, half), F32)
     for r in range(PIECES):
         for side in (own, partner):
-            g = jnp.where(keep, side[r] / mean_area, 0.0)
+            g = jnp.where(keep, side[r] * inverse, 0.0)
             squares = squares + g * g
     total = jnp.sum(jnp.sum(squares, axis=0, keepdims=True), axis=1, keepdims=True)
     total = total + jnp.sum(bias_grad * bias_grad, axis=1, keepdims=True)
@@ -180,8 +180,8 @@
             continue
         a, b = own[r, 0:n, :], partner[r, 0:n, :]
         left, right = jnp.where(first, a, b), jnp.where(first, b, a)
-        new_weight[low : low + n, :half] = weight[low : low + n, :half] - scale * (left / mean_area)
-        new_weight[low : low + n, half:] = weight[low : low + n, half:] - scale * (right / mean_area)
+        new_weight[low : low + n, :half] = weight[low : low + n, :half] - scale * (left * inverse)
+        new_weight[low : low + n, half:] = weight[low : low + n, half:] - scale * (right * inverse)
     new_bias[...] = intercept[...] - scale * bias_grad
 
 
@@ -194,7 +194,10 @@
     replicas = points * lax.axis_size("z") * lax.axis_size("x") * lax.axis_size("c") * GROUPS
     me, core = lax.axis_index("y"), lax.axis_index("c")
     where = jnp.stack([me, core]).astype(jnp.int32)
-    big = pltpu.CompilerParams(vmem_limit_bytes=BIG)
+
+    def grant(mib):
+        return pltpu.CompilerParams(vmem_limit_bytes=mib * MIB)
+
     intercept_row = decoder_intercept.reshape(1, variables)
     var_row = var_weight.reshape(1, variables)
 
@@ -202,44 +205,53 @@
         return value if k % GROUPS == 0 else lax.ppermute(value, "y", [(i, (i + k) % GROUPS) for i in range(GROUPS)])
 
     with jax.named_scope("forward"):
-        residual = pl.pallas_call(
+        *residual, half_weight = pl.pallas_call(
             forward_kernel,
-            out_shape=[jax.ShapeDtypeStruct((local, rows, chunk), F32)] * GROUPS,
-            in_specs=[SMEM, ANY, VMEM, VMEM, VMEM],
-            out_specs=[VMEM] * GROUPS,
+            out_shape=[jax.ShapeDtypeStruct((local, rows, chunk), F32)] * GROUPS
+            + [jax.ShapeDtypeStruct((rows, features), BF16)],
+            in_specs=[SMEM, HBM, HBM],
+            out_specs=[VMEM] * (GROUPS + 1),
             scratch_shapes=[
                 pltpu.VMEM((GROUPS, local, chunk, features), BF16),
-                pltpu.VMEM((rows, features), BF16),
+                pltpu.VMEM((variables, features), F32),
                 pltpu.SemaphoreType.DMA((GROUPS,)),
+                pltpu.SemaphoreType.DMA(()),
             ],
-            compiler_params=big,
+            compiler_params=grant(53),
             name="forward",
-        )(where, hidden, decoder_weight, intercept_row, analysis_truth)
+        )(where, hidden, decoder_weight)
     with jax.named_scope("residual_exchange"):
         gathered = [residual[0], None, None, None]
-        for k in (2, 1, 3):
+        for k in ORDER[:-1]:
             gathered[k] = turn(residual[k], k)
     with jax.named_scope("area"):
-        area = pl.pallas_call(
+        area, shift, held = pl.pallas_call(
             area_kernel,
-            out_shape=jax.ShapeDtypeStruct((1, points), F32),
-            in_specs=[VMEM, VMEM],
-            out_specs=VMEM,
+            out_shape=[
+                jax.ShapeDtypeStruct((1, points), F32),
+                jax.ShapeDtypeStruct((rows, chunk), F32),
+                jax.ShapeDtypeStruct((GROUPS, local, chunk, features), BF16),
+            ],
+            in_specs=[SMEM, HBM] + [VMEM] * 4,
+            out_specs=[VMEM] * 3,
+            scratch_shapes=[pltpu.SemaphoreType.DMA((GROUPS,))],
+            compiler_params=grant(46),
             name="area",
-        )(lat_weight.reshape(-1, 128), area_bin.reshape(1, points))
+        )(where, hidden, lat_weight.reshape(-1, 128), area_bin.reshape(1, points), intercept_row, analysis_truth)
+        gathered, area, shift, held = lax.optimization_barrier((gathered, area, shift, held))
     with jax.named_scope("pairs"):
         brackets = pl.pallas_call(
             lambda *refs: pairs_kernel(members, *refs),
             out_shape=[jax.ShapeDtypeStruct((local, rows, chunk), BF16)] * GROUPS,
-            in_specs=[VMEM] * GROUPS,
+            in_specs=[VMEM] * (GROUPS + 1),
             out_specs=[VMEM] * GROUPS,
             scratch_shapes=[pltpu.VMEM((members, rows, chunk), F32)],
-            compiler_params=big,
+            compiler_params=grant(6),
             name="pairs",
-        )(*gathered)
+        )(*gathered, shift)
     with jax.named_scope("bracket_exchange"):
         returned = [brackets[0], None, None, None]
-        for k in (2, 1, 3):
+        for k in ORDER[:-1]:
             returned[k] = turn(brackets[k], -k)
     with jax.named_scope("backward"):
         half = features // 2
@@ -250,16 +262,12 @@
                 jax.ShapeDtypeStruct((PIECES, 8, half), F32),
                 jax.ShapeDtypeStruct((PIECES, 8, half), F32),
             ],
-            in_specs=[SMEM, ANY] + [VMEM] * 6,
+            in_specs=[SMEM] + [VMEM] * 7,
             out_specs=[VMEM] * 3,
-            scratch_shapes=[
-                pltpu.VMEM((GROUPS, local, chunk, features), BF16),
-                pltpu.VMEM((PIECES * 8, features), F32),
-                pltpu.SemaphoreType.DMA((GROUPS,)),
-            ],
-            compiler_params=big,
+            scratch_shapes=[pltpu.VMEM((PIECES * 8, features), F32)],
+            compiler_params=grant(8),
             name="backward",
-        )(where, hidden, *returned, var_row, area)
+        )(where, held, *returned, var_row, area)
     with jax.named_scope("gradient_sum"):
         swap = [(0, 1), (1, 0)]
         part = mine + lax.ppermute(other, "c", swap)
@@ -269,7 +277,6 @@
         part = lax.all_to_all(part, "z", 0, 0, tiled=True)
         piece = jnp.sum(part, axis=0)
         own = lax.all_to_all(jnp.broadcast_to(piece, (PIECES, 8, half)), ("y", "x"), 0, 0, tiled=True)
-        partner = lax.ppermute(own, "c", swap)
     with jax.named_scope("grad_hidden"):
         grad_hidden = pl.pallas_call(
             lambda *refs: grad_hidden_kernel(*refs, replicas=replicas),
@@ -279,18 +286,20 @@
                 grid=(GROUPS,),
                 in_specs=[
                     pl.BlockSpec((1, rows, local * chunk), lambda g, s: (g, 0, 0)),
-                    pl.BlockSpec((variables, features), lambda g, s: (0, 0)),
+                    pl.BlockSpec((rows, features), lambda g, s: (0, 0)),
                     pl.BlockSpec((8, half), lambda g, s: (0, 0)),
                 ],
                 out_specs=pl.BlockSpec((local, chunk, features), lambda g, s: (0, lax.rem(s[0] + g, GROUPS), 0)),
-                scratch_shapes=[pltpu.VMEM((rows, features), BF16)],
             ),
-            compiler_params=big,
+            compiler_params=grant(12),
             cost_estimate=pl.CostEstimate(
                 flops=2 * rows * local * points * features, bytes_accessed=2 * hidden.size, transcendentals=0
             ),
             name="grad_hidden",
-        )(where, weighted, decoder_weight, piece)
+        )(where, weighted, half_weight, piece)
+        own, grad_hidden = lax.optimization_barrier((own, grad_hidden))
+    with jax.named_scope("last_swap"):
+        partner = lax.ppermute(own, "c", swap)
     with jax.named_scope("update"):
         new_weight, new_bias = pl.pallas_call(
             lambda *refs: update_kernel(*refs, replicas=replicas),
@@ -300,7 +309,7 @@
             ],
             in_specs=[SMEM, SMEM] + [VMEM] * 4,
             out_specs=[VMEM] * 2,
-            compiler_params=big,
+            compiler_params=grant(6),
             name="update",
         )(where, train_step, own, partner, decoder_weight, intercept_row)
     return grad_hidden, new_weight, new_bias.reshape(variables)

time: 92 us -> 82.9 us (0.901)
  blocking collectives: 39.1 us -> 28.9 us
  local copies, waits for them, and re-layouts: 7.7 us -> 0.77 us
  starting transfers between devices: 16.5 us -> 19.7 us
  waiting for transfers between devices: 12.9 us -> 15.7 us
  Pallas kernels: 13.9 us -> 15.9 us
    all_to_all x1 -> x0, blocking collectives: 10.1 us -> none  [on_device(): lax.all_to_all(jnp.broadcast_to(piece, (PIECES, 8, half)), ('y', 'x'), 0,...]
    unnamed x18 -> x14, local copies, waits for them, and re-layouts: 7.67 us -> 0.03 us
    all_to_all x0 -> x1, waiting for transfers between devices: none -> 3.58 us  [on_device(): lax.all_to_all(jnp.broadcast_to(piece, (PIECES, 8, half)), ('y', 'x'), 0,...]
    all_to_all x0 -> x1, starting transfers between devices: none -> 3.53 us  [on_device(): lax.all_to_all(jnp.broadcast_to(piece, (PIECES, 8, half)), ('y', 'x'), 0,...]
    pallas_call x1, Pallas kernels: 2.69 us -> 4.23 us  [on_device(): pl.pallas_call(forward_kernel, out_shape=[jax.ShapeDtypeStruct((local, ro...]
    ppermute x6, waiting for transfers between devices: 11.7 us -> 10.4 us  [turn(): lax.ppermute(value, 'y', [(i, (i + k) % GROUPS) for i in range(GROUPS)])]
    pallas_call x1, Pallas kernels: 1.52 us -> 2.77 us  [on_device(): pl.pallas_call(area_kernel, out_shape=[jax.ShapeDtypeStruct((1, points),...]
  transfers between devices with their start and end apart: 8 -> 9, of which waited for: 5 -> 7; matrix products, arithmetic and copies ran while one was open for 0% -> 0% of each run, Pallas kernels for 6% -> 8%
where the time goes in v2:
time: 82.9 us; the launch traced here: 82.6 us
  blocking collectives  28.9 us (35%)
  starting transfers between devices  19.7 us (24%)
  Pallas kernels  15.9 us (19%)
  waiting for transfers between devices  15.7 us (19%)
  between operations  1.41 us (2%)
    all_to_all x1, blocking collectives, on_device(): part = lax.all_to_all(part, 'z', 0, 0, tiled=True)  15.9 us
    all_to_all x1, blocking collectives, on_device(): part = lax.all_to_all(part, ('y', 'x'), 0, 0, tiled=True)  13 us
    ppermute x6, waiting for transfers between devices, turn(): lax.ppermute(value, 'y', [(i, (i + k) % GROUPS) for i in range(GROUPS)])  10.4 us
    ppermute x6, starting transfers between devices, turn(): lax.ppermute(value, 'y', [(i, (i + k) % GROUPS) for i in range(GROUPS)])  9.03 us
    pallas_call x1, Pallas kernels, on_device(): pl.pallas_call(forward_kernel, out_shape=[jax.ShapeDtypeStruct((local, ro...  4.23 us
    ppermute x1, starting transfers between devices, on_device(): partner = lax.ppermute(own, 'c', swap)  4.1 us
    pallas_call x1, Pallas kernels, on_device(): pl.pallas_call(lambda *refs: grad_hidden_kernel(*refs, replicas=replicas)...  3.92 us
    all_to_all x1, waiting for transfers between devices, on_device(): lax.all_to_all(jnp.broadcast_to(piece, (PIECES, 8, half)), ('y', 'x'), 0,...  3.58 us
  transfers between devices with their start and end apart: 9, of which 7 were waited for; matrix products, arithmetic and copies ran while one was open for 0% of the time, Pallas kernels for 8%

profile of v2, /device:TPU:1, one launch (start us, length us, event | category | flops | bytes accessed | tf_op | source)
XLA Modules:
  0.0 82.6 jit_solution(11282568717420214559)
XLA Ops:
  0.6 0.0 copy-start.5
  0.6 0.0 copy-start.3
  0.7 0.0 copy-start.4
  0.7 0.0 copy-start.2
  0.7 0.1 pad_add_fusion.where.refs_0_
  0.8 0.0 copy-start.6
  0.8 4.2 %forward.1 = (f32[4,104,128]{2,1,0:T(8,128)S(1)}, f32[4,104,128]{2,1,0:T(8,128)S(1)}, f32[4,104,128]{2,1,0:T(8,128)S(1)}, f32[4,104,128]{2,1,0:T(8,128)S(1)}, bf16[104,1024]{1,0:T(8,128)(2,1)}) custom-call(s32[2]{0:T(128)S(1)} %pad_add_fusion.where.refs_0_, bf16[4,512,1024]{2,1,0:T(8,128)(2,1)} %hidden.3, f32[99,1024]{1,0:T(8,128)} %refs_4_.1), custom_call_target="tpu_custom_call" | custom-call | tf_op jit(solution)/shard_map/forward/forward/pallas_call | solution.py:208
  5.0 2.2 %collective-permute-start = (f32[4,104,128]{2,1,0:T(8,128)S(1)}, f32[4,104,128]{2,1,0:T(8,128)S(1)}, u32[]{:S(2)}, u32[]{:S(2)}) collective-permute-start(f32[4,104,128]{2,1,0:T(8,128)S(1)} %get-tuple-element.30), channel_id=1, source_target_pairs={{0,64},{64,128},{128,192},{192,0},{1,65},{65,129},{129,193},{193,1... | collective-permute-start | bytes 638984 | tf_op jit(solution)/shard_map/residual_exchange/ppermute | solution.py:205
  7.2 2.6 %collective-permute-start.1 = (f32[4,104,128]{2,1,0:T(8,128)S(1)}, f32[4,104,128]{2,1,0:T(8,128)S(1)}, u32[]{:S(2)}, u32[]{:S(2)}) collective-permute-start(f32[4,104,128]{2,1,0:T(8,128)S(1)} %get-tuple-element.31), channel_id=1, source_target_pairs={{0,128},{64,192},{128,0},{192,64},{1,129},{65,193},{129,1},{193,65... | collective-permute-start | bytes 638984 | tf_op jit(solution)/shard_map/residual_exchange/ppermute | solution.py:205
  9.8 1.1 %collective-permute-start.2 = (f32[4,104,128]{2,1,0:T(8,128)S(1)}, f32[4,104,128]{2,1,0:T(8,128)S(1)}, u32[]{:S(2)}, u32[]{:S(2)}) collective-permute-start(f32[4,104,128]{2,1,0:T(8,128)S(1)} %get-tuple-element.32), channel_id=1, source_target_pairs={{0,192},{64,0},{128,64},{192,128},{1,193},{65,1},{129,65},{193,129... | collective-permute-start | bytes 638984 | tf_op jit(solution)/shard_map/residual_exchange/ppermute | solution.py:205
  10.9 0.0 copy-done.5
  10.9 0.0 copy-done.3
  10.9 0.0 copy-done.4
  10.9 0.0 copy-done.2
  10.9 2.8 %area.1 = (f32[1,512]{1,0:T(1,128)S(1)}, f32[104,128]{1,0:T(8,128)S(1)}, bf16[4,4,128,1024]{3,2,1,0:T(8,128)(2,1)S(1)}) custom-call(s32[2]{0:T(128)S(1)} %pad_add_fusion.where.refs_0_, bf16[4,512,1024]{2,1,0:T(8,128)(2,1)} %hidden.3, f32[5,128]{1,0:T(8,128)S(1)} %bitcast.7, s32[1,512]{1,0:T(1,128)S(1)} %bitcast.8, f32[1,99]{1,0:T(1,128)S(1)} %bitcast.9, ...), custom_call_target="tpu_custom_call" | custom-call | tf_op jit(solution)/shard_map/area/area/pallas_call | solution.py:228
  13.7 0.0 collective-permute-done.refs_1_
  13.7 5.3 %collective-permute-done.1.refs_2_ = f32[4,104,128]{2,1,0:T(8,128)S(1)} collective-permute-done((f32[4,104,128]{2,1,0:T(8,128)S(1)}, f32[4,104,128]{2,1,0:T(8,128)S(1)}, u32[]{:S(2)}, u32[]{:S(2)}) %collective-permute-start.1) | collective-permute-done | bytes 213024 | tf_op jit(solution)/shard_map/residual_exchange/ppermute | solution.py:205
  19.0 0.0 collective-permute-done.2.refs_3_
  19.0 0.0 copy-start.1
  19.1 1.8 %pairs.1 = (bf16[4,104,128]{2,1,0:T(8,128)(2,1)S(1)}, bf16[4,104,128]{2,1,0:T(8,128)(2,1)S(1)}, bf16[4,104,128]{2,1,0:T(8,128)(2,1)S(1)}, bf16[4,104,128]{2,1,0:T(8,128)(2,1)S(1)}) custom-call(f32[4,104,128]{2,1,0:T(8,128)S(1)} %get-tuple-element.37.refs_0_, f32[4,104,128]{2,1,0:T(8,128)S(1)} %collective-permute-done.refs_1_, ...), custom_call_target="tpu_custom_call" | custom-call | tf_op jit(solution)/shard_map/pairs/pairs/pallas_call | solution.py:243
  20.9 2.0 %collective-permute-start.3 = (bf16[4,104,128]{2,1,0:T(8,128)(2,1)S(1)}, bf16[4,104,128]{2,1,0:T(8,128)(2,1)S(1)}, u32[]{:S(2)}, u32[]{:S(2)}) collective-permute-start(bf16[4,104,128]{2,1,0:T(8,128)(2,1)S(1)} %get-tuple-element.43), channel_id=1, source_target_pairs={{0,192},{64,0},{128,64},{192,128},{1,193},{65,1},{129,65},{193,129... | collective-permute-start | bytes 319496 | tf_op jit(solution)/shard_map/bracket_exchange/ppermute | solution.py:205
  22.9 1.1 %collective-permute-start.4 = (bf16[4,104,128]{2,1,0:T(8,128)(2,1)S(1)}, bf16[4,104,128]{2,1,0:T(8,128)(2,1)S(1)}, u32[]{:S(2)}, u32[]{:S(2)}) collective-permute-start(bf16[4,104,128]{2,1,0:T(8,128)(2,1)S(1)} %get-tuple-element.44), channel_id=1, source_target_pairs={{0,128},{64,192},{128,0},{192,64},{1,129},{65,193},{129,1},{193,65... | collective-permute-start | bytes 319496 | tf_op jit(solution)/shard_map/bracket_exchange/ppermute | solution.py:205
  24.0 0.0 collective-permute-start.5
  24.0 1.4 %collective-permute-done.3.b1 = bf16[4,104,128]{2,1,0:T(8,128)(2,1)S(1)} collective-permute-done((bf16[4,104,128]{2,1,0:T(8,128)(2,1)S(1)}, bf16[4,104,128]{2,1,0:T(8,128)(2,1)S(1)}, u32[]{:S(2)}, u32[]{:S(2)}) %collective-permute-start.3) | collective-permute-done | bytes 106528 | tf_op jit(solution)/shard_map/bracket_exchange/ppermute | solution.py:205
  25.4 2.6 %collective-permute-done.4.b2 = bf16[4,104,128]{2,1,0:T(8,128)(2,1)S(1)} collective-permute-done((bf16[4,104,128]{2,1,0:T(8,128)(2,1)S(1)}, bf16[4,104,128]{2,1,0:T(8,128)(2,1)S(1)}, u32[]{:S(2)}, u32[]{:S(2)}) %collective-permute-start.4) | collective-permute-done | bytes 106528 | tf_op jit(solution)/shard_map/bracket_exchange/ppermute | solution.py:205
  28.0 1.1 %collective-permute-done.5.b3 = bf16[4,104,128]{2,1,0:T(8,128)(2,1)S(1)} collective-permute-done((bf16[4,104,128]{2,1,0:T(8,128)(2,1)S(1)}, bf16[4,104,128]{2,1,0:T(8,128)(2,1)S(1)}, u32[]{:S(2)}, u32[]{:S(2)}) %collective-permute-start.5) | collective-permute-done | bytes 106528 | tf_op jit(solution)/shard_map/bracket_exchange/ppermute | solution.py:205
  29.1 0.0 copy-done.6
  29.1 1.6 %backward.1 = (bf16[4,104,512]{2,1,0:T(8,128)(2,1)S(1)}, f32[16,8,512]{2,1,0:T(8,128)S(1)}, f32[16,8,512]{2,1,0:T(8,128)S(1)}) custom-call(s32[2]{0:T(128)S(1)} %pad_add_fusion.where.refs_0_, bf16[4,4,128,1024]{3,2,1,0:T(8,128)(2,1)S(1)} %get-tuple-element.36.held, bf16[4,104,128]{2,1,0:T(8,128)(2,1)S(1)} %get-tuple-element.42.b0, ...), custom_call_target="tpu_custom_call" | custom-call | tf_op jit(solution)/shard_map/backward/backward/pallas_call | solution.py:258
  30.7 0.0 copy-start
  30.7 3.1 %collective-permute-start.6 = (f32[16,8,512]{2,1,0:T(8,128)S(1)}, f32[16,8,512]{2,1,0:T(8,128)S(1)}, u32[]{:S(2)}, u32[]{:S(2)}) collective-permute-start(f32[16,8,512]{2,1,0:T(8,128)S(1)} %get-tuple-element.48), channel_id=1, source_target_pairs={{0,1},{1,0},{2,3},{3,2},{4,5},{5,4},{6,7},{7,6},{8,9},{9,8},{10,11... | collective-permute-start | bytes 786440 | tf_op jit(solution)/shard_map/gradient_sum/ppermute | solution.py:273
  33.7 1.2 %collective-permute-done.6 = f32[16,8,512]{2,1,0:T(8,128)S(1)} collective-permute-done((f32[16,8,512]{2,1,0:T(8,128)S(1)}, f32[16,8,512]{2,1,0:T(8,128)S(1)}, u32[]{:S(2)}, u32[]{:S(2)}) %collective-permute-start.6) | collective-permute-done | bytes 262176 | tf_op jit(solution)/shard_map/gradient_sum/ppermute | solution.py:273
  35.0 13.0 %all_to_all.15 = f32[16,8,512]{2,1,0:T(8,128)S(1)} all-to-all(f32[16,8,512]{2,1,0:T(8,128)S(1)} %add.3), channel_id=1, replica_groups=mesh['y'=4,'z'=8,'x'=4,'c'=2] {'y','x'}, dimensions={0} | all-to-all | bytes 524288 | tf_op jit(solution)/shard_map/gradient_sum/all_to_all | solution.py:274
  48.0 15.9 %all_to_all.16 = f32[8,8,512]{2,1,0:T(8,128)S(1)} all-to-all(f32[8,8,512]{2,1,0:T(8,128)S(1)} %broadcast_in_dim.6), channel_id=1, replica_groups=mesh['y'=4,'z'=8,'x'=4,'c'=2] {'z'}, dimensions={0} | all-to-all | bytes 262144 | tf_op jit(solution)/shard_map/gradient_sum/all_to_all | solution.py:277
  63.9 0.7 broadcast_in_dim.7
  64.6 3.5 %all-to-all-start.2 = ((f32[16,8,512]{2,1,0:T(8,128)}), f32[16,8,512]{2,1,0:T(8,128)S(1)}, u32[]{:S(2)}, u32[]{:S(2)}) async-start(f32[16,8,512]{2,1,0:T(8,128)} %broadcast_in_dim.7), calls=%async_computation.2 | async-start | bytes 524288 | tf_op jit(solution)/shard_map/gradient_sum/all_to_all | solution.py:279
  68.2 0.0 copy-done.1
  68.2 3.9 %grad_hidden.1 = bf16[4,512,1024]{2,1,0:T(8,128)(2,1)} custom-call(s32[2]{0:T(128)S(1)} %pad_add_fusion.where.refs_0_, bf16[4,104,512]{2,1,0:T(8,128)(2,1)S(1)} %get-tuple-element.49.refs_1_, bf16[104,1024]{1,0:T(8,128)(2,1)S(1)} %copy-done.1, f32[8,512]{1,0:T(8,128)S(1)} %reduce_sum.19.refs_3_), custom_call_target="tpu_custom_call" | custom-call | flops 436207616 | bytes 4194304 | tf_op jit(solution)/shard_map/grad_hidden/grad_hidden/pallas_call | solution.py:281
  72.1 3.6 %all-to-all-done.2.refs_2_ = f32[16,8,512]{2,1,0:T(8,128)S(1)} async-done(((f32[16,8,512]{2,1,0:T(8,128)}), f32[16,8,512]{2,1,0:T(8,128)S(1)}, u32[]{:S(2)}, u32[]{:S(2)}) %all-to-all-start.2) | async-done | bytes 262176 | tf_op jit(solution)/shard_map/gradient_sum/all_to_all | solution.py:279
  75.7 4.1 %collective-permute-start.7 = (f32[16,8,512]{2,1,0:T(8,128)S(1)}, f32[16,8,512]{2,1,0:T(8,128)S(1)}, u32[]{:S(2)}, u32[]{:S(2)}) collective-permute-start(f32[16,8,512]{2,1,0:T(8,128)S(1)} %all-to-all-done.2.refs_2_), channel_id=1, source_target_pairs={{0,1},{1,0},{2,3},{3,2},{4,5},{5,4},{6,7},{7,6},{8,9},{9,8},{10,11... | collective-permute-start | bytes 786440 | tf_op jit(solution)/shard_map/last_swap/ppermute | solution.py:302
  80.4 0.5 collective-permute-done.7.refs_3_
  81.0 0.0 copy-done
  81.0 1.6 %update.1 = (f32[99,1024]{1,0:T(8,128)}, f32[1,99]{1,0:T(1,128)}) custom-call(s32[2]{0:T(128)S(1)} %pad_add_fusion.where.refs_0_, s32[1]{0:T(128)S(6)} %copy.11.refs_1_, f32[16,8,512]{2,1,0:T(8,128)S(1)} %all-to-all-done.2.refs_2_, f32[16,8,512]{2,1,0:T(8,128)S(1)} %collective-permute-done.7.refs_3_, f32[99,1024]{1,0:T(8,128)S(1)} %copy-done, ...), custom_call_target="tpu_custom_call" | custom-call | tf_op jit(solution)/shard_map/update/update/pallas_call | solution.py:304
  (4 shorter events, 0.1 us)
Async XLA Ops:
  0.6 10.3 %copy-start.5 = (f32[99]{0:T(128)S(1)}, f32[99]{0:T(128)}, u32[]{:S(2)}) copy-start(f32[99]{0:T(128)} %param.10) | copy-start | bytes 1192
  0.6 10.3 %copy-start.3 = (f32[640]{0:T(1024)S(1)}, f32[640]{0:T(1024)}, u32[]{:S(2)}) copy-start(f32[640]{0:T(1024)} %param.13) | copy-start | bytes 7684
  0.7 10.3 %copy-start.4 = (s32[512]{0:T(512)S(1)}, s32[512]{0:T(512)}, u32[]{:S(2)}) copy-start(s32[512]{0:T(512)} %param.14) | copy-start | bytes 6148
  0.7 10.2 %copy-start.2 = (f32[99,512]{1,0:T(8,128)S(1)}, f32[99,512]{1,0:T(8,128)}, u32[]{:S(2)}) copy-start(f32[99,512]{1,0:T(8,128)} %truth.1) | copy-start | bytes 608260
  0.8 28.4 %copy-start.6 = (f32[99]{0:T(128)S(1)}, f32[99]{0:T(128)}, u32[]{:S(2)}) copy-start(f32[99]{0:T(128)} %param.12) | copy-start | bytes 1192
  5.0 8.7 %collective-permute-start = (f32[4,104,128]{2,1,0:T(8,128)S(1)}, f32[4,104,128]{2,1,0:T(8,128)S(1)}, u32[]{:S(2)}, u32[]{:S(2)}) collective-permute-start(f32[4,104,128]{2,1,0:T(8,128)S(1)} %get-tuple-element.30), channel_id=1, source_target_pairs={{0,64},{64,128},{128,192},{192,0},{1,65},{65,129},{129,193},{193,1... | collective-permute-start | bytes 638984 | tf_op jit(solution)/shard_map/residual_exchange/ppermute | solution.py:205
  7.2 11.8 %collective-permute-start.1 = (f32[4,104,128]{2,1,0:T(8,128)S(1)}, f32[4,104,128]{2,1,0:T(8,128)S(1)}, u32[]{:S(2)}, u32[]{:S(2)}) collective-permute-start(f32[4,104,128]{2,1,0:T(8,128)S(1)} %get-tuple-element.31), channel_id=1, source_target_pairs={{0,128},{64,192},{128,0},{192,64},{1,129},{65,193},{129,1},{193,65... | collective-permute-start | bytes 638984 | tf_op jit(solution)/shard_map/residual_exchange/ppermute | solution.py:205
  9.8 9.2 %collective-permute-start.2 = (f32[4,104,128]{2,1,0:T(8,128)S(1)}, f32[4,104,128]{2,1,0:T(8,128)S(1)}, u32[]{:S(2)}, u32[]{:S(2)}) collective-permute-start(f32[4,104,128]{2,1,0:T(8,128)S(1)} %get-tuple-element.32), channel_id=1, source_target_pairs={{0,192},{64,0},{128,64},{192,128},{1,193},{65,1},{129,65},{193,129... | collective-permute-start | bytes 638984 | tf_op jit(solution)/shard_map/residual_exchange/ppermute | solution.py:205
  19.0 49.1 %copy-start.1 = (bf16[104,1024]{1,0:T(8,128)(2,1)S(1)}, bf16[104,1024]{1,0:T(8,128)(2,1)}, u32[]{:S(2)}) copy-start(bf16[104,1024]{1,0:T(8,128)(2,1)} %get-tuple-element.50.refs_2_) | copy-start | bytes 638980
  20.9 4.6 %collective-permute-start.3 = (bf16[4,104,128]{2,1,0:T(8,128)(2,1)S(1)}, bf16[4,104,128]{2,1,0:T(8,128)(2,1)S(1)}, u32[]{:S(2)}, u32[]{:S(2)}) collective-permute-start(bf16[4,104,128]{2,1,0:T(8,128)(2,1)S(1)} %get-tuple-element.43), channel_id=1, source_target_pairs={{0,192},{64,0},{128,64},{192,128},{1,193},{65,1},{129,65},{193,129... | collective-permute-start | bytes 319496 | tf_op jit(solution)/shard_map/bracket_exchange/ppermute | solution.py:205
  22.9 5.1 %collective-permute-start.4 = (bf16[4,104,128]{2,1,0:T(8,128)(2,1)S(1)}, bf16[4,104,128]{2,1,0:T(8,128)(2,1)S(1)}, u32[]{:S(2)}, u32[]{:S(2)}) collective-permute-start(bf16[4,104,128]{2,1,0:T(8,128)(2,1)S(1)} %get-tuple-element.44), channel_id=1, source_target_pairs={{0,128},{64,192},{128,0},{192,64},{1,129},{65,193},{129,1},{193,65... | collective-permute-start | bytes 319496 | tf_op jit(solution)/shard_map/bracket_exchange/ppermute | solution.py:205
  24.0 5.1 %collective-permute-start.5 = (bf16[4,104,128]{2,1,0:T(8,128)(2,1)S(1)}, bf16[4,104,128]{2,1,0:T(8,128)(2,1)S(1)}, u32[]{:S(2)}, u32[]{:S(2)}) collective-permute-start(bf16[4,104,128]{2,1,0:T(8,128)(2,1)S(1)} %get-tuple-element.45), channel_id=1, source_target_pairs={{0,64},{64,128},{128,192},{192,0},{1,65},{65,129},{129,193},{193,1... | collective-permute-start | bytes 319496 | tf_op jit(solution)/shard_map/bracket_exchange/ppermute | solution.py:205
  30.7 50.3 %copy-start = (f32[99,1024]{1,0:T(8,128)S(1)}, f32[99,1024]{1,0:T(8,128)}, u32[]{:S(2)}) copy-start(f32[99,1024]{1,0:T(8,128)} %refs_4_.1) | copy-start | bytes 1216516
  30.7 4.2 %collective-permute-start.6 = (f32[16,8,512]{2,1,0:T(8,128)S(1)}, f32[16,8,512]{2,1,0:T(8,128)S(1)}, u32[]{:S(2)}, u32[]{:S(2)}) collective-permute-start(f32[16,8,512]{2,1,0:T(8,128)S(1)} %get-tuple-element.48), channel_id=1, source_target_pairs={{0,1},{1,0},{2,3},{3,2},{4,5},{5,4},{6,7},{7,6},{8,9},{9,8},{10,11... | collective-permute-start | bytes 786440 | tf_op jit(solution)/shard_map/gradient_sum/ppermute | solution.py:273
  64.6 11.0 %all-to-all-start.2 = ((f32[16,8,512]{2,1,0:T(8,128)}), f32[16,8,512]{2,1,0:T(8,128)S(1)}, u32[]{:S(2)}, u32[]{:S(2)}) async-start(f32[16,8,512]{2,1,0:T(8,128)} %broadcast_in_dim.7), calls=%async_computation.2 | async-start | bytes 524288 | tf_op jit(solution)/shard_map/gradient_sum/all_to_all | solution.py:279
  75.7 5.3 %collective-permute-start.7 = (f32[16,8,512]{2,1,0:T(8,128)S(1)}, f32[16,8,512]{2,1,0:T(8,128)S(1)}, u32[]{:S(2)}, u32[]{:S(2)}) collective-permute-start(f32[16,8,512]{2,1,0:T(8,128)S(1)} %all-to-all-done.2.refs_2_), channel_id=1, source_target_pairs={{0,1},{1,0},{2,3},{3,2},{4,5},{5,4},{6,7},{7,6},{8,9},{9,8},{10,11... | collective-permute-start | bytes 786440 | tf_op jit(solution)/shard_map/last_swap/ppermute | solution.py:302

commit v3 on v2

v3 whole, which is shorter than its diff:
```python
import jax
import jax.numpy as jnp
from jax import lax
from jax.experimental import pallas as pl
from jax.experimental.pallas import tpu as pltpu
from jax.sharding import Mesh, PartitionSpec as P

WARMUP = 1000
smooth_sq = 0.0025
fair_alpha = 0.95

GROUPS = 4
PIECES = 16
PIECE_ROWS = 7
MIB = 1024 * 1024
VMEM = pl.BlockSpec(memory_space=pltpu.VMEM)
SMEM = pl.BlockSpec(memory_space=pltpu.SMEM)
HBM = pl.BlockSpec(memory_space=pltpu.HBM)
F32 = jnp.float32
BF16 = jnp.bfloat16


def soft(d):
    return d * lax.rsqrt(d * d + smooth_sq)


def as_column(row, rows):
    n = row.shape[1]
    pick = lax.broadcasted_iota(jnp.int32, (rows, n), 0) == lax.broadcasted_iota(jnp.int32, (rows, n), 1)
    return jnp.sum(jnp.where(pick, jnp.broadcast_to(row, (rows, n)), 0.0), axis=1, keepdims=True)


def padded(value, rows):
    return jnp.concatenate([value, jnp.zeros((rows - value.shape[0], value.shape[1]), value.dtype)], axis=0)


def decode(half, features, out):
    for m in range(out.shape[0]):
        out[m] = lax.dot_general(half[...], features[m], (((1,), (1,)), ((), ())), preferred_element_type=F32)


def fetch_chunks(where, hidden, held, sem, ks):
    chunk = held.shape[2]
    copies = []
    for slot, k in enumerate(ks):
        start = pl.multiple_of(lax.rem(where[0] + k, GROUPS) * chunk, chunk)
        copies.append(pltpu.make_async_copy(hidden.at[:, pl.ds(start, chunk), :], held.at[slot], sem.at[slot]))
        copies[slot].start()
    return copies


def far_kernel(where, hidden, weight, out, half, held, w, sem, weight_sem):
    fetch = pltpu.make_async_copy(weight, w, weight_sem)
    fetch.start()
    copies = fetch_chunks(where, hidden, held, sem, (2,))
    fetch.wait()
    half[...] = padded(w[...], half.shape[0]).astype(BF16)
    copies[0].wait()
    decode(half, held.at[0], out)


def near_kernel(where, hidden, half, after, before, held, sem):
    copies = fetch_chunks(where, hidden, held, sem, (1, 3))
    for slot, out in enumerate((after, before)):
        copies[slot].wait()
        decode(half, held.at[slot], out)


def add_pair(total, i, j, s):
    total[i] = s if total[i] is None else total[i] + s
    total[j] = -s if total[j] is None else total[j] - s


def early_pairs_kernel(here, far, shift, out):
    local = here.shape[0]
    count = 2 * local

    def tile(t, carry):
        at = pl.ds(pl.multiple_of(t * 8, 8), 8)
        r = [ref[j, at, :] + shift[at, :] for ref in (here, far) for j in range(local)]
        total = [None] * count
        for i in range(count):
            for j in range(i + 1, count):
                add_pair(total, i, j, soft(r[i] - r[j]))
        for j in range(count):
            out[j, at, :] = total[j]
        return carry

    lax.fori_loop(0, here.shape[1] // 8, tile, 0)


def late_pairs_kernel(members, here, far, after, before, shift, early, *rest):
    ins, outs, scratch = (here, far, after, before), rest[:GROUPS], rest[GROUPS]
    local = here.shape[0]
    count = early.shape[0]
    eps = (1.0 - fair_alpha) / members
    normalizer = (1.0 - eps) / (members * (members - 1))

    def tile(t, carry):
        at = pl.ds(pl.multiple_of(t * 8, 8), 8)
        r = [ref[j, at, :] + shift[at, :] for ref in ins for j in range(local)]
        total = [early[j, at, :] for j in range(count)] + [None] * (members - count)
        for i in range(members):
            for j in range(max(i + 1, count), members):
                add_pair(total, i, j, soft(r[i] - r[j]))
        for j in range(members):
            scratch[j, at, :] = soft(r[j]) * (1.0 / members) - normalizer * total[j]
        return carry

    lax.fori_loop(0, here.shape[1] // 8, tile, 0)
    for j in range(members):
        outs[j // local][j % local] = scratch[j].astype(BF16)


def local_kernel(where, hidden, half, lat, area_bin, intercept, truth, out, area, shift, held, sem):
    chunk = held.shape[2]
    copies = fetch_chunks(where, hidden, held, sem, range(GROUPS))
    cells, width = lat.shape
    points = area_bin.shape[1]
    bins = jnp.broadcast_to(area_bin[...], (width, points))
    level = lax.broadcasted_iota(jnp.int32, (width, points), 0)
    total = jnp.zeros((width, points), F32)
    for q in range(cells):
        column = as_column(lat[q : q + 1, :], width)
        total = total + jnp.where(bins == level + q * width, column, 0.0)
    area[...] = jnp.sum(total, axis=0, keepdims=True)
    mine = pl.multiple_of(where[0] * chunk, chunk)
    shift[...] = as_column(intercept[...], shift.shape[0]) - padded(truth[:, pl.ds(mine, chunk)], shift.shape[0])
    copies[0].wait()
    decode(half, held.at[0], out)
    for copy in copies[1:]:
        copy.wait()


def pieces_of(acc, extra, out):
    last = lax.broadcasted_iota(jnp.int32, out.shape[1:], 0) == PIECE_ROWS
    for r in range(PIECES):
        out[r] = jnp.where(last, extra, acc[PIECE_ROWS * r : PIECE_ROWS * r + 8, :])


def gradient_half(side, weighted, held, acc):
    _, rows, depth = weighted.shape
    half = acc.shape[1]
    lanes = pl.ds(pl.multiple_of(side * half, half), half)
    total = None
    for k in range(GROUPS):
        part = jnp.dot(weighted[k], held[k, :, :, lanes].reshape(depth, half), preferred_element_type=F32)
        total = part if total is None else total + part
    acc[0:rows, :] = total
    acc[rows:, :] = jnp.zeros((acc.shape[0] - rows, half), F32)


def partner_half_kernel(where, held, b0, b1, b2, b3, var, area, weighted, extra_out, other, acc):
    brackets = (b0, b1, b2, b3)
    local, rows, chunk = b0.shape
    depth = local * chunk
    half = acc.shape[1]
    scale = as_column(var[...], rows)
    ones = jnp.ones((8, depth), BF16)
    bias = jnp.zeros((8, rows), F32)
    for k in range(GROUPS):
        start = pl.multiple_of(lax.rem(where[0] + k, GROUPS) * chunk, chunk)
        point_scale = area[:, pl.ds(start, chunk)] * scale
        w = jnp.concatenate(
            [(point_scale * brackets[k][m].astype(F32)).astype(BF16) for m in range(local)], axis=1
        )
        weighted[k] = w
        bias = bias + lax.dot_general(ones, w, (((1,), (1,)), ((), ())), preferred_element_type=F32)
    gradient_half(1 - where[1], weighted, held, acc)
    total = jnp.sum(area[...], axis=1, keepdims=True)
    extra = jnp.concatenate(
        [
            bias[0:1],
            jnp.zeros((1, 128 - rows), F32),
            jnp.broadcast_to(total, (1, 128)),
            jnp.zeros((1, half - 256), F32),
        ],
        axis=1,
    )
    extra_out[...] = jnp.broadcast_to(extra, (8, half))
    pieces_of(acc, extra_out[...], other)


def own_half_kernel(where, held, weighted, extra, mine, acc):
    gradient_half(where[1], weighted, held, acc)
    pieces_of(acc, extra[...], mine)


def grad_hidden_kernel(where, weighted, half, piece, out, *, replicas):
    inverse = 1.0 / (piece[PIECE_ROWS : PIECE_ROWS + 1, 128:129] * (1.0 / replicas))
    chunk = out.shape[1]
    for m in range(out.shape[0]):
        product = lax.dot_general(
            weighted[0, :, m * chunk : (m + 1) * chunk], half[...], (((0,), (0,)), ((), ())), preferred_element_type=F32
        )
        out[m] = (product * inverse).astype(BF16)


def squares_of(pieces, inverse):
    half = pieces.shape[2]
    keep = lax.broadcasted_iota(jnp.int32, (8, half), 0) < PIECE_ROWS
    squares = jnp.zeros((8, half), F32)
    for r in range(PIECES):
        g = jnp.where(keep, pieces[r] * inverse, 0.0)
        squares = squares + g * g
    return squares


def squares_kernel(own, out, *, replicas):
    inverse = 1.0 / (own[0, PIECE_ROWS : PIECE_ROWS + 1, 128:129] * (1.0 / replicas))
    out[...] = squares_of(own, inverse)


def update_kernel(where, step, own, partner, squares, weight, intercept, new_weight, new_bias, *, replicas):
    variables, features = weight.shape
    half = features // 2
    first = where[1] == 0
    mean_area = own[0, PIECE_ROWS : PIECE_ROWS + 1, 128:129] * (1.0 / replicas)
    inverse = 1.0 / mean_area
    bias_grad = own[0, PIECE_ROWS : PIECE_ROWS + 1, 0:variables] * inverse
    a, b = squares[...], squares_of(partner, inverse)
    both = jnp.where(first, a, b) + jnp.where(first, b, a)
    total = jnp.sum(jnp.sum(both, axis=0, keepdims=True), axis=1, keepdims=True)
    total = total + jnp.sum(bias_grad * bias_grad, axis=1, keepdims=True)
    count = variables * features + variables
    rms = jnp.sqrt(total / count + 1e-06)
    warm = (step[0] + 1).astype(F32) / WARMUP
    scale = warm * jnp.minimum(1.0, 1.0 / rms)
    for r in range(PIECES):
        low = PIECE_ROWS * r
        n = min(PIECE_ROWS, variables - low)
        if n <= 0:
            continue
        a, b = own[r, 0:n, :], partner[r, 0:n, :]
        left, right = jnp.where(first, a, b), jnp.where(first, b, a)
        new_weight[low : low + n, :half] = weight[low : low + n, :half] - scale * (left * inverse)
        new_weight[low : low + n, half:] = weight[low : low + n, half:] - scale * (right * inverse)
    new_bias[...] = intercept[...] - scale * bias_grad


def on_device(hidden, decoder_weight, decoder_intercept, analysis_truth, var_weight, lat_weight, area_bin, train_step):
    local, points, features = hidden.shape
    variables = decoder_weight.shape[0]
    rows = -(-variables // 8) * 8
    chunk = points // GROUPS
    members = local * GROUPS
    replicas = points * lax.axis_size("z") * lax.axis_size("x") * lax.axis_size("c") * GROUPS
    me, core = lax.axis_index("y"), lax.axis_index("c")
    where = jnp.stack([me, core]).astype(jnp.int32)

    def grant(mib):
        return pltpu.CompilerParams(vmem_limit_bytes=int(mib * MIB))

    intercept_row = decoder_intercept.reshape(1, variables)
    var_row = var_weight.reshape(1, variables)

    def turn(value, k):
        return value if k % GROUPS == 0 else lax.ppermute(value, "y", [(i, (i + k) % GROUPS) for i in range(GROUPS)])

    one_residual = jax.ShapeDtypeStruct((local, rows, chunk), F32)
    with jax.named_scope("forward_far"):
        far, half_weight = pl.pallas_call(
            far_kernel,
            out_shape=[one_residual, jax.ShapeDtypeStruct((rows, features), BF16)],
            in_specs=[SMEM, HBM, HBM],
            out_specs=[VMEM] * 2,
            scratch_shapes=[
                pltpu.VMEM((1, local, chunk, features), BF16),
                pltpu.VMEM((variables, features), F32),
                pltpu.SemaphoreType.DMA((1,)),
                pltpu.SemaphoreType.DMA(()),
            ],
            compiler_params=grant(53.4),
            name="forward_far",
        )(where, hidden, decoder_weight)
        far = turn(far, 2)
    with jax.named_scope("forward_near"):
        after, before = pl.pallas_call(
            near_kernel,
            out_shape=[one_residual] * 2,
            in_specs=[SMEM, HBM, VMEM],
            out_specs=[VMEM] * 2,
            scratch_shapes=[
                pltpu.VMEM((2, local, chunk, features), BF16),
                pltpu.SemaphoreType.DMA((2,)),
            ],
            compiler_params=grant(52),
            cost_estimate=pl.CostEstimate(
                flops=4 * rows * local * chunk * features, bytes_accessed=4 * local * chunk * features, transcendentals=0
            ),
            name="forward_near",
        )(where, hidden, half_weight)
        after, before = turn(after, 1), turn(before, 3)
    with jax.named_scope("forward_local"):
        here, area, shift, held = pl.pallas_call(
            local_kernel,
            out_shape=[
                one_residual,
                jax.ShapeDtypeStruct((1, points), F32),
                jax.ShapeDtypeStruct((rows, chunk), F32),
                jax.ShapeDtypeStruct((GROUPS, local, chunk, features), BF16),
            ],
            in_specs=[SMEM, HBM] + [VMEM] * 5,
            out_specs=[VMEM] * 4,
            scratch_shapes=[pltpu.SemaphoreType.DMA((GROUPS,))],
            compiler_params=grant(46),
            name="forward_local",
        )(where, hidden, half_weight, lat_weight.reshape(-1, 128), area_bin.reshape(1, points), intercept_row, analysis_truth)
    with jax.named_scope("early_pairs"):
        early = pl.pallas_call(
            early_pairs_kernel,
            out_shape=jax.ShapeDtypeStruct((2 * local, rows, chunk), F32),
            in_specs=[VMEM] * 3,
            out_specs=VMEM,
            compiler_params=grant(4),
            name="early_pairs",
        )(here, far, shift)
    after, before, early, area, held = lax.optimization_barrier((after, before, early, area, held))
    with jax.named_scope("late_pairs"):
        brackets = pl.pallas_call(
            lambda *refs: late_pairs_kernel(members, *refs),
            out_shape=[jax.ShapeDtypeStruct((local, rows, chunk), BF16)] * GROUPS,
            in_specs=[VMEM] * (GROUPS + 2),
            out_specs=[VMEM] * GROUPS,
            scratch_shapes=[pltpu.VMEM((members, rows, chunk), F32)],
            compiler_params=grant(6),
            name="late_pairs",
        )(here, far, after, before, shift, early)
    with jax.named_scope("bracket_exchange"):
        returned = [brackets[0], turn(brackets[2], -1), turn(brackets[1], -2), turn(brackets[3], -3)]
    half = features // 2
    pieces = jax.ShapeDtypeStruct((PIECES, 8, half), F32)
    sums = [pltpu.VMEM((PIECES * 8, half), F32)]
    with jax.named_scope("backward_partner_half"):
        weighted, extra, other = pl.pallas_call(
            partner_half_kernel,
            out_shape=[
                jax.ShapeDtypeStruct((GROUPS, rows, local * chunk), BF16),
                jax.ShapeDtypeStruct((8, half), F32),
                pieces,
            ],
            in_specs=[SMEM] + [VMEM] * 7,
            out_specs=[VMEM] * 3,
            scratch_shapes=sums,
            compiler_params=grant(8),
            name="backward_partner_half",
        )(where, held, *returned, var_row, area)
        swap = [(0, 1), (1, 0)]
        other = lax.ppermute(other, "c", swap)
    with jax.named_scope("backward_own_half"):
        mine = pl.pallas_call(
            own_half_kernel,
            out_shape=pieces,
            in_specs=[SMEM] + [VMEM] * 3,
            out_specs=VMEM,
            scratch_shapes=sums,
            compiler_params=grant(8),
            name="backward_own_half",
        )(where, held, weighted, extra)
    with jax.named_scope("gradient_sum"):
        part = mine + other
        part = lax.all_to_all(part, ("x", "y"), 0, 0, tiled=True)
        depth = lax.axis_size("z")
        part = jnp.broadcast_to(jnp.sum(part, axis=0), (depth, 8, half))
        part = lax.all_to_all(part, "z", 0, 0, tiled=True)
        piece = jnp.sum(part, axis=0)
        own = lax.all_to_all(jnp.broadcast_to(piece, (PIECES, 8, half)), ("x", "y"), 0, 0, tiled=True)
    with jax.named_scope("grad_hidden"):
        grad_hidden = pl.pallas_call(
            lambda *refs: grad_hidden_kernel(*refs, replicas=replicas),
            out_shape=jax.ShapeDtypeStruct(hidden.shape, BF16),
            grid_spec=pltpu.PrefetchScalarGridSpec(
                num_scalar_prefetch=1,
                grid=(GROUPS,),
                in_specs=[
                    pl.BlockSpec((1, rows, local * chunk), lambda g, s: (g, 0, 0)),
                    pl.BlockSpec((rows, features), lambda g, s: (0, 0)),
                    pl.BlockSpec((8, half), lambda g, s: (0, 0)),
                ],
                out_specs=pl.BlockSpec((local, chunk, features), lambda g, s: (0, lax.rem(s[0] + g, GROUPS), 0)),
            ),
            compiler_params=grant(12),
            cost_estimate=pl.CostEstimate(
                flops=2 * rows * local * points * features, bytes_accessed=2 * hidden.size, transcendentals=0
            ),
            name="grad_hidden",
        )(where, weighted, half_weight, piece)
        own, grad_hidden = lax.optimization_barrier((own, grad_hidden))
    with jax.named_scope("last_swap"):
        partner = lax.ppermute(own, "c", swap)
        squares = pl.pallas_call(
            lambda *refs: squares_kernel(*refs, replicas=replicas),
            out_shape=jax.ShapeDtypeStruct((8, half), F32),
            in_specs=[VMEM],
            out_specs=VMEM,
            compiler_params=grant(4),
            name="squares",
        )(own)
    with jax.named_scope("update"):
        new_weight, new_bias = pl.pallas_call(
            lambda *refs: update_kernel(*refs, replicas=replicas),
            out_shape=[
                jax.ShapeDtypeStruct((variables, features), F32),
                jax.ShapeDtypeStruct((1, variables), F32),
            ],
            in_specs=[SMEM, SMEM] + [VMEM] * 5,
            out_specs=[VMEM] * 2,
            compiler_params=grant(6),
            name="update",
        )(where, train_step, own, partner, squares, decoder_weight, intercept_row)
    return grad_hidden, new_weight, new_bias.reshape(variables)


def solution(mesh):
    fine = Mesh(mesh.devices.reshape(GROUPS, 8, 4, 2), ("y", "z", "x", "c"))
    space = ("z", "x", "c")
    return jax.shard_map(
        on_device,
        mesh=fine,
        in_specs=(P("y", space, None), P(), P(), P(None, space), P(), P(), P(space), P()),
        out_specs=(P("y", space, None), P(), P()),
        check_vma=False,
    )
```

time: 82.9 us -> 80 us (0.965)
  waiting for transfers between devices: 15.7 us -> 9.95 us
  starting transfers between devices: 19.7 us -> 21.6 us
  Pallas kernels: 15.9 us -> 17.6 us
    ppermute x6, waiting for transfers between devices: 10.4 us -> 6.03 us  [turn(): lax.ppermute(value, 'y', [(i, (i + k) % GROUPS) for i in range(GROUPS)])]
    pallas_call x4 -> x8, Pallas kernels: 10.4 us -> 12.1 us  [the longest x1 2.78 us: on_device(): pl.pallas_call(local_kernel, out_shape=[one_residual, jax.ShapeDtypeStruc...]
    ppermute x6, starting transfers between devices: 9.03 us -> 10.3 us  [turn(): lax.ppermute(value, 'y', [(i, (i + k) % GROUPS) for i in range(GROUPS)])]
    ppermute x1, waiting for transfers between devices: 1.16 us -> 0.12 us  [on_device(): other = lax.ppermute(other, 'c', swap)]
    all_to_all x1, blocking collectives: 13 us -> 12.1 us  [on_device(): part = lax.all_to_all(part, ('x', 'y'), 0, 0, tiled=True)]
  transfers between devices with their start and end apart: 9 -> 9, of which waited for: 7 -> 7; matrix products, arithmetic and copies ran while one was open for 0% -> 0% of each run, Pallas kernels for 8% -> 14%
where the time goes in v3:
time: 80 us; the launch traced here: 79.7 us
  blocking collectives  28.1 us (35%)
  starting transfers between devices  21.6 us (27%)
  Pallas kernels  17.6 us (22%)
  waiting for transfers between devices  9.95 us (12%)
  between operations  1.41 us (2%)
    all_to_all x1, blocking collectives, on_device(): part = lax.all_to_all(part, 'z', 0, 0, tiled=True)  16 us
    all_to_all x1, blocking collectives, on_device(): part = lax.all_to_all(part, ('x', 'y'), 0, 0, tiled=True)  12.1 us
    ppermute x6, starting transfers between devices, turn(): lax.ppermute(value, 'y', [(i, (i + k) % GROUPS) for i in range(GROUPS)])  10.3 us
    ppermute x6, waiting for transfers between devices, turn(): lax.ppermute(value, 'y', [(i, (i + k) % GROUPS) for i in range(GROUPS)])  6.03 us
    ppermute x1, starting transfers between devices, on_device(): partner = lax.ppermute(own, 'c', swap)  4.38 us
    pallas_call x1, Pallas kernels, on_device(): pl.pallas_call(lambda *refs: grad_hidden_kernel(*refs, replicas=replicas)...  3.92 us
    all_to_all x1, starting transfers between devices, on_device(): lax.all_to_all(jnp.broadcast_to(piece, (PIECES, 8, half)), ('x', 'y'), 0,...  3.62 us
    all_to_all x1, waiting for transfers between devices, on_device(): lax.all_to_all(jnp.broadcast_to(piece, (PIECES, 8, half)), ('x', 'y'), 0,...  3.4 us
  transfers between devices with their start and end apart: 9, of which 7 were waited for; matrix products, arithmetic and copies ran while one was open for 0% of the time, Pallas kernels for 14%

profile of v3, /device:TPU:1, one launch (start us, length us, event | category | flops | bytes accessed | tf_op | source)
XLA Modules:
  0.0 79.7 jit_solution(17771905163649680809)
XLA Ops:
  0.6 0.1 pad_add_fusion.where.refs_0_
  0.7 0.0 copy-start.1
  0.7 0.0 copy-start.2
  0.7 0.0 copy-start.3
  0.7 0.0 copy-start.4
  0.7 2.4 %forward_far.1 = (f32[4,104,128]{2,1,0:T(8,128)S(1)}, bf16[104,1024]{1,0:T(8,128)(2,1)S(1)}) custom-call(s32[2]{0:T(128)S(1)} %pad_add_fusion.where.refs_0_, bf16[4,512,1024]{2,1,0:T(8,128)(2,1)} %hidden.5, f32[99,1024]{1,0:T(8,128)} %refs_5_.1), custom_call_target="tpu_custom_call" | custom-call | tf_op jit(solution)/shard_map/forward_far/forward_far/pallas_call | solution.py:262
  3.1 3.8 %collective-permute-start.2 = (f32[4,104,128]{2,1,0:T(8,128)S(1)}, f32[4,104,128]{2,1,0:T(8,128)S(1)}, u32[]{:S(2)}, u32[]{:S(2)}) collective-permute-start(f32[4,104,128]{2,1,0:T(8,128)S(1)} %get-tuple-element.31), channel_id=1, source_target_pairs={{0,128},{64,192},{128,0},{192,64},{1,129},{65,193},{129,1},{193,65... | collective-permute-start | bytes 638984 | tf_op jit(solution)/shard_map/forward_far/ppermute | solution.py:258
  6.9 2.6 %forward_near.1 = (f32[4,104,128]{2,1,0:T(8,128)S(1)}, f32[4,104,128]{2,1,0:T(8,128)S(1)}) custom-call(s32[2]{0:T(128)S(1)} %pad_add_fusion.where.refs_0_, bf16[4,512,1024]{2,1,0:T(8,128)(2,1)} %hidden.5, bf16[104,1024]{1,0:T(8,128)(2,1)S(1)} %get-tuple-element.27.half.refs_2_), custom_call_target="tpu_custom_call" | custom-call | flops 218103808 | bytes 2097152 | tf_op jit(solution)/shard_map/forward_near/forward_near/pallas_call | solution.py:278
  9.6 0.0 copy-start.5
  9.6 0.5 collective-permute-start
  10.1 2.3 %collective-permute-start.1 = (f32[4,104,128]{2,1,0:T(8,128)S(1)}, f32[4,104,128]{2,1,0:T(8,128)S(1)}, u32[]{:S(2)}, u32[]{:S(2)}) collective-permute-start(f32[4,104,128]{2,1,0:T(8,128)S(1)} %get-tuple-element.29), channel_id=1, source_target_pairs={{0,192},{64,0},{128,64},{192,128},{1,193},{65,1},{129,65},{193,129... | collective-permute-start | bytes 638984 | tf_op jit(solution)/shard_map/forward_near/ppermute | solution.py:258
  12.3 0.0 copy-done.1
  12.3 0.0 copy-done.2
  12.3 0.0 copy-done.3
  12.3 0.0 copy-done.4
  12.3 2.8 %forward_local.1 = (f32[4,104,128]{2,1,0:T(8,128)S(1)}, f32[1,512]{1,0:T(1,128)S(1)}, f32[104,128]{1,0:T(8,128)S(1)}, bf16[4,4,128,1024]{3,2,1,0:T(8,128)(2,1)S(1)}) custom-call(s32[2]{0:T(128)S(1)} %pad_add_fusion.where.refs_0_, bf16[4,512,1024]{2,1,0:T(8,128)(2,1)} %hidden.5, bf16[104,1024]{1,0:T(8,128)(2,1)S(1)} %get-tuple-element.27.half.refs_2_, ...), custom_call_target="tpu_custom_call" | custom-call | tf_op jit(solution)/shard_map/forward_local/forward_local/pallas_call | solution.py:295
  15.1 0.0 collective-permute-done.2.far.refs_1_
  15.1 0.5 early_pairs.1.refs_5_
  15.6 1.3 %collective-permute-done.refs_2_ = f32[4,104,128]{2,1,0:T(8,128)S(1)} collective-permute-done((f32[4,104,128]{2,1,0:T(8,128)S(1)}, f32[4,104,128]{2,1,0:T(8,128)S(1)}, u32[]{:S(2)}, u32[]{:S(2)}) %collective-permute-start) | collective-permute-done | bytes 213024 | tf_op jit(solution)/shard_map/forward_near/ppermute | solution.py:258
  16.9 0.0 collective-permute-done.1.refs_3_
  16.9 1.5 %late_pairs.1 = (bf16[4,104,128]{2,1,0:T(8,128)(2,1)S(1)}, bf16[4,104,128]{2,1,0:T(8,128)(2,1)S(1)}, bf16[4,104,128]{2,1,0:T(8,128)(2,1)S(1)}, bf16[4,104,128]{2,1,0:T(8,128)(2,1)S(1)}) custom-call(f32[4,104,128]{2,1,0:T(8,128)S(1)} %get-tuple-element.30.here.refs_0_, f32[4,104,128]{2,1,0:T(8,128)S(1)} %collective-permute-done.2.far.refs_1_, ...), custom_call_target="tpu_custom_call" | custom-call | tf_op jit(solution)/shard_map/late_pairs/late_pairs/pallas_call | solution.py:320
  18.4 2.2 %collective-permute-start.3 = (bf16[4,104,128]{2,1,0:T(8,128)(2,1)S(1)}, bf16[4,104,128]{2,1,0:T(8,128)(2,1)S(1)}, u32[]{:S(2)}, u32[]{:S(2)}) collective-permute-start(bf16[4,104,128]{2,1,0:T(8,128)(2,1)S(1)} %get-tuple-element.40), channel_id=1, source_target_pairs={{0,192},{64,0},{128,64},{192,128},{1,193},{65,1},{129,65},{193,129... | collective-permute-start | bytes 319496 | tf_op jit(solution)/shard_map/bracket_exchange/ppermute | solution.py:258
  20.6 0.7 collective-permute-start.4
  21.3 0.8 collective-permute-start.5
  22.1 0.2 collective-permute-done.3.b1
  22.3 3.4 %collective-permute-done.4.b2 = bf16[4,104,128]{2,1,0:T(8,128)(2,1)S(1)} collective-permute-done((bf16[4,104,128]{2,1,0:T(8,128)(2,1)S(1)}, bf16[4,104,128]{2,1,0:T(8,128)(2,1)S(1)}, u32[]{:S(2)}, u32[]{:S(2)}) %collective-permute-start.4) | collective-permute-done | bytes 106528 | tf_op jit(solution)/shard_map/bracket_exchange/ppermute | solution.py:258
  25.7 1.1 %collective-permute-done.5.b3 = bf16[4,104,128]{2,1,0:T(8,128)(2,1)S(1)} collective-permute-done((bf16[4,104,128]{2,1,0:T(8,128)(2,1)S(1)}, bf16[4,104,128]{2,1,0:T(8,128)(2,1)S(1)}, u32[]{:S(2)}, u32[]{:S(2)}) %collective-permute-start.5) | collective-permute-done | bytes 106528 | tf_op jit(solution)/shard_map/bracket_exchange/ppermute | solution.py:258
  26.8 0.0 copy-done.5
  26.8 1.2 %backward_partner_half.1 = (bf16[4,104,512]{2,1,0:T(8,128)(2,1)S(1)}, f32[8,512]{1,0:T(8,128)S(1)}, f32[16,8,512]{2,1,0:T(8,128)S(1)}) custom-call(s32[2]{0:T(128)S(1)} %pad_add_fusion.where.refs_0_, bf16[4,4,128,1024]{3,2,1,0:T(8,128)(2,1)S(1)} %get-tuple-element.35.held, bf16[4,104,128]{2,1,0:T(8,128)(2,1)S(1)} %get-tuple-element.39.b0, ...), custom_call_target="tpu_custom_call" | custom-call | tf_op jit(solution)/shard_map/backward_partner_half/backward_partner_half/pallas_call | solution.py:335
  28.0 3.4 %collective-permute-start.6 = (f32[16,8,512]{2,1,0:T(8,128)S(1)}, f32[16,8,512]{2,1,0:T(8,128)S(1)}, u32[]{:S(2)}, u32[]{:S(2)}) collective-permute-start(f32[16,8,512]{2,1,0:T(8,128)S(1)} %get-tuple-element.46), channel_id=1, source_target_pairs={{0,1},{1,0},{2,3},{3,2},{4,5},{5,4},{6,7},{7,6},{8,9},{9,8},{10,11... | collective-permute-start | bytes 786440 | tf_op jit(solution)/shard_map/backward_partner_half/ppermute | solution.py:349
  31.4 1.0 %backward_own_half.1 = f32[16,8,512]{2,1,0:T(8,128)S(1)} custom-call(s32[2]{0:T(128)S(1)} %pad_add_fusion.where.refs_0_, bf16[4,4,128,1024]{3,2,1,0:T(8,128)(2,1)S(1)} %get-tuple-element.35.held, bf16[4,104,512]{2,1,0:T(8,128)(2,1)S(1)} %get-tuple-element.44.weighted.refs_1_, f32[8,512]{1,0:T(8,128)S(1)} %get-tuple-element.45.extra), custom_call_target="tpu_custom_call" | custom-call | tf_op jit(solution)/shard_map/backward_own_half/backward_own_half/pallas_call | solution.py:351
  32.4 0.0 copy-start
  32.4 0.1 collective-permute-done.6
  32.6 12.1 %all_to_all.15 = f32[16,8,512]{2,1,0:T(8,128)S(1)} all-to-all(f32[16,8,512]{2,1,0:T(8,128)S(1)} %add.3), channel_id=1, replica_groups=mesh['y'=4,'z'=8,'x'=4,'c'=2] {'x','y'}, dimensions={0} | all-to-all | bytes 524288 | tf_op jit(solution)/shard_map/gradient_sum/all_to_all | solution.py:362
  44.8 16.0 %all_to_all.16 = f32[8,8,512]{2,1,0:T(8,128)S(1)} all-to-all(f32[8,8,512]{2,1,0:T(8,128)S(1)} %broadcast_in_dim.6), channel_id=1, replica_groups=mesh['y'=4,'z'=8,'x'=4,'c'=2] {'z'}, dimensions={0} | all-to-all | bytes 262144 | tf_op jit(solution)/shard_map/gradient_sum/all_to_all | solution.py:365
  60.8 0.7 broadcast_in_dim.7
  61.5 3.6 %all-to-all-start.2 = ((f32[16,8,512]{2,1,0:T(8,128)}), f32[16,8,512]{2,1,0:T(8,128)S(1)}, u32[]{:S(2)}, u32[]{:S(2)}) async-start(f32[16,8,512]{2,1,0:T(8,128)} %broadcast_in_dim.7), calls=%async_computation.2 | async-start | bytes 524288 | tf_op jit(solution)/shard_map/gradient_sum/all_to_all | solution.py:367
  65.2 3.9 %grad_hidden.1 = bf16[4,512,1024]{2,1,0:T(8,128)(2,1)} custom-call(s32[2]{0:T(128)S(1)} %pad_add_fusion.where.refs_0_, bf16[4,104,512]{2,1,0:T(8,128)(2,1)S(1)} %get-tuple-element.44.weighted.refs_1_, bf16[104,1024]{1,0:T(8,128)(2,1)S(1)} %get-tuple-element.27.half.refs_2_, f32[8,512]{1,0:T(8,128)S(1)} %reduce_sum.19.refs_3_), custom_call_target="tpu_custom_call" | custom-call | flops 436207616 | bytes 4194304 | tf_op jit(solution)/shard_map/grad_hidden/grad_hidden/pallas_call | solution.py:369
  69.1 3.4 %all-to-all-done.2.refs_0_.refs_2_ = f32[16,8,512]{2,1,0:T(8,128)S(1)} async-done(((f32[16,8,512]{2,1,0:T(8,128)}), f32[16,8,512]{2,1,0:T(8,128)S(1)}, u32[]{:S(2)}, u32[]{:S(2)}) %all-to-all-start.2) | async-done | bytes 262176 | tf_op jit(solution)/shard_map/gradient_sum/all_to_all | solution.py:367
  72.5 4.4 %collective-permute-start.7 = (f32[16,8,512]{2,1,0:T(8,128)S(1)}, f32[16,8,512]{2,1,0:T(8,128)S(1)}, u32[]{:S(2)}, u32[]{:S(2)}) collective-permute-start(f32[16,8,512]{2,1,0:T(8,128)S(1)} %all-to-all-done.2.refs_0_.refs_2_), channel_id=1, source_target_pairs={{0,1},{1,0},{2,3},{3,2},{4,5},{5,4},{6,7},{7,6},{8,9},{9,8},{10,11... | collective-permute-start | bytes 786440 | tf_op jit(solution)/shard_map/last_swap/ppermute | solution.py:390
  77.5 0.1 squares.1.refs_4_
  77.6 0.4 collective-permute-done.7.refs_3_
  78.0 0.0 copy-done
  78.0 1.6 %update.1 = (f32[99,1024]{1,0:T(8,128)}, f32[1,99]{1,0:T(1,128)}) custom-call(s32[2]{0:T(128)S(1)} %pad_add_fusion.where.refs_0_, s32[1]{0:T(128)S(6)} %copy.11.refs_1_, f32[16,8,512]{2,1,0:T(8,128)S(1)} %all-to-all-done.2.refs_0_.refs_2_, f32[16,8,512]{2,1,0:T(8,128)S(1)} %collective-permute-done.7.refs_3_, f32[8,512]{1,0:T(8,128)S(1)} %squares.1.refs_4_, ...), custom_call_target="tpu_custom_call" | custom-call | tf_op jit(solution)/shard_map/update/update/pallas_call | solution.py:400
  (4 shorter events, 0.1 us)
Async XLA Ops:
  0.7 11.6 %copy-start.1 = (f32[99,512]{1,0:T(8,128)S(1)}, f32[99,512]{1,0:T(8,128)}, u32[]{:S(2)}) copy-start(f32[99,512]{1,0:T(8,128)} %truth.1) | copy-start | bytes 608260
  0.7 11.6 %copy-start.2 = (f32[640]{0:T(1024)S(1)}, f32[640]{0:T(1024)}, u32[]{:S(2)}) copy-start(f32[640]{0:T(1024)} %param.13) | copy-start | bytes 7684
  0.7 11.6 %copy-start.3 = (s32[512]{0:T(512)S(1)}, s32[512]{0:T(512)}, u32[]{:S(2)}) copy-start(s32[512]{0:T(512)} %param.14) | copy-start | bytes 6148
  0.7 11.6 %copy-start.4 = (f32[99]{0:T(128)S(1)}, f32[99]{0:T(128)}, u32[]{:S(2)}) copy-start(f32[99]{0:T(128)} %param.10) | copy-start | bytes 1192
  3.1 12.0 %collective-permute-start.2 = (f32[4,104,128]{2,1,0:T(8,128)S(1)}, f32[4,104,128]{2,1,0:T(8,128)S(1)}, u32[]{:S(2)}, u32[]{:S(2)}) collective-permute-start(f32[4,104,128]{2,1,0:T(8,128)S(1)} %get-tuple-element.31), channel_id=1, source_target_pairs={{0,128},{64,192},{128,0},{192,64},{1,129},{65,193},{129,1},{193,65... | collective-permute-start | bytes 638984 | tf_op jit(solution)/shard_map/forward_far/ppermute | solution.py:258
  9.6 17.2 %copy-start.5 = (f32[99]{0:T(128)S(1)}, f32[99]{0:T(128)}, u32[]{:S(2)}) copy-start(f32[99]{0:T(128)} %param.12) | copy-start | bytes 1192
  9.6 7.3 %collective-permute-start = (f32[4,104,128]{2,1,0:T(8,128)S(1)}, f32[4,104,128]{2,1,0:T(8,128)S(1)}, u32[]{:S(2)}, u32[]{:S(2)}) collective-permute-start(f32[4,104,128]{2,1,0:T(8,128)S(1)} %get-tuple-element.28), channel_id=1, source_target_pairs={{0,64},{64,128},{128,192},{192,0},{1,65},{65,129},{129,193},{193,1... | collective-permute-start | bytes 638984 | tf_op jit(solution)/shard_map/forward_near/ppermute | solution.py:258
  10.1 6.9 %collective-permute-start.1 = (f32[4,104,128]{2,1,0:T(8,128)S(1)}, f32[4,104,128]{2,1,0:T(8,128)S(1)}, u32[]{:S(2)}, u32[]{:S(2)}) collective-permute-start(f32[4,104,128]{2,1,0:T(8,128)S(1)} %get-tuple-element.29), channel_id=1, source_target_pairs={{0,192},{64,0},{128,64},{192,128},{1,193},{65,1},{129,65},{193,129... | collective-permute-start | bytes 638984 | tf_op jit(solution)/shard_map/forward_near/ppermute | solution.py:258
  18.4 3.9 %collective-permute-start.3 = (bf16[4,104,128]{2,1,0:T(8,128)(2,1)S(1)}, bf16[4,104,128]{2,1,0:T(8,128)(2,1)S(1)}, u32[]{:S(2)}, u32[]{:S(2)}) collective-permute-start(bf16[4,104,128]{2,1,0:T(8,128)(2,1)S(1)} %get-tuple-element.40), channel_id=1, source_target_pairs={{0,192},{64,0},{128,64},{192,128},{1,193},{65,1},{129,65},{193,129... | collective-permute-start | bytes 319496 | tf_op jit(solution)/shard_map/bracket_exchange/ppermute | solution.py:258
  20.6 5.1 %collective-permute-start.4 = (bf16[4,104,128]{2,1,0:T(8,128)(2,1)S(1)}, bf16[4,104,128]{2,1,0:T(8,128)(2,1)S(1)}, u32[]{:S(2)}, u32[]{:S(2)}) collective-permute-start(bf16[4,104,128]{2,1,0:T(8,128)(2,1)S(1)} %get-tuple-element.41), channel_id=1, source_target_pairs={{0,128},{64,192},{128,0},{192,64},{1,129},{65,193},{129,1},{193,65... | collective-permute-start | bytes 319496 | tf_op jit(solution)/shard_map/bracket_exchange/ppermute | solution.py:258
  21.3 5.5 %collective-permute-start.5 = (bf16[4,104,128]{2,1,0:T(8,128)(2,1)S(1)}, bf16[4,104,128]{2,1,0:T(8,128)(2,1)S(1)}, u32[]{:S(2)}, u32[]{:S(2)}) collective-permute-start(bf16[4,104,128]{2,1,0:T(8,128)(2,1)S(1)} %get-tuple-element.42), channel_id=1, source_target_pairs={{0,64},{64,128},{128,192},{192,0},{1,65},{65,129},{129,193},{193,1... | collective-permute-start | bytes 319496 | tf_op jit(solution)/shard_map/bracket_exchange/ppermute | solution.py:258
  28.0 4.5 %collective-permute-start.6 = (f32[16,8,512]{2,1,0:T(8,128)S(1)}, f32[16,8,512]{2,1,0:T(8,128)S(1)}, u32[]{:S(2)}, u32[]{:S(2)}) collective-permute-start(f32[16,8,512]{2,1,0:T(8,128)S(1)} %get-tuple-element.46), channel_id=1, source_target_pairs={{0,1},{1,0},{2,3},{3,2},{4,5},{5,4},{6,7},{7,6},{8,9},{9,8},{10,11... | collective-permute-start | bytes 786440 | tf_op jit(solution)/shard_map/backward_partner_half/ppermute | solution.py:349
  32.4 45.6 %copy-start = (f32[99,1024]{1,0:T(8,128)S(1)}, f32[99,1024]{1,0:T(8,128)}, u32[]{:S(2)}) copy-start(f32[99,1024]{1,0:T(8,128)} %refs_5_.1) | copy-start | bytes 1216516
  61.5 10.9 %all-to-all-start.2 = ((f32[16,8,512]{2,1,0:T(8,128)}), f32[16,8,512]{2,1,0:T(8,128)S(1)}, u32[]{:S(2)}, u32[]{:S(2)}) async-start(f32[16,8,512]{2,1,0:T(8,128)} %broadcast_in_dim.7), calls=%async_computation.2 | async-start | bytes 524288 | tf_op jit(solution)/shard_map/gradient_sum/all_to_all | solution.py:367
  72.5 5.5 %collective-permute-start.7 = (f32[16,8,512]{2,1,0:T(8,128)S(1)}, f32[16,8,512]{2,1,0:T(8,128)S(1)}, u32[]{:S(2)}, u32[]{:S(2)}) collective-permute-start(f32[16,8,512]{2,1,0:T(8,128)S(1)} %all-to-all-done.2.refs_0_.refs_2_), channel_id=1, source_target_pairs={{0,1},{1,0},{2,3},{3,2},{4,5},{5,4},{6,7},{7,6},{8,9},{9,8},{10,11... | collective-permute-start | bytes 786440 | tf_op jit(solution)/shard_map/last_swap/ppermute | solution.py:390

commit v4 on v3

--- a/solution.py
+++ b/solution.py
@@ -34,36 +34,43 @@
     return jnp.concatenate([value, jnp.zeros((rows - value.shape[0], value.shape[1]), value.dtype)], axis=0)
 
 
-def decode(half, features, out):
-    for m in range(out.shape[0]):
-        out[m] = lax.dot_general(half[...], features[m], (((1,), (1,)), ((), ())), preferred_element_type=F32)
+def decode(half, features):
+    return lax.dot_general(half[...], features, (((1,), (1,)), ((), ())), preferred_element_type=F32)
 
 
 def fetch_chunks(where, hidden, held, sem, ks):
-    chunk = held.shape[2]
+    local, chunk = held.shape[1:3]
     copies = []
     for slot, k in enumerate(ks):
         start = pl.multiple_of(lax.rem(where[0] + k, GROUPS) * chunk, chunk)
-        copies.append(pltpu.make_async_copy(hidden.at[:, pl.ds(start, chunk), :], held.at[slot], sem.at[slot]))
-        copies[slot].start()
+        copies.append(
+            [
+                pltpu.make_async_copy(hidden.at[m, pl.ds(start, chunk), :], held.at[slot, m], sem.at[slot, m])
+                for m in range(local)
+            ]
+        )
+        for copy in copies[slot]:
+            copy.start()
     return copies
 
 
 def far_kernel(where, hidden, weight, out, half, held, w, sem, weight_sem):
     fetch = pltpu.make_async_copy(weight, w, weight_sem)
     fetch.start()
-    copies = fetch_chunks(where, hidden, held, sem, (2,))
+    (copies,) = fetch_chunks(where, hidden, held, sem, (2,))
     fetch.wait()
     half[...] = padded(w[...], half.shape[0]).astype(BF16)
-    copies[0].wait()
-    decode(half, held.at[0], out)
+    for m, copy in enumerate(copies):
+        copy.wait()
+        out[m] = decode(half, held[0, m])
 
 
 def near_kernel(where, hidden, half, after, before, held, sem):
     copies = fetch_chunks(where, hidden, held, sem, (1, 3))
     for slot, out in enumerate((after, before)):
-        copies[slot].wait()
-        decode(half, held.at[slot], out)
+        for m, copy in enumerate(copies[slot]):
+            copy.wait()
+            out[m] = decode(half, held[slot, m])
 
 
 def add_pair(total, i, j, s):
@@ -126,10 +133,12 @@
     area[...] = jnp.sum(total, axis=0, keepdims=True)
     mine = pl.multiple_of(where[0] * chunk, chunk)
     shift[...] = as_column(intercept[...], shift.shape[0]) - padded(truth[:, pl.ds(mine, chunk)], shift.shape[0])
-    copies[0].wait()
-    decode(half, held.at[0], out)
-    for copy in copies[1:]:
+    for m, copy in enumerate(copies[0]):
         copy.wait()
+        out[m] = decode(half, held[0, m])
+    for chunk_copies in copies[1:]:
+        for copy in chunk_copies:
+            copy.wait()
 
 
 def pieces_of(acc, extra, out):
@@ -138,35 +147,51 @@
         out[r] = jnp.where(last, extra, acc[PIECE_ROWS * r : PIECE_ROWS * r + 8, :])
 
 
-def gradient_half(side, weighted, held, acc):
-    _, rows, depth = weighted.shape
+def weigh(where, k, bracket, area, scale):
+    local, _, chunk = bracket.shape
+    start = pl.multiple_of(lax.rem(where[0] + k, GROUPS) * chunk, chunk)
+    point_scale = area[:, pl.ds(start, chunk)] * scale
+    return jnp.concatenate([(point_scale * bracket[m].astype(F32)).astype(BF16) for m in range(local)], axis=1)
+
+
+def bias_of(w):
+    ones = jnp.ones((8, w.shape[1]), BF16)
+    return lax.dot_general(ones, w, (((1,), (1,)), ((), ())), preferred_element_type=F32)
+
+
+def early_backward_kernel(where, held, b0, b1, var, area, weighted, total, bias):
+    local, rows, chunk = b0.shape
+    depth, features = local * chunk, total.shape[1]
+    scale = as_column(var[...], rows)
+    w0 = weigh(where, 0, b0, area, scale)
+    w1 = weigh(where, 1, b1, area, scale)
+    weighted[0], weighted[1] = w0, w1
+    bias[...] = bias_of(w0) + bias_of(w1)
+    total[...] = jnp.dot(w0, held[0].reshape(depth, features), preferred_element_type=F32) + jnp.dot(
+        w1, held[1].reshape(depth, features), preferred_element_type=F32
+    )
+
+
+def late_half(side, w2, w3, held, early, acc):
+    rows, depth = w2.shape
     half = acc.shape[1]
     lanes = pl.ds(pl.multiple_of(side * half, half), half)
-    total = None
-    for k in range(GROUPS):
-        part = jnp.dot(weighted[k], held[k, :, :, lanes].reshape(depth, half), preferred_element_type=F32)
-        total = part if total is None else total + part
-    acc[0:rows, :] = total
+    acc[0:rows, :] = (
+        early[:, lanes]
+        + jnp.dot(w2, held[2, :, :, lanes].reshape(depth, half), preferred_element_type=F32)
+        + jnp.dot(w3, held[3, :, :, lanes].reshape(depth, half), preferred_element_type=F32)
+    )
     acc[rows:, :] = jnp.zeros((acc.shape[0] - rows, half), F32)
 
 
-def partner_half_kernel(where, held, b0, b1, b2, b3, var, area, weighted, extra_out, other, acc):
-    brackets = (b0, b1, b2, b3)
-    local, rows, chunk = b0.shape
-    depth = local * chunk
-    half = acc.shape[1]
+def partner_half_kernel(where, held, b2, b3, var, area, early, early_bias, weighted, extra_out, other, acc):
+    rows, half = b2.shape[1], acc.shape[1]
     scale = as_column(var[...], rows)
-    ones = jnp.ones((8, depth), BF16)
-    bias = jnp.zeros((8, rows), F32)
-    for k in range(GROUPS):
-        start = pl.multiple_of(lax.rem(where[0] + k, GROUPS) * chunk, chunk)
-        point_scale = area[:, pl.ds(start, chunk)] * scale
-        w = jnp.concatenate(
-            [(point_scale * brackets[k][m].astype(F32)).astype(BF16) for m in range(local)], axis=1
-        )
-        weighted[k] = w
-        bias = bias + lax.dot_general(ones, w, (((1,), (1,)), ((), ())), preferred_element_type=F32)
-    gradient_half(1 - where[1], weighted, held, acc)
+    w2 = weigh(where, 2, b2, area, scale)
+    w3 = weigh(where, 3, b3, area, scale)
+    weighted[0], weighted[1] = w2, w3
+    bias = early_bias[...] + bias_of(w2) + bias_of(w3)
+    late_half(1 - where[1], w2, w3, held, early, acc)
     total = jnp.sum(area[...], axis=1, keepdims=True)
     extra = jnp.concatenate(
         [
@@ -181,17 +206,19 @@
     pieces_of(acc, extra_out[...], other)
 
 
-def own_half_kernel(where, held, weighted, extra, mine, acc):
-    gradient_half(where[1], weighted, held, acc)
+def own_half_kernel(where, held, weighted, early, extra, mine, acc):
+    late_half(where[1], weighted[0], weighted[1], held, early, acc)
     pieces_of(acc, extra[...], mine)
 
 
-def grad_hidden_kernel(where, weighted, half, piece, out, *, replicas):
+def grad_hidden_kernel(where, early, late, half, piece, out, *, replicas):
+    first = pl.program_id(0) < GROUPS // 2
     inverse = 1.0 / (piece[PIECE_ROWS : PIECE_ROWS + 1, 128:129] * (1.0 / replicas))
     chunk = out.shape[1]
     for m in range(out.shape[0]):
+        lanes = slice(m * chunk, (m + 1) * chunk)
         product = lax.dot_general(
-            weighted[0, :, m * chunk : (m + 1) * chunk], half[...], (((0,), (0,)), ((), ())), preferred_element_type=F32
+            jnp.where(first, early[0, :, lanes], late[0, :, lanes]), half[...], (((0,), (0,)), ((), ())), preferred_element_type=F32
         )
         out[m] = (product * inverse).astype(BF16)
 
@@ -267,7 +294,7 @@
             scratch_shapes=[
                 pltpu.VMEM((1, local, chunk, features), BF16),
                 pltpu.VMEM((variables, features), F32),
-                pltpu.SemaphoreType.DMA((1,)),
+                pltpu.SemaphoreType.DMA((1, local)),
                 pltpu.SemaphoreType.DMA(()),
             ],
             compiler_params=grant(53.4),
@@ -282,7 +309,7 @@
             out_specs=[VMEM] * 2,
             scratch_shapes=[
                 pltpu.VMEM((2, local, chunk, features), BF16),
-                pltpu.SemaphoreType.DMA((2,)),
+                pltpu.SemaphoreType.DMA((2, local)),
             ],
             compiler_params=grant(52),
             cost_estimate=pl.CostEstimate(
@@ -302,7 +329,7 @@
             ],
             in_specs=[SMEM, HBM] + [VMEM] * 5,
             out_specs=[VMEM] * 4,
-            scratch_shapes=[pltpu.SemaphoreType.DMA((GROUPS,))],
+            scratch_shapes=[pltpu.SemaphoreType.DMA((GROUPS, local))],
             compiler_params=grant(46),
             name="forward_local",
         )(where, hidden, half_weight, lat_weight.reshape(-1, 128), area_bin.reshape(1, points), intercept_row, analysis_truth)
@@ -330,33 +357,43 @@
         returned = [brackets[0], turn(brackets[2], -1), turn(brackets[1], -2), turn(brackets[3], -3)]
     half = features // 2
     pieces = jax.ShapeDtypeStruct((PIECES, 8, half), F32)
+    two_weighted = jax.ShapeDtypeStruct((GROUPS // 2, rows, local * chunk), BF16)
     sums = [pltpu.VMEM((PIECES * 8, half), F32)]
+    with jax.named_scope("early_backward"):
+        weighted_early, early_sum, early_bias = pl.pallas_call(
+            early_backward_kernel,
+            out_shape=[
+                two_weighted,
+                jax.ShapeDtypeStruct((rows, features), F32),
+                jax.ShapeDtypeStruct((8, rows), F32),
+            ],
+            in_specs=[SMEM] + [VMEM] * 5,
+            out_specs=[VMEM] * 3,
+            compiler_params=grant(8),
+            name="early_backward",
+        )(where, held, returned[0], returned[1], var_row, area)
     with jax.named_scope("backward_partner_half"):
-        weighted, extra, other = pl.pallas_call(
+        weighted_late, extra, other = pl.pallas_call(
             partner_half_kernel,
-            out_shape=[
-                jax.ShapeDtypeStruct((GROUPS, rows, local * chunk), BF16),
-                jax.ShapeDtypeStruct((8, half), F32),
-                pieces,
-            ],
+            out_shape=[two_weighted, jax.ShapeDtypeStruct((8, half), F32), pieces],
             in_specs=[SMEM] + [VMEM] * 7,
             out_specs=[VMEM] * 3,
             scratch_shapes=sums,
             compiler_params=grant(8),
             name="backward_partner_half",
-        )(where, held, *returned, var_row, area)
+        )(where, held, returned[2], returned[3], var_row, area, early_sum, early_bias)
         swap = [(0, 1), (1, 0)]
         other = lax.ppermute(other, "c", swap)
     with jax.named_scope("backward_own_half"):
         mine = pl.pallas_call(
             own_half_kernel,
             out_shape=pieces,
-            in_specs=[SMEM] + [VMEM] * 3,
+            in_specs=[SMEM] + [VMEM] * 4,
             out_specs=VMEM,
             scratch_shapes=sums,
             compiler_params=grant(8),
             name="backward_own_half",
-        )(where, held, weighted, extra)
+        )(where, held, weighted_late, early_sum, extra)
     with jax.named_scope("gradient_sum"):
         part = mine + other
         part = lax.all_to_all(part, ("x", "y"), 0, 0, tiled=True)
@@ -373,7 +410,8 @@
                 num_scalar_prefetch=1,
                 grid=(GROUPS,),
                 in_specs=[
-                    pl.BlockSpec((1, rows, local * chunk), lambda g, s: (g, 0, 0)),
+                    pl.BlockSpec((1, rows, local * chunk), lambda g, s: (lax.rem(g, 2), 0, 0)),
+                    pl.BlockSpec((1, rows, local * chunk), lambda g, s: (lax.rem(g, 2), 0, 0)),
                     pl.BlockSpec((rows, features), lambda g, s: (0, 0)),
                     pl.BlockSpec((8, half), lambda g, s: (0, 0)),
                 ],
@@ -384,7 +422,7 @@
                 flops=2 * rows * local * points * features, bytes_accessed=2 * hidden.size, transcendentals=0
             ),
             name="grad_hidden",
-        )(where, weighted, half_weight, piece)
+        )(where, weighted_early, weighted_late, half_weight, piece)
         own, grad_hidden = lax.optimization_barrier((own, grad_hidden))
     with jax.named_scope("last_swap"):
         partner = lax.ppermute(own, "c", swap)

time: 80 us -> 81.3 us (1.016)
  Pallas kernels: 17.6 us -> 20 us
    pallas_call x1, Pallas kernels: 2.65 us -> 3.81 us  [on_device(): pl.pallas_call(near_kernel, out_shape=[one_residual] * 2, in_specs=[SMEM,...]
    ppermute x6, waiting for transfers between devices: 6.03 us -> 5.12 us  [turn(): lax.ppermute(value, 'y', [(i, (i + k) % GROUPS) for i in range(GROUPS)])]
    pallas_call x1 -> x2, Pallas kernels: 1.21 us -> 2.12 us  [the longest x1 1.11 us: on_device(): pl.pallas_call(early_backward_kernel, out_shape=[two_weighted, jax.ShapeD...]
  transfers between devices with their start and end apart: 9 -> 9, of which waited for: 7 -> 7; matrix products, arithmetic and copies ran while one was open for 0% -> 0% of each run, Pallas kernels for 14% -> 16%
where the time goes in v4:
time: 81.3 us; the launch traced here: 81 us
  blocking collectives  28.1 us (35%)
  starting transfers between devices  21.4 us (26%)
  Pallas kernels  20 us (25%)
  waiting for transfers between devices  9.17 us (11%)
  between operations  1.41 us (2%)
    all_to_all x1, blocking collectives, on_device(): part = lax.all_to_all(part, 'z', 0, 0, tiled=True)  16 us
    all_to_all x1, blocking collectives, on_device(): part = lax.all_to_all(part, ('x', 'y'), 0, 0, tiled=True)  12.1 us
    ppermute x6, starting transfers between devices, turn(): lax.ppermute(value, 'y', [(i, (i + k) % GROUPS) for i in range(GROUPS)])  9.72 us
    ppermute x6, waiting for transfers between devices, turn(): lax.ppermute(value, 'y', [(i, (i + k) % GROUPS) for i in range(GROUPS)])  5.12 us
    ppermute x1, starting transfers between devices, on_device(): partner = lax.ppermute(own, 'c', swap)  4.38 us
    pallas_call x1, Pallas kernels, on_device(): pl.pallas_call(lambda *refs: grad_hidden_kernel(*refs, replicas=replicas)...  3.93 us
    pallas_call x1, Pallas kernels, on_device(): pl.pallas_call(near_kernel, out_shape=[one_residual] * 2, in_specs=[SMEM,...  3.81 us
    ppermute x1, starting transfers between devices, on_device(): other = lax.ppermute(other, 'c', swap)  3.68 us
  transfers between devices with their start and end apart: 9, of which 7 were waited for; matrix products, arithmetic and copies ran while one was open for 0% of the time, Pallas kernels for 16%

profile of v4, /device:TPU:1, one launch (start us, length us, event | category | flops | bytes accessed | tf_op | source)
XLA Modules:
  0.0 81.0 jit_solution(9124025990488371290)
XLA Ops:
  0.6 0.1 pad_add_fusion.where.refs_0_
  0.7 0.0 copy-start.1
  0.7 0.0 copy-start.2
  0.7 0.0 copy-start.3
  0.7 0.0 copy-start.5
  0.7 2.8 %forward_far.1 = (f32[4,104,128]{2,1,0:T(8,128)S(1)}, bf16[104,1024]{1,0:T(8,128)(2,1)S(1)}) custom-call(s32[2]{0:T(128)S(1)} %pad_add_fusion.where.refs_0_, bf16[4,512,1024]{2,1,0:T(8,128)(2,1)} %hidden.5, f32[99,1024]{1,0:T(8,128)} %refs_5_.1), custom_call_target="tpu_custom_call" | custom-call | tf_op jit(solution)/shard_map/forward_far/forward_far/pallas_call | solution.py:289
  3.5 3.8 %collective-permute-start.2 = (f32[4,104,128]{2,1,0:T(8,128)S(1)}, f32[4,104,128]{2,1,0:T(8,128)S(1)}, u32[]{:S(2)}, u32[]{:S(2)}) collective-permute-start(f32[4,104,128]{2,1,0:T(8,128)S(1)} %get-tuple-element.34), channel_id=1, source_target_pairs={{0,128},{64,192},{128,0},{192,64},{1,129},{65,193},{129,1},{193,65... | collective-permute-start | bytes 638984 | tf_op jit(solution)/shard_map/forward_far/ppermute | solution.py:285
  7.3 3.8 %forward_near.1 = (f32[4,104,128]{2,1,0:T(8,128)S(1)}, f32[4,104,128]{2,1,0:T(8,128)S(1)}) custom-call(s32[2]{0:T(128)S(1)} %pad_add_fusion.where.refs_0_, bf16[4,512,1024]{2,1,0:T(8,128)(2,1)} %hidden.5, bf16[104,1024]{1,0:T(8,128)(2,1)S(1)} %get-tuple-element.30.half.refs_3_), custom_call_target="tpu_custom_call" | custom-call | flops 218103808 | bytes 2097152 | tf_op jit(solution)/shard_map/forward_near/forward_near/pallas_call | solution.py:305
  11.2 0.0 copy-start.4
  11.2 0.5 collective-permute-start
  11.6 2.3 %collective-permute-start.1 = (f32[4,104,128]{2,1,0:T(8,128)S(1)}, f32[4,104,128]{2,1,0:T(8,128)S(1)}, u32[]{:S(2)}, u32[]{:S(2)}) collective-permute-start(f32[4,104,128]{2,1,0:T(8,128)S(1)} %get-tuple-element.32), channel_id=1, source_target_pairs={{0,192},{64,0},{128,64},{192,128},{1,193},{65,1},{129,65},{193,129... | collective-permute-start | bytes 638984 | tf_op jit(solution)/shard_map/forward_near/ppermute | solution.py:285
  13.9 0.0 copy-done.1
  13.9 0.0 copy-done.2
  13.9 0.0 copy-done.3
  13.9 0.0 copy-done.5
  13.9 2.8 %forward_local.1 = (f32[4,104,128]{2,1,0:T(8,128)S(1)}, f32[1,512]{1,0:T(1,128)S(1)}, f32[104,128]{1,0:T(8,128)S(1)}, bf16[4,4,128,1024]{3,2,1,0:T(8,128)(2,1)S(1)}) custom-call(s32[2]{0:T(128)S(1)} %pad_add_fusion.where.refs_0_, bf16[4,512,1024]{2,1,0:T(8,128)(2,1)} %hidden.5, bf16[104,1024]{1,0:T(8,128)(2,1)S(1)} %get-tuple-element.30.half.refs_3_, ...), custom_call_target="tpu_custom_call" | custom-call | tf_op jit(solution)/shard_map/forward_local/forward_local/pallas_call | solution.py:322
  16.8 0.0 collective-permute-done.2.far.refs_1_
  16.8 0.5 early_pairs.1.refs_5_
  17.3 1.0 %collective-permute-done.refs_2_ = f32[4,104,128]{2,1,0:T(8,128)S(1)} collective-permute-done((f32[4,104,128]{2,1,0:T(8,128)S(1)}, f32[4,104,128]{2,1,0:T(8,128)S(1)}, u32[]{:S(2)}, u32[]{:S(2)}) %collective-permute-start) | collective-permute-done | bytes 213024 | tf_op jit(solution)/shard_map/forward_near/ppermute | solution.py:285
  18.3 0.0 collective-permute-done.1.refs_3_
  18.3 1.5 %late_pairs.1 = (bf16[4,104,128]{2,1,0:T(8,128)(2,1)S(1)}, bf16[4,104,128]{2,1,0:T(8,128)(2,1)S(1)}, bf16[4,104,128]{2,1,0:T(8,128)(2,1)S(1)}, bf16[4,104,128]{2,1,0:T(8,128)(2,1)S(1)}) custom-call(f32[4,104,128]{2,1,0:T(8,128)S(1)} %get-tuple-element.33.here.refs_0_, f32[4,104,128]{2,1,0:T(8,128)S(1)} %collective-permute-done.2.far.refs_1_, ...), custom_call_target="tpu_custom_call" | custom-call | tf_op jit(solution)/shard_map/late_pairs/late_pairs/pallas_call | solution.py:347
  19.7 2.5 %collective-permute-start.5 = (bf16[4,104,128]{2,1,0:T(8,128)(2,1)S(1)}, bf16[4,104,128]{2,1,0:T(8,128)(2,1)S(1)}, u32[]{:S(2)}, u32[]{:S(2)}) collective-permute-start(bf16[4,104,128]{2,1,0:T(8,128)(2,1)S(1)} %get-tuple-element.46), channel_id=1, source_target_pairs={{0,192},{64,0},{128,64},{192,128},{1,193},{65,1},{129,65},{193,129... | collective-permute-start | bytes 319496 | tf_op jit(solution)/shard_map/bracket_exchange/ppermute | solution.py:285
  22.2 0.0 collective-permute-start.3
  22.2 0.7 collective-permute-start.4
  22.9 2.1 %collective-permute-done.5.b1 = bf16[4,104,128]{2,1,0:T(8,128)(2,1)S(1)} collective-permute-done((bf16[4,104,128]{2,1,0:T(8,128)(2,1)S(1)}, bf16[4,104,128]{2,1,0:T(8,128)(2,1)S(1)}, u32[]{:S(2)}, u32[]{:S(2)}) %collective-permute-start.5) | collective-permute-done | bytes 106528 | tf_op jit(solution)/shard_map/bracket_exchange/ppermute | solution.py:285
  25.0 0.0 copy-done.4
  25.0 1.1 %early_backward.1 = (bf16[2,104,512]{2,1,0:T(8,128)(2,1)S(1)}, f32[104,1024]{1,0:T(8,128)S(1)}, f32[8,104]{1,0:T(8,128)S(1)}) custom-call(s32[2]{0:T(128)S(1)} %pad_add_fusion.where.refs_0_, bf16[4,4,128,1024]{3,2,1,0:T(8,128)(2,1)S(1)} %get-tuple-element.38.held, bf16[4,104,128]{2,1,0:T(8,128)(2,1)S(1)} %get-tuple-element.45.b0, ...), custom_call_target="tpu_custom_call" | custom-call | tf_op jit(solution)/shard_map/early_backward/early_backward/pallas_call | solution.py:363
  26.1 1.3 %collective-permute-done.3.b2 = bf16[4,104,128]{2,1,0:T(8,128)(2,1)S(1)} collective-permute-done((bf16[4,104,128]{2,1,0:T(8,128)(2,1)S(1)}, bf16[4,104,128]{2,1,0:T(8,128)(2,1)S(1)}, u32[]{:S(2)}, u32[]{:S(2)}) %collective-permute-start.3) | collective-permute-done | bytes 106528 | tf_op jit(solution)/shard_map/bracket_exchange/ppermute | solution.py:285
  27.4 0.7 collective-permute-done.4.b3
  28.1 1.0 %backward_partner_half.1 = (bf16[2,104,512]{2,1,0:T(8,128)(2,1)S(1)}, f32[8,512]{1,0:T(8,128)S(1)}, f32[16,8,512]{2,1,0:T(8,128)S(1)}) custom-call(s32[2]{0:T(128)S(1)} %pad_add_fusion.where.refs_0_, bf16[4,4,128,1024]{3,2,1,0:T(8,128)(2,1)S(1)} %get-tuple-element.38.held, bf16[4,104,128]{2,1,0:T(8,128)(2,1)S(1)} %collective-permute-done.3.b2, ...), custom_call_target="tpu_custom_call" | custom-call | tf_op jit(solution)/shard_map/backward_partner_half/backward_partner_half/pallas_call | solution.py:376
  29.1 3.7 %collective-permute-start.6 = (f32[16,8,512]{2,1,0:T(8,128)S(1)}, f32[16,8,512]{2,1,0:T(8,128)S(1)}, u32[]{:S(2)}, u32[]{:S(2)}) collective-permute-start(f32[16,8,512]{2,1,0:T(8,128)S(1)} %get-tuple-element.51), channel_id=1, source_target_pairs={{0,1},{1,0},{2,3},{3,2},{4,5},{5,4},{6,7},{7,6},{8,9},{9,8},{10,11... | collective-permute-start | bytes 786440 | tf_op jit(solution)/shard_map/backward_partner_half/ppermute | solution.py:386
  32.8 0.9 %backward_own_half.1 = f32[16,8,512]{2,1,0:T(8,128)S(1)} custom-call(s32[2]{0:T(128)S(1)} %pad_add_fusion.where.refs_0_, bf16[4,4,128,1024]{3,2,1,0:T(8,128)(2,1)S(1)} %get-tuple-element.38.held, bf16[2,104,512]{2,1,0:T(8,128)(2,1)S(1)} %get-tuple-element.49.weighted.refs_2_, f32[104,1024]{1,0:T(8,128)S(1)} %get-tuple-element.47.early, ...), custom_call_target="tpu_custom_call" | custom-call | tf_op jit(solution)/shard_map/backward_own_half/backward_own_half/pallas_call | solution.py:388
  33.7 0.0 copy-start
  33.7 0.3 collective-permute-done.6
  34.0 12.1 %all_to_all.15 = f32[16,8,512]{2,1,0:T(8,128)S(1)} all-to-all(f32[16,8,512]{2,1,0:T(8,128)S(1)} %add.3), channel_id=1, replica_groups=mesh['y'=4,'z'=8,'x'=4,'c'=2] {'x','y'}, dimensions={0} | all-to-all | bytes 524288 | tf_op jit(solution)/shard_map/gradient_sum/all_to_all | solution.py:399
  46.1 16.0 %all_to_all.16 = f32[8,8,512]{2,1,0:T(8,128)S(1)} all-to-all(f32[8,8,512]{2,1,0:T(8,128)S(1)} %broadcast_in_dim.6), channel_id=1, replica_groups=mesh['y'=4,'z'=8,'x'=4,'c'=2] {'z'}, dimensions={0} | all-to-all | bytes 262144 | tf_op jit(solution)/shard_map/gradient_sum/all_to_all | solution.py:402
  62.2 0.7 broadcast_in_dim.7
  62.9 3.6 %all-to-all-start.2 = ((f32[16,8,512]{2,1,0:T(8,128)}), f32[16,8,512]{2,1,0:T(8,128)S(1)}, u32[]{:S(2)}, u32[]{:S(2)}) async-start(f32[16,8,512]{2,1,0:T(8,128)} %broadcast_in_dim.7), calls=%async_computation.2 | async-start | bytes 524288 | tf_op jit(solution)/shard_map/gradient_sum/all_to_all | solution.py:404
  66.5 3.9 %grad_hidden.1 = bf16[4,512,1024]{2,1,0:T(8,128)(2,1)} custom-call(s32[2]{0:T(128)S(1)} %pad_add_fusion.where.refs_0_, bf16[2,104,512]{2,1,0:T(8,128)(2,1)S(1)} %get-tuple-element.52.refs_1_, bf16[2,104,512]{2,1,0:T(8,128)(2,1)S(1)} %get-tuple-element.49.weighted.refs_2_, bf16[104,1024]{1,0:T(8,128)(2,1)S(1)} %get-tuple-element.30.half.refs_3_, ...), custom_call_target="tpu_custom_call" | custom-call | flops 436207616 | bytes 4194304 | tf_op jit(solution)/shard_map/grad_hidden/grad_hidden/pallas_call | solution.py:406
  70.5 3.4 %all-to-all-done.2.refs_0_.refs_2_ = f32[16,8,512]{2,1,0:T(8,128)S(1)} async-done(((f32[16,8,512]{2,1,0:T(8,128)}), f32[16,8,512]{2,1,0:T(8,128)S(1)}, u32[]{:S(2)}, u32[]{:S(2)}) %all-to-all-start.2) | async-done | bytes 262176 | tf_op jit(solution)/shard_map/gradient_sum/all_to_all | solution.py:404
  73.8 4.4 %collective-permute-start.7 = (f32[16,8,512]{2,1,0:T(8,128)S(1)}, f32[16,8,512]{2,1,0:T(8,128)S(1)}, u32[]{:S(2)}, u32[]{:S(2)}) collective-permute-start(f32[16,8,512]{2,1,0:T(8,128)S(1)} %all-to-all-done.2.refs_0_.refs_2_), channel_id=1, source_target_pairs={{0,1},{1,0},{2,3},{3,2},{4,5},{5,4},{6,7},{7,6},{8,9},{9,8},{10,11... | collective-permute-start | bytes 786440 | tf_op jit(solution)/shard_map/last_swap/ppermute | solution.py:428
  78.9 0.1 squares.1.refs_4_
  79.0 0.4 collective-permute-done.7.refs_3_
  79.4 0.0 copy-done
  79.4 1.6 %update.1 = (f32[99,1024]{1,0:T(8,128)}, f32[1,99]{1,0:T(1,128)}) custom-call(s32[2]{0:T(128)S(1)} %pad_add_fusion.where.refs_0_, s32[1]{0:T(128)S(6)} %copy.11.refs_1_, f32[16,8,512]{2,1,0:T(8,128)S(1)} %all-to-all-done.2.refs_0_.refs_2_, f32[16,8,512]{2,1,0:T(8,128)S(1)} %collective-permute-done.7.refs_3_, f32[8,512]{1,0:T(8,128)S(1)} %squares.1.refs_4_, ...), custom_call_target="tpu_custom_call" | custom-call | tf_op jit(solution)/shard_map/update/update/pallas_call | solution.py:438
  (4 shorter events, 0.1 us)
Async XLA Ops:
  0.7 13.2 %copy-start.1 = (f32[99,512]{1,0:T(8,128)S(1)}, f32[99,512]{1,0:T(8,128)}, u32[]{:S(2)}) copy-start(f32[99,512]{1,0:T(8,128)} %truth.1) | copy-start | bytes 608260
  0.7 13.2 %copy-start.2 = (f32[640]{0:T(1024)S(1)}, f32[640]{0:T(1024)}, u32[]{:S(2)}) copy-start(f32[640]{0:T(1024)} %param.13) | copy-start | bytes 7684
  0.7 13.2 %copy-start.3 = (s32[512]{0:T(512)S(1)}, s32[512]{0:T(512)}, u32[]{:S(2)}) copy-start(s32[512]{0:T(512)} %param.14) | copy-start | bytes 6148
  0.7 13.2 %copy-start.5 = (f32[99]{0:T(128)S(1)}, f32[99]{0:T(128)}, u32[]{:S(2)}) copy-start(f32[99]{0:T(128)} %param.10) | copy-start | bytes 1192
  3.5 13.3 %collective-permute-start.2 = (f32[4,104,128]{2,1,0:T(8,128)S(1)}, f32[4,104,128]{2,1,0:T(8,128)S(1)}, u32[]{:S(2)}, u32[]{:S(2)}) collective-permute-start(f32[4,104,128]{2,1,0:T(8,128)S(1)} %get-tuple-element.34), channel_id=1, source_target_pairs={{0,128},{64,192},{128,0},{192,64},{1,129},{65,193},{129,1},{193,65... | collective-permute-start | bytes 638984 | tf_op jit(solution)/shard_map/forward_far/ppermute | solution.py:285
  11.2 13.8 %copy-start.4 = (f32[99]{0:T(128)S(1)}, f32[99]{0:T(128)}, u32[]{:S(2)}) copy-start(f32[99]{0:T(128)} %param.12) | copy-start | bytes 1192
  11.2 7.1 %collective-permute-start = (f32[4,104,128]{2,1,0:T(8,128)S(1)}, f32[4,104,128]{2,1,0:T(8,128)S(1)}, u32[]{:S(2)}, u32[]{:S(2)}) collective-permute-start(f32[4,104,128]{2,1,0:T(8,128)S(1)} %get-tuple-element.31), channel_id=1, source_target_pairs={{0,64},{64,128},{128,192},{192,0},{1,65},{65,129},{129,193},{193,1... | collective-permute-start | bytes 638984 | tf_op jit(solution)/shard_map/forward_near/ppermute | solution.py:285
  11.6 6.6 %collective-permute-start.1 = (f32[4,104,128]{2,1,0:T(8,128)S(1)}, f32[4,104,128]{2,1,0:T(8,128)S(1)}, u32[]{:S(2)}, u32[]{:S(2)}) collective-permute-start(f32[4,104,128]{2,1,0:T(8,128)S(1)} %get-tuple-element.32), channel_id=1, source_target_pairs={{0,192},{64,0},{128,64},{192,128},{1,193},{65,1},{129,65},{193,129... | collective-permute-start | bytes 638984 | tf_op jit(solution)/shard_map/forward_near/ppermute | solution.py:285
  19.7 5.2 %collective-permute-start.5 = (bf16[4,104,128]{2,1,0:T(8,128)(2,1)S(1)}, bf16[4,104,128]{2,1,0:T(8,128)(2,1)S(1)}, u32[]{:S(2)}, u32[]{:S(2)}) collective-permute-start(bf16[4,104,128]{2,1,0:T(8,128)(2,1)S(1)} %get-tuple-element.46), channel_id=1, source_target_pairs={{0,192},{64,0},{128,64},{192,128},{1,193},{65,1},{129,65},{193,129... | collective-permute-start | bytes 319496 | tf_op jit(solution)/shard_map/bracket_exchange/ppermute | solution.py:285
  22.2 5.2 %collective-permute-start.3 = (bf16[4,104,128]{2,1,0:T(8,128)(2,1)S(1)}, bf16[4,104,128]{2,1,0:T(8,128)(2,1)S(1)}, u32[]{:S(2)}, u32[]{:S(2)}) collective-permute-start(bf16[4,104,128]{2,1,0:T(8,128)(2,1)S(1)} %get-tuple-element.42), channel_id=1, source_target_pairs={{0,128},{64,192},{128,0},{192,64},{1,129},{65,193},{129,1},{193,65... | collective-permute-start | bytes 319496 | tf_op jit(solution)/shard_map/bracket_exchange/ppermute | solution.py:285
  22.2 5.9 %collective-permute-start.4 = (bf16[4,104,128]{2,1,0:T(8,128)(2,1)S(1)}, bf16[4,104,128]{2,1,0:T(8,128)(2,1)S(1)}, u32[]{:S(2)}, u32[]{:S(2)}) collective-permute-start(bf16[4,104,128]{2,1,0:T(8,128)(2,1)S(1)} %get-tuple-element.43), channel_id=1, source_target_pairs={{0,64},{64,128},{128,192},{192,0},{1,65},{65,129},{129,193},{193,1... | collective-permute-start | bytes 319496 | tf_op jit(solution)/shard_map/bracket_exchange/ppermute | solution.py:285
  29.1 4.8 %collective-permute-start.6 = (f32[16,8,512]{2,1,0:T(8,128)S(1)}, f32[16,8,512]{2,1,0:T(8,128)S(1)}, u32[]{:S(2)}, u32[]{:S(2)}) collective-permute-start(f32[16,8,512]{2,1,0:T(8,128)S(1)} %get-tuple-element.51), channel_id=1, source_target_pairs={{0,1},{1,0},{2,3},{3,2},{4,5},{5,4},{6,7},{7,6},{8,9},{9,8},{10,11... | collective-permute-start | bytes 786440 | tf_op jit(solution)/shard_map/backward_partner_half/ppermute | solution.py:386
  33.7 45.7 %copy-start = (f32[99,1024]{1,0:T(8,128)S(1)}, f32[99,1024]{1,0:T(8,128)}, u32[]{:S(2)}) copy-start(f32[99,1024]{1,0:T(8,128)} %refs_5_.1) | copy-start | bytes 1216516
  62.9 10.9 %all-to-all-start.2 = ((f32[16,8,512]{2,1,0:T(8,128)}), f32[16,8,512]{2,1,0:T(8,128)S(1)}, u32[]{:S(2)}, u32[]{:S(2)}) async-start(f32[16,8,512]{2,1,0:T(8,128)} %broadcast_in_dim.7), calls=%async_computation.2 | async-start | bytes 524288 | tf_op jit(solution)/shard_map/gradient_sum/all_to_all | solution.py:404
  73.8 5.5 %collective-permute-start.7 = (f32[16,8,512]{2,1,0:T(8,128)S(1)}, f32[16,8,512]{2,1,0:T(8,128)S(1)}, u32[]{:S(2)}, u32[]{:S(2)}) collective-permute-start(f32[16,8,512]{2,1,0:T(8,128)S(1)} %all-to-all-done.2.refs_0_.refs_2_), channel_id=1, source_target_pairs={{0,1},{1,0},{2,3},{3,2},{4,5},{5,4},{6,7},{7,6},{8,9},{9,8},{10,11... | collective-permute-start | bytes 786440 | tf_op jit(solution)/shard_map/last_swap/ppermute | solution.py:428

commit v5 on v4

--- a/solution.py
+++ b/solution.py
@@ -34,43 +34,35 @@
     return jnp.concatenate([value, jnp.zeros((rows - value.shape[0], value.shape[1]), value.dtype)], axis=0)
 
 
-def decode(half, features):
-    return lax.dot_general(half[...], features, (((1,), (1,)), ((), ())), preferred_element_type=F32)
-
-
-def fetch_chunks(where, hidden, held, sem, ks):
-    local, chunk = held.shape[1:3]
-    copies = []
-    for slot, k in enumerate(ks):
-        start = pl.multiple_of(lax.rem(where[0] + k, GROUPS) * chunk, chunk)
-        copies.append(
-            [
-                pltpu.make_async_copy(hidden.at[m, pl.ds(start, chunk), :], held.at[slot, m], sem.at[slot, m])
-                for m in range(local)
-            ]
-        )
-        for copy in copies[slot]:
-            copy.start()
-    return copies
-
-
-def far_kernel(where, hidden, weight, out, half, held, w, sem, weight_sem):
-    fetch = pltpu.make_async_copy(weight, w, weight_sem)
+def chunk_at(where, k, chunk):
+    return pl.ds(pl.multiple_of(lax.rem(where[0] + k, GROUPS) * chunk, chunk), chunk)
+
+
+def features_at(hidden, points):
+    return jnp.concatenate([hidden[m, points, :] for m in range(hidden.shape[0])], axis=0)
+
+
+def decode(half, features, out):
+    values = lax.dot_general(half[...], features, (((1,), (1,)), ((), ())), preferred_element_type=F32)
+    chunk = out.shape[2]
+    for m in range(out.shape[0]):
+        out[m] = values[:, m * chunk : (m + 1) * chunk]
+
+
+def far_kernel(where, hidden, weight, out, half, held, w, sem):
+    fetch = pltpu.make_async_copy(weight, w, sem.at[0])
     fetch.start()
-    (copies,) = fetch_chunks(where, hidden, held, sem, (2,))
+    copy = pltpu.make_async_copy(hidden.at[:, chunk_at(where, 2, out.shape[2]), :], held, sem.at[1])
+    copy.start()
     fetch.wait()
     half[...] = padded(w[...], half.shape[0]).astype(BF16)
-    for m, copy in enumerate(copies):
-        copy.wait()
-        out[m] = decode(half, held[0, m])
-
-
-def near_kernel(where, hidden, half, after, before, held, sem):
-    copies = fetch_chunks(where, hidden, held, sem, (1, 3))
-    for slot, out in enumerate((after, before)):
-        for m, copy in enumerate(copies[slot]):
-            copy.wait()
-            out[m] = decode(half, held[slot, m])
+    copy.wait()
+    decode(half, held[...].reshape(-1, held.shape[2]), out)
+
+
+def near_kernel(where, hidden, half, after, before):
+    for k, out in ((1, after), (3, before)):
+        decode(half, features_at(hidden, chunk_at(where, k, out.shape[2])), out)
 
 
 def add_pair(total, i, j, s):
@@ -119,9 +111,8 @@
         outs[j // local][j % local] = scratch[j].astype(BF16)
 
 
-def local_kernel(where, hidden, half, lat, area_bin, intercept, truth, out, area, shift, held, sem):
-    chunk = held.shape[2]
-    copies = fetch_chunks(where, hidden, held, sem, range(GROUPS))
+def local_kernel(where, hidden, half, lat, area_bin, intercept, truth, var, out, area, weight, shift):
+    rows, chunk = shift.shape
     cells, width = lat.shape
     points = area_bin.shape[1]
     bins = jnp.broadcast_to(area_bin[...], (width, points))
@@ -130,15 +121,12 @@
     for q in range(cells):
         column = as_column(lat[q : q + 1, :], width)
         total = total + jnp.where(bins == level + q * width, column, 0.0)
-    area[...] = jnp.sum(total, axis=0, keepdims=True)
-    mine = pl.multiple_of(where[0] * chunk, chunk)
-    shift[...] = as_column(intercept[...], shift.shape[0]) - padded(truth[:, pl.ds(mine, chunk)], shift.shape[0])
-    for m, copy in enumerate(copies[0]):
-        copy.wait()
-        out[m] = decode(half, held[0, m])
-    for chunk_copies in copies[1:]:
-        for copy in chunk_copies:
-            copy.wait()
+    by_point = jnp.sum(total, axis=0, keepdims=True)
+    area[...] = jnp.broadcast_to(jnp.sum(by_point, axis=1, keepdims=True), area.shape)
+    weight[...] = by_point * as_column(var[...], rows)
+    here = chunk_at(where, 0, chunk)
+    shift[...] = as_column(intercept[...], rows) - padded(truth[:, here], rows)
+    decode(half, features_at(hidden, here), out)
 
 
 def pieces_of(acc, extra, out):
@@ -147,11 +135,10 @@
         out[r] = jnp.where(last, extra, acc[PIECE_ROWS * r : PIECE_ROWS * r + 8, :])
 
 
-def weigh(where, k, bracket, area, scale):
+def weigh(where, k, bracket, weight):
     local, _, chunk = bracket.shape
-    start = pl.multiple_of(lax.rem(where[0] + k, GROUPS) * chunk, chunk)
-    point_scale = area[:, pl.ds(start, chunk)] * scale
-    return jnp.concatenate([(point_scale * bracket[m].astype(F32)).astype(BF16) for m in range(local)], axis=1)
+    scale = weight[:, chunk_at(where, k, chunk)]
+    return jnp.concatenate([(scale * bracket[m].astype(F32)).astype(BF16) for m in range(local)], axis=1)
 
 
 def bias_of(w):
@@ -159,56 +146,52 @@
     return lax.dot_general(ones, w, (((1,), (1,)), ((), ())), preferred_element_type=F32)
 
 
-def early_backward_kernel(where, held, b0, b1, var, area, weighted, total, bias):
-    local, rows, chunk = b0.shape
-    depth, features = local * chunk, total.shape[1]
-    scale = as_column(var[...], rows)
-    w0 = weigh(where, 0, b0, area, scale)
-    w1 = weigh(where, 1, b1, area, scale)
+def early_backward_kernel(where, hidden, b0, b1, weight, weighted, total, bias):
+    chunk = b0.shape[2]
+    w0 = weigh(where, 0, b0, weight)
+    w1 = weigh(where, 1, b1, weight)
     weighted[0], weighted[1] = w0, w1
     bias[...] = bias_of(w0) + bias_of(w1)
-    total[...] = jnp.dot(w0, held[0].reshape(depth, features), preferred_element_type=F32) + jnp.dot(
-        w1, held[1].reshape(depth, features), preferred_element_type=F32
-    )
-
-
-def late_half(side, w2, w3, held, early, acc):
+    total[...] = jnp.dot(
+        w0, features_at(hidden, chunk_at(where, 0, chunk)), preferred_element_type=F32
+    ) + jnp.dot(w1, features_at(hidden, chunk_at(where, 1, chunk)), preferred_element_type=F32)
+
+
+def late_half(where, side, w2, w3, hidden, early, acc):
     rows, depth = w2.shape
+    local = hidden.shape[0]
     half = acc.shape[1]
     lanes = pl.ds(pl.multiple_of(side * half, half), half)
-    acc[0:rows, :] = (
-        early[:, lanes]
-        + jnp.dot(w2, held[2, :, :, lanes].reshape(depth, half), preferred_element_type=F32)
-        + jnp.dot(w3, held[3, :, :, lanes].reshape(depth, half), preferred_element_type=F32)
-    )
+
+    def product(w, k):
+        points = chunk_at(where, k, depth // local)
+        part = jnp.concatenate([hidden[m, points, lanes] for m in range(local)], axis=0)
+        return jnp.dot(w, part, preferred_element_type=F32)
+
+    acc[0:rows, :] = early[:, lanes] + product(w2, 2) + product(w3, 3)
     acc[rows:, :] = jnp.zeros((acc.shape[0] - rows, half), F32)
 
 
-def partner_half_kernel(where, held, b2, b3, var, area, early, early_bias, weighted, extra_out, other, acc):
-    rows, half = b2.shape[1], acc.shape[1]
-    scale = as_column(var[...], rows)
-    w2 = weigh(where, 2, b2, area, scale)
-    w3 = weigh(where, 3, b3, area, scale)
+def extra_row(bias, area, half):
+    row = jnp.concatenate([bias, area, jnp.zeros((1, half - 256), F32)], axis=1)
+    return jnp.broadcast_to(row, (8, half))
+
+
+def partner_half_kernel(where, hidden, b2, b3, weight, area, early, weighted, other, acc):
+    w2 = weigh(where, 2, b2, weight)
+    w3 = weigh(where, 3, b3, weight)
     weighted[0], weighted[1] = w2, w3
+    late_half(where, 1 - where[1], w2, w3, hidden, early, acc)
+    pieces_of(acc, extra_row(jnp.zeros((1, 128), F32), area[...], acc.shape[1]), other)
+
+
+def own_half_kernel(where, hidden, weighted, early, early_bias, area, mine, acc):
+    rows = early.shape[0]
+    w2, w3 = weighted[0], weighted[1]
+    late_half(where, where[1], w2, w3, hidden, early, acc)
     bias = early_bias[...] + bias_of(w2) + bias_of(w3)
-    late_half(1 - where[1], w2, w3, held, early, acc)
-    total = jnp.sum(area[...], axis=1, keepdims=True)
-    extra = jnp.concatenate(
-        [
-            bias[0:1],
-            jnp.zeros((1, 128 - rows), F32),
-            jnp.broadcast_to(total, (1, 128)),
-            jnp.zeros((1, half - 256), F32),
-        ],
-        axis=1,
-    )
-    extra_out[...] = jnp.broadcast_to(extra, (8, half))
-    pieces_of(acc, extra_out[...], other)
-
-
-def own_half_kernel(where, held, weighted, early, extra, mine, acc):
-    late_half(where[1], weighted[0], weighted[1], held, early, acc)
-    pieces_of(acc, extra[...], mine)
+    bias = jnp.concatenate([bias[0:1], jnp.zeros((1, 128 - rows), F32)], axis=1)
+    pieces_of(acc, extra_row(bias, area[...], acc.shape[1]), mine)
 
 
 def grad_hidden_kernel(where, early, late, half, piece, out, *, replicas):
@@ -244,7 +227,8 @@
     first = where[1] == 0
     mean_area = own[0, PIECE_ROWS : PIECE_ROWS + 1, 128:129] * (1.0 / replicas)
     inverse = 1.0 / mean_area
-    bias_grad = own[0, PIECE_ROWS : PIECE_ROWS + 1, 0:variables] * inverse
+    a, b = (side[0, PIECE_ROWS : PIECE_ROWS + 1, 0:variables] for side in (own, partner))
+    bias_grad = (jnp.where(first, a, b) + jnp.where(first, b, a)) * inverse
     a, b = squares[...], squares_of(partner, inverse)
     both = jnp.where(first, a, b) + jnp.where(first, b, a)
     total = jnp.sum(jnp.sum(both, axis=0, keepdims=True), axis=1, keepdims=True)
@@ -292,10 +276,9 @@
             in_specs=[SMEM, HBM, HBM],
             out_specs=[VMEM] * 2,
             scratch_shapes=[
-                pltpu.VMEM((1, local, chunk, features), BF16),
+                pltpu.VMEM((local, chunk, features), BF16),
                 pltpu.VMEM((variables, features), F32),
-                pltpu.SemaphoreType.DMA((1, local)),
-                pltpu.SemaphoreType.DMA(()),
+                pltpu.SemaphoreType.DMA((2,)),
             ],
             compiler_params=grant(53.4),
             name="forward_far",
@@ -305,13 +288,9 @@
         after, before = pl.pallas_call(
             near_kernel,
             out_shape=[one_residual] * 2,
-            in_specs=[SMEM, HBM, VMEM],
+            in_specs=[SMEM, VMEM, VMEM],
             out_specs=[VMEM] * 2,
-            scratch_shapes=[
-                pltpu.VMEM((2, local, chunk, features), BF16),
-                pltpu.SemaphoreType.DMA((2, local)),
-            ],
-            compiler_params=grant(52),
+            compiler_params=grant(8),
             cost_estimate=pl.CostEstimate(
                 flops=4 * rows * local * chunk * features, bytes_accessed=4 * local * chunk * features, transcendentals=0
             ),
@@ -319,20 +298,19 @@
         )(where, hidden, half_weight)
         after, before = turn(after, 1), turn(before, 3)
     with jax.named_scope("forward_local"):
-        here, area, shift, held = pl.pallas_call(
+        here, area, point_weight, shift = pl.pallas_call(
             local_kernel,
             out_shape=[
                 one_residual,
-                jax.ShapeDtypeStruct((1, points), F32),
+                jax.ShapeDtypeStruct((1, 128), F32),
+                jax.ShapeDtypeStruct((rows, points), F32),
                 jax.ShapeDtypeStruct((rows, chunk), F32),
-                jax.ShapeDtypeStruct((GROUPS, local, chunk, features), BF16),
             ],
-            in_specs=[SMEM, HBM] + [VMEM] * 5,
+            in_specs=[SMEM] + [VMEM] * 7,
             out_specs=[VMEM] * 4,
-            scratch_shapes=[pltpu.SemaphoreType.DMA((GROUPS, local))],
-            compiler_params=grant(46),
+            compiler_params=grant(8),
             name="forward_local",
-        )(where, hidden, half_weight, lat_weight.reshape(-1, 128), area_bin.reshape(1, points), intercept_row, analysis_truth)
+        )(where, hidden, half_weight, lat_weight.reshape(-1, 128), area_bin.reshape(1, points), intercept_row, analysis_truth, var_row)
     with jax.named_scope("early_pairs"):
         early = pl.pallas_call(
             early_pairs_kernel,
@@ -342,7 +320,7 @@
             compiler_params=grant(4),
             name="early_pairs",
         )(here, far, shift)
-    after, before, early, area, held = lax.optimization_barrier((after, before, early, area, held))
+    after, before, early, point_weight = lax.optimization_barrier((after, before, early, point_weight))
     with jax.named_scope("late_pairs"):
         brackets = pl.pallas_call(
             lambda *refs: late_pairs_kernel(members, *refs),
@@ -367,33 +345,33 @@
                 jax.ShapeDtypeStruct((rows, features), F32),
                 jax.ShapeDtypeStruct((8, rows), F32),
             ],
-            in_specs=[SMEM] + [VMEM] * 5,
+            in_specs=[SMEM] + [VMEM] * 4,
             out_specs=[VMEM] * 3,
-            compiler_params=grant(8),
+            compiler_params=grant(10),
             name="early_backward",
-        )(where, held, returned[0], returned[1], var_row, area)
+        )(where, hidden, returned[0], returned[1], point_weight)
     with jax.named_scope("backward_partner_half"):
-        weighted_late, extra, other = pl.pallas_call(
+        weighted_late, other = pl.pallas_call(
             partner_half_kernel,
-            out_shape=[two_weighted, jax.ShapeDtypeStruct((8, half), F32), pieces],
-            in_specs=[SMEM] + [VMEM] * 7,
-            out_specs=[VMEM] * 3,
+            out_shape=[two_weighted, pieces],
+            in_specs=[SMEM] + [VMEM] * 6,
+            out_specs=[VMEM] * 2,
             scratch_shapes=sums,
-            compiler_params=grant(8),
+            compiler_params=grant(10),
             name="backward_partner_half",
-        )(where, held, returned[2], returned[3], var_row, area, early_sum, early_bias)
+        )(where, hidden, returned[2], returned[3], point_weight, area, early_sum)
         swap = [(0, 1), (1, 0)]
         other = lax.ppermute(other, "c", swap)
     with jax.named_scope("backward_own_half"):
         mine = pl.pallas_call(
             own_half_kernel,
             out_shape=pieces,
-            in_specs=[SMEM] + [VMEM] * 4,
+            in_specs=[SMEM] + [VMEM] * 5,
             out_specs=VMEM,
             scratch_shapes=sums,
-            compiler_params=grant(8),
+            compiler_params=grant(10),
             name="backward_own_half",
-        )(where, held, weighted_late, early_sum, extra)
+        )(where, hidden, weighted_late, early_sum, early_bias, area)
     with jax.named_scope("gradient_sum"):
         part = mine + other
         part = lax.all_to_all(part, ("x", "y"), 0, 0, tiled=True)

time: 81.3 us -> 80.2 us (0.986)
  Pallas kernels: 20 us -> 15.5 us
  waiting for transfers between devices: 9.17 us -> 13.3 us
  starting transfers between devices: 21.4 us -> 20.4 us
    ppermute x6, waiting for transfers between devices: 5.12 us -> 9.34 us  [turn(): lax.ppermute(value, 'y', [(i, (i + k) % GROUPS) for i in range(GROUPS)])]
    pallas_call x1, Pallas kernels: 3.81 us -> 1.34 us  [on_device(): pl.pallas_call(near_kernel, out_shape=[one_residual] * 2, in_specs=[SMEM,...]
    pallas_call x1, Pallas kernels: 2.84 us -> 1.04 us  [on_device(): pl.pallas_call(local_kernel, out_shape=[one_residual, jax.ShapeDtypeStruc...]
    ppermute x1, starting transfers between devices: 3.68 us -> 2.3 us  [on_device(): other = lax.ppermute(other, 'c', swap)]
  transfers between devices with their start and end apart: 9 -> 9, of which waited for: 7 -> 7; matrix products, arithmetic and copies ran while one was open for 0% -> 0% of each run, Pallas kernels for 16% -> 11%
where the time goes in v5:
time: 80.2 us; the launch traced here: 79.9 us
  blocking collectives  28.3 us (35%)
  starting transfers between devices  20.4 us (25%)
  Pallas kernels  15.5 us (19%)
  waiting for transfers between devices  13.3 us (17%)
  between operations  1.43 us (2%)
    all_to_all x1, blocking collectives, on_device(): part = lax.all_to_all(part, 'z', 0, 0, tiled=True)  16 us
    all_to_all x1, blocking collectives, on_device(): part = lax.all_to_all(part, ('x', 'y'), 0, 0, tiled=True)  12.2 us
    ppermute x6, starting transfers between devices, turn(): lax.ppermute(value, 'y', [(i, (i + k) % GROUPS) for i in range(GROUPS)])  10.1 us
    ppermute x6, waiting for transfers between devices, turn(): lax.ppermute(value, 'y', [(i, (i + k) % GROUPS) for i in range(GROUPS)])  9.34 us
    ppermute x1, starting transfers between devices, on_device(): partner = lax.ppermute(own, 'c', swap)  4.38 us
    pallas_call x1, Pallas kernels, on_device(): pl.pallas_call(lambda *refs: grad_hidden_kernel(*refs, replicas=replicas)...  3.94 us
    all_to_all x1, starting transfers between devices, on_device(): lax.all_to_all(jnp.broadcast_to(piece, (PIECES, 8, half)), ('x', 'y'), 0,...  3.62 us
    all_to_all x1, waiting for transfers between devices, on_device(): lax.all_to_all(jnp.broadcast_to(piece, (PIECES, 8, half)), ('x', 'y'), 0,...  3.38 us
  transfers between devices with their start and end apart: 9, of which 7 were waited for; matrix products, arithmetic and copies ran while one was open for 0% of the time, Pallas kernels for 11%

profile of v5, /device:TPU:1, one launch (start us, length us, event | category | flops | bytes accessed | tf_op | source)
XLA Modules:
  0.0 79.9 jit_solution(6713698112004209)
XLA Ops:
  0.6 0.0 copy-start
  0.6 0.1 pad_add_fusion.where.refs_0_
  0.7 0.0 copy-start.2
  0.7 0.0 copy-start.3
  0.7 0.0 copy-start.4
  0.7 0.0 copy-start.5
  0.7 0.0 copy-start.6
  0.7 2.7 %forward_far.1 = (f32[4,104,128]{2,1,0:T(8,128)S(1)}, bf16[104,1024]{1,0:T(8,128)(2,1)S(1)}) custom-call(s32[2]{0:T(128)S(1)} %pad_add_fusion.where.refs_0_, bf16[4,512,1024]{2,1,0:T(8,128)(2,1)} %hidden.11, f32[99,1024]{1,0:T(8,128)} %refs_5_.1), custom_call_target="tpu_custom_call" | custom-call | tf_op jit(solution)/shard_map/forward_far/forward_far/pallas_call | solution.py:273
  3.4 3.8 %collective-permute-start = (f32[4,104,128]{2,1,0:T(8,128)S(1)}, f32[4,104,128]{2,1,0:T(8,128)S(1)}, u32[]{:S(2)}, u32[]{:S(2)}) collective-permute-start(f32[4,104,128]{2,1,0:T(8,128)S(1)} %get-tuple-element.30), channel_id=1, source_target_pairs={{0,128},{64,192},{128,0},{192,64},{1,129},{65,193},{129,1},{193,65... | collective-permute-start | bytes 638984 | tf_op jit(solution)/shard_map/forward_far/ppermute | solution.py:269
  7.3 0.0 copy-done
  7.3 1.3 %forward_near.1 = (f32[4,104,128]{2,1,0:T(8,128)S(1)}, f32[4,104,128]{2,1,0:T(8,128)S(1)}) custom-call(s32[2]{0:T(128)S(1)} %pad_add_fusion.where.refs_0_, bf16[4,512,1024]{2,1,0:T(8,128)(2,1)S(1)} %copy-done, bf16[104,1024]{1,0:T(8,128)(2,1)S(1)} %get-tuple-element.28.half.refs_3_), custom_call_target="tpu_custom_call" | custom-call | flops 218103808 | bytes 2097152 | tf_op jit(solution)/shard_map/forward_near/forward_near/pallas_call | solution.py:288
  8.6 0.5 collective-permute-start.1
  9.1 2.3 %collective-permute-start.2 = (f32[4,104,128]{2,1,0:T(8,128)S(1)}, f32[4,104,128]{2,1,0:T(8,128)S(1)}, u32[]{:S(2)}, u32[]{:S(2)}) collective-permute-start(f32[4,104,128]{2,1,0:T(8,128)S(1)} %get-tuple-element.32), channel_id=1, source_target_pairs={{0,192},{64,0},{128,64},{192,128},{1,193},{65,1},{129,65},{193,129... | collective-permute-start | bytes 638984 | tf_op jit(solution)/shard_map/forward_near/ppermute | solution.py:269
  11.4 0.0 copy-done.2
  11.4 0.0 copy-done.3
  11.4 0.0 copy-done.4
  11.4 0.0 copy-done.5
  11.4 0.0 copy-done.6
  11.4 1.0 %forward_local.1 = (f32[4,104,128]{2,1,0:T(8,128)S(1)}, f32[1,128]{1,0:T(1,128)S(1)}, f32[104,512]{1,0:T(8,128)S(1)}, f32[104,128]{1,0:T(8,128)S(1)}) custom-call(s32[2]{0:T(128)S(1)} %pad_add_fusion.where.refs_0_, bf16[4,512,1024]{2,1,0:T(8,128)(2,1)S(1)} %copy-done, bf16[104,1024]{1,0:T(8,128)(2,1)S(1)} %get-tuple-element.28.half.refs_3_, ...), custom_call_target="tpu_custom_call" | custom-call | tf_op jit(solution)/shard_map/forward_local/forward_local/pallas_call | solution.py:301
  12.5 0.0 collective-permute-done.far.refs_1_
  12.5 0.5 early_pairs.1.refs_5_
  12.9 5.0 %collective-permute-done.1.refs_2_ = f32[4,104,128]{2,1,0:T(8,128)S(1)} collective-permute-done((f32[4,104,128]{2,1,0:T(8,128)S(1)}, f32[4,104,128]{2,1,0:T(8,128)S(1)}, u32[]{:S(2)}, u32[]{:S(2)}) %collective-permute-start.1) | collective-permute-done | bytes 213024 | tf_op jit(solution)/shard_map/forward_near/ppermute | solution.py:269
  17.9 0.0 collective-permute-done.2.refs_3_
  17.9 1.5 %late_pairs.1 = (bf16[4,104,128]{2,1,0:T(8,128)(2,1)S(1)}, bf16[4,104,128]{2,1,0:T(8,128)(2,1)S(1)}, bf16[4,104,128]{2,1,0:T(8,128)(2,1)S(1)}, bf16[4,104,128]{2,1,0:T(8,128)(2,1)S(1)}) custom-call(f32[4,104,128]{2,1,0:T(8,128)S(1)} %get-tuple-element.29.here.refs_0_, f32[4,104,128]{2,1,0:T(8,128)S(1)} %collective-permute-done.far.refs_1_, ...), custom_call_target="tpu_custom_call" | custom-call | tf_op jit(solution)/shard_map/late_pairs/late_pairs/pallas_call | solution.py:325
  19.4 2.0 %collective-permute-start.5 = (bf16[4,104,128]{2,1,0:T(8,128)(2,1)S(1)}, bf16[4,104,128]{2,1,0:T(8,128)(2,1)S(1)}, u32[]{:S(2)}, u32[]{:S(2)}) collective-permute-start(bf16[4,104,128]{2,1,0:T(8,128)(2,1)S(1)} %get-tuple-element.43), channel_id=1, source_target_pairs={{0,192},{64,0},{128,64},{192,128},{1,193},{65,1},{129,65},{193,129... | collective-permute-start | bytes 319496 | tf_op jit(solution)/shard_map/bracket_exchange/ppermute | solution.py:269
  21.4 0.8 %collective-permute-start.3 = (bf16[4,104,128]{2,1,0:T(8,128)(2,1)S(1)}, bf16[4,104,128]{2,1,0:T(8,128)(2,1)S(1)}, u32[]{:S(2)}, u32[]{:S(2)}) collective-permute-start(bf16[4,104,128]{2,1,0:T(8,128)(2,1)S(1)} %get-tuple-element.38), channel_id=1, source_target_pairs={{0,128},{64,192},{128,0},{192,64},{1,129},{65,193},{129,1},{193,65... | collective-permute-start | bytes 319496 | tf_op jit(solution)/shard_map/bracket_exchange/ppermute | solution.py:269
  22.2 0.8 collective-permute-start.4
  22.9 0.1 collective-permute-done.5.b1
  23.1 1.0 %early_backward.1 = (bf16[2,104,512]{2,1,0:T(8,128)(2,1)S(1)}, f32[104,1024]{1,0:T(8,128)S(1)}, f32[8,104]{1,0:T(8,128)S(1)}) custom-call(s32[2]{0:T(128)S(1)} %pad_add_fusion.where.refs_0_, bf16[4,512,1024]{2,1,0:T(8,128)(2,1)S(1)} %copy-done, bf16[4,104,128]{2,1,0:T(8,128)(2,1)S(1)} %get-tuple-element.42.b0, ...), custom_call_target="tpu_custom_call" | custom-call | tf_op jit(solution)/shard_map/early_backward/early_backward/pallas_call | solution.py:341
  24.1 2.4 %collective-permute-done.3.b2 = bf16[4,104,128]{2,1,0:T(8,128)(2,1)S(1)} collective-permute-done((bf16[4,104,128]{2,1,0:T(8,128)(2,1)S(1)}, bf16[4,104,128]{2,1,0:T(8,128)(2,1)S(1)}, u32[]{:S(2)}, u32[]{:S(2)}) %collective-permute-start.3) | collective-permute-done | bytes 106528 | tf_op jit(solution)/shard_map/bracket_exchange/ppermute | solution.py:269
  26.5 1.8 %collective-permute-done.4.b3 = bf16[4,104,128]{2,1,0:T(8,128)(2,1)S(1)} collective-permute-done((bf16[4,104,128]{2,1,0:T(8,128)(2,1)S(1)}, bf16[4,104,128]{2,1,0:T(8,128)(2,1)S(1)}, u32[]{:S(2)}, u32[]{:S(2)}) %collective-permute-start.4) | collective-permute-done | bytes 106528 | tf_op jit(solution)/shard_map/bracket_exchange/ppermute | solution.py:269
  28.3 0.9 %backward_partner_half.1 = (bf16[2,104,512]{2,1,0:T(8,128)(2,1)S(1)}, f32[16,8,512]{2,1,0:T(8,128)S(1)}) custom-call(s32[2]{0:T(128)S(1)} %pad_add_fusion.where.refs_0_, bf16[4,512,1024]{2,1,0:T(8,128)(2,1)S(1)} %copy-done, bf16[4,104,128]{2,1,0:T(8,128)(2,1)S(1)} %collective-permute-done.3.b2, bf16[4,104,128]{2,1,0:T(8,128)(2,1)S(1)} %collective-permute-done.4.b3, ...), custom_call_target="tpu_custom_call" | custom-call | tf_op jit(solution)/shard_map/backward_partner_half/backward_partner_half/pallas_call | solution.py:354
  29.2 2.3 %collective-permute-start.6 = (f32[16,8,512]{2,1,0:T(8,128)S(1)}, f32[16,8,512]{2,1,0:T(8,128)S(1)}, u32[]{:S(2)}, u32[]{:S(2)}) collective-permute-start(f32[16,8,512]{2,1,0:T(8,128)S(1)} %get-tuple-element.47), channel_id=1, source_target_pairs={{0,1},{1,0},{2,3},{3,2},{4,5},{5,4},{6,7},{7,6},{8,9},{9,8},{10,11... | collective-permute-start | bytes 786440 | tf_op jit(solution)/shard_map/backward_partner_half/ppermute | solution.py:364
  31.5 0.9 %backward_own_half.1 = f32[16,8,512]{2,1,0:T(8,128)S(1)} custom-call(s32[2]{0:T(128)S(1)} %pad_add_fusion.where.refs_0_, bf16[4,512,1024]{2,1,0:T(8,128)(2,1)S(1)} %copy-done, bf16[2,104,512]{2,1,0:T(8,128)(2,1)S(1)} %get-tuple-element.45.weighted.refs_2_, f32[104,1024]{1,0:T(8,128)S(1)} %get-tuple-element.44.early, ...), custom_call_target="tpu_custom_call" | custom-call | tf_op jit(solution)/shard_map/backward_own_half/backward_own_half/pallas_call | solution.py:366
  32.4 0.0 copy-start.1
  32.4 0.2 collective-permute-done.6
  32.7 12.2 %all_to_all.15 = f32[16,8,512]{2,1,0:T(8,128)S(1)} all-to-all(f32[16,8,512]{2,1,0:T(8,128)S(1)} %add.3), channel_id=1, replica_groups=mesh['y'=4,'z'=8,'x'=4,'c'=2] {'x','y'}, dimensions={0} | all-to-all | bytes 524288 | tf_op jit(solution)/shard_map/gradient_sum/all_to_all | solution.py:377
  45.0 16.0 %all_to_all.16 = f32[8,8,512]{2,1,0:T(8,128)S(1)} all-to-all(f32[8,8,512]{2,1,0:T(8,128)S(1)} %broadcast_in_dim.6), channel_id=1, replica_groups=mesh['y'=4,'z'=8,'x'=4,'c'=2] {'z'}, dimensions={0} | all-to-all | bytes 262144 | tf_op jit(solution)/shard_map/gradient_sum/all_to_all | solution.py:380
  61.0 0.7 broadcast_in_dim.7
  61.8 3.6 %all-to-all-start.2 = ((f32[16,8,512]{2,1,0:T(8,128)}), f32[16,8,512]{2,1,0:T(8,128)S(1)}, u32[]{:S(2)}, u32[]{:S(2)}) async-start(f32[16,8,512]{2,1,0:T(8,128)} %broadcast_in_dim.7), calls=%async_computation.2 | async-start | bytes 524288 | tf_op jit(solution)/shard_map/gradient_sum/all_to_all | solution.py:382
  65.4 3.9 %grad_hidden.1 = bf16[4,512,1024]{2,1,0:T(8,128)(2,1)} custom-call(s32[2]{0:T(128)S(1)} %pad_add_fusion.where.refs_0_, bf16[2,104,512]{2,1,0:T(8,128)(2,1)S(1)} %get-tuple-element.48.refs_1_, bf16[2,104,512]{2,1,0:T(8,128)(2,1)S(1)} %get-tuple-element.45.weighted.refs_2_, bf16[104,1024]{1,0:T(8,128)(2,1)S(1)} %get-tuple-element.28.half.refs_3_, ...), custom_call_target="tpu_custom_call" | custom-call | flops 436207616 | bytes 4194304 | tf_op jit(solution)/shard_map/grad_hidden/grad_hidden/pallas_call | solution.py:384
  69.3 3.4 %all-to-all-done.2.refs_0_.refs_2_ = f32[16,8,512]{2,1,0:T(8,128)S(1)} async-done(((f32[16,8,512]{2,1,0:T(8,128)}), f32[16,8,512]{2,1,0:T(8,128)S(1)}, u32[]{:S(2)}, u32[]{:S(2)}) %all-to-all-start.2) | async-done | bytes 262176 | tf_op jit(solution)/shard_map/gradient_sum/all_to_all | solution.py:382
  72.7 4.4 %collective-permute-start.7 = (f32[16,8,512]{2,1,0:T(8,128)S(1)}, f32[16,8,512]{2,1,0:T(8,128)S(1)}, u32[]{:S(2)}, u32[]{:S(2)}) collective-permute-start(f32[16,8,512]{2,1,0:T(8,128)S(1)} %all-to-all-done.2.refs_0_.refs_2_), channel_id=1, source_target_pairs={{0,1},{1,0},{2,3},{3,2},{4,5},{5,4},{6,7},{7,6},{8,9},{9,8},{10,11... | collective-permute-start | bytes 786440 | tf_op jit(solution)/shard_map/last_swap/ppermute | solution.py:406
  77.7 0.1 squares.1.refs_4_
  77.9 0.4 collective-permute-done.7.refs_3_
  78.3 0.0 copy-done.1
  78.3 1.6 %update.1 = (f32[99,1024]{1,0:T(8,128)}, f32[1,99]{1,0:T(1,128)}) custom-call(s32[2]{0:T(128)S(1)} %pad_add_fusion.where.refs_0_, s32[1]{0:T(128)S(6)} %copy.11.refs_1_, f32[16,8,512]{2,1,0:T(8,128)S(1)} %all-to-all-done.2.refs_0_.refs_2_, f32[16,8,512]{2,1,0:T(8,128)S(1)} %collective-permute-done.7.refs_3_, f32[8,512]{1,0:T(8,128)S(1)} %squares.1.refs_4_, ...), custom_call_target="tpu_custom_call" | custom-call | tf_op jit(solution)/shard_map/update/update/pallas_call | solution.py:416
  (4 shorter events, 0.1 us)
Async XLA Ops:
  0.6 6.6 %copy-start = (bf16[4,512,1024]{2,1,0:T(8,128)(2,1)S(1)}, bf16[4,512,1024]{2,1,0:T(8,128)(2,1)}, u32[]{:S(2)}) copy-start(bf16[4,512,1024]{2,1,0:T(8,128)(2,1)} %hidden.11) | copy-start | bytes 12582916
  0.7 10.7 %copy-start.2 = (f32[99,512]{1,0:T(8,128)S(1)}, f32[99,512]{1,0:T(8,128)}, u32[]{:S(2)}) copy-start(f32[99,512]{1,0:T(8,128)} %truth.1) | copy-start | bytes 608260
  0.7 10.7 %copy-start.3 = (f32[640]{0:T(1024)S(1)}, f32[640]{0:T(1024)}, u32[]{:S(2)}) copy-start(f32[640]{0:T(1024)} %param.13) | copy-start | bytes 7684
  0.7 10.7 %copy-start.4 = (s32[512]{0:T(512)S(1)}, s32[512]{0:T(512)}, u32[]{:S(2)}) copy-start(s32[512]{0:T(512)} %param.14) | copy-start | bytes 6148
  0.7 10.7 %copy-start.5 = (f32[99]{0:T(128)S(1)}, f32[99]{0:T(128)}, u32[]{:S(2)}) copy-start(f32[99]{0:T(128)} %param.10) | copy-start | bytes 1192
  0.7 10.7 %copy-start.6 = (f32[99]{0:T(128)S(1)}, f32[99]{0:T(128)}, u32[]{:S(2)}) copy-start(f32[99]{0:T(128)} %param.12) | copy-start | bytes 1192
  3.4 9.0 %collective-permute-start = (f32[4,104,128]{2,1,0:T(8,128)S(1)}, f32[4,104,128]{2,1,0:T(8,128)S(1)}, u32[]{:S(2)}, u32[]{:S(2)}) collective-permute-start(f32[4,104,128]{2,1,0:T(8,128)S(1)} %get-tuple-element.30), channel_id=1, source_target_pairs={{0,128},{64,192},{128,0},{192,64},{1,129},{65,193},{129,1},{193,65... | collective-permute-start | bytes 638984 | tf_op jit(solution)/shard_map/forward_far/ppermute | solution.py:269
  8.6 9.3 %collective-permute-start.1 = (f32[4,104,128]{2,1,0:T(8,128)S(1)}, f32[4,104,128]{2,1,0:T(8,128)S(1)}, u32[]{:S(2)}, u32[]{:S(2)}) collective-permute-start(f32[4,104,128]{2,1,0:T(8,128)S(1)} %get-tuple-element.31), channel_id=1, source_target_pairs={{0,64},{64,128},{128,192},{192,0},{1,65},{65,129},{129,193},{193,1... | collective-permute-start | bytes 638984 | tf_op jit(solution)/shard_map/forward_near/ppermute | solution.py:269
  9.1 8.8 %collective-permute-start.2 = (f32[4,104,128]{2,1,0:T(8,128)S(1)}, f32[4,104,128]{2,1,0:T(8,128)S(1)}, u32[]{:S(2)}, u32[]{:S(2)}) collective-permute-start(f32[4,104,128]{2,1,0:T(8,128)S(1)} %get-tuple-element.32), channel_id=1, source_target_pairs={{0,192},{64,0},{128,64},{192,128},{1,193},{65,1},{129,65},{193,129... | collective-permute-start | bytes 638984 | tf_op jit(solution)/shard_map/forward_near/ppermute | solution.py:269
  19.4 3.7 %collective-permute-start.5 = (bf16[4,104,128]{2,1,0:T(8,128)(2,1)S(1)}, bf16[4,104,128]{2,1,0:T(8,128)(2,1)S(1)}, u32[]{:S(2)}, u32[]{:S(2)}) collective-permute-start(bf16[4,104,128]{2,1,0:T(8,128)(2,1)S(1)} %get-tuple-element.43), channel_id=1, source_target_pairs={{0,192},{64,0},{128,64},{192,128},{1,193},{65,1},{129,65},{193,129... | collective-permute-start | bytes 319496 | tf_op jit(solution)/shard_map/bracket_exchange/ppermute | solution.py:269
  21.4 5.1 %collective-permute-start.3 = (bf16[4,104,128]{2,1,0:T(8,128)(2,1)S(1)}, bf16[4,104,128]{2,1,0:T(8,128)(2,1)S(1)}, u32[]{:S(2)}, u32[]{:S(2)}) collective-permute-start(bf16[4,104,128]{2,1,0:T(8,128)(2,1)S(1)} %get-tuple-element.38), channel_id=1, source_target_pairs={{0,128},{64,192},{128,0},{192,64},{1,129},{65,193},{129,1},{193,65... | collective-permute-start | bytes 319496 | tf_op jit(solution)/shard_map/bracket_exchange/ppermute | solution.py:269
  22.2 6.1 %collective-permute-start.4 = (bf16[4,104,128]{2,1,0:T(8,128)(2,1)S(1)}, bf16[4,104,128]{2,1,0:T(8,128)(2,1)S(1)}, u32[]{:S(2)}, u32[]{:S(2)}) collective-permute-start(bf16[4,104,128]{2,1,0:T(8,128)(2,1)S(1)} %get-tuple-element.39), channel_id=1, source_target_pairs={{0,64},{64,128},{128,192},{192,0},{1,65},{65,129},{129,193},{193,1... | collective-permute-start | bytes 319496 | tf_op jit(solution)/shard_map/bracket_exchange/ppermute | solution.py:269
  29.2 3.5 %collective-permute-start.6 = (f32[16,8,512]{2,1,0:T(8,128)S(1)}, f32[16,8,512]{2,1,0:T(8,128)S(1)}, u32[]{:S(2)}, u32[]{:S(2)}) collective-permute-start(f32[16,8,512]{2,1,0:T(8,128)S(1)} %get-tuple-element.47), channel_id=1, source_target_pairs={{0,1},{1,0},{2,3},{3,2},{4,5},{5,4},{6,7},{7,6},{8,9},{9,8},{10,11... | collective-permute-start | bytes 786440 | tf_op jit(solution)/shard_map/backward_partner_half/ppermute | solution.py:364
  32.4 45.8 %copy-start.1 = (f32[99,1024]{1,0:T(8,128)S(1)}, f32[99,1024]{1,0:T(8,128)}, u32[]{:S(2)}) copy-start(f32[99,1024]{1,0:T(8,128)} %refs_5_.1) | copy-start | bytes 1216516
  61.8 10.9 %all-to-all-start.2 = ((f32[16,8,512]{2,1,0:T(8,128)}), f32[16,8,512]{2,1,0:T(8,128)S(1)}, u32[]{:S(2)}, u32[]{:S(2)}) async-start(f32[16,8,512]{2,1,0:T(8,128)} %broadcast_in_dim.7), calls=%async_computation.2 | async-start | bytes 524288 | tf_op jit(solution)/shard_map/gradient_sum/all_to_all | solution.py:382
  72.7 5.5 %collective-permute-start.7 = (f32[16,8,512]{2,1,0:T(8,128)S(1)}, f32[16,8,512]{2,1,0:T(8,128)S(1)}, u32[]{:S(2)}, u32[]{:S(2)}) collective-permute-start(f32[16,8,512]{2,1,0:T(8,128)S(1)} %all-to-all-done.2.refs_0_.refs_2_), channel_id=1, source_target_pairs={{0,1},{1,0},{2,3},{3,2},{4,5},{5,4},{6,7},{7,6},{8,9},{9,8},{10,11... | collective-permute-start | bytes 786440 | tf_op jit(solution)/shard_map/last_swap/ppermute | solution.py:406

commit v6 on v5

--- a/solution.py
+++ b/solution.py
@@ -38,31 +38,43 @@
     return pl.ds(pl.multiple_of(lax.rem(where[0] + k, GROUPS) * chunk, chunk), chunk)
 
 
-def features_at(hidden, points):
-    return jnp.concatenate([hidden[m, points, :] for m in range(hidden.shape[0])], axis=0)
-
-
-def decode(half, features, out):
-    values = lax.dot_general(half[...], features, (((1,), (1,)), ((), ())), preferred_element_type=F32)
+def fetch_chunks(where, hidden, held, sem, ks):
+    local, chunk = held.shape[1:3]
+    copies = []
+    for slot, k in enumerate(ks):
+        points = chunk_at(where, k, chunk)
+        copies.append(
+            [pltpu.make_async_copy(hidden.at[m, points, :], held.at[slot, m], sem.at[slot, m]) for m in range(local)]
+        )
+        for copy in copies[slot]:
+            copy.start()
+    return copies
+
+
+def decode_chunk(copies, held, half, out):
+    for copy in copies:
+        copy.wait()
+    values = lax.dot_general(
+        half[...], held[...].reshape(-1, held.shape[2]), (((1,), (1,)), ((), ())), preferred_element_type=F32
+    )
     chunk = out.shape[2]
     for m in range(out.shape[0]):
         out[m] = values[:, m * chunk : (m + 1) * chunk]
 
 
-def far_kernel(where, hidden, weight, out, half, held, w, sem):
-    fetch = pltpu.make_async_copy(weight, w, sem.at[0])
+def far_kernel(where, hidden, weight, out, half, held, w, sem, weight_sem):
+    fetch = pltpu.make_async_copy(weight, w, weight_sem)
     fetch.start()
-    copy = pltpu.make_async_copy(hidden.at[:, chunk_at(where, 2, out.shape[2]), :], held, sem.at[1])
-    copy.start()
+    (copies,) = fetch_chunks(where, hidden, held, sem, (2,))
     fetch.wait()
     half[...] = padded(w[...], half.shape[0]).astype(BF16)
-    copy.wait()
-    decode(half, held[...].reshape(-1, held.shape[2]), out)
-
-
-def near_kernel(where, hidden, half, after, before):
-    for k, out in ((1, after), (3, before)):
-        decode(half, features_at(hidden, chunk_at(where, k, out.shape[2])), out)
+    decode_chunk(copies, held.at[0], half, out)
+
+
+def near_kernel(where, hidden, half, after, before, held, sem):
+    copies = fetch_chunks(where, hidden, held, sem, (1, 3))
+    for slot, out in enumerate((after, before)):
+        decode_chunk(copies[slot], held.at[slot], half, out)
 
 
 def add_pair(total, i, j, s):
@@ -111,7 +123,8 @@
         outs[j // local][j % local] = scratch[j].astype(BF16)
 
 
-def local_kernel(where, hidden, half, lat, area_bin, intercept, truth, var, out, area, weight, shift):
+def local_kernel(where, hidden, half, lat, area_bin, intercept, truth, var, out, area, weight, shift, held, sem):
+    copies = fetch_chunks(where, hidden, held, sem, range(GROUPS))
     rows, chunk = shift.shape
     cells, width = lat.shape
     points = area_bin.shape[1]
@@ -126,7 +139,10 @@
     weight[...] = by_point * as_column(var[...], rows)
     here = chunk_at(where, 0, chunk)
     shift[...] = as_column(intercept[...], rows) - padded(truth[:, here], rows)
-    decode(half, features_at(hidden, here), out)
+    decode_chunk(copies[0], held.at[0], half, out)
+    for chunk_copies in copies[1:]:
+        for copy in chunk_copies:
+            copy.wait()
 
 
 def pieces_of(acc, extra, out):
@@ -146,29 +162,26 @@
     return lax.dot_general(ones, w, (((1,), (1,)), ((), ())), preferred_element_type=F32)
 
 
-def early_backward_kernel(where, hidden, b0, b1, weight, weighted, total, bias):
-    chunk = b0.shape[2]
+def early_backward_kernel(where, held, b0, b1, weight, weighted, total, bias):
+    features = held.shape[3]
     w0 = weigh(where, 0, b0, weight)
     w1 = weigh(where, 1, b1, weight)
     weighted[0], weighted[1] = w0, w1
     bias[...] = bias_of(w0) + bias_of(w1)
     total[...] = jnp.dot(
-        w0, features_at(hidden, chunk_at(where, 0, chunk)), preferred_element_type=F32
-    ) + jnp.dot(w1, features_at(hidden, chunk_at(where, 1, chunk)), preferred_element_type=F32)
-
-
-def late_half(where, side, w2, w3, hidden, early, acc):
-    rows, depth = w2.shape
-    local = hidden.shape[0]
+        w0, held[0].reshape(-1, features), preferred_element_type=F32
+    ) + jnp.dot(w1, held[1].reshape(-1, features), preferred_element_type=F32)
+
+
+def late_half(side, w2, w3, held, early, acc):
+    rows = w2.shape[0]
     half = acc.shape[1]
     lanes = pl.ds(pl.multiple_of(side * half, half), half)
-
-    def product(w, k):
-        points = chunk_at(where, k, depth // local)
-        part = jnp.concatenate([hidden[m, points, lanes] for m in range(local)], axis=0)
-        return jnp.dot(w, part, preferred_element_type=F32)
-
-    acc[0:rows, :] = early[:, lanes] + product(w2, 2) + product(w3, 3)
+    acc[0:rows, :] = (
+        early[:, lanes]
+        + jnp.dot(w2, held[2, :, :, lanes].reshape(-1, half), preferred_element_type=F32)
+        + jnp.dot(w3, held[3, :, :, lanes].reshape(-1, half), preferred_element_type=F32)
+    )
     acc[rows:, :] = jnp.zeros((acc.shape[0] - rows, half), F32)
 
 
@@ -177,18 +190,18 @@
     return jnp.broadcast_to(row, (8, half))
 
 
-def partner_half_kernel(where, hidden, b2, b3, weight, area, early, weighted, other, acc):
+def partner_half_kernel(where, held, b2, b3, weight, area, early, weighted, other, acc):
     w2 = weigh(where, 2, b2, weight)
     w3 = weigh(where, 3, b3, weight)
     weighted[0], weighted[1] = w2, w3
-    late_half(where, 1 - where[1], w2, w3, hidden, early, acc)
+    late_half(1 - where[1], w2, w3, held, early, acc)
     pieces_of(acc, extra_row(jnp.zeros((1, 128), F32), area[...], acc.shape[1]), other)
 
 
-def own_half_kernel(where, hidden, weighted, early, early_bias, area, mine, acc):
+def own_half_kernel(where, held, weighted, early, early_bias, area, mine, acc):
     rows = early.shape[0]
     w2, w3 = weighted[0], weighted[1]
-    late_half(where, where[1], w2, w3, hidden, early, acc)
+    late_half(where[1], w2, w3, held, early, acc)
     bias = early_bias[...] + bias_of(w2) + bias_of(w3)
     bias = jnp.concatenate([bias[0:1], jnp.zeros((1, 128 - rows), F32)], axis=1)
     pieces_of(acc, extra_row(bias, area[...], acc.shape[1]), mine)
@@ -221,7 +234,7 @@
     out[...] = squares_of(own, inverse)
 
 
-def update_kernel(where, step, own, partner, squares, weight, intercept, new_weight, new_bias, *, replicas):
+def update_kernel(where, step, own, partner, squares, weight, intercept, new_weight, new_bias, result, sem, *, replicas):
     variables, features = weight.shape
     half = features // 2
     first = where[1] == 0
@@ -237,16 +250,22 @@
     rms = jnp.sqrt(total / count + 1e-06)
     warm = (step[0] + 1).astype(F32) / WARMUP
     scale = warm * jnp.minimum(1.0, 1.0 / rms)
-    for r in range(PIECES):
-        low = PIECE_ROWS * r
-        n = min(PIECE_ROWS, variables - low)
-        if n <= 0:
-            continue
-        a, b = own[r, 0:n, :], partner[r, 0:n, :]
-        left, right = jnp.where(first, a, b), jnp.where(first, b, a)
-        new_weight[low : low + n, :half] = weight[low : low + n, :half] - scale * (left * inverse)
-        new_weight[low : low + n, half:] = weight[low : low + n, half:] - scale * (right * inverse)
+    copies = []
+    for side in range(2):
+        lanes = slice(side * half, (side + 1) * half)
+        this_core = where[1] == side
+        for r in range(PIECES):
+            low = PIECE_ROWS * r
+            n = min(PIECE_ROWS, variables - low)
+            if n <= 0:
+                continue
+            g = jnp.where(this_core, own[r, 0:n, :], partner[r, 0:n, :])
+            result[low : low + n, lanes] = weight[low : low + n, lanes] - scale * (g * inverse)
+        copies.append(pltpu.make_async_copy(result.at[:, lanes], new_weight.at[:, lanes], sem.at[side]))
+        copies[side].start()
     new_bias[...] = intercept[...] - scale * bias_grad
+    for copy in copies:
+        copy.wait()
 
 
 def on_device(hidden, decoder_weight, decoder_intercept, analysis_truth, var_weight, lat_weight, area_bin, train_step):
@@ -276,9 +295,10 @@
             in_specs=[SMEM, HBM, HBM],
             out_specs=[VMEM] * 2,
             scratch_shapes=[
-                pltpu.VMEM((local, chunk, features), BF16),
+                pltpu.VMEM((1, local, chunk, features), BF16),
                 pltpu.VMEM((variables, features), F32),
-                pltpu.SemaphoreType.DMA((2,)),
+                pltpu.SemaphoreType.DMA((1, local)),
+                pltpu.SemaphoreType.DMA(()),
             ],
             compiler_params=grant(53.4),
             name="forward_far",
@@ -288,9 +308,13 @@
         after, before = pl.pallas_call(
             near_kernel,
             out_shape=[one_residual] * 2,
-            in_specs=[SMEM, VMEM, VMEM],
+            in_specs=[SMEM, HBM, VMEM],
             out_specs=[VMEM] * 2,
-            compiler_params=grant(8),
+            scratch_shapes=[
+                pltpu.VMEM((2, local, chunk, features), BF16),
+                pltpu.SemaphoreType.DMA((2, local)),
+            ],
+            compiler_params=grant(52),
             cost_estimate=pl.CostEstimate(
                 flops=4 * rows * local * chunk * features, bytes_accessed=4 * local * chunk * features, transcendentals=0
             ),
@@ -298,17 +322,19 @@
         )(where, hidden, half_weight)
         after, before = turn(after, 1), turn(before, 3)
     with jax.named_scope("forward_local"):
-        here, area, point_weight, shift = pl.pallas_call(
+        here, area, point_weight, shift, held = pl.pallas_call(
             local_kernel,
             out_shape=[
                 one_residual,
                 jax.ShapeDtypeStruct((1, 128), F32),
                 jax.ShapeDtypeStruct((rows, points), F32),
                 jax.ShapeDtypeStruct((rows, chunk), F32),
+                jax.ShapeDtypeStruct((GROUPS, local, chunk, features), BF16),
             ],
-            in_specs=[SMEM] + [VMEM] * 7,
-            out_specs=[VMEM] * 4,
-            compiler_params=grant(8),
+            in_specs=[SMEM, HBM] + [VMEM] * 6,
+            out_specs=[VMEM] * 5,
+            scratch_shapes=[pltpu.SemaphoreType.DMA((GROUPS, local))],
+            compiler_params=grant(46),
             name="forward_local",
         )(where, hidden, half_weight, lat_weight.reshape(-1, 128), area_bin.reshape(1, points), intercept_row, analysis_truth, var_row)
     with jax.named_scope("early_pairs"):
@@ -320,7 +346,7 @@
             compiler_params=grant(4),
             name="early_pairs",
         )(here, far, shift)
-    after, before, early, point_weight = lax.optimization_barrier((after, before, early, point_weight))
+    after, before, early, point_weight, held = lax.optimization_barrier((after, before, early, point_weight, held))
     with jax.named_scope("late_pairs"):
         brackets = pl.pallas_call(
             lambda *refs: late_pairs_kernel(members, *refs),
@@ -349,7 +375,7 @@
             out_specs=[VMEM] * 3,
             compiler_params=grant(10),
             name="early_backward",
-        )(where, hidden, returned[0], returned[1], point_weight)
+        )(where, held, returned[0], returned[1], point_weight)
     with jax.named_scope("backward_partner_half"):
         weighted_late, other = pl.pallas_call(
             partner_half_kernel,
@@ -359,7 +385,7 @@
             scratch_shapes=sums,
             compiler_params=grant(10),
             name="backward_partner_half",
-        )(where, hidden, returned[2], returned[3], point_weight, area, early_sum)
+        )(where, held, returned[2], returned[3], point_weight, area, early_sum)
         swap = [(0, 1), (1, 0)]
         other = lax.ppermute(other, "c", swap)
     with jax.named_scope("backward_own_half"):
@@ -371,7 +397,7 @@
             scratch_shapes=sums,
             compiler_params=grant(10),
             name="backward_own_half",
-        )(where, hidden, weighted_late, early_sum, early_bias, area)
+        )(where, held, weighted_late, early_sum, early_bias, area)
     with jax.named_scope("gradient_sum"):
         part = mine + other
         part = lax.all_to_all(part, ("x", "y"), 0, 0, tiled=True)
@@ -420,7 +446,8 @@
                 jax.ShapeDtypeStruct((1, variables), F32),
             ],
             in_specs=[SMEM, SMEM] + [VMEM] * 5,
-            out_specs=[VMEM] * 2,
+            out_specs=[HBM, VMEM],
+            scratch_shapes=[pltpu.VMEM((variables, features), F32), pltpu.SemaphoreType.DMA((2,))],
             compiler_params=grant(6),
             name="update",
         )(where, train_step, own, partner, squares, decoder_weight, intercept_row)

time: 80.2 us -> 80.7 us (level)
  waiting for transfers between devices: 13.3 us -> 8.63 us
  Pallas kernels: 15.5 us -> 19.1 us
  starting transfers between devices: 20.4 us -> 21.7 us
    ppermute x6, waiting for transfers between devices: 9.34 us -> 4.64 us  [turn(): lax.ppermute(value, 'y', [(i, (i + k) % GROUPS) for i in range(GROUPS)])]
    pallas_call x1, Pallas kernels: 1.04 us -> 3.05 us  [on_device(): pl.pallas_call(local_kernel, out_shape=[one_residual, jax.ShapeDtypeStruc...]
    pallas_call x1, Pallas kernels: 1.34 us -> 2.74 us  [on_device(): pl.pallas_call(near_kernel, out_shape=[one_residual] * 2, in_specs=[SMEM,...]
    ppermute x1, starting transfers between devices: 2.3 us -> 3.37 us  [on_device(): other = lax.ppermute(other, 'c', swap)]
  transfers between devices with their start and end apart: 9 -> 9, of which waited for: 7 -> 7; matrix products, arithmetic and copies ran while one was open for 0% -> 0% of each run, Pallas kernels for 11% -> 15%
where the time goes in v6:
time: 80.7 us; the launch traced here: 80.4 us
  blocking collectives  28.6 us (35%)
  starting transfers between devices  21.7 us (27%)
  Pallas kernels  19.1 us (24%)
  waiting for transfers between devices  8.63 us (11%)
  between operations  1.43 us (2%)
    all_to_all x1, blocking collectives, on_device(): part = lax.all_to_all(part, 'z', 0, 0, tiled=True)  16 us
    all_to_all x1, blocking collectives, on_device(): part = lax.all_to_all(part, ('x', 'y'), 0, 0, tiled=True)  12.6 us
    ppermute x6, starting transfers between devices, turn(): lax.ppermute(value, 'y', [(i, (i + k) % GROUPS) for i in range(GROUPS)])  10.4 us
    ppermute x6, waiting for transfers between devices, turn(): lax.ppermute(value, 'y', [(i, (i + k) % GROUPS) for i in range(GROUPS)])  4.64 us
    ppermute x1, starting transfers between devices, on_device(): partner = lax.ppermute(own, 'c', swap)  4.38 us
    pallas_call x1, Pallas kernels, on_device(): pl.pallas_call(lambda *refs: grad_hidden_kernel(*refs, replicas=replicas)...  3.96 us
    all_to_all x1, starting transfers between devices, on_device(): lax.all_to_all(jnp.broadcast_to(piece, (PIECES, 8, half)), ('x', 'y'), 0,...  3.62 us
    ppermute x1, starting transfers between devices, on_device(): other = lax.ppermute(other, 'c', swap)  3.37 us
  transfers between devices with their start and end apart: 9, of which 7 were waited for; matrix products, arithmetic and copies ran while one was open for 0% of the time, Pallas kernels for 15%

profile of v6, /device:TPU:1, one launch (start us, length us, event | category | flops | bytes accessed | tf_op | source)
XLA Modules:
  0.0 80.4 jit_solution(10877699038299344878)
XLA Ops:
  0.6 0.1 pad_add_fusion.where.refs_0_
  0.7 0.0 copy-start.1
  0.7 0.0 copy-start.2
  0.7 0.0 copy-start.3
  0.7 0.0 copy-start.4
  0.7 0.0 copy-start.5
  0.7 2.4 %forward_far.1 = (f32[4,104,128]{2,1,0:T(8,128)S(1)}, bf16[104,1024]{1,0:T(8,128)(2,1)S(1)}) custom-call(s32[2]{0:T(128)S(1)} %pad_add_fusion.where.refs_0_, bf16[4,512,1024]{2,1,0:T(8,128)(2,1)} %hidden.5, f32[99,1024]{1,0:T(8,128)} %refs_5_.1), custom_call_target="tpu_custom_call" | custom-call | tf_op jit(solution)/shard_map/forward_far/forward_far/pallas_call | solution.py:292
  3.1 3.8 %collective-permute-start.2 = (f32[4,104,128]{2,1,0:T(8,128)S(1)}, f32[4,104,128]{2,1,0:T(8,128)S(1)}, u32[]{:S(2)}, u32[]{:S(2)}) collective-permute-start(f32[4,104,128]{2,1,0:T(8,128)S(1)} %get-tuple-element.34), channel_id=1, source_target_pairs={{0,128},{64,192},{128,0},{192,64},{1,129},{65,193},{129,1},{193,65... | collective-permute-start | bytes 638984 | tf_op jit(solution)/shard_map/forward_far/ppermute | solution.py:288
  6.9 2.7 %forward_near.1 = (f32[4,104,128]{2,1,0:T(8,128)S(1)}, f32[4,104,128]{2,1,0:T(8,128)S(1)}) custom-call(s32[2]{0:T(128)S(1)} %pad_add_fusion.where.refs_0_, bf16[4,512,1024]{2,1,0:T(8,128)(2,1)} %hidden.5, bf16[104,1024]{1,0:T(8,128)(2,1)S(1)} %get-tuple-element.30.half.refs_3_), custom_call_target="tpu_custom_call" | custom-call | flops 218103808 | bytes 2097152 | tf_op jit(solution)/shard_map/forward_near/forward_near/pallas_call | solution.py:308
  9.7 0.5 collective-permute-start
  10.2 2.3 %collective-permute-start.1 = (f32[4,104,128]{2,1,0:T(8,128)S(1)}, f32[4,104,128]{2,1,0:T(8,128)S(1)}, u32[]{:S(2)}, u32[]{:S(2)}) collective-permute-start(f32[4,104,128]{2,1,0:T(8,128)S(1)} %get-tuple-element.32), channel_id=1, source_target_pairs={{0,192},{64,0},{128,64},{192,128},{1,193},{65,1},{129,65},{193,129... | collective-permute-start | bytes 638984 | tf_op jit(solution)/shard_map/forward_near/ppermute | solution.py:288
  12.4 0.0 copy-done.1
  12.4 0.0 copy-done.2
  12.4 0.0 copy-done.3
  12.5 0.0 copy-done.4
  12.5 0.0 copy-done.5
  12.5 3.0 %forward_local.1 = (f32[4,104,128]{2,1,0:T(8,128)S(1)}, f32[1,128]{1,0:T(1,128)S(1)}, f32[104,512]{1,0:T(8,128)S(1)}, f32[104,128]{1,0:T(8,128)S(1)}, bf16[4,4,128,1024]{3,2,1,0:T(8,128)(2,1)S(1)}) custom-call(s32[2]{0:T(128)S(1)} %pad_add_fusion.where.refs_0_, bf16[4,512,1024]{2,1,0:T(8,128)(2,1)} %hidden.5, ...), custom_call_target="tpu_custom_call" | custom-call | tf_op jit(solution)/shard_map/forward_local/forward_local/pallas_call | solution.py:325
  15.5 0.0 collective-permute-done.2.far.refs_1_
  15.5 0.5 early_pairs.1.refs_5_
  16.0 0.8 %collective-permute-done.refs_2_ = f32[4,104,128]{2,1,0:T(8,128)S(1)} collective-permute-done((f32[4,104,128]{2,1,0:T(8,128)S(1)}, f32[4,104,128]{2,1,0:T(8,128)S(1)}, u32[]{:S(2)}, u32[]{:S(2)}) %collective-permute-start) | collective-permute-done | bytes 213024 | tf_op jit(solution)/shard_map/forward_near/ppermute | solution.py:288
  16.8 0.0 collective-permute-done.1.refs_3_
  16.8 1.5 %late_pairs.1 = (bf16[4,104,128]{2,1,0:T(8,128)(2,1)S(1)}, bf16[4,104,128]{2,1,0:T(8,128)(2,1)S(1)}, bf16[4,104,128]{2,1,0:T(8,128)(2,1)S(1)}, bf16[4,104,128]{2,1,0:T(8,128)(2,1)S(1)}) custom-call(f32[4,104,128]{2,1,0:T(8,128)S(1)} %get-tuple-element.33.here.refs_0_, f32[4,104,128]{2,1,0:T(8,128)S(1)} %collective-permute-done.2.far.refs_1_, ...), custom_call_target="tpu_custom_call" | custom-call | tf_op jit(solution)/shard_map/late_pairs/late_pairs/pallas_call | solution.py:351
  18.3 2.4 %collective-permute-start.5 = (bf16[4,104,128]{2,1,0:T(8,128)(2,1)S(1)}, bf16[4,104,128]{2,1,0:T(8,128)(2,1)S(1)}, u32[]{:S(2)}, u32[]{:S(2)}) collective-permute-start(bf16[4,104,128]{2,1,0:T(8,128)(2,1)S(1)} %get-tuple-element.47), channel_id=1, source_target_pairs={{0,192},{64,0},{128,64},{192,128},{1,193},{65,1},{129,65},{193,129... | collective-permute-start | bytes 319496 | tf_op jit(solution)/shard_map/bracket_exchange/ppermute | solution.py:288
  20.7 0.6 collective-permute-start.3
  21.3 0.8 collective-permute-start.4
  22.1 0.4 collective-permute-done.5.b1
  22.4 1.0 %early_backward.1 = (bf16[2,104,512]{2,1,0:T(8,128)(2,1)S(1)}, f32[104,1024]{1,0:T(8,128)S(1)}, f32[8,104]{1,0:T(8,128)S(1)}) custom-call(s32[2]{0:T(128)S(1)} %pad_add_fusion.where.refs_0_, bf16[4,4,128,1024]{3,2,1,0:T(8,128)(2,1)S(1)} %get-tuple-element.38.held, bf16[4,104,128]{2,1,0:T(8,128)(2,1)S(1)} %get-tuple-element.46.b0, ...), custom_call_target="tpu_custom_call" | custom-call | tf_op jit(solution)/shard_map/early_backward/early_backward/pallas_call | solution.py:367
  23.5 2.4 %collective-permute-done.3.b2 = bf16[4,104,128]{2,1,0:T(8,128)(2,1)S(1)} collective-permute-done((bf16[4,104,128]{2,1,0:T(8,128)(2,1)S(1)}, bf16[4,104,128]{2,1,0:T(8,128)(2,1)S(1)}, u32[]{:S(2)}, u32[]{:S(2)}) %collective-permute-start.3) | collective-permute-done | bytes 106528 | tf_op jit(solution)/shard_map/bracket_exchange/ppermute | solution.py:288
  25.9 1.1 %collective-permute-done.4.b3 = bf16[4,104,128]{2,1,0:T(8,128)(2,1)S(1)} collective-permute-done((bf16[4,104,128]{2,1,0:T(8,128)(2,1)S(1)}, bf16[4,104,128]{2,1,0:T(8,128)(2,1)S(1)}, u32[]{:S(2)}, u32[]{:S(2)}) %collective-permute-start.4) | collective-permute-done | bytes 106528 | tf_op jit(solution)/shard_map/bracket_exchange/ppermute | solution.py:288
  26.9 0.9 %backward_partner_half.1 = (bf16[2,104,512]{2,1,0:T(8,128)(2,1)S(1)}, f32[16,8,512]{2,1,0:T(8,128)S(1)}) custom-call(s32[2]{0:T(128)S(1)} %pad_add_fusion.where.refs_0_, bf16[4,4,128,1024]{3,2,1,0:T(8,128)(2,1)S(1)} %get-tuple-element.38.held, bf16[4,104,128]{2,1,0:T(8,128)(2,1)S(1)} %collective-permute-done.3.b2, ...), custom_call_target="tpu_custom_call" | custom-call | tf_op jit(solution)/shard_map/backward_partner_half/backward_partner_half/pallas_call | solution.py:380
  27.8 3.4 %collective-permute-start.6 = (f32[16,8,512]{2,1,0:T(8,128)S(1)}, f32[16,8,512]{2,1,0:T(8,128)S(1)}, u32[]{:S(2)}, u32[]{:S(2)}) collective-permute-start(f32[16,8,512]{2,1,0:T(8,128)S(1)} %get-tuple-element.51), channel_id=1, source_target_pairs={{0,1},{1,0},{2,3},{3,2},{4,5},{5,4},{6,7},{7,6},{8,9},{9,8},{10,11... | collective-permute-start | bytes 786440 | tf_op jit(solution)/shard_map/backward_partner_half/ppermute | solution.py:390
  31.2 0.9 %backward_own_half.1 = f32[16,8,512]{2,1,0:T(8,128)S(1)} custom-call(s32[2]{0:T(128)S(1)} %pad_add_fusion.where.refs_0_, bf16[4,4,128,1024]{3,2,1,0:T(8,128)(2,1)S(1)} %get-tuple-element.38.held, bf16[2,104,512]{2,1,0:T(8,128)(2,1)S(1)} %get-tuple-element.49.weighted.refs_2_, f32[104,1024]{1,0:T(8,128)S(1)} %get-tuple-element.48.early, ...), custom_call_target="tpu_custom_call" | custom-call | tf_op jit(solution)/shard_map/backward_own_half/backward_own_half/pallas_call | solution.py:392
  32.1 0.0 copy-start
  32.1 0.2 collective-permute-done.6
  32.4 12.6 %all_to_all.15 = f32[16,8,512]{2,1,0:T(8,128)S(1)} all-to-all(f32[16,8,512]{2,1,0:T(8,128)S(1)} %add.3), channel_id=1, replica_groups=mesh['y'=4,'z'=8,'x'=4,'c'=2] {'x','y'}, dimensions={0} | all-to-all | bytes 524288 | tf_op jit(solution)/shard_map/gradient_sum/all_to_all | solution.py:403
  45.0 16.0 %all_to_all.16 = f32[8,8,512]{2,1,0:T(8,128)S(1)} all-to-all(f32[8,8,512]{2,1,0:T(8,128)S(1)} %broadcast_in_dim.6), channel_id=1, replica_groups=mesh['y'=4,'z'=8,'x'=4,'c'=2] {'z'}, dimensions={0} | all-to-all | bytes 262144 | tf_op jit(solution)/shard_map/gradient_sum/all_to_all | solution.py:406
  61.1 0.7 broadcast_in_dim.7
  61.8 3.6 %all-to-all-start.2 = ((f32[16,8,512]{2,1,0:T(8,128)}), f32[16,8,512]{2,1,0:T(8,128)S(1)}, u32[]{:S(2)}, u32[]{:S(2)}) async-start(f32[16,8,512]{2,1,0:T(8,128)} %broadcast_in_dim.7), calls=%async_computation.2 | async-start | bytes 524288 | tf_op jit(solution)/shard_map/gradient_sum/all_to_all | solution.py:408
  65.4 4.0 %grad_hidden.1 = bf16[4,512,1024]{2,1,0:T(8,128)(2,1)} custom-call(s32[2]{0:T(128)S(1)} %pad_add_fusion.where.refs_0_, bf16[2,104,512]{2,1,0:T(8,128)(2,1)S(1)} %get-tuple-element.52.refs_1_, bf16[2,104,512]{2,1,0:T(8,128)(2,1)S(1)} %get-tuple-element.49.weighted.refs_2_, bf16[104,1024]{1,0:T(8,128)(2,1)S(1)} %get-tuple-element.30.half.refs_3_, ...), custom_call_target="tpu_custom_call" | custom-call | flops 436207616 | bytes 4194304 | tf_op jit(solution)/shard_map/grad_hidden/grad_hidden/pallas_call | solution.py:410
  69.4 3.4 %all-to-all-done.2.refs_0_.refs_2_ = f32[16,8,512]{2,1,0:T(8,128)S(1)} async-done(((f32[16,8,512]{2,1,0:T(8,128)}), f32[16,8,512]{2,1,0:T(8,128)S(1)}, u32[]{:S(2)}, u32[]{:S(2)}) %all-to-all-start.2) | async-done | bytes 262176 | tf_op jit(solution)/shard_map/gradient_sum/all_to_all | solution.py:408
  72.7 4.4 %collective-permute-start.7 = (f32[16,8,512]{2,1,0:T(8,128)S(1)}, f32[16,8,512]{2,1,0:T(8,128)S(1)}, u32[]{:S(2)}, u32[]{:S(2)}) collective-permute-start(f32[16,8,512]{2,1,0:T(8,128)S(1)} %all-to-all-done.2.refs_0_.refs_2_), channel_id=1, source_target_pairs={{0,1},{1,0},{2,3},{3,2},{4,5},{5,4},{6,7},{7,6},{8,9},{9,8},{10,11... | collective-permute-start | bytes 786440 | tf_op jit(solution)/shard_map/last_swap/ppermute | solution.py:432
  77.8 0.1 squares.1.refs_4_
  77.9 0.4 collective-permute-done.7.refs_3_
  78.3 0.0 copy-done
  78.3 2.1 %update.1 = (f32[99,1024]{1,0:T(8,128)}, f32[1,99]{1,0:T(1,128)}) custom-call(s32[2]{0:T(128)S(1)} %pad_add_fusion.where.refs_0_, s32[1]{0:T(128)S(6)} %copy.11.refs_1_, f32[16,8,512]{2,1,0:T(8,128)S(1)} %all-to-all-done.2.refs_0_.refs_2_, f32[16,8,512]{2,1,0:T(8,128)S(1)} %collective-permute-done.7.refs_3_, f32[8,512]{1,0:T(8,128)S(1)} %squares.1.refs_4_, ...), custom_call_target="tpu_custom_call" | custom-call | tf_op jit(solution)/shard_map/update/update/pallas_call | solution.py:442
  (4 shorter events, 0.1 us)
Async XLA Ops:
  0.7 11.7 %copy-start.1 = (f32[99,512]{1,0:T(8,128)S(1)}, f32[99,512]{1,0:T(8,128)}, u32[]{:S(2)}) copy-start(f32[99,512]{1,0:T(8,128)} %truth.1) | copy-start | bytes 608260
  0.7 11.7 %copy-start.2 = (f32[640]{0:T(1024)S(1)}, f32[640]{0:T(1024)}, u32[]{:S(2)}) copy-start(f32[640]{0:T(1024)} %param.13) | copy-start | bytes 7684
  0.7 11.7 %copy-start.3 = (s32[512]{0:T(512)S(1)}, s32[512]{0:T(512)}, u32[]{:S(2)}) copy-start(s32[512]{0:T(512)} %param.14) | copy-start | bytes 6148
  0.7 11.7 %copy-start.4 = (f32[99]{0:T(128)S(1)}, f32[99]{0:T(128)}, u32[]{:S(2)}) copy-start(f32[99]{0:T(128)} %param.10) | copy-start | bytes 1192
  0.7 11.7 %copy-start.5 = (f32[99]{0:T(128)S(1)}, f32[99]{0:T(128)}, u32[]{:S(2)}) copy-start(f32[99]{0:T(128)} %param.12) | copy-start | bytes 1192
  3.1 12.4 %collective-permute-start.2 = (f32[4,104,128]{2,1,0:T(8,128)S(1)}, f32[4,104,128]{2,1,0:T(8,128)S(1)}, u32[]{:S(2)}, u32[]{:S(2)}) collective-permute-start(f32[4,104,128]{2,1,0:T(8,128)S(1)} %get-tuple-element.34), channel_id=1, source_target_pairs={{0,128},{64,192},{128,0},{192,64},{1,129},{65,193},{129,1},{193,65... | collective-permute-start | bytes 638984 | tf_op jit(solution)/shard_map/forward_far/ppermute | solution.py:288
  9.7 7.1 %collective-permute-start = (f32[4,104,128]{2,1,0:T(8,128)S(1)}, f32[4,104,128]{2,1,0:T(8,128)S(1)}, u32[]{:S(2)}, u32[]{:S(2)}) collective-permute-start(f32[4,104,128]{2,1,0:T(8,128)S(1)} %get-tuple-element.31), channel_id=1, source_target_pairs={{0,64},{64,128},{128,192},{192,0},{1,65},{65,129},{129,193},{193,1... | collective-permute-start | bytes 638984 | tf_op jit(solution)/shard_map/forward_near/ppermute | solution.py:288
  10.2 6.7 %collective-permute-start.1 = (f32[4,104,128]{2,1,0:T(8,128)S(1)}, f32[4,104,128]{2,1,0:T(8,128)S(1)}, u32[]{:S(2)}, u32[]{:S(2)}) collective-permute-start(f32[4,104,128]{2,1,0:T(8,128)S(1)} %get-tuple-element.32), channel_id=1, source_target_pairs={{0,192},{64,0},{128,64},{192,128},{1,193},{65,1},{129,65},{193,129... | collective-permute-start | bytes 638984 | tf_op jit(solution)/shard_map/forward_near/ppermute | solution.py:288
  18.3 4.1 %collective-permute-start.5 = (bf16[4,104,128]{2,1,0:T(8,128)(2,1)S(1)}, bf16[4,104,128]{2,1,0:T(8,128)(2,1)S(1)}, u32[]{:S(2)}, u32[]{:S(2)}) collective-permute-start(bf16[4,104,128]{2,1,0:T(8,128)(2,1)S(1)} %get-tuple-element.47), channel_id=1, source_target_pairs={{0,192},{64,0},{128,64},{192,128},{1,193},{65,1},{129,65},{193,129... | collective-permute-start | bytes 319496 | tf_op jit(solution)/shard_map/bracket_exchange/ppermute | solution.py:288
  20.7 5.1 %collective-permute-start.3 = (bf16[4,104,128]{2,1,0:T(8,128)(2,1)S(1)}, bf16[4,104,128]{2,1,0:T(8,128)(2,1)S(1)}, u32[]{:S(2)}, u32[]{:S(2)}) collective-permute-start(bf16[4,104,128]{2,1,0:T(8,128)(2,1)S(1)} %get-tuple-element.42), channel_id=1, source_target_pairs={{0,128},{64,192},{128,0},{192,64},{1,129},{65,193},{129,1},{193,65... | collective-permute-start | bytes 319496 | tf_op jit(solution)/shard_map/bracket_exchange/ppermute | solution.py:288
  21.3 5.6 %collective-permute-start.4 = (bf16[4,104,128]{2,1,0:T(8,128)(2,1)S(1)}, bf16[4,104,128]{2,1,0:T(8,128)(2,1)S(1)}, u32[]{:S(2)}, u32[]{:S(2)}) collective-permute-start(bf16[4,104,128]{2,1,0:T(8,128)(2,1)S(1)} %get-tuple-element.43), channel_id=1, source_target_pairs={{0,64},{64,128},{128,192},{192,0},{1,65},{65,129},{129,193},{193,1... | collective-permute-start | bytes 319496 | tf_op jit(solution)/shard_map/bracket_exchange/ppermute | solution.py:288
  27.8 4.5 %collective-permute-start.6 = (f32[16,8,512]{2,1,0:T(8,128)S(1)}, f32[16,8,512]{2,1,0:T(8,128)S(1)}, u32[]{:S(2)}, u32[]{:S(2)}) collective-permute-start(f32[16,8,512]{2,1,0:T(8,128)S(1)} %get-tuple-element.51), channel_id=1, source_target_pairs={{0,1},{1,0},{2,3},{3,2},{4,5},{5,4},{6,7},{7,6},{8,9},{9,8},{10,11... | collective-permute-start | bytes 786440 | tf_op jit(solution)/shard_map/backward_partner_half/ppermute | solution.py:390
  32.1 46.2 %copy-start = (f32[99,1024]{1,0:T(8,128)S(1)}, f32[99,1024]{1,0:T(8,128)}, u32[]{:S(2)}) copy-start(f32[99,1024]{1,0:T(8,128)} %refs_5_.1) | copy-start | bytes 1216516
  61.8 10.9 %all-to-all-start.2 = ((f32[16,8,512]{2,1,0:T(8,128)}), f32[16,8,512]{2,1,0:T(8,128)S(1)}, u32[]{:S(2)}, u32[]{:S(2)}) async-start(f32[16,8,512]{2,1,0:T(8,128)} %broadcast_in_dim.7), calls=%async_computation.2 | async-start | bytes 524288 | tf_op jit(solution)/shard_map/gradient_sum/all_to_all | solution.py:408
  72.7 5.5 %collective-permute-start.7 = (f32[16,8,512]{2,1,0:T(8,128)S(1)}, f32[16,8,512]{2,1,0:T(8,128)S(1)}, u32[]{:S(2)}, u32[]{:S(2)}) collective-permute-start(f32[16,8,512]{2,1,0:T(8,128)S(1)} %all-to-all-done.2.refs_0_.refs_2_), channel_id=1, source_target_pairs={{0,1},{1,0},{2,3},{3,2},{4,5},{5,4},{6,7},{7,6},{8,9},{9,8},{10,11... | collective-permute-start | bytes 786440 | tf_op jit(solution)/shard_map/last_swap/ppermute | solution.py:432

commit v7 on v6

--- a/solution.py
+++ b/solution.py
@@ -162,24 +162,24 @@
     return lax.dot_general(ones, w, (((1,), (1,)), ((), ())), preferred_element_type=F32)
 
 
-def early_backward_kernel(where, held, b0, b1, weight, weighted, total, bias):
+def early_backward_kernel(where, held, b0, b2, weight, weighted, total, bias):
     features = held.shape[3]
     w0 = weigh(where, 0, b0, weight)
-    w1 = weigh(where, 1, b1, weight)
-    weighted[0], weighted[1] = w0, w1
-    bias[...] = bias_of(w0) + bias_of(w1)
+    w2 = weigh(where, 2, b2, weight)
+    weighted[0], weighted[1] = w0, w2
+    bias[...] = bias_of(w0) + bias_of(w2)
     total[...] = jnp.dot(
         w0, held[0].reshape(-1, features), preferred_element_type=F32
-    ) + jnp.dot(w1, held[1].reshape(-1, features), preferred_element_type=F32)
-
-
-def late_half(side, w2, w3, held, early, acc):
-    rows = w2.shape[0]
+    ) + jnp.dot(w2, held[2].reshape(-1, features), preferred_element_type=F32)
+
+
+def late_half(side, w1, w3, held, early, acc):
+    rows = w1.shape[0]
     half = acc.shape[1]
     lanes = pl.ds(pl.multiple_of(side * half, half), half)
     acc[0:rows, :] = (
         early[:, lanes]
-        + jnp.dot(w2, held[2, :, :, lanes].reshape(-1, half), preferred_element_type=F32)
+        + jnp.dot(w1, held[1, :, :, lanes].reshape(-1, half), preferred_element_type=F32)
         + jnp.dot(w3, held[3, :, :, lanes].reshape(-1, half), preferred_element_type=F32)
     )
     acc[rows:, :] = jnp.zeros((acc.shape[0] - rows, half), F32)
@@ -190,25 +190,25 @@
     return jnp.broadcast_to(row, (8, half))
 
 
-def partner_half_kernel(where, held, b2, b3, weight, area, early, weighted, other, acc):
-    w2 = weigh(where, 2, b2, weight)
+def partner_half_kernel(where, held, b1, b3, weight, area, early, weighted, other, acc):
+    w1 = weigh(where, 1, b1, weight)
     w3 = weigh(where, 3, b3, weight)
-    weighted[0], weighted[1] = w2, w3
-    late_half(1 - where[1], w2, w3, held, early, acc)
+    weighted[0], weighted[1] = w1, w3
+    late_half(1 - where[1], w1, w3, held, early, acc)
     pieces_of(acc, extra_row(jnp.zeros((1, 128), F32), area[...], acc.shape[1]), other)
 
 
 def own_half_kernel(where, held, weighted, early, early_bias, area, mine, acc):
     rows = early.shape[0]
-    w2, w3 = weighted[0], weighted[1]
-    late_half(where[1], w2, w3, held, early, acc)
-    bias = early_bias[...] + bias_of(w2) + bias_of(w3)
+    w1, w3 = weighted[0], weighted[1]
+    late_half(where[1], w1, w3, held, early, acc)
+    bias = early_bias[...] + bias_of(w1) + bias_of(w3)
     bias = jnp.concatenate([bias[0:1], jnp.zeros((1, 128 - rows), F32)], axis=1)
     pieces_of(acc, extra_row(bias, area[...], acc.shape[1]), mine)
 
 
 def grad_hidden_kernel(where, early, late, half, piece, out, *, replicas):
-    first = pl.program_id(0) < GROUPS // 2
+    first = lax.rem(pl.program_id(0), 2) == 0
     inverse = 1.0 / (piece[PIECE_ROWS : PIECE_ROWS + 1, 128:129] * (1.0 / replicas))
     chunk = out.shape[1]
     for m in range(out.shape[0]):
@@ -229,19 +229,30 @@
     return squares
 
 
-def squares_kernel(own, out, *, replicas):
+def in_order(pieces, inverse, out):
+    for r in range(PIECES):
+        low = PIECE_ROWS * r
+        n = min(PIECE_ROWS, out.shape[0] - low)
+        if n > 0:
+            out[low : low + n, :] = pieces[r, 0:n, :] * inverse
+
+
+def own_gradient_kernel(own, gradient, squares, *, replicas):
     inverse = 1.0 / (own[0, PIECE_ROWS : PIECE_ROWS + 1, 128:129] * (1.0 / replicas))
-    out[...] = squares_of(own, inverse)
-
-
-def update_kernel(where, step, own, partner, squares, weight, intercept, new_weight, new_bias, result, sem, *, replicas):
+    squares[...] = squares_of(own, inverse)
+    in_order(own, inverse, gradient)
+
+
+def update_kernel(
+    where, step, own, gradient, partner, squares, weight, intercept, new_weight, new_bias, other, *, replicas
+):
     variables, features = weight.shape
     half = features // 2
     first = where[1] == 0
-    mean_area = own[0, PIECE_ROWS : PIECE_ROWS + 1, 128:129] * (1.0 / replicas)
-    inverse = 1.0 / mean_area
+    inverse = 1.0 / (own[0, PIECE_ROWS : PIECE_ROWS + 1, 128:129] * (1.0 / replicas))
     a, b = (side[0, PIECE_ROWS : PIECE_ROWS + 1, 0:variables] for side in (own, partner))
     bias_grad = (jnp.where(first, a, b) + jnp.where(first, b, a)) * inverse
+    in_order(partner, inverse, other)
     a, b = squares[...], squares_of(partner, inverse)
     both = jnp.where(first, a, b) + jnp.where(first, b, a)
     total = jnp.sum(jnp.sum(both, axis=0, keepdims=True), axis=1, keepdims=True)
@@ -250,22 +261,10 @@
     rms = jnp.sqrt(total / count + 1e-06)
     warm = (step[0] + 1).astype(F32) / WARMUP
     scale = warm * jnp.minimum(1.0, 1.0 / rms)
-    copies = []
-    for side in range(2):
-        lanes = slice(side * half, (side + 1) * half)
-        this_core = where[1] == side
-        for r in range(PIECES):
-            low = PIECE_ROWS * r
-            n = min(PIECE_ROWS, variables - low)
-            if n <= 0:
-                continue
-            g = jnp.where(this_core, own[r, 0:n, :], partner[r, 0:n, :])
-            result[low : low + n, lanes] = weight[low : low + n, lanes] - scale * (g * inverse)
-        copies.append(pltpu.make_async_copy(result.at[:, lanes], new_weight.at[:, lanes], sem.at[side]))
-        copies[side].start()
+    a, b = gradient[...], other[...]
+    new_weight[:, :half] = weight[:, :half] - scale * jnp.where(first, a, b)
+    new_weight[:, half:] = weight[:, half:] - scale * jnp.where(first, b, a)
     new_bias[...] = intercept[...] - scale * bias_grad
-    for copy in copies:
-        copy.wait()
 
 
 def on_device(hidden, decoder_weight, decoder_intercept, analysis_truth, var_weight, lat_weight, area_bin, train_step):
@@ -375,7 +374,7 @@
             out_specs=[VMEM] * 3,
             compiler_params=grant(10),
             name="early_backward",
-        )(where, held, returned[0], returned[1], point_weight)
+        )(where, held, returned[0], returned[2], point_weight)
     with jax.named_scope("backward_partner_half"):
         weighted_late, other = pl.pallas_call(
             partner_half_kernel,
@@ -385,7 +384,7 @@
             scratch_shapes=sums,
             compiler_params=grant(10),
             name="backward_partner_half",
-        )(where, held, returned[2], returned[3], point_weight, area, early_sum)
+        )(where, held, returned[1], returned[3], point_weight, area, early_sum)
         swap = [(0, 1), (1, 0)]
         other = lax.ppermute(other, "c", swap)
     with jax.named_scope("backward_own_half"):
@@ -414,8 +413,8 @@
                 num_scalar_prefetch=1,
                 grid=(GROUPS,),
                 in_specs=[
-                    pl.BlockSpec((1, rows, local * chunk), lambda g, s: (lax.rem(g, 2), 0, 0)),
-                    pl.BlockSpec((1, rows, local * chunk), lambda g, s: (lax.rem(g, 2), 0, 0)),
+                    pl.BlockSpec((1, rows, local * chunk), lambda g, s: (lax.div(g, 2), 0, 0)),
+                    pl.BlockSpec((1, rows, local * chunk), lambda g, s: (lax.div(g, 2), 0, 0)),
                     pl.BlockSpec((rows, features), lambda g, s: (0, 0)),
                     pl.BlockSpec((8, half), lambda g, s: (0, 0)),
                 ],
@@ -430,13 +429,13 @@
         own, grad_hidden = lax.optimization_barrier((own, grad_hidden))
     with jax.named_scope("last_swap"):
         partner = lax.ppermute(own, "c", swap)
-        squares = pl.pallas_call(
-            lambda *refs: squares_kernel(*refs, replicas=replicas),
-            out_shape=jax.ShapeDtypeStruct((8, half), F32),
+        gradient, squares = pl.pallas_call(
+            lambda *refs: own_gradient_kernel(*refs, replicas=replicas),
+            out_shape=[jax.ShapeDtypeStruct((variables, half), F32), jax.ShapeDtypeStruct((8, half), F32)],
             in_specs=[VMEM],
-            out_specs=VMEM,
+            out_specs=[VMEM] * 2,
             compiler_params=grant(4),
-            name="squares",
+            name="own_gradient",
         )(own)
     with jax.named_scope("update"):
         new_weight, new_bias = pl.pallas_call(
@@ -445,12 +444,12 @@
                 jax.ShapeDtypeStruct((variables, features), F32),
                 jax.ShapeDtypeStruct((1, variables), F32),
             ],
-            in_specs=[SMEM, SMEM] + [VMEM] * 5,
-            out_specs=[HBM, VMEM],
-            scratch_shapes=[pltpu.VMEM((variables, features), F32), pltpu.SemaphoreType.DMA((2,))],
+            in_specs=[SMEM, SMEM] + [VMEM] * 6,
+            out_specs=[VMEM] * 2,
+            scratch_shapes=[pltpu.VMEM((variables, half), F32)],
             compiler_params=grant(6),
             name="update",
-        )(where, train_step, own, partner, squares, decoder_weight, intercept_row)
+        )(where, train_step, own, gradient, partner, squares, decoder_weight, intercept_row)
     return grad_hidden, new_weight, new_bias.reshape(variables)
 
 

time: 80.7 us -> 79.5 us (0.985)
    ppermute x1, starting transfers between devices: 3.37 us -> 2.51 us  [on_device(): other = lax.ppermute(other, 'c', swap)]
where the time goes in v7:
time: 79.5 us; the launch traced here: 79.2 us
  blocking collectives  28.5 us (36%)
  starting transfers between devices  21.5 us (27%)
  Pallas kernels  18.6 us (23%)
  waiting for transfers between devices  8.26 us (10%)
  between operations  1.43 us (2%)
    all_to_all x1, blocking collectives, on_device(): part = lax.all_to_all(part, 'z', 0, 0, tiled=True)  16 us
    all_to_all x1, blocking collectives, on_device(): part = lax.all_to_all(part, ('x', 'y'), 0, 0, tiled=True)  12.5 us
    ppermute x6, starting transfers between devices, turn(): lax.ppermute(value, 'y', [(i, (i + k) % GROUPS) for i in range(GROUPS)])  11 us
    ppermute x1, starting transfers between devices, on_device(): partner = lax.ppermute(own, 'c', swap)  4.38 us
    ppermute x6, waiting for transfers between devices, turn(): lax.ppermute(value, 'y', [(i, (i + k) % GROUPS) for i in range(GROUPS)])  4.28 us
    pallas_call x1, Pallas kernels, on_device(): pl.pallas_call(lambda *refs: grad_hidden_kernel(*refs, replicas=replicas)...  3.94 us
    all_to_all x1, starting transfers between devices, on_device(): lax.all_to_all(jnp.broadcast_to(piece, (PIECES, 8, half)), ('x', 'y'), 0,...  3.62 us
    all_to_all x1, waiting for transfers between devices, on_device(): lax.all_to_all(jnp.broadcast_to(piece, (PIECES, 8, half)), ('x', 'y'), 0,...  3.38 us
  transfers between devices with their start and end apart: 9, of which 7 were waited for; matrix products, arithmetic and copies ran while one was open for 0% of the time, Pallas kernels for 15%

profile of v7, /device:TPU:1, one launch (start us, length us, event | category | flops | bytes accessed | tf_op | source)
XLA Modules:
  0.0 79.2 jit_solution(4545652717053273913)
XLA Ops:
  0.6 0.1 pad_add_fusion.where.refs_0_
  0.7 0.0 copy-start.1
  0.7 0.0 copy-start.2
  0.7 0.0 copy-start.3
  0.7 0.0 copy-start.4
  0.7 0.0 copy-start.5
  0.7 2.4 %forward_far.1 = (f32[4,104,128]{2,1,0:T(8,128)S(1)}, bf16[104,1024]{1,0:T(8,128)(2,1)S(1)}) custom-call(s32[2]{0:T(128)S(1)} %pad_add_fusion.where.refs_0_, bf16[4,512,1024]{2,1,0:T(8,128)(2,1)} %hidden.5, f32[99,1024]{1,0:T(8,128)} %refs_6_.1), custom_call_target="tpu_custom_call" | custom-call | tf_op jit(solution)/shard_map/forward_far/forward_far/pallas_call | solution.py:291
  3.1 3.8 %collective-permute-start.2 = (f32[4,104,128]{2,1,0:T(8,128)S(1)}, f32[4,104,128]{2,1,0:T(8,128)S(1)}, u32[]{:S(2)}, u32[]{:S(2)}) collective-permute-start(f32[4,104,128]{2,1,0:T(8,128)S(1)} %get-tuple-element.36), channel_id=1, source_target_pairs={{0,128},{64,192},{128,0},{192,64},{1,129},{65,193},{129,1},{193,65... | collective-permute-start | bytes 638984 | tf_op jit(solution)/shard_map/forward_far/ppermute | solution.py:287
  6.9 2.7 %forward_near.1 = (f32[4,104,128]{2,1,0:T(8,128)S(1)}, f32[4,104,128]{2,1,0:T(8,128)S(1)}) custom-call(s32[2]{0:T(128)S(1)} %pad_add_fusion.where.refs_0_, bf16[4,512,1024]{2,1,0:T(8,128)(2,1)} %hidden.5, bf16[104,1024]{1,0:T(8,128)(2,1)S(1)} %get-tuple-element.32.half.refs_3_), custom_call_target="tpu_custom_call" | custom-call | flops 218103808 | bytes 2097152 | tf_op jit(solution)/shard_map/forward_near/forward_near/pallas_call | solution.py:307
  9.7 0.5 collective-permute-start
  10.2 2.3 %collective-permute-start.1 = (f32[4,104,128]{2,1,0:T(8,128)S(1)}, f32[4,104,128]{2,1,0:T(8,128)S(1)}, u32[]{:S(2)}, u32[]{:S(2)}) collective-permute-start(f32[4,104,128]{2,1,0:T(8,128)S(1)} %get-tuple-element.34), channel_id=1, source_target_pairs={{0,192},{64,0},{128,64},{192,128},{1,193},{65,1},{129,65},{193,129... | collective-permute-start | bytes 638984 | tf_op jit(solution)/shard_map/forward_near/ppermute | solution.py:287
  12.4 0.0 copy-done.1
  12.4 0.0 copy-done.2
  12.4 0.0 copy-done.3
  12.5 0.0 copy-done.4
  12.5 0.0 copy-done.5
  12.5 3.0 %forward_local.1 = (f32[4,104,128]{2,1,0:T(8,128)S(1)}, f32[1,128]{1,0:T(1,128)S(1)}, f32[104,512]{1,0:T(8,128)S(1)}, f32[104,128]{1,0:T(8,128)S(1)}, bf16[4,4,128,1024]{3,2,1,0:T(8,128)(2,1)S(1)}) custom-call(s32[2]{0:T(128)S(1)} %pad_add_fusion.where.refs_0_, bf16[4,512,1024]{2,1,0:T(8,128)(2,1)} %hidden.5, ...), custom_call_target="tpu_custom_call" | custom-call | tf_op jit(solution)/shard_map/forward_local/forward_local/pallas_call | solution.py:324
  15.5 0.0 collective-permute-done.2.far.refs_1_
  15.5 0.5 early_pairs.1.refs_5_
  16.0 0.8 %collective-permute-done.refs_2_ = f32[4,104,128]{2,1,0:T(8,128)S(1)} collective-permute-done((f32[4,104,128]{2,1,0:T(8,128)S(1)}, f32[4,104,128]{2,1,0:T(8,128)S(1)}, u32[]{:S(2)}, u32[]{:S(2)}) %collective-permute-start) | collective-permute-done | bytes 213024 | tf_op jit(solution)/shard_map/forward_near/ppermute | solution.py:287
  16.8 0.0 collective-permute-done.1.refs_3_
  16.8 1.5 %late_pairs.1 = (bf16[4,104,128]{2,1,0:T(8,128)(2,1)S(1)}, bf16[4,104,128]{2,1,0:T(8,128)(2,1)S(1)}, bf16[4,104,128]{2,1,0:T(8,128)(2,1)S(1)}, bf16[4,104,128]{2,1,0:T(8,128)(2,1)S(1)}) custom-call(f32[4,104,128]{2,1,0:T(8,128)S(1)} %get-tuple-element.35.here.refs_0_, f32[4,104,128]{2,1,0:T(8,128)S(1)} %collective-permute-done.2.far.refs_1_, ...), custom_call_target="tpu_custom_call" | custom-call | tf_op jit(solution)/shard_map/late_pairs/late_pairs/pallas_call | solution.py:350
  18.3 2.9 %collective-permute-start.5 = (bf16[4,104,128]{2,1,0:T(8,128)(2,1)S(1)}, bf16[4,104,128]{2,1,0:T(8,128)(2,1)S(1)}, u32[]{:S(2)}, u32[]{:S(2)}) collective-permute-start(bf16[4,104,128]{2,1,0:T(8,128)(2,1)S(1)} %get-tuple-element.49), channel_id=1, source_target_pairs={{0,128},{64,192},{128,0},{192,64},{1,129},{65,193},{129,1},{193,65... | collective-permute-start | bytes 319496 | tf_op jit(solution)/shard_map/bracket_exchange/ppermute | solution.py:287
  21.2 0.4 collective-permute-start.3
  21.6 1.1 %collective-permute-start.4 = (bf16[4,104,128]{2,1,0:T(8,128)(2,1)S(1)}, bf16[4,104,128]{2,1,0:T(8,128)(2,1)S(1)}, u32[]{:S(2)}, u32[]{:S(2)}) collective-permute-start(bf16[4,104,128]{2,1,0:T(8,128)(2,1)S(1)} %get-tuple-element.45), channel_id=1, source_target_pairs={{0,64},{64,128},{128,192},{192,0},{1,65},{65,129},{129,193},{193,1... | collective-permute-start | bytes 319496 | tf_op jit(solution)/shard_map/bracket_exchange/ppermute | solution.py:287
  22.7 0.8 collective-permute-done.5.b2
  23.5 1.0 %early_backward.1 = (bf16[2,104,512]{2,1,0:T(8,128)(2,1)S(1)}, f32[104,1024]{1,0:T(8,128)S(1)}, f32[8,104]{1,0:T(8,128)S(1)}) custom-call(s32[2]{0:T(128)S(1)} %pad_add_fusion.where.refs_0_, bf16[4,4,128,1024]{3,2,1,0:T(8,128)(2,1)S(1)} %get-tuple-element.40.held, bf16[4,104,128]{2,1,0:T(8,128)(2,1)S(1)} %get-tuple-element.48.b0, ...), custom_call_target="tpu_custom_call" | custom-call | tf_op jit(solution)/shard_map/early_backward/early_backward/pallas_call | solution.py:366
  24.5 0.6 collective-permute-done.3.b1
  25.1 2.1 %collective-permute-done.4.b3 = bf16[4,104,128]{2,1,0:T(8,128)(2,1)S(1)} collective-permute-done((bf16[4,104,128]{2,1,0:T(8,128)(2,1)S(1)}, bf16[4,104,128]{2,1,0:T(8,128)(2,1)S(1)}, u32[]{:S(2)}, u32[]{:S(2)}) %collective-permute-start.4) | collective-permute-done | bytes 106528 | tf_op jit(solution)/shard_map/bracket_exchange/ppermute | solution.py:287
  27.2 0.9 %backward_partner_half.1 = (bf16[2,104,512]{2,1,0:T(8,128)(2,1)S(1)}, f32[16,8,512]{2,1,0:T(8,128)S(1)}) custom-call(s32[2]{0:T(128)S(1)} %pad_add_fusion.where.refs_0_, bf16[4,4,128,1024]{3,2,1,0:T(8,128)(2,1)S(1)} %get-tuple-element.40.held, bf16[4,104,128]{2,1,0:T(8,128)(2,1)S(1)} %collective-permute-done.3.b1, ...), custom_call_target="tpu_custom_call" | custom-call | tf_op jit(solution)/shard_map/backward_partner_half/backward_partner_half/pallas_call | solution.py:379
  28.1 2.5 %collective-permute-start.6 = (f32[16,8,512]{2,1,0:T(8,128)S(1)}, f32[16,8,512]{2,1,0:T(8,128)S(1)}, u32[]{:S(2)}, u32[]{:S(2)}) collective-permute-start(f32[16,8,512]{2,1,0:T(8,128)S(1)} %get-tuple-element.53), channel_id=1, source_target_pairs={{0,1},{1,0},{2,3},{3,2},{4,5},{5,4},{6,7},{7,6},{8,9},{9,8},{10,11... | collective-permute-start | bytes 786440 | tf_op jit(solution)/shard_map/backward_partner_half/ppermute | solution.py:389
  30.6 0.9 %backward_own_half.1 = f32[16,8,512]{2,1,0:T(8,128)S(1)} custom-call(s32[2]{0:T(128)S(1)} %pad_add_fusion.where.refs_0_, bf16[4,4,128,1024]{3,2,1,0:T(8,128)(2,1)S(1)} %get-tuple-element.40.held, bf16[2,104,512]{2,1,0:T(8,128)(2,1)S(1)} %get-tuple-element.51.weighted.refs_2_, f32[104,1024]{1,0:T(8,128)S(1)} %get-tuple-element.50.early, ...), custom_call_target="tpu_custom_call" | custom-call | tf_op jit(solution)/shard_map/backward_own_half/backward_own_half/pallas_call | solution.py:391
  31.5 0.0 copy-start
  31.5 0.2 collective-permute-done.6
  31.8 12.5 %all_to_all.15 = f32[16,8,512]{2,1,0:T(8,128)S(1)} all-to-all(f32[16,8,512]{2,1,0:T(8,128)S(1)} %add.3), channel_id=1, replica_groups=mesh['y'=4,'z'=8,'x'=4,'c'=2] {'x','y'}, dimensions={0} | all-to-all | bytes 524288 | tf_op jit(solution)/shard_map/gradient_sum/all_to_all | solution.py:402
  44.4 16.0 %all_to_all.16 = f32[8,8,512]{2,1,0:T(8,128)S(1)} all-to-all(f32[8,8,512]{2,1,0:T(8,128)S(1)} %broadcast_in_dim.6), channel_id=1, replica_groups=mesh['y'=4,'z'=8,'x'=4,'c'=2] {'z'}, dimensions={0} | all-to-all | bytes 262144 | tf_op jit(solution)/shard_map/gradient_sum/all_to_all | solution.py:405
  60.4 0.7 broadcast_in_dim.7
  61.1 3.6 %all-to-all-start.2 = ((f32[16,8,512]{2,1,0:T(8,128)}), f32[16,8,512]{2,1,0:T(8,128)S(1)}, u32[]{:S(2)}, u32[]{:S(2)}) async-start(f32[16,8,512]{2,1,0:T(8,128)} %broadcast_in_dim.7), calls=%async_computation.2 | async-start | bytes 524288 | tf_op jit(solution)/shard_map/gradient_sum/all_to_all | solution.py:407
  64.7 3.9 %grad_hidden.1 = bf16[4,512,1024]{2,1,0:T(8,128)(2,1)} custom-call(s32[2]{0:T(128)S(1)} %pad_add_fusion.where.refs_0_, bf16[2,104,512]{2,1,0:T(8,128)(2,1)S(1)} %get-tuple-element.54.refs_1_, bf16[2,104,512]{2,1,0:T(8,128)(2,1)S(1)} %get-tuple-element.51.weighted.refs_2_, bf16[104,1024]{1,0:T(8,128)(2,1)S(1)} %get-tuple-element.32.half.refs_3_, ...), custom_call_target="tpu_custom_call" | custom-call | flops 436207616 | bytes 4194304 | tf_op jit(solution)/shard_map/grad_hidden/grad_hidden/pallas_call | solution.py:409
  68.7 3.4 %all-to-all-done.2.refs_0_.refs_2_ = f32[16,8,512]{2,1,0:T(8,128)S(1)} async-done(((f32[16,8,512]{2,1,0:T(8,128)}), f32[16,8,512]{2,1,0:T(8,128)S(1)}, u32[]{:S(2)}, u32[]{:S(2)}) %all-to-all-start.2) | async-done | bytes 262176 | tf_op jit(solution)/shard_map/gradient_sum/all_to_all | solution.py:407
  72.1 4.4 %collective-permute-start.7 = (f32[16,8,512]{2,1,0:T(8,128)S(1)}, f32[16,8,512]{2,1,0:T(8,128)S(1)}, u32[]{:S(2)}, u32[]{:S(2)}) collective-permute-start(f32[16,8,512]{2,1,0:T(8,128)S(1)} %all-to-all-done.2.refs_0_.refs_2_), channel_id=1, source_target_pairs={{0,1},{1,0},{2,3},{3,2},{4,5},{5,4},{6,7},{7,6},{8,9},{9,8},{10,11... | collective-permute-start | bytes 786440 | tf_op jit(solution)/shard_map/last_swap/ppermute | solution.py:431
  77.1 0.1 own_gradient.1
  77.2 0.4 collective-permute-done.7.refs_4_
  77.6 0.0 copy-done
  77.6 1.6 %update.1 = (f32[99,1024]{1,0:T(8,128)}, f32[1,99]{1,0:T(1,128)}) custom-call(s32[2]{0:T(128)S(1)} %pad_add_fusion.where.refs_0_, s32[1]{0:T(128)S(6)} %copy.11.refs_1_, f32[16,8,512]{2,1,0:T(8,128)S(1)} %all-to-all-done.2.refs_0_.refs_2_, f32[99,512]{1,0:T(8,128)S(1)} %get-tuple-element.57.refs_3_, f32[16,8,512]{2,1,0:T(8,128)S(1)} %collective-permute-done.7.refs_4_, ...), custom_call_target="tpu_custom_call" | custom-call | tf_op jit(solution)/shard_map/update/update/pallas_call | solution.py:441
  (4 shorter events, 0.1 us)
Async XLA Ops:
  0.7 11.7 %copy-start.1 = (f32[99,512]{1,0:T(8,128)S(1)}, f32[99,512]{1,0:T(8,128)}, u32[]{:S(2)}) copy-start(f32[99,512]{1,0:T(8,128)} %truth.1) | copy-start | bytes 608260
  0.7 11.7 %copy-start.2 = (f32[640]{0:T(1024)S(1)}, f32[640]{0:T(1024)}, u32[]{:S(2)}) copy-start(f32[640]{0:T(1024)} %param.13) | copy-start | bytes 7684
  0.7 11.7 %copy-start.3 = (f32[99]{0:T(128)S(1)}, f32[99]{0:T(128)}, u32[]{:S(2)}) copy-start(f32[99]{0:T(128)} %param.10) | copy-start | bytes 1192
  0.7 11.7 %copy-start.4 = (s32[512]{0:T(512)S(1)}, s32[512]{0:T(512)}, u32[]{:S(2)}) copy-start(s32[512]{0:T(512)} %param.14) | copy-start | bytes 6148
  0.7 11.7 %copy-start.5 = (f32[99]{0:T(128)S(1)}, f32[99]{0:T(128)}, u32[]{:S(2)}) copy-start(f32[99]{0:T(128)} %param.12) | copy-start | bytes 1192
  3.1 12.4 %collective-permute-start.2 = (f32[4,104,128]{2,1,0:T(8,128)S(1)}, f32[4,104,128]{2,1,0:T(8,128)S(1)}, u32[]{:S(2)}, u32[]{:S(2)}) collective-permute-start(f32[4,104,128]{2,1,0:T(8,128)S(1)} %get-tuple-element.36), channel_id=1, source_target_pairs={{0,128},{64,192},{128,0},{192,64},{1,129},{65,193},{129,1},{193,65... | collective-permute-start | bytes 638984 | tf_op jit(solution)/shard_map/forward_far/ppermute | solution.py:287
  9.7 7.1 %collective-permute-start = (f32[4,104,128]{2,1,0:T(8,128)S(1)}, f32[4,104,128]{2,1,0:T(8,128)S(1)}, u32[]{:S(2)}, u32[]{:S(2)}) collective-permute-start(f32[4,104,128]{2,1,0:T(8,128)S(1)} %get-tuple-element.33), channel_id=1, source_target_pairs={{0,64},{64,128},{128,192},{192,0},{1,65},{65,129},{129,193},{193,1... | collective-permute-start | bytes 638984 | tf_op jit(solution)/shard_map/forward_near/ppermute | solution.py:287
  10.2 6.7 %collective-permute-start.1 = (f32[4,104,128]{2,1,0:T(8,128)S(1)}, f32[4,104,128]{2,1,0:T(8,128)S(1)}, u32[]{:S(2)}, u32[]{:S(2)}) collective-permute-start(f32[4,104,128]{2,1,0:T(8,128)S(1)} %get-tuple-element.34), channel_id=1, source_target_pairs={{0,192},{64,0},{128,64},{192,128},{1,193},{65,1},{129,65},{193,129... | collective-permute-start | bytes 638984 | tf_op jit(solution)/shard_map/forward_near/ppermute | solution.py:287
  18.3 5.1 %collective-permute-start.5 = (bf16[4,104,128]{2,1,0:T(8,128)(2,1)S(1)}, bf16[4,104,128]{2,1,0:T(8,128)(2,1)S(1)}, u32[]{:S(2)}, u32[]{:S(2)}) collective-permute-start(bf16[4,104,128]{2,1,0:T(8,128)(2,1)S(1)} %get-tuple-element.49), channel_id=1, source_target_pairs={{0,128},{64,192},{128,0},{192,64},{1,129},{65,193},{129,1},{193,65... | collective-permute-start | bytes 319496 | tf_op jit(solution)/shard_map/bracket_exchange/ppermute | solution.py:287
  21.2 3.9 %collective-permute-start.3 = (bf16[4,104,128]{2,1,0:T(8,128)(2,1)S(1)}, bf16[4,104,128]{2,1,0:T(8,128)(2,1)S(1)}, u32[]{:S(2)}, u32[]{:S(2)}) collective-permute-start(bf16[4,104,128]{2,1,0:T(8,128)(2,1)S(1)} %get-tuple-element.44), channel_id=1, source_target_pairs={{0,192},{64,0},{128,64},{192,128},{1,193},{65,1},{129,65},{193,129... | collective-permute-start | bytes 319496 | tf_op jit(solution)/shard_map/bracket_exchange/ppermute | solution.py:287
  21.6 5.6 %collective-permute-start.4 = (bf16[4,104,128]{2,1,0:T(8,128)(2,1)S(1)}, bf16[4,104,128]{2,1,0:T(8,128)(2,1)S(1)}, u32[]{:S(2)}, u32[]{:S(2)}) collective-permute-start(bf16[4,104,128]{2,1,0:T(8,128)(2,1)S(1)} %get-tuple-element.45), channel_id=1, source_target_pairs={{0,64},{64,128},{128,192},{192,0},{1,65},{65,129},{129,193},{193,1... | collective-permute-start | bytes 319496 | tf_op jit(solution)/shard_map/bracket_exchange/ppermute | solution.py:287
  28.1 3.7 %collective-permute-start.6 = (f32[16,8,512]{2,1,0:T(8,128)S(1)}, f32[16,8,512]{2,1,0:T(8,128)S(1)}, u32[]{:S(2)}, u32[]{:S(2)}) collective-permute-start(f32[16,8,512]{2,1,0:T(8,128)S(1)} %get-tuple-element.53), channel_id=1, source_target_pairs={{0,1},{1,0},{2,3},{3,2},{4,5},{5,4},{6,7},{7,6},{8,9},{9,8},{10,11... | collective-permute-start | bytes 786440 | tf_op jit(solution)/shard_map/backward_partner_half/ppermute | solution.py:389
  31.5 46.1 %copy-start = (f32[99,1024]{1,0:T(8,128)S(1)}, f32[99,1024]{1,0:T(8,128)}, u32[]{:S(2)}) copy-start(f32[99,1024]{1,0:T(8,128)} %refs_6_.1) | copy-start | bytes 1216516
  61.1 10.9 %all-to-all-start.2 = ((f32[16,8,512]{2,1,0:T(8,128)}), f32[16,8,512]{2,1,0:T(8,128)S(1)}, u32[]{:S(2)}, u32[]{:S(2)}) async-start(f32[16,8,512]{2,1,0:T(8,128)} %broadcast_in_dim.7), calls=%async_computation.2 | async-start | bytes 524288 | tf_op jit(solution)/shard_map/gradient_sum/all_to_all | solution.py:407
  72.1 5.5 %collective-permute-start.7 = (f32[16,8,512]{2,1,0:T(8,128)S(1)}, f32[16,8,512]{2,1,0:T(8,128)S(1)}, u32[]{:S(2)}, u32[]{:S(2)}) collective-permute-start(f32[16,8,512]{2,1,0:T(8,128)S(1)} %all-to-all-done.2.refs_0_.refs_2_), channel_id=1, source_target_pairs={{0,1},{1,0},{2,3},{3,2},{4,5},{5,4},{6,7},{7,6},{8,9},{9,8},{10,11... | collective-permute-start | bytes 786440 | tf_op jit(solution)/shard_map/last_swap/ppermute | solution.py:431

commit v8 on v7

--- a/solution.py
+++ b/solution.py
@@ -82,7 +82,13 @@
     total[j] = -s if total[j] is None else total[j] - s
 
 
-def early_pairs_kernel(here, far, shift, out):
+def pair_normalizer(members):
+    eps = (1.0 - fair_alpha) / members
+    return (1.0 - eps) / (members * (members - 1))
+
+
+def early_pairs_kernel(members, here, far, shift, out):
+    normalizer = pair_normalizer(members)
     local = here.shape[0]
     count = 2 * local
 
@@ -94,7 +100,7 @@
             for j in range(i + 1, count):
                 add_pair(total, i, j, soft(r[i] - r[j]))
         for j in range(count):
-            out[j, at, :] = total[j]
+            out[j, at, :] = soft(r[j]) * (1.0 / members) - normalizer * total[j]
         return carry
 
     lax.fori_loop(0, here.shape[1] // 8, tile, 0)
@@ -104,18 +110,18 @@
     ins, outs, scratch = (here, far, after, before), rest[:GROUPS], rest[GROUPS]
     local = here.shape[0]
     count = early.shape[0]
-    eps = (1.0 - fair_alpha) / members
-    normalizer = (1.0 - eps) / (members * (members - 1))
+    normalizer = pair_normalizer(members)
 
     def tile(t, carry):
         at = pl.ds(pl.multiple_of(t * 8, 8), 8)
         r = [ref[j, at, :] + shift[at, :] for ref in ins for j in range(local)]
-        total = [early[j, at, :] for j in range(count)] + [None] * (members - count)
+        total = [None] * members
         for i in range(members):
             for j in range(max(i + 1, count), members):
                 add_pair(total, i, j, soft(r[i] - r[j]))
         for j in range(members):
-            scratch[j, at, :] = soft(r[j]) * (1.0 / members) - normalizer * total[j]
+            base = early[j, at, :] if j < count else soft(r[j]) * (1.0 / members)
+            scratch[j, at, :] = base - normalizer * total[j]
         return carry
 
     lax.fori_loop(0, here.shape[1] // 8, tile, 0)
@@ -205,6 +211,18 @@
     bias = early_bias[...] + bias_of(w1) + bias_of(w3)
     bias = jnp.concatenate([bias[0:1], jnp.zeros((1, 128 - rows), F32)], axis=1)
     pieces_of(acc, extra_row(bias, area[...], acc.shape[1]), mine)
+
+
+def sum_kernel(parts, piece, copies_out, sem):
+    total = parts[0]
+    for k in range(1, parts.shape[0]):
+        total = total + parts[k]
+    piece[...] = total
+    copies = [pltpu.make_async_copy(piece, copies_out.at[r], sem.at[r]) for r in range(PIECES)]
+    for copy in copies:
+        copy.start()
+    for copy in copies:
+        copy.wait()
 
 
 def grad_hidden_kernel(where, early, late, half, piece, out, *, replicas):
@@ -338,7 +356,7 @@
         )(where, hidden, half_weight, lat_weight.reshape(-1, 128), area_bin.reshape(1, points), intercept_row, analysis_truth, var_row)
     with jax.named_scope("early_pairs"):
         early = pl.pallas_call(
-            early_pairs_kernel,
+            lambda *refs: early_pairs_kernel(members, *refs),
             out_shape=jax.ShapeDtypeStruct((2 * local, rows, chunk), F32),
             in_specs=[VMEM] * 3,
             out_specs=VMEM,
@@ -403,8 +421,16 @@
         depth = lax.axis_size("z")
         part = jnp.broadcast_to(jnp.sum(part, axis=0), (depth, 8, half))
         part = lax.all_to_all(part, "z", 0, 0, tiled=True)
-        piece = jnp.sum(part, axis=0)
-        own = lax.all_to_all(jnp.broadcast_to(piece, (PIECES, 8, half)), ("x", "y"), 0, 0, tiled=True)
+        piece, outgoing = pl.pallas_call(
+            sum_kernel,
+            out_shape=[jax.ShapeDtypeStruct((8, half), F32), pieces],
+            in_specs=[VMEM],
+            out_specs=[VMEM, HBM],
+            scratch_shapes=[pltpu.SemaphoreType.DMA((PIECES,))],
+            compiler_params=grant(4),
+            name="sum_pieces",
+        )(part)
+        own = lax.all_to_all(outgoing, ("x", "y"), 0, 0, tiled=True)
     with jax.named_scope("grad_hidden"):
         grad_hidden = pl.pallas_call(
             lambda *refs: grad_hidden_kernel(*refs, replicas=replicas),

time: 79.5 us -> 79.5 us (level)
  Pallas kernels: 18.6 us -> 19.4 us
    pallas_call x1 -> x2, Pallas kernels: 0.45 us -> 1.38 us  [the longest x1 0.84 us: on_device(): pl.pallas_call(sum_kernel, out_shape=[jax.ShapeDtypeStruct((8, half), F32...]
  transfers between devices with their start and end apart: 9 -> 9, of which waited for: 7 -> 7; matrix products, arithmetic and copies ran while one was open for 0% -> 0% of each run, Pallas kernels for 15% -> 16%
where the time goes in v8:
time: 79.5 us; the launch traced here: 79.2 us
  blocking collectives  28.5 us (36%)
  starting transfers between devices  21.5 us (27%)
  Pallas kernels  19.4 us (24%)
  waiting for transfers between devices  8.17 us (10%)
  between operations  1.43 us (2%)
    all_to_all x1, blocking collectives, on_device(): part = lax.all_to_all(part, 'z', 0, 0, tiled=True)  16 us
    all_to_all x1, blocking collectives, on_device(): part = lax.all_to_all(part, ('x', 'y'), 0, 0, tiled=True)  12.5 us
    ppermute x6, starting transfers between devices, turn(): lax.ppermute(value, 'y', [(i, (i + k) % GROUPS) for i in range(GROUPS)])  11 us
    ppermute x1, starting transfers between devices, on_device(): partner = lax.ppermute(own, 'c', swap)  4.38 us
    ppermute x6, waiting for transfers between devices, turn(): lax.ppermute(value, 'y', [(i, (i + k) % GROUPS) for i in range(GROUPS)])  4.19 us
    pallas_call x1, Pallas kernels, on_device(): pl.pallas_call(lambda *refs: grad_hidden_kernel(*refs, replicas=replicas)...  3.94 us
    all_to_all x1, starting transfers between devices, on_device(): own = lax.all_to_all(outgoing, ('x', 'y'), 0, 0, tiled=True)  3.63 us
    all_to_all x1, waiting for transfers between devices, on_device(): own = lax.all_to_all(outgoing, ('x', 'y'), 0, 0, tiled=True)  3.38 us
  transfers between devices with their start and end apart: 9, of which 7 were waited for; matrix products, arithmetic and copies ran while one was open for 0% of the time, Pallas kernels for 16%

profile of v8, /device:TPU:1, one launch (start us, length us, event | category | flops | bytes accessed | tf_op | source)
XLA Modules:
  0.0 79.2 jit_solution(8208824185342265992)
XLA Ops:
  0.6 0.1 pad_add_fusion.where.refs_0_
  0.7 0.0 copy-start.1
  0.7 0.0 copy-start.2
  0.7 0.0 copy-start.3
  0.7 0.0 copy-start.4
  0.7 0.0 copy-start.5
  0.7 2.4 %forward_far.1 = (f32[4,104,128]{2,1,0:T(8,128)S(1)}, bf16[104,1024]{1,0:T(8,128)(2,1)S(1)}) custom-call(s32[2]{0:T(128)S(1)} %pad_add_fusion.where.refs_0_, bf16[4,512,1024]{2,1,0:T(8,128)(2,1)} %hidden.5, f32[99,1024]{1,0:T(8,128)} %refs_6_.1), custom_call_target="tpu_custom_call" | custom-call | tf_op jit(solution)/shard_map/forward_far/forward_far/pallas_call | solution.py:309
  3.1 3.8 %collective-permute-start.2 = (f32[4,104,128]{2,1,0:T(8,128)S(1)}, f32[4,104,128]{2,1,0:T(8,128)S(1)}, u32[]{:S(2)}, u32[]{:S(2)}) collective-permute-start(f32[4,104,128]{2,1,0:T(8,128)S(1)} %get-tuple-element.38), channel_id=1, source_target_pairs={{0,128},{64,192},{128,0},{192,64},{1,129},{65,193},{129,1},{193,65... | collective-permute-start | bytes 638984 | tf_op jit(solution)/shard_map/forward_far/ppermute | solution.py:305
  6.9 2.7 %forward_near.1 = (f32[4,104,128]{2,1,0:T(8,128)S(1)}, f32[4,104,128]{2,1,0:T(8,128)S(1)}) custom-call(s32[2]{0:T(128)S(1)} %pad_add_fusion.where.refs_0_, bf16[4,512,1024]{2,1,0:T(8,128)(2,1)} %hidden.5, bf16[104,1024]{1,0:T(8,128)(2,1)S(1)} %get-tuple-element.34.half.refs_3_), custom_call_target="tpu_custom_call" | custom-call | flops 218103808 | bytes 2097152 | tf_op jit(solution)/shard_map/forward_near/forward_near/pallas_call | solution.py:325
  9.7 0.5 collective-permute-start
  10.2 2.3 %collective-permute-start.1 = (f32[4,104,128]{2,1,0:T(8,128)S(1)}, f32[4,104,128]{2,1,0:T(8,128)S(1)}, u32[]{:S(2)}, u32[]{:S(2)}) collective-permute-start(f32[4,104,128]{2,1,0:T(8,128)S(1)} %get-tuple-element.36), channel_id=1, source_target_pairs={{0,192},{64,0},{128,64},{192,128},{1,193},{65,1},{129,65},{193,129... | collective-permute-start | bytes 638984 | tf_op jit(solution)/shard_map/forward_near/ppermute | solution.py:305
  12.4 0.0 copy-done.1
  12.4 0.0 copy-done.2
  12.4 0.0 copy-done.3
  12.5 0.0 copy-done.4
  12.5 0.0 copy-done.5
  12.5 3.0 %forward_local.1 = (f32[4,104,128]{2,1,0:T(8,128)S(1)}, f32[1,128]{1,0:T(1,128)S(1)}, f32[104,512]{1,0:T(8,128)S(1)}, f32[104,128]{1,0:T(8,128)S(1)}, bf16[4,4,128,1024]{3,2,1,0:T(8,128)(2,1)S(1)}) custom-call(s32[2]{0:T(128)S(1)} %pad_add_fusion.where.refs_0_, bf16[4,512,1024]{2,1,0:T(8,128)(2,1)} %hidden.5, ...), custom_call_target="tpu_custom_call" | custom-call | tf_op jit(solution)/shard_map/forward_local/forward_local/pallas_call | solution.py:342
  15.5 0.0 collective-permute-done.2.refs_1_
  15.5 0.5 early_pairs.1.refs_5_
  16.1 0.8 collective-permute-done.refs_2_
  16.8 0.0 collective-permute-done.1.refs_3_
  16.8 1.4 %late_pairs.1 = (bf16[4,104,128]{2,1,0:T(8,128)(2,1)S(1)}, bf16[4,104,128]{2,1,0:T(8,128)(2,1)S(1)}, bf16[4,104,128]{2,1,0:T(8,128)(2,1)S(1)}, bf16[4,104,128]{2,1,0:T(8,128)(2,1)S(1)}) custom-call(f32[4,104,128]{2,1,0:T(8,128)S(1)} %get-tuple-element.37.refs_0_, f32[4,104,128]{2,1,0:T(8,128)S(1)} %collective-permute-done.2.refs_1_, ...), custom_call_target="tpu_custom_call" | custom-call | tf_op jit(solution)/shard_map/late_pairs/late_pairs/pallas_call | solution.py:368
  18.2 2.9 %collective-permute-start.5 = (bf16[4,104,128]{2,1,0:T(8,128)(2,1)S(1)}, bf16[4,104,128]{2,1,0:T(8,128)(2,1)S(1)}, u32[]{:S(2)}, u32[]{:S(2)}) collective-permute-start(bf16[4,104,128]{2,1,0:T(8,128)(2,1)S(1)} %get-tuple-element.51), channel_id=1, source_target_pairs={{0,128},{64,192},{128,0},{192,64},{1,129},{65,193},{129,1},{193,65... | collective-permute-start | bytes 319496 | tf_op jit(solution)/shard_map/bracket_exchange/ppermute | solution.py:305
  21.1 0.4 collective-permute-start.3
  21.5 1.1 %collective-permute-start.4 = (bf16[4,104,128]{2,1,0:T(8,128)(2,1)S(1)}, bf16[4,104,128]{2,1,0:T(8,128)(2,1)S(1)}, u32[]{:S(2)}, u32[]{:S(2)}) collective-permute-start(bf16[4,104,128]{2,1,0:T(8,128)(2,1)S(1)} %get-tuple-element.47), channel_id=1, source_target_pairs={{0,64},{64,128},{128,192},{192,0},{1,65},{65,129},{129,193},{193,1... | collective-permute-start | bytes 319496 | tf_op jit(solution)/shard_map/bracket_exchange/ppermute | solution.py:305
  22.6 0.8 collective-permute-done.5.b2
  23.4 1.0 %early_backward.1 = (bf16[2,104,512]{2,1,0:T(8,128)(2,1)S(1)}, f32[104,1024]{1,0:T(8,128)S(1)}, f32[8,104]{1,0:T(8,128)S(1)}) custom-call(s32[2]{0:T(128)S(1)} %pad_add_fusion.where.refs_0_, bf16[4,4,128,1024]{3,2,1,0:T(8,128)(2,1)S(1)} %get-tuple-element.42.held, bf16[4,104,128]{2,1,0:T(8,128)(2,1)S(1)} %get-tuple-element.50.b0, ...), custom_call_target="tpu_custom_call" | custom-call | tf_op jit(solution)/shard_map/early_backward/early_backward/pallas_call | solution.py:384
  24.4 0.6 collective-permute-done.3.b1
  25.0 2.1 %collective-permute-done.4.b3 = bf16[4,104,128]{2,1,0:T(8,128)(2,1)S(1)} collective-permute-done((bf16[4,104,128]{2,1,0:T(8,128)(2,1)S(1)}, bf16[4,104,128]{2,1,0:T(8,128)(2,1)S(1)}, u32[]{:S(2)}, u32[]{:S(2)}) %collective-permute-start.4) | collective-permute-done | bytes 106528 | tf_op jit(solution)/shard_map/bracket_exchange/ppermute | solution.py:305
  27.1 0.9 %backward_partner_half.1 = (bf16[2,104,512]{2,1,0:T(8,128)(2,1)S(1)}, f32[16,8,512]{2,1,0:T(8,128)S(1)}) custom-call(s32[2]{0:T(128)S(1)} %pad_add_fusion.where.refs_0_, bf16[4,4,128,1024]{3,2,1,0:T(8,128)(2,1)S(1)} %get-tuple-element.42.held, bf16[4,104,128]{2,1,0:T(8,128)(2,1)S(1)} %collective-permute-done.3.b1, ...), custom_call_target="tpu_custom_call" | custom-call | tf_op jit(solution)/shard_map/backward_partner_half/backward_partner_half/pallas_call | solution.py:397
  28.0 2.5 %collective-permute-start.6 = (f32[16,8,512]{2,1,0:T(8,128)S(1)}, f32[16,8,512]{2,1,0:T(8,128)S(1)}, u32[]{:S(2)}, u32[]{:S(2)}) collective-permute-start(f32[16,8,512]{2,1,0:T(8,128)S(1)} %get-tuple-element.55), channel_id=1, source_target_pairs={{0,1},{1,0},{2,3},{3,2},{4,5},{5,4},{6,7},{7,6},{8,9},{9,8},{10,11... | collective-permute-start | bytes 786440 | tf_op jit(solution)/shard_map/backward_partner_half/ppermute | solution.py:407
  30.5 0.9 %backward_own_half.1 = f32[16,8,512]{2,1,0:T(8,128)S(1)} custom-call(s32[2]{0:T(128)S(1)} %pad_add_fusion.where.refs_0_, bf16[4,4,128,1024]{3,2,1,0:T(8,128)(2,1)S(1)} %get-tuple-element.42.held, bf16[2,104,512]{2,1,0:T(8,128)(2,1)S(1)} %get-tuple-element.53.weighted.refs_2_, f32[104,1024]{1,0:T(8,128)S(1)} %get-tuple-element.52.early, ...), custom_call_target="tpu_custom_call" | custom-call | tf_op jit(solution)/shard_map/backward_own_half/backward_own_half/pallas_call | solution.py:409
  31.4 0.0 copy-start
  31.4 0.2 collective-permute-done.6
  31.7 12.5 %all_to_all.15 = f32[16,8,512]{2,1,0:T(8,128)S(1)} all-to-all(f32[16,8,512]{2,1,0:T(8,128)S(1)} %add.3), channel_id=1, replica_groups=mesh['y'=4,'z'=8,'x'=4,'c'=2] {'x','y'}, dimensions={0} | all-to-all | bytes 524288 | tf_op jit(solution)/shard_map/gradient_sum/all_to_all | solution.py:420
  44.3 16.0 %all_to_all.16.parts = f32[8,8,512]{2,1,0:T(8,128)S(1)} all-to-all(f32[8,8,512]{2,1,0:T(8,128)S(1)} %broadcast_in_dim.3), channel_id=1, replica_groups=mesh['y'=4,'z'=8,'x'=4,'c'=2] {'z'}, dimensions={0} | all-to-all | bytes 262144 | tf_op jit(solution)/shard_map/gradient_sum/all_to_all | solution.py:423
  60.3 0.8 %sum_pieces.1 = (f32[8,512]{1,0:T(8,128)S(1)}, f32[16,8,512]{2,1,0:T(8,128)}) custom-call(f32[8,8,512]{2,1,0:T(8,128)S(1)} %all_to_all.16.parts), custom_call_target="tpu_custom_call" | custom-call | tf_op jit(solution)/shard_map/gradient_sum/sum_pieces/pallas_call | solution.py:424
  61.1 3.6 %all-to-all-start.2 = ((f32[16,8,512]{2,1,0:T(8,128)}), f32[16,8,512]{2,1,0:T(8,128)S(1)}, u32[]{:S(2)}, u32[]{:S(2)}) async-start(f32[16,8,512]{2,1,0:T(8,128)} %get-tuple-element.56), calls=%async_computation.2 | async-start | bytes 524288 | tf_op jit(solution)/shard_map/gradient_sum/all_to_all | solution.py:433
  64.8 3.9 %grad_hidden.1 = bf16[4,512,1024]{2,1,0:T(8,128)(2,1)} custom-call(s32[2]{0:T(128)S(1)} %pad_add_fusion.where.refs_0_, bf16[2,104,512]{2,1,0:T(8,128)(2,1)S(1)} %get-tuple-element.57.refs_1_, bf16[2,104,512]{2,1,0:T(8,128)(2,1)S(1)} %get-tuple-element.53.weighted.refs_2_, bf16[104,1024]{1,0:T(8,128)(2,1)S(1)} %get-tuple-element.34.half.refs_3_, ...), custom_call_target="tpu_custom_call" | custom-call | flops 436207616 | bytes 4194304 | tf_op jit(solution)/shard_map/grad_hidden/grad_hidden/pallas_call | solution.py:435
  68.7 3.4 %all-to-all-done.2.refs_0_.refs_2_ = f32[16,8,512]{2,1,0:T(8,128)S(1)} async-done(((f32[16,8,512]{2,1,0:T(8,128)}), f32[16,8,512]{2,1,0:T(8,128)S(1)}, u32[]{:S(2)}, u32[]{:S(2)}) %all-to-all-start.2) | async-done | bytes 262176 | tf_op jit(solution)/shard_map/gradient_sum/all_to_all | solution.py:433
  72.1 4.4 %collective-permute-start.7 = (f32[16,8,512]{2,1,0:T(8,128)S(1)}, f32[16,8,512]{2,1,0:T(8,128)S(1)}, u32[]{:S(2)}, u32[]{:S(2)}) collective-permute-start(f32[16,8,512]{2,1,0:T(8,128)S(1)} %all-to-all-done.2.refs_0_.refs_2_), channel_id=1, source_target_pairs={{0,1},{1,0},{2,3},{3,2},{4,5},{5,4},{6,7},{7,6},{8,9},{9,8},{10,11... | collective-permute-start | bytes 786440 | tf_op jit(solution)/shard_map/last_swap/ppermute | solution.py:457
  77.1 0.1 own_gradient.1
  77.3 0.4 collective-permute-done.7.refs_4_
  77.7 0.0 copy-done
  77.7 1.6 %update.1 = (f32[99,1024]{1,0:T(8,128)}, f32[1,99]{1,0:T(1,128)}) custom-call(s32[2]{0:T(128)S(1)} %pad_add_fusion.where.refs_0_, s32[1]{0:T(128)S(6)} %copy.11.refs_1_, f32[16,8,512]{2,1,0:T(8,128)S(1)} %all-to-all-done.2.refs_0_.refs_2_, f32[99,512]{1,0:T(8,128)S(1)} %get-tuple-element.61.refs_3_, f32[16,8,512]{2,1,0:T(8,128)S(1)} %collective-permute-done.7.refs_4_, ...), custom_call_target="tpu_custom_call" | custom-call | tf_op jit(solution)/shard_map/update/update/pallas_call | solution.py:467
  (3 shorter events, 0.1 us)
Async XLA Ops:
  0.7 11.7 %copy-start.1 = (f32[99,512]{1,0:T(8,128)S(1)}, f32[99,512]{1,0:T(8,128)}, u32[]{:S(2)}) copy-start(f32[99,512]{1,0:T(8,128)} %truth.1) | copy-start | bytes 608260
  0.7 11.7 %copy-start.2 = (f32[640]{0:T(1024)S(1)}, f32[640]{0:T(1024)}, u32[]{:S(2)}) copy-start(f32[640]{0:T(1024)} %param.13) | copy-start | bytes 7684
  0.7 11.7 %copy-start.3 = (f32[99]{0:T(128)S(1)}, f32[99]{0:T(128)}, u32[]{:S(2)}) copy-start(f32[99]{0:T(128)} %param.10) | copy-start | bytes 1192
  0.7 11.7 %copy-start.4 = (s32[512]{0:T(512)S(1)}, s32[512]{0:T(512)}, u32[]{:S(2)}) copy-start(s32[512]{0:T(512)} %param.14) | copy-start | bytes 6148
  0.7 11.7 %copy-start.5 = (f32[99]{0:T(128)S(1)}, f32[99]{0:T(128)}, u32[]{:S(2)}) copy-start(f32[99]{0:T(128)} %param.12) | copy-start | bytes 1192
  3.1 12.4 %collective-permute-start.2 = (f32[4,104,128]{2,1,0:T(8,128)S(1)}, f32[4,104,128]{2,1,0:T(8,128)S(1)}, u32[]{:S(2)}, u32[]{:S(2)}) collective-permute-start(f32[4,104,128]{2,1,0:T(8,128)S(1)} %get-tuple-element.38), channel_id=1, source_target_pairs={{0,128},{64,192},{128,0},{192,64},{1,129},{65,193},{129,1},{193,65... | collective-permute-start | bytes 638984 | tf_op jit(solution)/shard_map/forward_far/ppermute | solution.py:305
  9.7 7.1 %collective-permute-start = (f32[4,104,128]{2,1,0:T(8,128)S(1)}, f32[4,104,128]{2,1,0:T(8,128)S(1)}, u32[]{:S(2)}, u32[]{:S(2)}) collective-permute-start(f32[4,104,128]{2,1,0:T(8,128)S(1)} %get-tuple-element.35), channel_id=1, source_target_pairs={{0,64},{64,128},{128,192},{192,0},{1,65},{65,129},{129,193},{193,1... | collective-permute-start | bytes 638984 | tf_op jit(solution)/shard_map/forward_near/ppermute | solution.py:305
  10.2 6.7 %collective-permute-start.1 = (f32[4,104,128]{2,1,0:T(8,128)S(1)}, f32[4,104,128]{2,1,0:T(8,128)S(1)}, u32[]{:S(2)}, u32[]{:S(2)}) collective-permute-start(f32[4,104,128]{2,1,0:T(8,128)S(1)} %get-tuple-element.36), channel_id=1, source_target_pairs={{0,192},{64,0},{128,64},{192,128},{1,193},{65,1},{129,65},{193,129... | collective-permute-start | bytes 638984 | tf_op jit(solution)/shard_map/forward_near/ppermute | solution.py:305
  18.2 5.1 %collective-permute-start.5 = (bf16[4,104,128]{2,1,0:T(8,128)(2,1)S(1)}, bf16[4,104,128]{2,1,0:T(8,128)(2,1)S(1)}, u32[]{:S(2)}, u32[]{:S(2)}) collective-permute-start(bf16[4,104,128]{2,1,0:T(8,128)(2,1)S(1)} %get-tuple-element.51), channel_id=1, source_target_pairs={{0,128},{64,192},{128,0},{192,64},{1,129},{65,193},{129,1},{193,65... | collective-permute-start | bytes 319496 | tf_op jit(solution)/shard_map/bracket_exchange/ppermute | solution.py:305
  21.1 3.9 %collective-permute-start.3 = (bf16[4,104,128]{2,1,0:T(8,128)(2,1)S(1)}, bf16[4,104,128]{2,1,0:T(8,128)(2,1)S(1)}, u32[]{:S(2)}, u32[]{:S(2)}) collective-permute-start(bf16[4,104,128]{2,1,0:T(8,128)(2,1)S(1)} %get-tuple-element.46), channel_id=1, source_target_pairs={{0,192},{64,0},{128,64},{192,128},{1,193},{65,1},{129,65},{193,129... | collective-permute-start | bytes 319496 | tf_op jit(solution)/shard_map/bracket_exchange/ppermute | solution.py:305
  21.5 5.6 %collective-permute-start.4 = (bf16[4,104,128]{2,1,0:T(8,128)(2,1)S(1)}, bf16[4,104,128]{2,1,0:T(8,128)(2,1)S(1)}, u32[]{:S(2)}, u32[]{:S(2)}) collective-permute-start(bf16[4,104,128]{2,1,0:T(8,128)(2,1)S(1)} %get-tuple-element.47), channel_id=1, source_target_pairs={{0,64},{64,128},{128,192},{192,0},{1,65},{65,129},{129,193},{193,1... | collective-permute-start | bytes 319496 | tf_op jit(solution)/shard_map/bracket_exchange/ppermute | solution.py:305
  28.0 3.7 %collective-permute-start.6 = (f32[16,8,512]{2,1,0:T(8,128)S(1)}, f32[16,8,512]{2,1,0:T(8,128)S(1)}, u32[]{:S(2)}, u32[]{:S(2)}) collective-permute-start(f32[16,8,512]{2,1,0:T(8,128)S(1)} %get-tuple-element.55), channel_id=1, source_target_pairs={{0,1},{1,0},{2,3},{3,2},{4,5},{5,4},{6,7},{7,6},{8,9},{9,8},{10,11... | collective-permute-start | bytes 786440 | tf_op jit(solution)/shard_map/backward_partner_half/ppermute | solution.py:407
  31.4 46.2 %copy-start = (f32[99,1024]{1,0:T(8,128)S(1)}, f32[99,1024]{1,0:T(8,128)}, u32[]{:S(2)}) copy-start(f32[99,1024]{1,0:T(8,128)} %refs_6_.1) | copy-start | bytes 1216516
  61.1 11.0 %all-to-all-start.2 = ((f32[16,8,512]{2,1,0:T(8,128)}), f32[16,8,512]{2,1,0:T(8,128)S(1)}, u32[]{:S(2)}, u32[]{:S(2)}) async-start(f32[16,8,512]{2,1,0:T(8,128)} %get-tuple-element.56), calls=%async_computation.2 | async-start | bytes 524288 | tf_op jit(solution)/shard_map/gradient_sum/all_to_all | solution.py:433
  72.1 5.5 %collective-permute-start.7 = (f32[16,8,512]{2,1,0:T(8,128)S(1)}, f32[16,8,512]{2,1,0:T(8,128)S(1)}, u32[]{:S(2)}, u32[]{:S(2)}) collective-permute-start(f32[16,8,512]{2,1,0:T(8,128)S(1)} %all-to-all-done.2.refs_0_.refs_2_), channel_id=1, source_target_pairs={{0,1},{1,0},{2,3},{3,2},{4,5},{5,4},{6,7},{7,6},{8,9},{9,8},{10,11... | collective-permute-start | bytes 786440 | tf_op jit(solution)/shard_map/last_swap/ppermute | solution.py:457

commit v9 on v7

--- a/solution.py
+++ b/solution.py
@@ -82,7 +82,13 @@
     total[j] = -s if total[j] is None else total[j] - s
 
 
-def early_pairs_kernel(here, far, shift, out):
+def pair_normalizer(members):
+    eps = (1.0 - fair_alpha) / members
+    return (1.0 - eps) / (members * (members - 1))
+
+
+def early_pairs_kernel(members, here, far, shift, out):
+    normalizer = pair_normalizer(members)
     local = here.shape[0]
     count = 2 * local
 
@@ -94,7 +100,7 @@
             for j in range(i + 1, count):
                 add_pair(total, i, j, soft(r[i] - r[j]))
         for j in range(count):
-            out[j, at, :] = total[j]
+            out[j, at, :] = soft(r[j]) * (1.0 / members) - normalizer * total[j]
         return carry
 
     lax.fori_loop(0, here.shape[1] // 8, tile, 0)
@@ -104,18 +110,18 @@
     ins, outs, scratch = (here, far, after, before), rest[:GROUPS], rest[GROUPS]
     local = here.shape[0]
     count = early.shape[0]
-    eps = (1.0 - fair_alpha) / members
-    normalizer = (1.0 - eps) / (members * (members - 1))
+    normalizer = pair_normalizer(members)
 
     def tile(t, carry):
         at = pl.ds(pl.multiple_of(t * 8, 8), 8)
         r = [ref[j, at, :] + shift[at, :] for ref in ins for j in range(local)]
-        total = [early[j, at, :] for j in range(count)] + [None] * (members - count)
+        total = [None] * members
         for i in range(members):
             for j in range(max(i + 1, count), members):
                 add_pair(total, i, j, soft(r[i] - r[j]))
         for j in range(members):
-            scratch[j, at, :] = soft(r[j]) * (1.0 / members) - normalizer * total[j]
+            base = early[j, at, :] if j < count else soft(r[j]) * (1.0 / members)
+            scratch[j, at, :] = base - normalizer * total[j]
         return carry
 
     lax.fori_loop(0, here.shape[1] // 8, tile, 0)
@@ -162,26 +168,21 @@
     return lax.dot_general(ones, w, (((1,), (1,)), ((), ())), preferred_element_type=F32)
 
 
-def early_backward_kernel(where, held, b0, b2, weight, weighted, total, bias):
-    features = held.shape[3]
-    w0 = weigh(where, 0, b0, weight)
-    w2 = weigh(where, 2, b2, weight)
-    weighted[0], weighted[1] = w0, w2
-    bias[...] = bias_of(w0) + bias_of(w2)
-    total[...] = jnp.dot(
-        w0, held[0].reshape(-1, features), preferred_element_type=F32
-    ) + jnp.dot(w2, held[2].reshape(-1, features), preferred_element_type=F32)
-
-
-def late_half(side, w1, w3, held, early, acc):
-    rows = w1.shape[0]
+def early_backward_kernel(where, held, b0, weight, weighted, total, bias):
+    w = weigh(where, 0, b0, weight)
+    weighted[0] = w
+    bias[...] = bias_of(w)
+    total[...] = jnp.dot(w, held[0].reshape(-1, held.shape[3]), preferred_element_type=F32)
+
+
+def late_half(side, ws, held, early, acc):
+    rows = early.shape[0]
     half = acc.shape[1]
     lanes = pl.ds(pl.multiple_of(side * half, half), half)
-    acc[0:rows, :] = (
-        early[:, lanes]
-        + jnp.dot(w1, held[1, :, :, lanes].reshape(-1, half), preferred_element_type=F32)
-        + jnp.dot(w3, held[3, :, :, lanes].reshape(-1, half), preferred_element_type=F32)
-    )
+    total = early[:, lanes]
+    for k, w in enumerate(ws, 1):
+        total = total + jnp.dot(w, held[k, :, :, lanes].reshape(-1, half), preferred_element_type=F32)
+    acc[0:rows, :] = total
     acc[rows:, :] = jnp.zeros((acc.shape[0] - rows, half), F32)
 
 
@@ -190,25 +191,27 @@
     return jnp.broadcast_to(row, (8, half))
 
 
-def partner_half_kernel(where, held, b1, b3, weight, area, early, weighted, other, acc):
-    w1 = weigh(where, 1, b1, weight)
-    w3 = weigh(where, 3, b3, weight)
-    weighted[0], weighted[1] = w1, w3
-    late_half(1 - where[1], w1, w3, held, early, acc)
+def partner_half_kernel(where, held, b1, b2, b3, weight, area, early, weighted, other, acc):
+    ws = [weigh(where, k, bracket, weight) for k, bracket in enumerate((b1, b2, b3), 1)]
+    for k, w in enumerate(ws):
+        weighted[k] = w
+    late_half(1 - where[1], ws, held, early, acc)
     pieces_of(acc, extra_row(jnp.zeros((1, 128), F32), area[...], acc.shape[1]), other)
 
 
 def own_half_kernel(where, held, weighted, early, early_bias, area, mine, acc):
     rows = early.shape[0]
-    w1, w3 = weighted[0], weighted[1]
-    late_half(where[1], w1, w3, held, early, acc)
-    bias = early_bias[...] + bias_of(w1) + bias_of(w3)
+    ws = [weighted[k] for k in range(GROUPS - 1)]
+    late_half(where[1], ws, held, early, acc)
+    bias = early_bias[...]
+    for w in ws:
+        bias = bias + bias_of(w)
     bias = jnp.concatenate([bias[0:1], jnp.zeros((1, 128 - rows), F32)], axis=1)
     pieces_of(acc, extra_row(bias, area[...], acc.shape[1]), mine)
 
 
 def grad_hidden_kernel(where, early, late, half, piece, out, *, replicas):
-    first = lax.rem(pl.program_id(0), 2) == 0
+    first = pl.program_id(0) == 0
     inverse = 1.0 / (piece[PIECE_ROWS : PIECE_ROWS + 1, 128:129] * (1.0 / replicas))
     chunk = out.shape[1]
     for m in range(out.shape[0]):
@@ -338,7 +341,7 @@
         )(where, hidden, half_weight, lat_weight.reshape(-1, 128), area_bin.reshape(1, points), intercept_row, analysis_truth, var_row)
     with jax.named_scope("early_pairs"):
         early = pl.pallas_call(
-            early_pairs_kernel,
+            lambda *refs: early_pairs_kernel(members, *refs),
             out_shape=jax.ShapeDtypeStruct((2 * local, rows, chunk), F32),
             in_specs=[VMEM] * 3,
             out_specs=VMEM,
@@ -360,31 +363,30 @@
         returned = [brackets[0], turn(brackets[2], -1), turn(brackets[1], -2), turn(brackets[3], -3)]
     half = features // 2
     pieces = jax.ShapeDtypeStruct((PIECES, 8, half), F32)
-    two_weighted = jax.ShapeDtypeStruct((GROUPS // 2, rows, local * chunk), BF16)
     sums = [pltpu.VMEM((PIECES * 8, half), F32)]
     with jax.named_scope("early_backward"):
         weighted_early, early_sum, early_bias = pl.pallas_call(
             early_backward_kernel,
             out_shape=[
-                two_weighted,
+                jax.ShapeDtypeStruct((1, rows, local * chunk), BF16),
                 jax.ShapeDtypeStruct((rows, features), F32),
                 jax.ShapeDtypeStruct((8, rows), F32),
             ],
-            in_specs=[SMEM] + [VMEM] * 4,
+            in_specs=[SMEM] + [VMEM] * 3,
             out_specs=[VMEM] * 3,
             compiler_params=grant(10),
             name="early_backward",
-        )(where, held, returned[0], returned[2], point_weight)
+        )(where, held, returned[0], point_weight)
     with jax.named_scope("backward_partner_half"):
         weighted_late, other = pl.pallas_call(
             partner_half_kernel,
-            out_shape=[two_weighted, pieces],
-            in_specs=[SMEM] + [VMEM] * 6,
+            out_shape=[jax.ShapeDtypeStruct((GROUPS - 1, rows, local * chunk), BF16), pieces],
+            in_specs=[SMEM] + [VMEM] * 7,
             out_specs=[VMEM] * 2,
             scratch_shapes=sums,
             compiler_params=grant(10),
             name="backward_partner_half",
-        )(where, held, returned[1], returned[3], point_weight, area, early_sum)
+        )(where, held, *returned[1:], point_weight, area, early_sum)
         swap = [(0, 1), (1, 0)]
         other = lax.ppermute(other, "c", swap)
     with jax.named_scope("backward_own_half"):
@@ -413,8 +415,8 @@
                 num_scalar_prefetch=1,
                 grid=(GROUPS,),
                 in_specs=[
-                    pl.BlockSpec((1, rows, local * chunk), lambda g, s: (lax.div(g, 2), 0, 0)),
-                    pl.BlockSpec((1, rows, local * chunk), lambda g, s: (lax.div(g, 2), 0, 0)),
+                    pl.BlockSpec((1, rows, local * chunk), lambda g, s: (0, 0, 0)),
+                    pl.BlockSpec((1, rows, local * chunk), lambda g, s: (lax.max(g - 1, 0), 0, 0)),
                     pl.BlockSpec((rows, features), lambda g, s: (0, 0)),
                     pl.BlockSpec((8, half), lambda g, s: (0, 0)),
                 ],

time: 79.5 us -> 79.7 us (level)
    ppermute x1, starting transfers between devices: 2.51 us -> 3.38 us  [on_device(): other = lax.ppermute(other, 'c', swap)]
  transfers between devices with their start and end apart: 9 -> 9, of which waited for: 7 -> 6; matrix products, arithmetic and copies ran while one was open for 0% -> 0% of each run, Pallas kernels for 15% -> 16%
where the time goes in v9:
time: 79.7 us; the launch traced here: 79.4 us
  blocking collectives  28.1 us (35%)
  starting transfers between devices  21.7 us (27%)
  Pallas kernels  18.6 us (23%)
  waiting for transfers between devices  8.55 us (11%)
  between operations  1.44 us (2%)
    all_to_all x1, blocking collectives, on_device(): part = lax.all_to_all(part, 'z', 0, 0, tiled=True)  16 us
    all_to_all x1, blocking collectives, on_device(): part = lax.all_to_all(part, ('x', 'y'), 0, 0, tiled=True)  12.1 us
    ppermute x6, starting transfers between devices, turn(): lax.ppermute(value, 'y', [(i, (i + k) % GROUPS) for i in range(GROUPS)])  10.4 us
    ppermute x6, waiting for transfers between devices, turn(): lax.ppermute(value, 'y', [(i, (i + k) % GROUPS) for i in range(GROUPS)])  4.7 us
    ppermute x1, starting transfers between devices, on_device(): partner = lax.ppermute(own, 'c', swap)  4.38 us
    pallas_call x1, Pallas kernels, on_device(): pl.pallas_call(lambda *refs: grad_hidden_kernel(*refs, replicas=replicas)...  3.95 us
    all_to_all x1, starting transfers between devices, on_device(): lax.all_to_all(jnp.broadcast_to(piece, (PIECES, 8, half)), ('x', 'y'), 0,...  3.62 us
    ppermute x1, starting transfers between devices, on_device(): other = lax.ppermute(other, 'c', swap)  3.38 us
  transfers between devices with their start and end apart: 9, of which 6 were waited for; matrix products, arithmetic and copies ran while one was open for 0% of the time, Pallas kernels for 16%

profile of v9, /device:TPU:1, one launch (start us, length us, event | category | flops | bytes accessed | tf_op | source)
XLA Modules:
  0.0 79.4 jit_solution(17758549924803241886)
XLA Ops:
  0.6 0.1 pad_add_fusion.where.refs_0_
  0.7 0.0 copy-start.1
  0.7 0.0 copy-start.2
  0.7 0.0 copy-start.3
  0.7 0.0 copy-start.4
  0.7 0.0 copy-start.5
  0.7 2.4 %forward_far.1 = (f32[4,104,128]{2,1,0:T(8,128)S(1)}, bf16[104,1024]{1,0:T(8,128)(2,1)S(1)}) custom-call(s32[2]{0:T(128)S(1)} %pad_add_fusion.where.refs_0_, bf16[4,512,1024]{2,1,0:T(8,128)(2,1)} %hidden.5, f32[99,1024]{1,0:T(8,128)} %refs_6_.1), custom_call_target="tpu_custom_call" | custom-call | tf_op jit(solution)/shard_map/forward_far/forward_far/pallas_call | solution.py:294
  3.1 3.8 %collective-permute-start.2 = (f32[4,104,128]{2,1,0:T(8,128)S(1)}, f32[4,104,128]{2,1,0:T(8,128)S(1)}, u32[]{:S(2)}, u32[]{:S(2)}) collective-permute-start(f32[4,104,128]{2,1,0:T(8,128)S(1)} %get-tuple-element.36), channel_id=1, source_target_pairs={{0,128},{64,192},{128,0},{192,64},{1,129},{65,193},{129,1},{193,65... | collective-permute-start | bytes 638984 | tf_op jit(solution)/shard_map/forward_far/ppermute | solution.py:290
  6.9 2.7 %forward_near.1 = (f32[4,104,128]{2,1,0:T(8,128)S(1)}, f32[4,104,128]{2,1,0:T(8,128)S(1)}) custom-call(s32[2]{0:T(128)S(1)} %pad_add_fusion.where.refs_0_, bf16[4,512,1024]{2,1,0:T(8,128)(2,1)} %hidden.5, bf16[104,1024]{1,0:T(8,128)(2,1)S(1)} %get-tuple-element.32.half.refs_3_), custom_call_target="tpu_custom_call" | custom-call | flops 218103808 | bytes 2097152 | tf_op jit(solution)/shard_map/forward_near/forward_near/pallas_call | solution.py:310
  9.7 0.5 collective-permute-start
  10.2 2.3 %collective-permute-start.1 = (f32[4,104,128]{2,1,0:T(8,128)S(1)}, f32[4,104,128]{2,1,0:T(8,128)S(1)}, u32[]{:S(2)}, u32[]{:S(2)}) collective-permute-start(f32[4,104,128]{2,1,0:T(8,128)S(1)} %get-tuple-element.34), channel_id=1, source_target_pairs={{0,192},{64,0},{128,64},{192,128},{1,193},{65,1},{129,65},{193,129... | collective-permute-start | bytes 638984 | tf_op jit(solution)/shard_map/forward_near/ppermute | solution.py:290
  12.4 0.0 copy-done.1
  12.4 0.0 copy-done.2
  12.4 0.0 copy-done.3
  12.5 0.0 copy-done.4
  12.5 0.0 copy-done.5
  12.5 3.0 %forward_local.1 = (f32[4,104,128]{2,1,0:T(8,128)S(1)}, f32[1,128]{1,0:T(1,128)S(1)}, f32[104,512]{1,0:T(8,128)S(1)}, f32[104,128]{1,0:T(8,128)S(1)}, bf16[4,4,128,1024]{3,2,1,0:T(8,128)(2,1)S(1)}) custom-call(s32[2]{0:T(128)S(1)} %pad_add_fusion.where.refs_0_, bf16[4,512,1024]{2,1,0:T(8,128)(2,1)} %hidden.5, ...), custom_call_target="tpu_custom_call" | custom-call | tf_op jit(solution)/shard_map/forward_local/forward_local/pallas_call | solution.py:327
  15.5 0.0 collective-permute-done.2.refs_1_
  15.5 0.5 early_pairs.1.refs_5_
  16.1 0.8 collective-permute-done.refs_2_
  16.8 0.0 collective-permute-done.1.refs_3_
  16.8 1.4 %late_pairs.1 = (bf16[4,104,128]{2,1,0:T(8,128)(2,1)S(1)}, bf16[4,104,128]{2,1,0:T(8,128)(2,1)S(1)}, bf16[4,104,128]{2,1,0:T(8,128)(2,1)S(1)}, bf16[4,104,128]{2,1,0:T(8,128)(2,1)S(1)}) custom-call(f32[4,104,128]{2,1,0:T(8,128)S(1)} %get-tuple-element.35.refs_0_, f32[4,104,128]{2,1,0:T(8,128)S(1)} %collective-permute-done.2.refs_1_, ...), custom_call_target="tpu_custom_call" | custom-call | tf_op jit(solution)/shard_map/late_pairs/late_pairs/pallas_call | solution.py:353
  18.2 2.4 %collective-permute-start.3 = (bf16[4,104,128]{2,1,0:T(8,128)(2,1)S(1)}, bf16[4,104,128]{2,1,0:T(8,128)(2,1)S(1)}, u32[]{:S(2)}, u32[]{:S(2)}) collective-permute-start(bf16[4,104,128]{2,1,0:T(8,128)(2,1)S(1)} %get-tuple-element.44), channel_id=1, source_target_pairs={{0,192},{64,0},{128,64},{192,128},{1,193},{65,1},{129,65},{193,129... | collective-permute-start | bytes 319496 | tf_op jit(solution)/shard_map/bracket_exchange/ppermute | solution.py:290
  20.6 0.6 collective-permute-start.4
  21.2 0.8 collective-permute-start.5
  22.0 0.9 %early_backward.1 = (bf16[1,104,512]{2,1,0:T(8,128)(2,1)S(1)}, f32[104,1024]{1,0:T(8,128)S(1)}, f32[8,104]{1,0:T(8,128)S(1)}) custom-call(s32[2]{0:T(128)S(1)} %pad_add_fusion.where.refs_0_, bf16[4,4,128,1024]{3,2,1,0:T(8,128)(2,1)S(1)} %get-tuple-element.40.held, bf16[4,104,128]{2,1,0:T(8,128)(2,1)S(1)} %get-tuple-element.49.b0, ...), custom_call_target="tpu_custom_call" | custom-call | tf_op jit(solution)/shard_map/early_backward/early_backward/pallas_call | solution.py:368
  22.9 0.0 collective-permute-done.3.b1
  22.9 2.9 %collective-permute-done.4.b2 = bf16[4,104,128]{2,1,0:T(8,128)(2,1)S(1)} collective-permute-done((bf16[4,104,128]{2,1,0:T(8,128)(2,1)S(1)}, bf16[4,104,128]{2,1,0:T(8,128)(2,1)S(1)}, u32[]{:S(2)}, u32[]{:S(2)}) %collective-permute-start.4) | collective-permute-done | bytes 106528 | tf_op jit(solution)/shard_map/bracket_exchange/ppermute | solution.py:290
  25.8 1.1 %collective-permute-done.5.b3 = bf16[4,104,128]{2,1,0:T(8,128)(2,1)S(1)} collective-permute-done((bf16[4,104,128]{2,1,0:T(8,128)(2,1)S(1)}, bf16[4,104,128]{2,1,0:T(8,128)(2,1)S(1)}, u32[]{:S(2)}, u32[]{:S(2)}) %collective-permute-start.5) | collective-permute-done | bytes 106528 | tf_op jit(solution)/shard_map/bracket_exchange/ppermute | solution.py:290
  26.8 1.0 %backward_partner_half.1 = (bf16[3,104,512]{2,1,0:T(8,128)(2,1)S(1)}, f32[16,8,512]{2,1,0:T(8,128)S(1)}) custom-call(s32[2]{0:T(128)S(1)} %pad_add_fusion.where.refs_0_, bf16[4,4,128,1024]{3,2,1,0:T(8,128)(2,1)S(1)} %get-tuple-element.40.held, bf16[4,104,128]{2,1,0:T(8,128)(2,1)S(1)} %collective-permute-done.3.b1, ...), custom_call_target="tpu_custom_call" | custom-call | tf_op jit(solution)/shard_map/backward_partner_half/backward_partner_half/pallas_call | solution.py:381
  27.8 3.4 %collective-permute-start.6 = (f32[16,8,512]{2,1,0:T(8,128)S(1)}, f32[16,8,512]{2,1,0:T(8,128)S(1)}, u32[]{:S(2)}, u32[]{:S(2)}) collective-permute-start(f32[16,8,512]{2,1,0:T(8,128)S(1)} %get-tuple-element.53), channel_id=1, source_target_pairs={{0,1},{1,0},{2,3},{3,2},{4,5},{5,4},{6,7},{7,6},{8,9},{9,8},{10,11... | collective-permute-start | bytes 786440 | tf_op jit(solution)/shard_map/backward_partner_half/ppermute | solution.py:391
  31.2 1.0 %backward_own_half.1 = f32[16,8,512]{2,1,0:T(8,128)S(1)} custom-call(s32[2]{0:T(128)S(1)} %pad_add_fusion.where.refs_0_, bf16[4,4,128,1024]{3,2,1,0:T(8,128)(2,1)S(1)} %get-tuple-element.40.held, bf16[3,104,512]{2,1,0:T(8,128)(2,1)S(1)} %get-tuple-element.51.weighted.refs_2_, f32[104,1024]{1,0:T(8,128)S(1)} %get-tuple-element.50.early, ...), custom_call_target="tpu_custom_call" | custom-call | tf_op jit(solution)/shard_map/backward_own_half/backward_own_half/pallas_call | solution.py:393
  32.2 0.0 copy-start
  32.2 0.1 collective-permute-done.6
  32.4 12.1 %all_to_all.15 = f32[16,8,512]{2,1,0:T(8,128)S(1)} all-to-all(f32[16,8,512]{2,1,0:T(8,128)S(1)} %add.3), channel_id=1, replica_groups=mesh['y'=4,'z'=8,'x'=4,'c'=2] {'x','y'}, dimensions={0} | all-to-all | bytes 524288 | tf_op jit(solution)/shard_map/gradient_sum/all_to_all | solution.py:404
  44.5 16.0 %all_to_all.16 = f32[8,8,512]{2,1,0:T(8,128)S(1)} all-to-all(f32[8,8,512]{2,1,0:T(8,128)S(1)} %broadcast_in_dim.6), channel_id=1, replica_groups=mesh['y'=4,'z'=8,'x'=4,'c'=2] {'z'}, dimensions={0} | all-to-all | bytes 262144 | tf_op jit(solution)/shard_map/gradient_sum/all_to_all | solution.py:407
  60.6 0.7 broadcast_in_dim.7
  61.3 3.6 %all-to-all-start.2 = ((f32[16,8,512]{2,1,0:T(8,128)}), f32[16,8,512]{2,1,0:T(8,128)S(1)}, u32[]{:S(2)}, u32[]{:S(2)}) async-start(f32[16,8,512]{2,1,0:T(8,128)} %broadcast_in_dim.7), calls=%async_computation.2 | async-start | bytes 524288 | tf_op jit(solution)/shard_map/gradient_sum/all_to_all | solution.py:409
  64.9 3.9 %grad_hidden.1 = bf16[4,512,1024]{2,1,0:T(8,128)(2,1)} custom-call(s32[2]{0:T(128)S(1)} %pad_add_fusion.where.refs_0_, bf16[1,104,512]{2,1,0:T(8,128)(2,1)S(1)} %get-tuple-element.54.refs_1_, bf16[3,104,512]{2,1,0:T(8,128)(2,1)S(1)} %get-tuple-element.51.weighted.refs_2_, bf16[104,1024]{1,0:T(8,128)(2,1)S(1)} %get-tuple-element.32.half.refs_3_, ...), custom_call_target="tpu_custom_call" | custom-call | flops 436207616 | bytes 4194304 | tf_op jit(solution)/shard_map/grad_hidden/grad_hidden/pallas_call | solution.py:411
  68.9 3.4 %all-to-all-done.2.refs_0_.refs_2_ = f32[16,8,512]{2,1,0:T(8,128)S(1)} async-done(((f32[16,8,512]{2,1,0:T(8,128)}), f32[16,8,512]{2,1,0:T(8,128)S(1)}, u32[]{:S(2)}, u32[]{:S(2)}) %all-to-all-start.2) | async-done | bytes 262176 | tf_op jit(solution)/shard_map/gradient_sum/all_to_all | solution.py:409
  72.2 4.4 %collective-permute-start.7 = (f32[16,8,512]{2,1,0:T(8,128)S(1)}, f32[16,8,512]{2,1,0:T(8,128)S(1)}, u32[]{:S(2)}, u32[]{:S(2)}) collective-permute-start(f32[16,8,512]{2,1,0:T(8,128)S(1)} %all-to-all-done.2.refs_0_.refs_2_), channel_id=1, source_target_pairs={{0,1},{1,0},{2,3},{3,2},{4,5},{5,4},{6,7},{7,6},{8,9},{9,8},{10,11... | collective-permute-start | bytes 786440 | tf_op jit(solution)/shard_map/last_swap/ppermute | solution.py:433
  77.3 0.1 own_gradient.1
  77.4 0.4 collective-permute-done.7.refs_4_
  77.8 0.0 copy-done
  77.8 1.6 %update.1 = (f32[99,1024]{1,0:T(8,128)}, f32[1,99]{1,0:T(1,128)}) custom-call(s32[2]{0:T(128)S(1)} %pad_add_fusion.where.refs_0_, s32[1]{0:T(128)S(6)} %copy.11.refs_1_, f32[16,8,512]{2,1,0:T(8,128)S(1)} %all-to-all-done.2.refs_0_.refs_2_, f32[99,512]{1,0:T(8,128)S(1)} %get-tuple-element.57.refs_3_, f32[16,8,512]{2,1,0:T(8,128)S(1)} %collective-permute-done.7.refs_4_, ...), custom_call_target="tpu_custom_call" | custom-call | tf_op jit(solution)/shard_map/update/update/pallas_call | solution.py:443
  (4 shorter events, 0.1 us)
Async XLA Ops:
  0.7 11.7 %copy-start.1 = (f32[99,512]{1,0:T(8,128)S(1)}, f32[99,512]{1,0:T(8,128)}, u32[]{:S(2)}) copy-start(f32[99,512]{1,0:T(8,128)} %truth.1) | copy-start | bytes 608260
  0.7 11.7 %copy-start.2 = (f32[640]{0:T(1024)S(1)}, f32[640]{0:T(1024)}, u32[]{:S(2)}) copy-start(f32[640]{0:T(1024)} %param.13) | copy-start | bytes 7684
  0.7 11.7 %copy-start.3 = (f32[99]{0:T(128)S(1)}, f32[99]{0:T(128)}, u32[]{:S(2)}) copy-start(f32[99]{0:T(128)} %param.10) | copy-start | bytes 1192
  0.7 11.7 %copy-start.4 = (s32[512]{0:T(512)S(1)}, s32[512]{0:T(512)}, u32[]{:S(2)}) copy-start(s32[512]{0:T(512)} %param.14) | copy-start | bytes 6148
  0.7 11.7 %copy-start.5 = (f32[99]{0:T(128)S(1)}, f32[99]{0:T(128)}, u32[]{:S(2)}) copy-start(f32[99]{0:T(128)} %param.12) | copy-start | bytes 1192
  3.1 12.4 %collective-permute-start.2 = (f32[4,104,128]{2,1,0:T(8,128)S(1)}, f32[4,104,128]{2,1,0:T(8,128)S(1)}, u32[]{:S(2)}, u32[]{:S(2)}) collective-permute-start(f32[4,104,128]{2,1,0:T(8,128)S(1)} %get-tuple-element.36), channel_id=1, source_target_pairs={{0,128},{64,192},{128,0},{192,64},{1,129},{65,193},{129,1},{193,65... | collective-permute-start | bytes 638984 | tf_op jit(solution)/shard_map/forward_far/ppermute | solution.py:290
  9.7 7.1 %collective-permute-start = (f32[4,104,128]{2,1,0:T(8,128)S(1)}, f32[4,104,128]{2,1,0:T(8,128)S(1)}, u32[]{:S(2)}, u32[]{:S(2)}) collective-permute-start(f32[4,104,128]{2,1,0:T(8,128)S(1)} %get-tuple-element.33), channel_id=1, source_target_pairs={{0,64},{64,128},{128,192},{192,0},{1,65},{65,129},{129,193},{193,1... | collective-permute-start | bytes 638984 | tf_op jit(solution)/shard_map/forward_near/ppermute | solution.py:290
  10.2 6.7 %collective-permute-start.1 = (f32[4,104,128]{2,1,0:T(8,128)S(1)}, f32[4,104,128]{2,1,0:T(8,128)S(1)}, u32[]{:S(2)}, u32[]{:S(2)}) collective-permute-start(f32[4,104,128]{2,1,0:T(8,128)S(1)} %get-tuple-element.34), channel_id=1, source_target_pairs={{0,192},{64,0},{128,64},{192,128},{1,193},{65,1},{129,65},{193,129... | collective-permute-start | bytes 638984 | tf_op jit(solution)/shard_map/forward_near/ppermute | solution.py:290
  18.2 4.7 %collective-permute-start.3 = (bf16[4,104,128]{2,1,0:T(8,128)(2,1)S(1)}, bf16[4,104,128]{2,1,0:T(8,128)(2,1)S(1)}, u32[]{:S(2)}, u32[]{:S(2)}) collective-permute-start(bf16[4,104,128]{2,1,0:T(8,128)(2,1)S(1)} %get-tuple-element.44), channel_id=1, source_target_pairs={{0,192},{64,0},{128,64},{192,128},{1,193},{65,1},{129,65},{193,129... | collective-permute-start | bytes 319496 | tf_op jit(solution)/shard_map/bracket_exchange/ppermute | solution.py:290
  20.6 5.1 %collective-permute-start.4 = (bf16[4,104,128]{2,1,0:T(8,128)(2,1)S(1)}, bf16[4,104,128]{2,1,0:T(8,128)(2,1)S(1)}, u32[]{:S(2)}, u32[]{:S(2)}) collective-permute-start(bf16[4,104,128]{2,1,0:T(8,128)(2,1)S(1)} %get-tuple-element.45), channel_id=1, source_target_pairs={{0,128},{64,192},{128,0},{192,64},{1,129},{65,193},{129,1},{193,65... | collective-permute-start | bytes 319496 | tf_op jit(solution)/shard_map/bracket_exchange/ppermute | solution.py:290
  21.2 5.6 %collective-permute-start.5 = (bf16[4,104,128]{2,1,0:T(8,128)(2,1)S(1)}, bf16[4,104,128]{2,1,0:T(8,128)(2,1)S(1)}, u32[]{:S(2)}, u32[]{:S(2)}) collective-permute-start(bf16[4,104,128]{2,1,0:T(8,128)(2,1)S(1)} %get-tuple-element.46), channel_id=1, source_target_pairs={{0,64},{64,128},{128,192},{192,0},{1,65},{65,129},{129,193},{193,1... | collective-permute-start | bytes 319496 | tf_op jit(solution)/shard_map/bracket_exchange/ppermute | solution.py:290
  27.8 4.5 %collective-permute-start.6 = (f32[16,8,512]{2,1,0:T(8,128)S(1)}, f32[16,8,512]{2,1,0:T(8,128)S(1)}, u32[]{:S(2)}, u32[]{:S(2)}) collective-permute-start(f32[16,8,512]{2,1,0:T(8,128)S(1)} %get-tuple-element.53), channel_id=1, source_target_pairs={{0,1},{1,0},{2,3},{3,2},{4,5},{5,4},{6,7},{7,6},{8,9},{9,8},{10,11... | collective-permute-start | bytes 786440 | tf_op jit(solution)/shard_map/backward_partner_half/ppermute | solution.py:391
  32.2 45.6 %copy-start = (f32[99,1024]{1,0:T(8,128)S(1)}, f32[99,1024]{1,0:T(8,128)}, u32[]{:S(2)}) copy-start(f32[99,1024]{1,0:T(8,128)} %refs_6_.1) | copy-start | bytes 1216516
  61.3 10.9 %all-to-all-start.2 = ((f32[16,8,512]{2,1,0:T(8,128)}), f32[16,8,512]{2,1,0:T(8,128)S(1)}, u32[]{:S(2)}, u32[]{:S(2)}) async-start(f32[16,8,512]{2,1,0:T(8,128)} %broadcast_in_dim.7), calls=%async_computation.2 | async-start | bytes 524288 | tf_op jit(solution)/shard_map/gradient_sum/all_to_all | solution.py:409
  72.2 5.5 %collective-permute-start.7 = (f32[16,8,512]{2,1,0:T(8,128)S(1)}, f32[16,8,512]{2,1,0:T(8,128)S(1)}, u32[]{:S(2)}, u32[]{:S(2)}) collective-permute-start(f32[16,8,512]{2,1,0:T(8,128)S(1)} %all-to-all-done.2.refs_0_.refs_2_), channel_id=1, source_target_pairs={{0,1},{1,0},{2,3},{3,2},{4,5},{5,4},{6,7},{7,6},{8,9},{9,8},{10,11... | collective-permute-start | bytes 786440 | tf_op jit(solution)/shard_map/last_swap/ppermute | solution.py:433

commit v10 on v7

--- a/solution.py
+++ b/solution.py
@@ -82,44 +82,73 @@
     total[j] = -s if total[j] is None else total[j] - s
 
 
-def early_pairs_kernel(here, far, shift, out):
+def pair_normalizer(members):
+    eps = (1.0 - fair_alpha) / members
+    return (1.0 - eps) / (members * (members - 1))
+
+
+def row_tiles(rows, body):
+    def tile(t, carry):
+        body(pl.ds(pl.multiple_of(t * 8, 8), 8))
+        return carry
+
+    lax.fori_loop(0, rows // 8, tile, 0)
+
+
+def early_pairs_kernel(members, here, far, shift, out):
     local = here.shape[0]
     count = 2 * local
-
-    def tile(t, carry):
-        at = pl.ds(pl.multiple_of(t * 8, 8), 8)
+    normalizer = pair_normalizer(members)
+
+    def body(at):
         r = [ref[j, at, :] + shift[at, :] for ref in (here, far) for j in range(local)]
         total = [None] * count
         for i in range(count):
             for j in range(i + 1, count):
                 add_pair(total, i, j, soft(r[i] - r[j]))
         for j in range(count):
-            out[j, at, :] = total[j]
-        return carry
-
-    lax.fori_loop(0, here.shape[1] // 8, tile, 0)
-
-
-def late_pairs_kernel(members, here, far, after, before, shift, early, *rest):
-    ins, outs, scratch = (here, far, after, before), rest[:GROUPS], rest[GROUPS]
+            out[j, at, :] = soft(r[j]) * (1.0 / members) - normalizer * total[j]
+
+    row_tiles(here.shape[1], body)
+
+
+def far_pairs_kernel(members, far, after, before, shift, early, bracket, near, scratch):
+    local = far.shape[0]
+    normalizer = pair_normalizer(members)
+
+    def body(at):
+        r = [ref[j, at, :] + shift[at, :] for ref in (far, after, before) for j in range(local)]
+        total = [None] * (3 * local)
+        for i in range(local):
+            for j in range(local, 3 * local):
+                add_pair(total, i, j, soft(r[i] - r[j]))
+        for j in range(local):
+            scratch[j, at, :] = early[local + j, at, :] - normalizer * total[j]
+        for j in range(2 * local):
+            near[j, at, :] = total[local + j]
+
+    row_tiles(far.shape[1], body)
+    for j in range(local):
+        bracket[j] = scratch[j].astype(BF16)
+
+
+def near_pairs_kernel(members, here, after, before, shift, early, near, *rest):
+    outs, scratch = rest[:3], rest[3]
     local = here.shape[0]
-    count = early.shape[0]
-    eps = (1.0 - fair_alpha) / members
-    normalizer = (1.0 - eps) / (members * (members - 1))
-
-    def tile(t, carry):
-        at = pl.ds(pl.multiple_of(t * 8, 8), 8)
-        r = [ref[j, at, :] + shift[at, :] for ref in ins for j in range(local)]
-        total = [early[j, at, :] for j in range(count)] + [None] * (members - count)
-        for i in range(members):
-            for j in range(max(i + 1, count), members):
+    normalizer = pair_normalizer(members)
+
+    def body(at):
+        r = [ref[j, at, :] + shift[at, :] for ref in (here, after, before) for j in range(local)]
+        total = [None] * local + [near[j, at, :] for j in range(2 * local)]
+        for i in range(3 * local):
+            for j in range(max(i + 1, local), 3 * local):
                 add_pair(total, i, j, soft(r[i] - r[j]))
-        for j in range(members):
-            scratch[j, at, :] = soft(r[j]) * (1.0 / members) - normalizer * total[j]
-        return carry
-
-    lax.fori_loop(0, here.shape[1] // 8, tile, 0)
-    for j in range(members):
+        for j in range(3 * local):
+            base = early[j, at, :] if j < local else soft(r[j]) * (1.0 / members)
+            scratch[j, at, :] = base - normalizer * total[j]
+
+    row_tiles(here.shape[1], body)
+    for j in range(3 * local):
         outs[j // local][j % local] = scratch[j].astype(BF16)
 
 
@@ -338,7 +367,7 @@
         )(where, hidden, half_weight, lat_weight.reshape(-1, 128), area_bin.reshape(1, points), intercept_row, analysis_truth, var_row)
     with jax.named_scope("early_pairs"):
         early = pl.pallas_call(
-            early_pairs_kernel,
+            lambda *refs: early_pairs_kernel(members, *refs),
             out_shape=jax.ShapeDtypeStruct((2 * local, rows, chunk), F32),
             in_specs=[VMEM] * 3,
             out_specs=VMEM,
@@ -346,18 +375,30 @@
             name="early_pairs",
         )(here, far, shift)
     after, before, early, point_weight, held = lax.optimization_barrier((after, before, early, point_weight, held))
-    with jax.named_scope("late_pairs"):
-        brackets = pl.pallas_call(
-            lambda *refs: late_pairs_kernel(members, *refs),
-            out_shape=[jax.ShapeDtypeStruct((local, rows, chunk), BF16)] * GROUPS,
-            in_specs=[VMEM] * (GROUPS + 2),
-            out_specs=[VMEM] * GROUPS,
-            scratch_shapes=[pltpu.VMEM((members, rows, chunk), F32)],
+    one_bracket = jax.ShapeDtypeStruct((local, rows, chunk), BF16)
+    with jax.named_scope("far_pairs"):
+        far_bracket, near_sums = pl.pallas_call(
+            lambda *refs: far_pairs_kernel(members, *refs),
+            out_shape=[one_bracket, jax.ShapeDtypeStruct((2 * local, rows, chunk), F32)],
+            in_specs=[VMEM] * 5,
+            out_specs=[VMEM] * 2,
+            scratch_shapes=[pltpu.VMEM((local, rows, chunk), F32)],
             compiler_params=grant(6),
-            name="late_pairs",
-        )(here, far, after, before, shift, early)
-    with jax.named_scope("bracket_exchange"):
-        returned = [brackets[0], turn(brackets[2], -1), turn(brackets[1], -2), turn(brackets[3], -3)]
+            name="far_pairs",
+        )(far, after, before, shift, early)
+        far_bracket = turn(far_bracket, -2)
+    with jax.named_scope("near_pairs"):
+        here_bracket, after_bracket, before_bracket = pl.pallas_call(
+            lambda *refs: near_pairs_kernel(members, *refs),
+            out_shape=[one_bracket] * 3,
+            in_specs=[VMEM] * 6,
+            out_specs=[VMEM] * 3,
+            scratch_shapes=[pltpu.VMEM((3 * local, rows, chunk), F32)],
+            compiler_params=grant(6),
+            cost_estimate=pl.CostEstimate(flops=600 * rows * chunk, bytes_accessed=64 * rows * chunk, transcendentals=60 * rows * chunk),
+            name="near_pairs",
+        )(here, after, before, shift, early, near_sums)
+        returned = [here_bracket, turn(after_bracket, -1), far_bracket, turn(before_bracket, -3)]
     half = features // 2
     pieces = jax.ShapeDtypeStruct((PIECES, 8, half), F32)
     two_weighted = jax.ShapeDtypeStruct((GROUPS // 2, rows, local * chunk), BF16)

time: 79.5 us -> 79.2 us (level)
  waiting for transfers between devices: 8.26 us -> 7.44 us
  starting transfers between devices: 21.5 us -> 22.3 us
    ppermute x6, waiting for transfers between devices: 4.28 us -> 3.46 us  [turn(): lax.ppermute(value, 'y', [(i, (i + k) % GROUPS) for i in range(GROUPS)])]
    pallas_call x2 -> x3, Pallas kernels: 1.91 us -> 2.06 us  [the longest x1 1 us: on_device(): pl.pallas_call(lambda *refs: near_pairs_kernel(members, *refs), out_shape...]
  transfers between devices with their start and end apart: 9 -> 9, of which waited for: 7 -> 6; matrix products, arithmetic and copies ran while one was open for 0% -> 0% of each run, Pallas kernels for 15% -> 17%
where the time goes in v10:
time: 79.2 us; the launch traced here: 78.9 us
  blocking collectives  28.1 us (35%)
  starting transfers between devices  22.3 us (28%)
  Pallas kernels  18.7 us (24%)
  waiting for transfers between devices  7.44 us (9%)
  between operations  1.43 us (2%)
    all_to_all x1, blocking collectives, on_device(): part = lax.all_to_all(part, 'z', 0, 0, tiled=True)  16 us
    all_to_all x1, blocking collectives, on_device(): part = lax.all_to_all(part, ('x', 'y'), 0, 0, tiled=True)  12.1 us
    ppermute x6, starting transfers between devices, turn(): lax.ppermute(value, 'y', [(i, (i + k) % GROUPS) for i in range(GROUPS)])  11 us
    ppermute x1, starting transfers between devices, on_device(): partner = lax.ppermute(own, 'c', swap)  4.38 us
    pallas_call x1, Pallas kernels, on_device(): pl.pallas_call(lambda *refs: grad_hidden_kernel(*refs, replicas=replicas)...  3.94 us
    all_to_all x1, starting transfers between devices, on_device(): lax.all_to_all(jnp.broadcast_to(piece, (PIECES, 8, half)), ('x', 'y'), 0,...  3.62 us
    ppermute x6, waiting for transfers between devices, turn(): lax.ppermute(value, 'y', [(i, (i + k) % GROUPS) for i in range(GROUPS)])  3.46 us
    all_to_all x1, waiting for transfers between devices, on_device(): lax.all_to_all(jnp.broadcast_to(piece, (PIECES, 8, half)), ('x', 'y'), 0,...  3.38 us
  transfers between devices with their start and end apart: 9, of which 6 were waited for; matrix products, arithmetic and copies ran while one was open for 0% of the time, Pallas kernels for 17%

profile of v10, /device:TPU:1, one launch (start us, length us, event | category | flops | bytes accessed | tf_op | source)
XLA Modules:
  0.0 78.9 jit_solution(7959861297033534718)
XLA Ops:
  0.6 0.1 pad_add_fusion.where.refs_0_
  0.7 0.0 copy-start.1
  0.7 0.0 copy-start.2
  0.7 0.0 copy-start.3
  0.7 0.0 copy-start.4
  0.7 0.0 copy-start.5
  0.7 2.4 %forward_far.1 = (f32[4,104,128]{2,1,0:T(8,128)S(1)}, bf16[104,1024]{1,0:T(8,128)(2,1)S(1)}) custom-call(s32[2]{0:T(128)S(1)} %pad_add_fusion.where.refs_0_, bf16[4,512,1024]{2,1,0:T(8,128)(2,1)} %hidden.5, f32[99,1024]{1,0:T(8,128)} %refs_6_.1), custom_call_target="tpu_custom_call" | custom-call | tf_op jit(solution)/shard_map/forward_far/forward_far/pallas_call | solution.py:320
  3.1 3.8 %collective-permute-start.2 = (f32[4,104,128]{2,1,0:T(8,128)S(1)}, f32[4,104,128]{2,1,0:T(8,128)S(1)}, u32[]{:S(2)}, u32[]{:S(2)}) collective-permute-start(f32[4,104,128]{2,1,0:T(8,128)S(1)} %get-tuple-element.37), channel_id=1, source_target_pairs={{0,128},{64,192},{128,0},{192,64},{1,129},{65,193},{129,1},{193,65... | collective-permute-start | bytes 638984 | tf_op jit(solution)/shard_map/forward_far/ppermute | solution.py:316
  6.9 2.7 %forward_near.1 = (f32[4,104,128]{2,1,0:T(8,128)S(1)}, f32[4,104,128]{2,1,0:T(8,128)S(1)}) custom-call(s32[2]{0:T(128)S(1)} %pad_add_fusion.where.refs_0_, bf16[4,512,1024]{2,1,0:T(8,128)(2,1)} %hidden.5, bf16[104,1024]{1,0:T(8,128)(2,1)S(1)} %get-tuple-element.33.half.refs_3_), custom_call_target="tpu_custom_call" | custom-call | flops 218103808 | bytes 2097152 | tf_op jit(solution)/shard_map/forward_near/forward_near/pallas_call | solution.py:336
  9.7 0.5 collective-permute-start
  10.2 2.3 %collective-permute-start.1 = (f32[4,104,128]{2,1,0:T(8,128)S(1)}, f32[4,104,128]{2,1,0:T(8,128)S(1)}, u32[]{:S(2)}, u32[]{:S(2)}) collective-permute-start(f32[4,104,128]{2,1,0:T(8,128)S(1)} %get-tuple-element.35), channel_id=1, source_target_pairs={{0,192},{64,0},{128,64},{192,128},{1,193},{65,1},{129,65},{193,129... | collective-permute-start | bytes 638984 | tf_op jit(solution)/shard_map/forward_near/ppermute | solution.py:316
  12.4 0.0 copy-done.1
  12.4 0.0 copy-done.2
  12.4 0.0 copy-done.3
  12.5 0.0 copy-done.4
  12.5 0.0 copy-done.5
  12.5 3.0 %forward_local.1 = (f32[4,104,128]{2,1,0:T(8,128)S(1)}, f32[1,128]{1,0:T(1,128)S(1)}, f32[104,512]{1,0:T(8,128)S(1)}, f32[104,128]{1,0:T(8,128)S(1)}, bf16[4,4,128,1024]{3,2,1,0:T(8,128)(2,1)S(1)}) custom-call(s32[2]{0:T(128)S(1)} %pad_add_fusion.where.refs_0_, bf16[4,512,1024]{2,1,0:T(8,128)(2,1)} %hidden.5, ...), custom_call_target="tpu_custom_call" | custom-call | tf_op jit(solution)/shard_map/forward_local/forward_local/pallas_call | solution.py:353
  15.5 0.0 collective-permute-done.2.refs_1_.refs_0_
  15.5 0.5 early_pairs.1.refs_4_
  16.1 0.8 collective-permute-done.refs_1_
  16.8 0.0 collective-permute-done.1.refs_2_
  16.8 0.5 far_pairs.1
  17.4 2.9 %collective-permute-start.5 = (bf16[4,104,128]{2,1,0:T(8,128)(2,1)S(1)}, bf16[4,104,128]{2,1,0:T(8,128)(2,1)S(1)}, u32[]{:S(2)}, u32[]{:S(2)}) collective-permute-start(bf16[4,104,128]{2,1,0:T(8,128)(2,1)S(1)} %get-tuple-element.51), channel_id=1, source_target_pairs={{0,128},{64,192},{128,0},{192,64},{1,129},{65,193},{129,1},{193,65... | collective-permute-start | bytes 319496 | tf_op jit(solution)/shard_map/far_pairs/ppermute | solution.py:316
  20.3 1.0 %near_pairs.1 = (bf16[4,104,128]{2,1,0:T(8,128)(2,1)S(1)}, bf16[4,104,128]{2,1,0:T(8,128)(2,1)S(1)}, bf16[4,104,128]{2,1,0:T(8,128)(2,1)S(1)}) custom-call(f32[4,104,128]{2,1,0:T(8,128)S(1)} %get-tuple-element.36.refs_0_, f32[4,104,128]{2,1,0:T(8,128)S(1)} %collective-permute-done.refs_1_, f32[4,104,128]{2,1,0:T(8,128)S(1)} %collective-permute-done.1.refs_2_, ...), custom_call_target="tpu_custom_call" | custom-call | flops 7987200 | bytes 851968 | tf_op jit(solution)/shard_map/near_pairs/near_pairs/pallas_call | solution.py:391
  21.3 0.4 collective-permute-start.3
  21.7 1.1 %collective-permute-start.4 = (bf16[4,104,128]{2,1,0:T(8,128)(2,1)S(1)}, bf16[4,104,128]{2,1,0:T(8,128)(2,1)S(1)}, u32[]{:S(2)}, u32[]{:S(2)}) collective-permute-start(bf16[4,104,128]{2,1,0:T(8,128)(2,1)S(1)} %get-tuple-element.47), channel_id=1, source_target_pairs={{0,64},{64,128},{128,192},{192,0},{1,65},{65,129},{129,193},{193,1... | collective-permute-start | bytes 319496 | tf_op jit(solution)/shard_map/near_pairs/ppermute | solution.py:316
  22.8 0.0 collective-permute-done.5.b2
  22.8 1.0 %early_backward.1 = (bf16[2,104,512]{2,1,0:T(8,128)(2,1)S(1)}, f32[104,1024]{1,0:T(8,128)S(1)}, f32[8,104]{1,0:T(8,128)S(1)}) custom-call(s32[2]{0:T(128)S(1)} %pad_add_fusion.where.refs_0_, bf16[4,4,128,1024]{3,2,1,0:T(8,128)(2,1)S(1)} %get-tuple-element.41.held, bf16[4,104,128]{2,1,0:T(8,128)(2,1)S(1)} %get-tuple-element.50.b0, ...), custom_call_target="tpu_custom_call" | custom-call | tf_op jit(solution)/shard_map/early_backward/early_backward/pallas_call | solution.py:407
  23.9 2.0 %collective-permute-done.3.b1 = bf16[4,104,128]{2,1,0:T(8,128)(2,1)S(1)} collective-permute-done((bf16[4,104,128]{2,1,0:T(8,128)(2,1)S(1)}, bf16[4,104,128]{2,1,0:T(8,128)(2,1)S(1)}, u32[]{:S(2)}, u32[]{:S(2)}) %collective-permute-start.3) | collective-permute-done | bytes 106528 | tf_op jit(solution)/shard_map/near_pairs/ppermute | solution.py:316
  25.9 0.7 collective-permute-done.4.b3
  26.6 0.9 %backward_partner_half.1 = (bf16[2,104,512]{2,1,0:T(8,128)(2,1)S(1)}, f32[16,8,512]{2,1,0:T(8,128)S(1)}) custom-call(s32[2]{0:T(128)S(1)} %pad_add_fusion.where.refs_0_, bf16[4,4,128,1024]{3,2,1,0:T(8,128)(2,1)S(1)} %get-tuple-element.41.held, bf16[4,104,128]{2,1,0:T(8,128)(2,1)S(1)} %collective-permute-done.3.b1, ...), custom_call_target="tpu_custom_call" | custom-call | tf_op jit(solution)/shard_map/backward_partner_half/backward_partner_half/pallas_call | solution.py:420
  27.5 3.3 %collective-permute-start.6 = (f32[16,8,512]{2,1,0:T(8,128)S(1)}, f32[16,8,512]{2,1,0:T(8,128)S(1)}, u32[]{:S(2)}, u32[]{:S(2)}) collective-permute-start(f32[16,8,512]{2,1,0:T(8,128)S(1)} %get-tuple-element.55), channel_id=1, source_target_pairs={{0,1},{1,0},{2,3},{3,2},{4,5},{5,4},{6,7},{7,6},{8,9},{9,8},{10,11... | collective-permute-start | bytes 786440 | tf_op jit(solution)/shard_map/backward_partner_half/ppermute | solution.py:430
  30.7 0.9 %backward_own_half.1 = f32[16,8,512]{2,1,0:T(8,128)S(1)} custom-call(s32[2]{0:T(128)S(1)} %pad_add_fusion.where.refs_0_, bf16[4,4,128,1024]{3,2,1,0:T(8,128)(2,1)S(1)} %get-tuple-element.41.held, bf16[2,104,512]{2,1,0:T(8,128)(2,1)S(1)} %get-tuple-element.53.weighted.refs_2_, f32[104,1024]{1,0:T(8,128)S(1)} %get-tuple-element.52.early, ...), custom_call_target="tpu_custom_call" | custom-call | tf_op jit(solution)/shard_map/backward_own_half/backward_own_half/pallas_call | solution.py:432
  31.6 0.0 copy-start
  31.7 0.2 collective-permute-done.6
  31.9 12.1 %all_to_all.15 = f32[16,8,512]{2,1,0:T(8,128)S(1)} all-to-all(f32[16,8,512]{2,1,0:T(8,128)S(1)} %add.3), channel_id=1, replica_groups=mesh['y'=4,'z'=8,'x'=4,'c'=2] {'x','y'}, dimensions={0} | all-to-all | bytes 524288 | tf_op jit(solution)/shard_map/gradient_sum/all_to_all | solution.py:443
  44.1 16.0 %all_to_all.16 = f32[8,8,512]{2,1,0:T(8,128)S(1)} all-to-all(f32[8,8,512]{2,1,0:T(8,128)S(1)} %broadcast_in_dim.6), channel_id=1, replica_groups=mesh['y'=4,'z'=8,'x'=4,'c'=2] {'z'}, dimensions={0} | all-to-all | bytes 262144 | tf_op jit(solution)/shard_map/gradient_sum/all_to_all | solution.py:446
  60.1 0.7 broadcast_in_dim.7
  60.8 3.6 %all-to-all-start.2 = ((f32[16,8,512]{2,1,0:T(8,128)}), f32[16,8,512]{2,1,0:T(8,128)S(1)}, u32[]{:S(2)}, u32[]{:S(2)}) async-start(f32[16,8,512]{2,1,0:T(8,128)} %broadcast_in_dim.7), calls=%async_computation.2 | async-start | bytes 524288 | tf_op jit(solution)/shard_map/gradient_sum/all_to_all | solution.py:448
  64.5 3.9 %grad_hidden.1 = bf16[4,512,1024]{2,1,0:T(8,128)(2,1)} custom-call(s32[2]{0:T(128)S(1)} %pad_add_fusion.where.refs_0_, bf16[2,104,512]{2,1,0:T(8,128)(2,1)S(1)} %get-tuple-element.56.refs_1_, bf16[2,104,512]{2,1,0:T(8,128)(2,1)S(1)} %get-tuple-element.53.weighted.refs_2_, bf16[104,1024]{1,0:T(8,128)(2,1)S(1)} %get-tuple-element.33.half.refs_3_, ...), custom_call_target="tpu_custom_call" | custom-call | flops 436207616 | bytes 4194304 | tf_op jit(solution)/shard_map/grad_hidden/grad_hidden/pallas_call | solution.py:450
  68.4 3.4 %all-to-all-done.2.refs_0_.refs_2_ = f32[16,8,512]{2,1,0:T(8,128)S(1)} async-done(((f32[16,8,512]{2,1,0:T(8,128)}), f32[16,8,512]{2,1,0:T(8,128)S(1)}, u32[]{:S(2)}, u32[]{:S(2)}) %all-to-all-start.2) | async-done | bytes 262176 | tf_op jit(solution)/shard_map/gradient_sum/all_to_all | solution.py:448
  71.8 4.4 %collective-permute-start.7 = (f32[16,8,512]{2,1,0:T(8,128)S(1)}, f32[16,8,512]{2,1,0:T(8,128)S(1)}, u32[]{:S(2)}, u32[]{:S(2)}) collective-permute-start(f32[16,8,512]{2,1,0:T(8,128)S(1)} %all-to-all-done.2.refs_0_.refs_2_), channel_id=1, source_target_pairs={{0,1},{1,0},{2,3},{3,2},{4,5},{5,4},{6,7},{7,6},{8,9},{9,8},{10,11... | collective-permute-start | bytes 786440 | tf_op jit(solution)/shard_map/last_swap/ppermute | solution.py:472
  76.8 0.1 own_gradient.1
  77.0 0.4 collective-permute-done.7.refs_4_
  77.3 0.0 copy-done
  77.3 1.6 %update.1 = (f32[99,1024]{1,0:T(8,128)}, f32[1,99]{1,0:T(1,128)}) custom-call(s32[2]{0:T(128)S(1)} %pad_add_fusion.where.refs_0_, s32[1]{0:T(128)S(6)} %copy.11.refs_1_, f32[16,8,512]{2,1,0:T(8,128)S(1)} %all-to-all-done.2.refs_0_.refs_2_, f32[99,512]{1,0:T(8,128)S(1)} %get-tuple-element.59.refs_3_, f32[16,8,512]{2,1,0:T(8,128)S(1)} %collective-permute-done.7.refs_4_, ...), custom_call_target="tpu_custom_call" | custom-call | tf_op jit(solution)/shard_map/update/update/pallas_call | solution.py:482
  (4 shorter events, 0.1 us)
Async XLA Ops:
  0.7 11.7 %copy-start.1 = (f32[99,512]{1,0:T(8,128)S(1)}, f32[99,512]{1,0:T(8,128)}, u32[]{:S(2)}) copy-start(f32[99,512]{1,0:T(8,128)} %truth.1) | copy-start | bytes 608260
  0.7 11.7 %copy-start.2 = (f32[640]{0:T(1024)S(1)}, f32[640]{0:T(1024)}, u32[]{:S(2)}) copy-start(f32[640]{0:T(1024)} %param.13) | copy-start | bytes 7684
  0.7 11.7 %copy-start.3 = (f32[99]{0:T(128)S(1)}, f32[99]{0:T(128)}, u32[]{:S(2)}) copy-start(f32[99]{0:T(128)} %param.10) | copy-start | bytes 1192
  0.7 11.7 %copy-start.4 = (s32[512]{0:T(512)S(1)}, s32[512]{0:T(512)}, u32[]{:S(2)}) copy-start(s32[512]{0:T(512)} %param.14) | copy-start | bytes 6148
  0.7 11.7 %copy-start.5 = (f32[99]{0:T(128)S(1)}, f32[99]{0:T(128)}, u32[]{:S(2)}) copy-start(f32[99]{0:T(128)} %param.12) | copy-start | bytes 1192
  3.1 12.4 %collective-permute-start.2 = (f32[4,104,128]{2,1,0:T(8,128)S(1)}, f32[4,104,128]{2,1,0:T(8,128)S(1)}, u32[]{:S(2)}, u32[]{:S(2)}) collective-permute-start(f32[4,104,128]{2,1,0:T(8,128)S(1)} %get-tuple-element.37), channel_id=1, source_target_pairs={{0,128},{64,192},{128,0},{192,64},{1,129},{65,193},{129,1},{193,65... | collective-permute-start | bytes 638984 | tf_op jit(solution)/shard_map/forward_far/ppermute | solution.py:316
  9.7 7.1 %collective-permute-start = (f32[4,104,128]{2,1,0:T(8,128)S(1)}, f32[4,104,128]{2,1,0:T(8,128)S(1)}, u32[]{:S(2)}, u32[]{:S(2)}) collective-permute-start(f32[4,104,128]{2,1,0:T(8,128)S(1)} %get-tuple-element.34), channel_id=1, source_target_pairs={{0,64},{64,128},{128,192},{192,0},{1,65},{65,129},{129,193},{193,1... | collective-permute-start | bytes 638984 | tf_op jit(solution)/shard_map/forward_near/ppermute | solution.py:316
  10.2 6.7 %collective-permute-start.1 = (f32[4,104,128]{2,1,0:T(8,128)S(1)}, f32[4,104,128]{2,1,0:T(8,128)S(1)}, u32[]{:S(2)}, u32[]{:S(2)}) collective-permute-start(f32[4,104,128]{2,1,0:T(8,128)S(1)} %get-tuple-element.35), channel_id=1, source_target_pairs={{0,192},{64,0},{128,64},{192,128},{1,193},{65,1},{129,65},{193,129... | collective-permute-start | bytes 638984 | tf_op jit(solution)/shard_map/forward_near/ppermute | solution.py:316
  17.4 5.5 %collective-permute-start.5 = (bf16[4,104,128]{2,1,0:T(8,128)(2,1)S(1)}, bf16[4,104,128]{2,1,0:T(8,128)(2,1)S(1)}, u32[]{:S(2)}, u32[]{:S(2)}) collective-permute-start(bf16[4,104,128]{2,1,0:T(8,128)(2,1)S(1)} %get-tuple-element.51), channel_id=1, source_target_pairs={{0,128},{64,192},{128,0},{192,64},{1,129},{65,193},{129,1},{193,65... | collective-permute-start | bytes 319496 | tf_op jit(solution)/shard_map/far_pairs/ppermute | solution.py:316
  21.3 4.6 %collective-permute-start.3 = (bf16[4,104,128]{2,1,0:T(8,128)(2,1)S(1)}, bf16[4,104,128]{2,1,0:T(8,128)(2,1)S(1)}, u32[]{:S(2)}, u32[]{:S(2)}) collective-permute-start(bf16[4,104,128]{2,1,0:T(8,128)(2,1)S(1)} %get-tuple-element.46), channel_id=1, source_target_pairs={{0,192},{64,0},{128,64},{192,128},{1,193},{65,1},{129,65},{193,129... | collective-permute-start | bytes 319496 | tf_op jit(solution)/shard_map/near_pairs/ppermute | solution.py:316
  21.7 4.9 %collective-permute-start.4 = (bf16[4,104,128]{2,1,0:T(8,128)(2,1)S(1)}, bf16[4,104,128]{2,1,0:T(8,128)(2,1)S(1)}, u32[]{:S(2)}, u32[]{:S(2)}) collective-permute-start(bf16[4,104,128]{2,1,0:T(8,128)(2,1)S(1)} %get-tuple-element.47), channel_id=1, source_target_pairs={{0,64},{64,128},{128,192},{192,0},{1,65},{65,129},{129,193},{193,1... | collective-permute-start | bytes 319496 | tf_op jit(solution)/shard_map/near_pairs/ppermute | solution.py:316
  27.5 4.4 %collective-permute-start.6 = (f32[16,8,512]{2,1,0:T(8,128)S(1)}, f32[16,8,512]{2,1,0:T(8,128)S(1)}, u32[]{:S(2)}, u32[]{:S(2)}) collective-permute-start(f32[16,8,512]{2,1,0:T(8,128)S(1)} %get-tuple-element.55), channel_id=1, source_target_pairs={{0,1},{1,0},{2,3},{3,2},{4,5},{5,4},{6,7},{7,6},{8,9},{9,8},{10,11... | collective-permute-start | bytes 786440 | tf_op jit(solution)/shard_map/backward_partner_half/ppermute | solution.py:430
  31.6 45.7 %copy-start = (f32[99,1024]{1,0:T(8,128)S(1)}, f32[99,1024]{1,0:T(8,128)}, u32[]{:S(2)}) copy-start(f32[99,1024]{1,0:T(8,128)} %refs_6_.1) | copy-start | bytes 1216516
  60.8 10.9 %all-to-all-start.2 = ((f32[16,8,512]{2,1,0:T(8,128)}), f32[16,8,512]{2,1,0:T(8,128)S(1)}, u32[]{:S(2)}, u32[]{:S(2)}) async-start(f32[16,8,512]{2,1,0:T(8,128)} %broadcast_in_dim.7), calls=%async_computation.2 | async-start | bytes 524288 | tf_op jit(solution)/shard_map/gradient_sum/all_to_all | solution.py:448
  71.8 5.5 %collective-permute-start.7 = (f32[16,8,512]{2,1,0:T(8,128)S(1)}, f32[16,8,512]{2,1,0:T(8,128)S(1)}, u32[]{:S(2)}, u32[]{:S(2)}) collective-permute-start(f32[16,8,512]{2,1,0:T(8,128)S(1)} %all-to-all-done.2.refs_0_.refs_2_), channel_id=1, source_target_pairs={{0,1},{1,0},{2,3},{3,2},{4,5},{5,4},{6,7},{7,6},{8,9},{9,8},{10,11... | collective-permute-start | bytes 786440 | tf_op jit(solution)/shard_map/last_swap/ppermute | solution.py:472

commit v11 on v10

--- a/solution.py
+++ b/solution.py
@@ -54,12 +54,8 @@
 def decode_chunk(copies, held, half, out):
     for copy in copies:
         copy.wait()
-    values = lax.dot_general(
-        half[...], held[...].reshape(-1, held.shape[2]), (((1,), (1,)), ((), ())), preferred_element_type=F32
-    )
-    chunk = out.shape[2]
     for m in range(out.shape[0]):
-        out[m] = values[:, m * chunk : (m + 1) * chunk]
+        out[m] = lax.dot_general(half[...], held[m], (((1,), (1,)), ((), ())), preferred_element_type=F32)
 
 
 def far_kernel(where, hidden, weight, out, half, held, w, sem, weight_sem):

time: 79.2 us -> 79.2 us (level)
  no operation moved by 1% of the time
where the time goes in v11:
time: 79.2 us; the launch traced here: 78.8 us
  blocking collectives  28.1 us (35%)
  starting transfers between devices  22.2 us (28%)
  Pallas kernels  18.6 us (23%)
  waiting for transfers between devices  7.57 us (10%)
  between operations  1.43 us (2%)
    all_to_all x1, blocking collectives, on_device(): part = lax.all_to_all(part, 'z', 0, 0, tiled=True)  16 us
    all_to_all x1, blocking collectives, on_device(): part = lax.all_to_all(part, ('x', 'y'), 0, 0, tiled=True)  12 us
    ppermute x6, starting transfers between devices, turn(): lax.ppermute(value, 'y', [(i, (i + k) % GROUPS) for i in range(GROUPS)])  11 us
    ppermute x1, starting transfers between devices, on_device(): partner = lax.ppermute(own, 'c', swap)  4.38 us
    pallas_call x1, Pallas kernels, on_device(): pl.pallas_call(lambda *refs: grad_hidden_kernel(*refs, replicas=replicas)...  3.94 us
    all_to_all x1, starting transfers between devices, on_device(): lax.all_to_all(jnp.broadcast_to(piece, (PIECES, 8, half)), ('x', 'y'), 0,...  3.62 us
    ppermute x6, waiting for transfers between devices, turn(): lax.ppermute(value, 'y', [(i, (i + k) % GROUPS) for i in range(GROUPS)])  3.59 us
    all_to_all x1, waiting for transfers between devices, on_device(): lax.all_to_all(jnp.broadcast_to(piece, (PIECES, 8, half)), ('x', 'y'), 0,...  3.38 us
  transfers between devices with their start and end apart: 9, of which 6 were waited for; matrix products, arithmetic and copies ran while one was open for 0% of the time, Pallas kernels for 17%

profile of v11, /device:TPU:1, one launch (start us, length us, event | category | flops | bytes accessed | tf_op | source)
XLA Modules:
  0.0 78.8 jit_solution(18383944894848485729)
XLA Ops:
  0.6 0.1 pad_add_fusion.where.refs_0_
  0.7 0.0 copy-start.1
  0.7 0.0 copy-start.2
  0.7 0.0 copy-start.3
  0.7 0.0 copy-start.4
  0.7 0.0 copy-start.5
  0.7 2.3 %forward_far.1 = (f32[4,104,128]{2,1,0:T(8,128)S(1)}, bf16[104,1024]{1,0:T(8,128)(2,1)S(1)}) custom-call(s32[2]{0:T(128)S(1)} %pad_add_fusion.where.refs_0_, bf16[4,512,1024]{2,1,0:T(8,128)(2,1)} %hidden.5, f32[99,1024]{1,0:T(8,128)} %refs_6_.1), custom_call_target="tpu_custom_call" | custom-call | tf_op jit(solution)/shard_map/forward_far/forward_far/pallas_call | solution.py:316
  3.1 3.8 %collective-permute-start.2 = (f32[4,104,128]{2,1,0:T(8,128)S(1)}, f32[4,104,128]{2,1,0:T(8,128)S(1)}, u32[]{:S(2)}, u32[]{:S(2)}) collective-permute-start(f32[4,104,128]{2,1,0:T(8,128)S(1)} %get-tuple-element.37), channel_id=1, source_target_pairs={{0,128},{64,192},{128,0},{192,64},{1,129},{65,193},{129,1},{193,65... | collective-permute-start | bytes 638984 | tf_op jit(solution)/shard_map/forward_far/ppermute | solution.py:312
  6.9 2.7 %forward_near.1 = (f32[4,104,128]{2,1,0:T(8,128)S(1)}, f32[4,104,128]{2,1,0:T(8,128)S(1)}) custom-call(s32[2]{0:T(128)S(1)} %pad_add_fusion.where.refs_0_, bf16[4,512,1024]{2,1,0:T(8,128)(2,1)} %hidden.5, bf16[104,1024]{1,0:T(8,128)(2,1)S(1)} %get-tuple-element.33.half.refs_3_), custom_call_target="tpu_custom_call" | custom-call | flops 218103808 | bytes 2097152 | tf_op jit(solution)/shard_map/forward_near/forward_near/pallas_call | solution.py:332
  9.6 0.5 collective-permute-start
  10.1 2.3 %collective-permute-start.1 = (f32[4,104,128]{2,1,0:T(8,128)S(1)}, f32[4,104,128]{2,1,0:T(8,128)S(1)}, u32[]{:S(2)}, u32[]{:S(2)}) collective-permute-start(f32[4,104,128]{2,1,0:T(8,128)S(1)} %get-tuple-element.35), channel_id=1, source_target_pairs={{0,192},{64,0},{128,64},{192,128},{1,193},{65,1},{129,65},{193,129... | collective-permute-start | bytes 638984 | tf_op jit(solution)/shard_map/forward_near/ppermute | solution.py:312
  12.4 0.0 copy-done.1
  12.4 0.0 copy-done.2
  12.4 0.0 copy-done.3
  12.4 0.0 copy-done.4
  12.4 0.0 copy-done.5
  12.4 3.0 %forward_local.1 = (f32[4,104,128]{2,1,0:T(8,128)S(1)}, f32[1,128]{1,0:T(1,128)S(1)}, f32[104,512]{1,0:T(8,128)S(1)}, f32[104,128]{1,0:T(8,128)S(1)}, bf16[4,4,128,1024]{3,2,1,0:T(8,128)(2,1)S(1)}) custom-call(s32[2]{0:T(128)S(1)} %pad_add_fusion.where.refs_0_, bf16[4,512,1024]{2,1,0:T(8,128)(2,1)} %hidden.5, ...), custom_call_target="tpu_custom_call" | custom-call | tf_op jit(solution)/shard_map/forward_local/forward_local/pallas_call | solution.py:349
  15.4 0.0 collective-permute-done.2.refs_1_.refs_0_
  15.4 0.5 early_pairs.1.refs_4_
  16.0 0.9 %collective-permute-done.refs_1_ = f32[4,104,128]{2,1,0:T(8,128)S(1)} collective-permute-done((f32[4,104,128]{2,1,0:T(8,128)S(1)}, f32[4,104,128]{2,1,0:T(8,128)S(1)}, u32[]{:S(2)}, u32[]{:S(2)}) %collective-permute-start) | collective-permute-done | bytes 213024 | tf_op jit(solution)/shard_map/forward_near/ppermute | solution.py:312
  16.9 0.0 collective-permute-done.1.refs_2_
  16.9 0.5 far_pairs.1
  17.4 2.9 %collective-permute-start.5 = (bf16[4,104,128]{2,1,0:T(8,128)(2,1)S(1)}, bf16[4,104,128]{2,1,0:T(8,128)(2,1)S(1)}, u32[]{:S(2)}, u32[]{:S(2)}) collective-permute-start(bf16[4,104,128]{2,1,0:T(8,128)(2,1)S(1)} %get-tuple-element.51), channel_id=1, source_target_pairs={{0,128},{64,192},{128,0},{192,64},{1,129},{65,193},{129,1},{193,65... | collective-permute-start | bytes 319496 | tf_op jit(solution)/shard_map/far_pairs/ppermute | solution.py:312
  20.3 1.0 %near_pairs.1 = (bf16[4,104,128]{2,1,0:T(8,128)(2,1)S(1)}, bf16[4,104,128]{2,1,0:T(8,128)(2,1)S(1)}, bf16[4,104,128]{2,1,0:T(8,128)(2,1)S(1)}) custom-call(f32[4,104,128]{2,1,0:T(8,128)S(1)} %get-tuple-element.36.refs_0_, f32[4,104,128]{2,1,0:T(8,128)S(1)} %collective-permute-done.refs_1_, f32[4,104,128]{2,1,0:T(8,128)S(1)} %collective-permute-done.1.refs_2_, ...), custom_call_target="tpu_custom_call" | custom-call | flops 7987200 | bytes 851968 | tf_op jit(solution)/shard_map/near_pairs/near_pairs/pallas_call | solution.py:387
  21.3 0.4 collective-permute-start.3
  21.7 1.1 %collective-permute-start.4 = (bf16[4,104,128]{2,1,0:T(8,128)(2,1)S(1)}, bf16[4,104,128]{2,1,0:T(8,128)(2,1)S(1)}, u32[]{:S(2)}, u32[]{:S(2)}) collective-permute-start(bf16[4,104,128]{2,1,0:T(8,128)(2,1)S(1)} %get-tuple-element.47), channel_id=1, source_target_pairs={{0,64},{64,128},{128,192},{192,0},{1,65},{65,129},{129,193},{193,1... | collective-permute-start | bytes 319496 | tf_op jit(solution)/shard_map/near_pairs/ppermute | solution.py:312
  22.9 0.0 collective-permute-done.5.b2
  22.9 1.0 %early_backward.1 = (bf16[2,104,512]{2,1,0:T(8,128)(2,1)S(1)}, f32[104,1024]{1,0:T(8,128)S(1)}, f32[8,104]{1,0:T(8,128)S(1)}) custom-call(s32[2]{0:T(128)S(1)} %pad_add_fusion.where.refs_0_, bf16[4,4,128,1024]{3,2,1,0:T(8,128)(2,1)S(1)} %get-tuple-element.41.held, bf16[4,104,128]{2,1,0:T(8,128)(2,1)S(1)} %get-tuple-element.50.b0, ...), custom_call_target="tpu_custom_call" | custom-call | tf_op jit(solution)/shard_map/early_backward/early_backward/pallas_call | solution.py:403
  23.9 2.1 %collective-permute-done.3.b1 = bf16[4,104,128]{2,1,0:T(8,128)(2,1)S(1)} collective-permute-done((bf16[4,104,128]{2,1,0:T(8,128)(2,1)S(1)}, bf16[4,104,128]{2,1,0:T(8,128)(2,1)S(1)}, u32[]{:S(2)}, u32[]{:S(2)}) %collective-permute-start.3) | collective-permute-done | bytes 106528 | tf_op jit(solution)/shard_map/near_pairs/ppermute | solution.py:312
  26.0 0.5 collective-permute-done.4.b3
  26.6 0.9 %backward_partner_half.1 = (bf16[2,104,512]{2,1,0:T(8,128)(2,1)S(1)}, f32[16,8,512]{2,1,0:T(8,128)S(1)}) custom-call(s32[2]{0:T(128)S(1)} %pad_add_fusion.where.refs_0_, bf16[4,4,128,1024]{3,2,1,0:T(8,128)(2,1)S(1)} %get-tuple-element.41.held, bf16[4,104,128]{2,1,0:T(8,128)(2,1)S(1)} %collective-permute-done.3.b1, ...), custom_call_target="tpu_custom_call" | custom-call | tf_op jit(solution)/shard_map/backward_partner_half/backward_partner_half/pallas_call | solution.py:416
  27.5 3.2 %collective-permute-start.6 = (f32[16,8,512]{2,1,0:T(8,128)S(1)}, f32[16,8,512]{2,1,0:T(8,128)S(1)}, u32[]{:S(2)}, u32[]{:S(2)}) collective-permute-start(f32[16,8,512]{2,1,0:T(8,128)S(1)} %get-tuple-element.55), channel_id=1, source_target_pairs={{0,1},{1,0},{2,3},{3,2},{4,5},{5,4},{6,7},{7,6},{8,9},{9,8},{10,11... | collective-permute-start | bytes 786440 | tf_op jit(solution)/shard_map/backward_partner_half/ppermute | solution.py:426
  30.7 0.9 %backward_own_half.1 = f32[16,8,512]{2,1,0:T(8,128)S(1)} custom-call(s32[2]{0:T(128)S(1)} %pad_add_fusion.where.refs_0_, bf16[4,4,128,1024]{3,2,1,0:T(8,128)(2,1)S(1)} %get-tuple-element.41.held, bf16[2,104,512]{2,1,0:T(8,128)(2,1)S(1)} %get-tuple-element.53.weighted.refs_2_, f32[104,1024]{1,0:T(8,128)S(1)} %get-tuple-element.52.early, ...), custom_call_target="tpu_custom_call" | custom-call | tf_op jit(solution)/shard_map/backward_own_half/backward_own_half/pallas_call | solution.py:428
  31.6 0.0 copy-start
  31.6 0.2 collective-permute-done.6
  31.9 12.0 %all_to_all.15 = f32[16,8,512]{2,1,0:T(8,128)S(1)} all-to-all(f32[16,8,512]{2,1,0:T(8,128)S(1)} %add.3), channel_id=1, replica_groups=mesh['y'=4,'z'=8,'x'=4,'c'=2] {'x','y'}, dimensions={0} | all-to-all | bytes 524288 | tf_op jit(solution)/shard_map/gradient_sum/all_to_all | solution.py:439
  44.0 16.0 %all_to_all.16 = f32[8,8,512]{2,1,0:T(8,128)S(1)} all-to-all(f32[8,8,512]{2,1,0:T(8,128)S(1)} %broadcast_in_dim.6), channel_id=1, replica_groups=mesh['y'=4,'z'=8,'x'=4,'c'=2] {'z'}, dimensions={0} | all-to-all | bytes 262144 | tf_op jit(solution)/shard_map/gradient_sum/all_to_all | solution.py:442
  60.0 0.7 broadcast_in_dim.7
  60.8 3.6 %all-to-all-start.2 = ((f32[16,8,512]{2,1,0:T(8,128)}), f32[16,8,512]{2,1,0:T(8,128)S(1)}, u32[]{:S(2)}, u32[]{:S(2)}) async-start(f32[16,8,512]{2,1,0:T(8,128)} %broadcast_in_dim.7), calls=%async_computation.2 | async-start | bytes 524288 | tf_op jit(solution)/shard_map/gradient_sum/all_to_all | solution.py:444
  64.4 3.9 %grad_hidden.1 = bf16[4,512,1024]{2,1,0:T(8,128)(2,1)} custom-call(s32[2]{0:T(128)S(1)} %pad_add_fusion.where.refs_0_, bf16[2,104,512]{2,1,0:T(8,128)(2,1)S(1)} %get-tuple-element.56.refs_1_, bf16[2,104,512]{2,1,0:T(8,128)(2,1)S(1)} %get-tuple-element.53.weighted.refs_2_, bf16[104,1024]{1,0:T(8,128)(2,1)S(1)} %get-tuple-element.33.half.refs_3_, ...), custom_call_target="tpu_custom_call" | custom-call | flops 436207616 | bytes 4194304 | tf_op jit(solution)/shard_map/grad_hidden/grad_hidden/pallas_call | solution.py:446
  68.3 3.4 %all-to-all-done.2.refs_0_.refs_2_ = f32[16,8,512]{2,1,0:T(8,128)S(1)} async-done(((f32[16,8,512]{2,1,0:T(8,128)}), f32[16,8,512]{2,1,0:T(8,128)S(1)}, u32[]{:S(2)}, u32[]{:S(2)}) %all-to-all-start.2) | async-done | bytes 262176 | tf_op jit(solution)/shard_map/gradient_sum/all_to_all | solution.py:444
  71.7 4.4 %collective-permute-start.7 = (f32[16,8,512]{2,1,0:T(8,128)S(1)}, f32[16,8,512]{2,1,0:T(8,128)S(1)}, u32[]{:S(2)}, u32[]{:S(2)}) collective-permute-start(f32[16,8,512]{2,1,0:T(8,128)S(1)} %all-to-all-done.2.refs_0_.refs_2_), channel_id=1, source_target_pairs={{0,1},{1,0},{2,3},{3,2},{4,5},{5,4},{6,7},{7,6},{8,9},{9,8},{10,11... | collective-permute-start | bytes 786440 | tf_op jit(solution)/shard_map/last_swap/ppermute | solution.py:468
  76.7 0.1 own_gradient.1
  76.9 0.4 collective-permute-done.7.refs_4_
  77.3 0.0 copy-done
  77.3 1.6 %update.1 = (f32[99,1024]{1,0:T(8,128)}, f32[1,99]{1,0:T(1,128)}) custom-call(s32[2]{0:T(128)S(1)} %pad_add_fusion.where.refs_0_, s32[1]{0:T(128)S(6)} %copy.11.refs_1_, f32[16,8,512]{2,1,0:T(8,128)S(1)} %all-to-all-done.2.refs_0_.refs_2_, f32[99,512]{1,0:T(8,128)S(1)} %get-tuple-element.59.refs_3_, f32[16,8,512]{2,1,0:T(8,128)S(1)} %collective-permute-done.7.refs_4_, ...), custom_call_target="tpu_custom_call" | custom-call | tf_op jit(solution)/shard_map/update/update/pallas_call | solution.py:478
  (4 shorter events, 0.1 us)
Async XLA Ops:
  0.7 11.6 %copy-start.1 = (f32[99,512]{1,0:T(8,128)S(1)}, f32[99,512]{1,0:T(8,128)}, u32[]{:S(2)}) copy-start(f32[99,512]{1,0:T(8,128)} %truth.1) | copy-start | bytes 608260
  0.7 11.6 %copy-start.2 = (f32[640]{0:T(1024)S(1)}, f32[640]{0:T(1024)}, u32[]{:S(2)}) copy-start(f32[640]{0:T(1024)} %param.13) | copy-start | bytes 7684
  0.7 11.6 %copy-start.3 = (f32[99]{0:T(128)S(1)}, f32[99]{0:T(128)}, u32[]{:S(2)}) copy-start(f32[99]{0:T(128)} %param.10) | copy-start | bytes 1192
  0.7 11.6 %copy-start.4 = (s32[512]{0:T(512)S(1)}, s32[512]{0:T(512)}, u32[]{:S(2)}) copy-start(s32[512]{0:T(512)} %param.14) | copy-start | bytes 6148
  0.7 11.6 %copy-start.5 = (f32[99]{0:T(128)S(1)}, f32[99]{0:T(128)}, u32[]{:S(2)}) copy-start(f32[99]{0:T(128)} %param.12) | copy-start | bytes 1192
  3.1 12.4 %collective-permute-start.2 = (f32[4,104,128]{2,1,0:T(8,128)S(1)}, f32[4,104,128]{2,1,0:T(8,128)S(1)}, u32[]{:S(2)}, u32[]{:S(2)}) collective-permute-start(f32[4,104,128]{2,1,0:T(8,128)S(1)} %get-tuple-element.37), channel_id=1, source_target_pairs={{0,128},{64,192},{128,0},{192,64},{1,129},{65,193},{129,1},{193,65... | collective-permute-start | bytes 638984 | tf_op jit(solution)/shard_map/forward_far/ppermute | solution.py:312
  9.6 7.3 %collective-permute-start = (f32[4,104,128]{2,1,0:T(8,128)S(1)}, f32[4,104,128]{2,1,0:T(8,128)S(1)}, u32[]{:S(2)}, u32[]{:S(2)}) collective-permute-start(f32[4,104,128]{2,1,0:T(8,128)S(1)} %get-tuple-element.34), channel_id=1, source_target_pairs={{0,64},{64,128},{128,192},{192,0},{1,65},{65,129},{129,193},{193,1... | collective-permute-start | bytes 638984 | tf_op jit(solution)/shard_map/forward_near/ppermute | solution.py:312
  10.1 6.8 %collective-permute-start.1 = (f32[4,104,128]{2,1,0:T(8,128)S(1)}, f32[4,104,128]{2,1,0:T(8,128)S(1)}, u32[]{:S(2)}, u32[]{:S(2)}) collective-permute-start(f32[4,104,128]{2,1,0:T(8,128)S(1)} %get-tuple-element.35), channel_id=1, source_target_pairs={{0,192},{64,0},{128,64},{192,128},{1,193},{65,1},{129,65},{193,129... | collective-permute-start | bytes 638984 | tf_op jit(solution)/shard_map/forward_near/ppermute | solution.py:312
  17.4 5.4 %collective-permute-start.5 = (bf16[4,104,128]{2,1,0:T(8,128)(2,1)S(1)}, bf16[4,104,128]{2,1,0:T(8,128)(2,1)S(1)}, u32[]{:S(2)}, u32[]{:S(2)}) collective-permute-start(bf16[4,104,128]{2,1,0:T(8,128)(2,1)S(1)} %get-tuple-element.51), channel_id=1, source_target_pairs={{0,128},{64,192},{128,0},{192,64},{1,129},{65,193},{129,1},{193,65... | collective-permute-start | bytes 319496 | tf_op jit(solution)/shard_map/far_pairs/ppermute | solution.py:312
  21.3 4.7 %collective-permute-start.3 = (bf16[4,104,128]{2,1,0:T(8,128)(2,1)S(1)}, bf16[4,104,128]{2,1,0:T(8,128)(2,1)S(1)}, u32[]{:S(2)}, u32[]{:S(2)}) collective-permute-start(bf16[4,104,128]{2,1,0:T(8,128)(2,1)S(1)} %get-tuple-element.46), channel_id=1, source_target_pairs={{0,192},{64,0},{128,64},{192,128},{1,193},{65,1},{129,65},{193,129... | collective-permute-start | bytes 319496 | tf_op jit(solution)/shard_map/near_pairs/ppermute | solution.py:312
  21.7 4.9 %collective-permute-start.4 = (bf16[4,104,128]{2,1,0:T(8,128)(2,1)S(1)}, bf16[4,104,128]{2,1,0:T(8,128)(2,1)S(1)}, u32[]{:S(2)}, u32[]{:S(2)}) collective-permute-start(bf16[4,104,128]{2,1,0:T(8,128)(2,1)S(1)} %get-tuple-element.47), channel_id=1, source_target_pairs={{0,64},{64,128},{128,192},{192,0},{1,65},{65,129},{129,193},{193,1... | collective-permute-start | bytes 319496 | tf_op jit(solution)/shard_map/near_pairs/ppermute | solution.py:312
  27.5 4.4 %collective-permute-start.6 = (f32[16,8,512]{2,1,0:T(8,128)S(1)}, f32[16,8,512]{2,1,0:T(8,128)S(1)}, u32[]{:S(2)}, u32[]{:S(2)}) collective-permute-start(f32[16,8,512]{2,1,0:T(8,128)S(1)} %get-tuple-element.55), channel_id=1, source_target_pairs={{0,1},{1,0},{2,3},{3,2},{4,5},{5,4},{6,7},{7,6},{8,9},{9,8},{10,11... | collective-permute-start | bytes 786440 | tf_op jit(solution)/shard_map/backward_partner_half/ppermute | solution.py:426
  31.6 45.6 %copy-start = (f32[99,1024]{1,0:T(8,128)S(1)}, f32[99,1024]{1,0:T(8,128)}, u32[]{:S(2)}) copy-start(f32[99,1024]{1,0:T(8,128)} %refs_6_.1) | copy-start | bytes 1216516
  60.8 10.9 %all-to-all-start.2 = ((f32[16,8,512]{2,1,0:T(8,128)}), f32[16,8,512]{2,1,0:T(8,128)S(1)}, u32[]{:S(2)}, u32[]{:S(2)}) async-start(f32[16,8,512]{2,1,0:T(8,128)} %broadcast_in_dim.7), calls=%async_computation.2 | async-start | bytes 524288 | tf_op jit(solution)/shard_map/gradient_sum/all_to_all | solution.py:444
  71.7 5.5 %collective-permute-start.7 = (f32[16,8,512]{2,1,0:T(8,128)S(1)}, f32[16,8,512]{2,1,0:T(8,128)S(1)}, u32[]{:S(2)}, u32[]{:S(2)}) collective-permute-start(f32[16,8,512]{2,1,0:T(8,128)S(1)} %all-to-all-done.2.refs_0_.refs_2_), channel_id=1, source_target_pairs={{0,1},{1,0},{2,3},{3,2},{4,5},{5,4},{6,7},{7,6},{8,9},{9,8},{10,11... | collective-permute-start | bytes 786440 | tf_op jit(solution)/shard_map/last_swap/ppermute | solution.py:468

commit v12 on v10

--- a/solution.py
+++ b/solution.py
@@ -202,13 +202,19 @@
     ) + jnp.dot(w2, held[2].reshape(-1, features), preferred_element_type=F32)
 
 
-def late_half(side, w1, w3, held, early, acc):
-    rows = w1.shape[0]
+def next_backward_kernel(where, held, b1, weight, early, early_bias, weighted, total, bias):
+    w1 = weigh(where, 1, b1, weight)
+    weighted[0] = w1
+    bias[...] = early_bias[...] + bias_of(w1)
+    total[...] = early[...] + jnp.dot(w1, held[1].reshape(-1, held.shape[3]), preferred_element_type=F32)
+
+
+def late_half(side, w3, held, early, acc):
+    rows = w3.shape[0]
     half = acc.shape[1]
     lanes = pl.ds(pl.multiple_of(side * half, half), half)
     acc[0:rows, :] = (
         early[:, lanes]
-        + jnp.dot(w1, held[1, :, :, lanes].reshape(-1, half), preferred_element_type=F32)
         + jnp.dot(w3, held[3, :, :, lanes].reshape(-1, half), preferred_element_type=F32)
     )
     acc[rows:, :] = jnp.zeros((acc.shape[0] - rows, half), F32)
@@ -219,19 +225,18 @@
     return jnp.broadcast_to(row, (8, half))
 
 
-def partner_half_kernel(where, held, b1, b3, weight, area, early, weighted, other, acc):
-    w1 = weigh(where, 1, b1, weight)
+def partner_half_kernel(where, held, b3, weight, area, early, weighted, other, acc):
     w3 = weigh(where, 3, b3, weight)
-    weighted[0], weighted[1] = w1, w3
-    late_half(1 - where[1], w1, w3, held, early, acc)
+    weighted[0] = w3
+    late_half(1 - where[1], w3, held, early, acc)
     pieces_of(acc, extra_row(jnp.zeros((1, 128), F32), area[...], acc.shape[1]), other)
 
 
 def own_half_kernel(where, held, weighted, early, early_bias, area, mine, acc):
     rows = early.shape[0]
-    w1, w3 = weighted[0], weighted[1]
-    late_half(where[1], w1, w3, held, early, acc)
-    bias = early_bias[...] + bias_of(w1) + bias_of(w3)
+    w3 = weighted[0]
+    late_half(where[1], w3, held, early, acc)
+    bias = early_bias[...] + bias_of(w3)
     bias = jnp.concatenate([bias[0:1], jnp.zeros((1, 128 - rows), F32)], axis=1)
     pieces_of(acc, extra_row(bias, area[...], acc.shape[1]), mine)
 
@@ -416,16 +421,30 @@
             compiler_params=grant(10),
             name="early_backward",
         )(where, held, returned[0], returned[2], point_weight)
+    one_weighted = jax.ShapeDtypeStruct((1, rows, local * chunk), BF16)
+    with jax.named_scope("next_backward"):
+        weighted_next, early_sum, early_bias = pl.pallas_call(
+            next_backward_kernel,
+            out_shape=[
+                one_weighted,
+                jax.ShapeDtypeStruct((rows, features), F32),
+                jax.ShapeDtypeStruct((8, rows), F32),
+            ],
+            in_specs=[SMEM] + [VMEM] * 5,
+            out_specs=[VMEM] * 3,
+            compiler_params=grant(10),
+            name="next_backward",
+        )(where, held, returned[1], point_weight, early_sum, early_bias)
     with jax.named_scope("backward_partner_half"):
         weighted_late, other = pl.pallas_call(
             partner_half_kernel,
-            out_shape=[two_weighted, pieces],
-            in_specs=[SMEM] + [VMEM] * 6,
+            out_shape=[one_weighted, pieces],
+            in_specs=[SMEM] + [VMEM] * 5,
             out_specs=[VMEM] * 2,
             scratch_shapes=sums,
             compiler_params=grant(10),
             name="backward_partner_half",
-        )(where, held, returned[1], returned[3], point_weight, area, early_sum)
+        )(where, held, returned[3], point_weight, area, early_sum)
         swap = [(0, 1), (1, 0)]
         other = lax.ppermute(other, "c", swap)
     with jax.named_scope("backward_own_half"):
@@ -466,7 +485,7 @@
                 flops=2 * rows * local * points * features, bytes_accessed=2 * hidden.size, transcendentals=0
             ),
             name="grad_hidden",
-        )(where, weighted_early, weighted_late, half_weight, piece)
+        )(where, weighted_early, jnp.concatenate([weighted_next, weighted_late]), half_weight, piece)
         own, grad_hidden = lax.optimization_barrier((own, grad_hidden))
     with jax.named_scope("last_swap"):
         partner = lax.ppermute(own, "c", swap)

time: 79.2 us -> 79.6 us (level)
    pallas_call x1 -> x2, Pallas kernels: 0.88 us -> 1.7 us  [the longest x1 0.89 us: on_device(): pl.pallas_call(next_backward_kernel, out_shape=[one_weighted, jax.ShapeDt...]
  transfers between devices with their start and end apart: 9 -> 9, of which waited for: 6 -> 5; matrix products, arithmetic and copies ran while one was open for 0% -> 0% of each run, Pallas kernels for 17% -> 18%
where the time goes in v12:
time: 79.6 us; the launch traced here: 79.3 us
  blocking collectives  28.6 us (36%)
  starting transfers between devices  22.1 us (28%)
  Pallas kernels  19.4 us (24%)
  waiting for transfers between devices  6.85 us (9%)
  between operations  1.46 us (2%)
    all_to_all x1, blocking collectives, on_device(): part = lax.all_to_all(part, 'z', 0, 0, tiled=True)  16 us
    all_to_all x1, blocking collectives, on_device(): part = lax.all_to_all(part, ('x', 'y'), 0, 0, tiled=True)  12.6 us
    ppermute x6, starting transfers between devices, turn(): lax.ppermute(value, 'y', [(i, (i + k) % GROUPS) for i in range(GROUPS)])  11 us
    ppermute x1, starting transfers between devices, on_device(): partner = lax.ppermute(own, 'c', swap)  4.38 us
    pallas_call x1, Pallas kernels, on_device(): pl.pallas_call(lambda *refs: grad_hidden_kernel(*refs, replicas=replicas)...  3.94 us
    all_to_all x1, starting transfers between devices, on_device(): lax.all_to_all(jnp.broadcast_to(piece, (PIECES, 8, half)), ('x', 'y'), 0,...  3.62 us
    all_to_all x1, waiting for transfers between devices, on_device(): lax.all_to_all(jnp.broadcast_to(piece, (PIECES, 8, half)), ('x', 'y'), 0,...  3.35 us
    pallas_call x1, Pallas kernels, on_device(): pl.pallas_call(local_kernel, out_shape=[one_residual, jax.ShapeDtypeStruc...  3.05 us
  transfers between devices with their start and end apart: 9, of which 5 were waited for; matrix products, arithmetic and copies ran while one was open for 0% of the time, Pallas kernels for 18%

profile of v12, /device:TPU:1, one launch (start us, length us, event | category | flops | bytes accessed | tf_op | source)
XLA Modules:
  0.0 79.3 jit_solution(66948476775375915)
XLA Ops:
  0.6 0.1 pad_add_fusion.where.refs_0_
  0.7 0.0 copy-start.1
  0.7 0.0 copy-start.2
  0.7 0.0 copy-start.3
  0.7 0.0 copy-start.4
  0.7 0.0 copy-start.5
  0.7 2.4 %forward_far.1 = (f32[4,104,128]{2,1,0:T(8,128)S(1)}, bf16[104,1024]{1,0:T(8,128)(2,1)S(1)}) custom-call(s32[2]{0:T(128)S(1)} %pad_add_fusion.where.refs_0_, bf16[4,512,1024]{2,1,0:T(8,128)(2,1)} %hidden.5, f32[99,1024]{1,0:T(8,128)} %refs_6_.1), custom_call_target="tpu_custom_call" | custom-call | tf_op jit(solution)/shard_map/forward_far/forward_far/pallas_call | solution.py:325
  3.1 3.8 %collective-permute-start.2 = (f32[4,104,128]{2,1,0:T(8,128)S(1)}, f32[4,104,128]{2,1,0:T(8,128)S(1)}, u32[]{:S(2)}, u32[]{:S(2)}) collective-permute-start(f32[4,104,128]{2,1,0:T(8,128)S(1)} %get-tuple-element.40), channel_id=1, source_target_pairs={{0,128},{64,192},{128,0},{192,64},{1,129},{65,193},{129,1},{193,65... | collective-permute-start | bytes 638984 | tf_op jit(solution)/shard_map/forward_far/ppermute | solution.py:321
  6.9 2.7 %forward_near.1 = (f32[4,104,128]{2,1,0:T(8,128)S(1)}, f32[4,104,128]{2,1,0:T(8,128)S(1)}) custom-call(s32[2]{0:T(128)S(1)} %pad_add_fusion.where.refs_0_, bf16[4,512,1024]{2,1,0:T(8,128)(2,1)} %hidden.5, bf16[104,1024]{1,0:T(8,128)(2,1)S(1)} %get-tuple-element.36.half.refs_3_), custom_call_target="tpu_custom_call" | custom-call | flops 218103808 | bytes 2097152 | tf_op jit(solution)/shard_map/forward_near/forward_near/pallas_call | solution.py:341
  9.7 0.5 collective-permute-start
  10.2 2.3 %collective-permute-start.1 = (f32[4,104,128]{2,1,0:T(8,128)S(1)}, f32[4,104,128]{2,1,0:T(8,128)S(1)}, u32[]{:S(2)}, u32[]{:S(2)}) collective-permute-start(f32[4,104,128]{2,1,0:T(8,128)S(1)} %get-tuple-element.38), channel_id=1, source_target_pairs={{0,192},{64,0},{128,64},{192,128},{1,193},{65,1},{129,65},{193,129... | collective-permute-start | bytes 638984 | tf_op jit(solution)/shard_map/forward_near/ppermute | solution.py:321
  12.4 0.0 copy-done.1
  12.4 0.0 copy-done.2
  12.4 0.0 copy-done.3
  12.5 0.0 copy-done.4
  12.5 0.0 copy-done.5
  12.5 3.0 %forward_local.1 = (f32[4,104,128]{2,1,0:T(8,128)S(1)}, f32[1,128]{1,0:T(1,128)S(1)}, f32[104,512]{1,0:T(8,128)S(1)}, f32[104,128]{1,0:T(8,128)S(1)}, bf16[4,4,128,1024]{3,2,1,0:T(8,128)(2,1)S(1)}) custom-call(s32[2]{0:T(128)S(1)} %pad_add_fusion.where.refs_0_, bf16[4,512,1024]{2,1,0:T(8,128)(2,1)} %hidden.5, ...), custom_call_target="tpu_custom_call" | custom-call | tf_op jit(solution)/shard_map/forward_local/forward_local/pallas_call | solution.py:358
  15.5 0.0 collective-permute-done.2.refs_1_.refs_0_
  15.5 0.5 early_pairs.1.refs_4_
  16.1 0.8 collective-permute-done.refs_1_
  16.8 0.0 collective-permute-done.1.refs_2_
  16.8 0.5 far_pairs.1
  17.4 2.9 %collective-permute-start.5 = (bf16[4,104,128]{2,1,0:T(8,128)(2,1)S(1)}, bf16[4,104,128]{2,1,0:T(8,128)(2,1)S(1)}, u32[]{:S(2)}, u32[]{:S(2)}) collective-permute-start(bf16[4,104,128]{2,1,0:T(8,128)(2,1)S(1)} %get-tuple-element.54), channel_id=1, source_target_pairs={{0,128},{64,192},{128,0},{192,64},{1,129},{65,193},{129,1},{193,65... | collective-permute-start | bytes 319496 | tf_op jit(solution)/shard_map/far_pairs/ppermute | solution.py:321
  20.3 1.0 %near_pairs.1 = (bf16[4,104,128]{2,1,0:T(8,128)(2,1)S(1)}, bf16[4,104,128]{2,1,0:T(8,128)(2,1)S(1)}, bf16[4,104,128]{2,1,0:T(8,128)(2,1)S(1)}) custom-call(f32[4,104,128]{2,1,0:T(8,128)S(1)} %get-tuple-element.39.refs_0_, f32[4,104,128]{2,1,0:T(8,128)S(1)} %collective-permute-done.refs_1_, f32[4,104,128]{2,1,0:T(8,128)S(1)} %collective-permute-done.1.refs_2_, ...), custom_call_target="tpu_custom_call" | custom-call | flops 7987200 | bytes 851968 | tf_op jit(solution)/shard_map/near_pairs/near_pairs/pallas_call | solution.py:396
  21.3 0.4 collective-permute-start.4
  21.7 1.1 %collective-permute-start.3 = (bf16[4,104,128]{2,1,0:T(8,128)(2,1)S(1)}, bf16[4,104,128]{2,1,0:T(8,128)(2,1)S(1)}, u32[]{:S(2)}, u32[]{:S(2)}) collective-permute-start(bf16[4,104,128]{2,1,0:T(8,128)(2,1)S(1)} %get-tuple-element.49), channel_id=1, source_target_pairs={{0,64},{64,128},{128,192},{192,0},{1,65},{65,129},{129,193},{193,1... | collective-permute-start | bytes 319496 | tf_op jit(solution)/shard_map/near_pairs/ppermute | solution.py:321
  22.8 0.0 collective-permute-done.5.b2
  22.8 1.0 %early_backward.1 = (bf16[2,104,512]{2,1,0:T(8,128)(2,1)S(1)}, f32[104,1024]{1,0:T(8,128)S(1)}, f32[8,104]{1,0:T(8,128)S(1)}) custom-call(s32[2]{0:T(128)S(1)} %pad_add_fusion.where.refs_0_, bf16[4,4,128,1024]{3,2,1,0:T(8,128)(2,1)S(1)} %get-tuple-element.44.held, bf16[4,104,128]{2,1,0:T(8,128)(2,1)S(1)} %get-tuple-element.53.b0, ...), custom_call_target="tpu_custom_call" | custom-call | tf_op jit(solution)/shard_map/early_backward/early_backward/pallas_call | solution.py:412
  23.9 2.0 %collective-permute-done.4.b1 = bf16[4,104,128]{2,1,0:T(8,128)(2,1)S(1)} collective-permute-done((bf16[4,104,128]{2,1,0:T(8,128)(2,1)S(1)}, bf16[4,104,128]{2,1,0:T(8,128)(2,1)S(1)}, u32[]{:S(2)}, u32[]{:S(2)}) %collective-permute-start.4) | collective-permute-done | bytes 106528 | tf_op jit(solution)/shard_map/near_pairs/ppermute | solution.py:321
  25.9 0.9 %next_backward.1 = (bf16[1,104,512]{2,1,0:T(8,128)(2,1)S(1)}, f32[104,1024]{1,0:T(8,128)S(1)}, f32[8,104]{1,0:T(8,128)S(1)}) custom-call(s32[2]{0:T(128)S(1)} %pad_add_fusion.where.refs_0_, bf16[4,4,128,1024]{3,2,1,0:T(8,128)(2,1)S(1)} %get-tuple-element.44.held, bf16[4,104,128]{2,1,0:T(8,128)(2,1)S(1)} %collective-permute-done.4.b1, ...), custom_call_target="tpu_custom_call" | custom-call | tf_op jit(solution)/shard_map/next_backward/next_backward/pallas_call | solution.py:426
  26.8 0.0 collective-permute-done.3.b3
  26.8 0.8 %backward_partner_half.1 = (bf16[1,104,512]{2,1,0:T(8,128)(2,1)S(1)}, f32[16,8,512]{2,1,0:T(8,128)S(1)}) custom-call(s32[2]{0:T(128)S(1)} %pad_add_fusion.where.refs_0_, bf16[4,4,128,1024]{3,2,1,0:T(8,128)(2,1)S(1)} %get-tuple-element.44.held, bf16[4,104,128]{2,1,0:T(8,128)(2,1)S(1)} %collective-permute-done.3.b3, f32[104,512]{1,0:T(8,128)S(1)} %get-tuple-element.50.weight, ...), custom_call_target="tpu_custom_call" | custom-call | tf_op jit(solution)/shard_map/backward_partner_half/backward_partner_half/pallas_call | solution.py:439
  27.6 3.0 %collective-permute-start.6 = (f32[16,8,512]{2,1,0:T(8,128)S(1)}, f32[16,8,512]{2,1,0:T(8,128)S(1)}, u32[]{:S(2)}, u32[]{:S(2)}) collective-permute-start(f32[16,8,512]{2,1,0:T(8,128)S(1)} %get-tuple-element.60), channel_id=1, source_target_pairs={{0,1},{1,0},{2,3},{3,2},{4,5},{5,4},{6,7},{7,6},{8,9},{9,8},{10,11... | collective-permute-start | bytes 786440 | tf_op jit(solution)/shard_map/backward_partner_half/ppermute | solution.py:449
  30.6 0.8 %backward_own_half.1 = f32[16,8,512]{2,1,0:T(8,128)S(1)} custom-call(s32[2]{0:T(128)S(1)} %pad_add_fusion.where.refs_0_, bf16[4,4,128,1024]{3,2,1,0:T(8,128)(2,1)S(1)} %get-tuple-element.44.held, bf16[1,104,512]{2,1,0:T(8,128)(2,1)S(1)} %get-tuple-element.58.weighted, f32[104,1024]{1,0:T(8,128)S(1)} %get-tuple-element.57.early, ...), custom_call_target="tpu_custom_call" | custom-call | tf_op jit(solution)/shard_map/backward_own_half/backward_own_half/pallas_call | solution.py:451
  31.5 0.0 copy-start
  31.5 0.3 collective-permute-done.6
  31.8 12.6 %all_to_all.15 = f32[16,8,512]{2,1,0:T(8,128)S(1)} all-to-all(f32[16,8,512]{2,1,0:T(8,128)S(1)} %add.3), channel_id=1, replica_groups=mesh['y'=4,'z'=8,'x'=4,'c'=2] {'x','y'}, dimensions={0} | all-to-all | bytes 524288 | tf_op jit(solution)/shard_map/gradient_sum/all_to_all | solution.py:462
  44.5 16.0 %all_to_all.16 = f32[8,8,512]{2,1,0:T(8,128)S(1)} all-to-all(f32[8,8,512]{2,1,0:T(8,128)S(1)} %broadcast_in_dim.6), channel_id=1, replica_groups=mesh['y'=4,'z'=8,'x'=4,'c'=2] {'z'}, dimensions={0} | all-to-all | bytes 262144 | tf_op jit(solution)/shard_map/gradient_sum/all_to_all | solution.py:465
  60.5 0.7 broadcast_in_dim.7
  61.2 3.6 %all-to-all-start.2 = ((f32[16,8,512]{2,1,0:T(8,128)}), f32[16,8,512]{2,1,0:T(8,128)S(1)}, u32[]{:S(2)}, u32[]{:S(2)}) async-start(f32[16,8,512]{2,1,0:T(8,128)} %broadcast_in_dim.7), calls=%async_computation.2 | async-start | bytes 524288 | tf_op jit(solution)/shard_map/gradient_sum/all_to_all | solution.py:467
  64.9 3.9 %grad_hidden.1 = bf16[4,512,1024]{2,1,0:T(8,128)(2,1)} custom-call(s32[2]{0:T(128)S(1)} %pad_add_fusion.where.refs_0_, bf16[2,104,512]{2,1,0:T(8,128)(2,1)S(1)} %get-tuple-element.61.refs_1_, bf16[2,104,512]{2,1,0:T(8,128)(2,1)S(1)} %pad_maximum_fusion.refs_2_, bf16[104,1024]{1,0:T(8,128)(2,1)S(1)} %get-tuple-element.36.half.refs_3_, ...), custom_call_target="tpu_custom_call" | custom-call | flops 436207616 | bytes 4194304 | tf_op jit(solution)/shard_map/grad_hidden/grad_hidden/pallas_call | solution.py:469
  68.8 3.4 %all-to-all-done.2.refs_0_.refs_2_ = f32[16,8,512]{2,1,0:T(8,128)S(1)} async-done(((f32[16,8,512]{2,1,0:T(8,128)}), f32[16,8,512]{2,1,0:T(8,128)S(1)}, u32[]{:S(2)}, u32[]{:S(2)}) %all-to-all-start.2) | async-done | bytes 262176 | tf_op jit(solution)/shard_map/gradient_sum/all_to_all | solution.py:467
  72.2 4.4 %collective-permute-start.7 = (f32[16,8,512]{2,1,0:T(8,128)S(1)}, f32[16,8,512]{2,1,0:T(8,128)S(1)}, u32[]{:S(2)}, u32[]{:S(2)}) collective-permute-start(f32[16,8,512]{2,1,0:T(8,128)S(1)} %all-to-all-done.2.refs_0_.refs_2_), channel_id=1, source_target_pairs={{0,1},{1,0},{2,3},{3,2},{4,5},{5,4},{6,7},{7,6},{8,9},{9,8},{10,11... | collective-permute-start | bytes 786440 | tf_op jit(solution)/shard_map/last_swap/ppermute | solution.py:491
  77.2 0.1 own_gradient.1
  77.3 0.4 collective-permute-done.7.refs_4_
  77.7 0.0 copy-done
  77.7 1.6 %update.1 = (f32[99,1024]{1,0:T(8,128)}, f32[1,99]{1,0:T(1,128)}) custom-call(s32[2]{0:T(128)S(1)} %pad_add_fusion.where.refs_0_, s32[1]{0:T(128)S(6)} %copy.11.refs_1_, f32[16,8,512]{2,1,0:T(8,128)S(1)} %all-to-all-done.2.refs_0_.refs_2_, f32[99,512]{1,0:T(8,128)S(1)} %get-tuple-element.65.refs_3_, f32[16,8,512]{2,1,0:T(8,128)S(1)} %collective-permute-done.7.refs_4_, ...), custom_call_target="tpu_custom_call" | custom-call | tf_op jit(solution)/shard_map/update/update/pallas_call | solution.py:501
  (5 shorter events, 0.1 us)
Async XLA Ops:
  0.7 11.7 %copy-start.1 = (f32[99,512]{1,0:T(8,128)S(1)}, f32[99,512]{1,0:T(8,128)}, u32[]{:S(2)}) copy-start(f32[99,512]{1,0:T(8,128)} %truth.1) | copy-start | bytes 608260
  0.7 11.7 %copy-start.2 = (f32[640]{0:T(1024)S(1)}, f32[640]{0:T(1024)}, u32[]{:S(2)}) copy-start(f32[640]{0:T(1024)} %param.13) | copy-start | bytes 7684
  0.7 11.7 %copy-start.3 = (f32[99]{0:T(128)S(1)}, f32[99]{0:T(128)}, u32[]{:S(2)}) copy-start(f32[99]{0:T(128)} %param.10) | copy-start | bytes 1192
  0.7 11.7 %copy-start.4 = (s32[512]{0:T(512)S(1)}, s32[512]{0:T(512)}, u32[]{:S(2)}) copy-start(s32[512]{0:T(512)} %param.14) | copy-start | bytes 6148
  0.7 11.7 %copy-start.5 = (f32[99]{0:T(128)S(1)}, f32[99]{0:T(128)}, u32[]{:S(2)}) copy-start(f32[99]{0:T(128)} %param.12) | copy-start | bytes 1192
  3.1 12.4 %collective-permute-start.2 = (f32[4,104,128]{2,1,0:T(8,128)S(1)}, f32[4,104,128]{2,1,0:T(8,128)S(1)}, u32[]{:S(2)}, u32[]{:S(2)}) collective-permute-start(f32[4,104,128]{2,1,0:T(8,128)S(1)} %get-tuple-element.40), channel_id=1, source_target_pairs={{0,128},{64,192},{128,0},{192,64},{1,129},{65,193},{129,1},{193,65... | collective-permute-start | bytes 638984 | tf_op jit(solution)/shard_map/forward_far/ppermute | solution.py:321
  9.7 7.1 %collective-permute-start = (f32[4,104,128]{2,1,0:T(8,128)S(1)}, f32[4,104,128]{2,1,0:T(8,128)S(1)}, u32[]{:S(2)}, u32[]{:S(2)}) collective-permute-start(f32[4,104,128]{2,1,0:T(8,128)S(1)} %get-tuple-element.37), channel_id=1, source_target_pairs={{0,64},{64,128},{128,192},{192,0},{1,65},{65,129},{129,193},{193,1... | collective-permute-start | bytes 638984 | tf_op jit(solution)/shard_map/forward_near/ppermute | solution.py:321
  10.2 6.7 %collective-permute-start.1 = (f32[4,104,128]{2,1,0:T(8,128)S(1)}, f32[4,104,128]{2,1,0:T(8,128)S(1)}, u32[]{:S(2)}, u32[]{:S(2)}) collective-permute-start(f32[4,104,128]{2,1,0:T(8,128)S(1)} %get-tuple-element.38), channel_id=1, source_target_pairs={{0,192},{64,0},{128,64},{192,128},{1,193},{65,1},{129,65},{193,129... | collective-permute-start | bytes 638984 | tf_op jit(solution)/shard_map/forward_near/ppermute | solution.py:321
  17.4 5.5 %collective-permute-start.5 = (bf16[4,104,128]{2,1,0:T(8,128)(2,1)S(1)}, bf16[4,104,128]{2,1,0:T(8,128)(2,1)S(1)}, u32[]{:S(2)}, u32[]{:S(2)}) collective-permute-start(bf16[4,104,128]{2,1,0:T(8,128)(2,1)S(1)} %get-tuple-element.54), channel_id=1, source_target_pairs={{0,128},{64,192},{128,0},{192,64},{1,129},{65,193},{129,1},{193,65... | collective-permute-start | bytes 319496 | tf_op jit(solution)/shard_map/far_pairs/ppermute | solution.py:321
  21.3 4.6 %collective-permute-start.4 = (bf16[4,104,128]{2,1,0:T(8,128)(2,1)S(1)}, bf16[4,104,128]{2,1,0:T(8,128)(2,1)S(1)}, u32[]{:S(2)}, u32[]{:S(2)}) collective-permute-start(bf16[4,104,128]{2,1,0:T(8,128)(2,1)S(1)} %get-tuple-element.52), channel_id=1, source_target_pairs={{0,192},{64,0},{128,64},{192,128},{1,193},{65,1},{129,65},{193,129... | collective-permute-start | bytes 319496 | tf_op jit(solution)/shard_map/near_pairs/ppermute | solution.py:321
  21.7 5.1 %collective-permute-start.3 = (bf16[4,104,128]{2,1,0:T(8,128)(2,1)S(1)}, bf16[4,104,128]{2,1,0:T(8,128)(2,1)S(1)}, u32[]{:S(2)}, u32[]{:S(2)}) collective-permute-start(bf16[4,104,128]{2,1,0:T(8,128)(2,1)S(1)} %get-tuple-element.49), channel_id=1, source_target_pairs={{0,64},{64,128},{128,192},{192,0},{1,65},{65,129},{129,193},{193,1... | collective-permute-start | bytes 319496 | tf_op jit(solution)/shard_map/near_pairs/ppermute | solution.py:321
  27.6 4.2 %collective-permute-start.6 = (f32[16,8,512]{2,1,0:T(8,128)S(1)}, f32[16,8,512]{2,1,0:T(8,128)S(1)}, u32[]{:S(2)}, u32[]{:S(2)}) collective-permute-start(f32[16,8,512]{2,1,0:T(8,128)S(1)} %get-tuple-element.60), channel_id=1, source_target_pairs={{0,1},{1,0},{2,3},{3,2},{4,5},{5,4},{6,7},{7,6},{8,9},{9,8},{10,11... | collective-permute-start | bytes 786440 | tf_op jit(solution)/shard_map/backward_partner_half/ppermute | solution.py:449
  31.5 46.3 %copy-start = (f32[99,1024]{1,0:T(8,128)S(1)}, f32[99,1024]{1,0:T(8,128)}, u32[]{:S(2)}) copy-start(f32[99,1024]{1,0:T(8,128)} %refs_6_.1) | copy-start | bytes 1216516
  61.2 10.9 %all-to-all-start.2 = ((f32[16,8,512]{2,1,0:T(8,128)}), f32[16,8,512]{2,1,0:T(8,128)S(1)}, u32[]{:S(2)}, u32[]{:S(2)}) async-start(f32[16,8,512]{2,1,0:T(8,128)} %broadcast_in_dim.7), calls=%async_computation.2 | async-start | bytes 524288 | tf_op jit(solution)/shard_map/gradient_sum/all_to_all | solution.py:467
  72.2 5.5 %collective-permute-start.7 = (f32[16,8,512]{2,1,0:T(8,128)S(1)}, f32[16,8,512]{2,1,0:T(8,128)S(1)}, u32[]{:S(2)}, u32[]{:S(2)}) collective-permute-start(f32[16,8,512]{2,1,0:T(8,128)S(1)} %all-to-all-done.2.refs_0_.refs_2_), channel_id=1, source_target_pairs={{0,1},{1,0},{2,3},{3,2},{4,5},{5,4},{6,7},{7,6},{8,9},{9,8},{10,11... | collective-permute-start | bytes 786440 | tf_op jit(solution)/shard_map/last_swap/ppermute | solution.py:491
